TPU v7x, 32 devices: a whole 2x2x4 slice. The times are simulated.
32 devices in a mesh: video: 4 (over y, x), context: 8 (over z, core).
Axes of the slice: x: 2, y: 2, z: 4, core: 2. Of those that a mesh axis runs over, the one named last changes fastest.
Arguments:
- queries: bfloat16 [4096, 4096], P(('video', 'context')), parts along dimension 0, may hold values from -135 to 135
- keys: bfloat16 [4096, 4096], P(('video', 'context')), parts along dimension 0, may hold values from -5 to 5
- values: bfloat16 [4096, 4096], P(('video', 'context')), parts along dimension 0, may hold values from -6 to 6
- value_layer_input: bfloat16 [4096, 4096], P(('video', 'context')), parts along dimension 0, may hold values from -6 to 6
- adapter_down_weight: bfloat16 [4096, 64], replicated, may hold values from -0.09375 to 0.09375
- adapter_up_weight: bfloat16 [4096, 64], replicated, may hold values from -0.75 to 0.75
- neighbors: int32 [64, 4], P(('video', 'context')), parts along dimension 0, may hold values from 0 to 15, as said below
Outputs:
- student_out: bfloat16 [4096, 4096], P(('video', 'context')), parts along dimension 0
- grad_down: float32 [16384, 64], P(('video', 'context')), parts along dimension 0
- grad_up: float32 [16384, 64], P(('video', 'context')), parts along dimension 0
There are 4 independent parts, one for each index of `video`. A program takes and returns all parts, laid end to end along the dimension named above; an argument that names none is the same for every part. Nothing has to cross between parts.
Inputs may be any that keep to these rules, and one draw needn't show every extreme that they name: `neighbors`: row i begins with i itself; its 4 entries are distinct tiles of the slab of tile i, the slab before or the slab after, where slab = tile // 2.
All inputs are finite; a program needn't handle non-finite values.
Results may differ from a plain program's by a relative error of at most 0.008.
Values may be sent and summed in bfloat16 or wider, within the bound.
No kernel may reach another device: no remote copies, remote signals or barrier semaphores. Data moves between devices by JAX's collectives and lax.ppermute only.
A program may use at most 64 MiB of HBM per device.

v0:
```python
import jax
import jax.numpy as jnp
from jax import lax
from jax.sharding import PartitionSpec as P

H = 32


def padded(block, sides, width):
    for axis, dim in sides:
        count = lax.axis_size(axis)
        forward = [(i, i + 1) for i in range(count - 1)]
        backward = [(target, source) for source, target in forward]
        low = lax.ppermute(
            lax.slice_in_dim(block, block.shape[dim] - width, None, axis=dim), axis, forward
        )
        high = lax.ppermute(lax.slice_in_dim(block, 0, width, axis=dim), axis, backward)
        block = jnp.concatenate([low, block, high], axis=dim)
    return block


def teacher_heads(pieces):
    queries, keys, values = pieces
    total = queries.shape[0]
    heads = queries.shape[2]
    width = queries.shape[3]
    queries = queries.reshape(total, heads, width)
    keys = keys.reshape(total, heads, width)
    values = values.reshape(total, heads, width)
    block = min(512, total)
    scale = width ** (-0.5)

    def one_block(query_block):
        scores = (
            jnp.einsum("qhd,khd->hqk", query_block, keys, preferred_element_type=jnp.float32)
            * scale
        )
        top = jnp.max(scores, axis=2, keepdims=True)
        expo = jnp.exp(scores - top)
        weights = (expo / jnp.sum(expo, axis=2, keepdims=True)).astype(jnp.bfloat16)
        return jnp.einsum(
            "hqk,khd->qhd", weights, values, preferred_element_type=jnp.float32
        ).astype(jnp.bfloat16)

    outputs = lax.map(one_block, queries.reshape(total // block, block, heads, width))
    return outputs.reshape(total, 1, heads, width)


def contract_rows(left, right):
    return lax.dot_general(
        left,
        right,
        (((0,), (0,)), ((), ())),
        precision=lax.Precision.HIGHEST,
        preferred_element_type=jnp.float32,
    )


def local(
    queries, keys, values, value_layer_input, adapter_down_weight, adapter_up_weight, neighbors
):
    tok = queries.shape[0]
    width = queries.shape[1]
    adapter_rank = adapter_down_weight.shape[1]
    groups = lax.axis_size("context")
    head_size = width // H
    per_group = H // groups

    def split_heads(array):
        return array.reshape(tok, groups, per_group, head_size)

    teacher = teacher_heads(
        (
            lax.all_to_all(
                split_heads(queries), "context", split_axis=1, concat_axis=0, tiled=True
            ),
            lax.all_to_all(split_heads(keys), "context", split_axis=1, concat_axis=0, tiled=True),
            lax.all_to_all(split_heads(values), "context", split_axis=1, concat_axis=0, tiled=True),
        )
    )
    teacher = lax.all_to_all(teacher, "context", split_axis=0, concat_axis=1, tiled=True).reshape(
        tok, width
    )
    adapter_down_rows = jnp.dot(
        value_layer_input, adapter_down_weight, preferred_element_type=jnp.float32
    ).astype(jnp.bfloat16)
    adapter_value_term = lax.dot_general(
        adapter_down_rows,
        adapter_up_weight,
        (((1,), (1,)), ((), ())),
        preferred_element_type=jnp.float32,
    )
    learner_values = (values.astype(jnp.float32) + adapter_value_term).astype(jnp.bfloat16)
    up_float = adapter_up_weight.astype(jnp.float32)
    window = padded(jnp.stack([keys, learner_values, value_layer_input]), (("context", 1),), tok)
    window_input = window[2]
    window_keys = window[0].reshape(3 * tok, H, head_size)
    window_values = window[1].reshape(3 * tok, H, head_size)
    tile_count = neighbors.shape[0]
    tile = tok // tile_count
    slab = lax.axis_index("context")
    offsets = neighbors - (slab - 1) * tile_count
    slots = jnp.arange(3 * tile_count, dtype=jnp.int32)
    tile_mask = jnp.any(offsets[:, :, None] == slots[None, None, :], axis=1)
    token_mask = jnp.broadcast_to(
        tile_mask[:, None, :, None], (tile_count, tile, 3 * tile_count, tile)
    ).reshape(tok, 3 * tok)
    scale = head_size ** (-0.5)
    scores = (
        jnp.einsum(
            "qhd,khd->hqk",
            queries.reshape(tok, H, head_size),
            window_keys,
            preferred_element_type=jnp.float32,
        )
        * scale
    )
    scores = jnp.where(token_mask[None], scores, -1e30)
    top = jnp.max(scores, axis=2, keepdims=True)
    expo = jnp.exp(scores - top)
    weights = (expo / jnp.sum(expo, axis=2, keepdims=True)).astype(jnp.bfloat16)
    student = jnp.einsum(
        "hqk,khd->qhd", weights, window_values, preferred_element_type=jnp.float32
    ).reshape(tok, width)
    student_out = student.astype(jnp.bfloat16)
    factor = (tok * groups) ** (-0.5)
    output_grad = ((student - teacher.astype(jnp.float32)) * factor).astype(jnp.bfloat16)
    window_grad = jnp.einsum(
        "hqk,qhd->khd",
        weights,
        output_grad.reshape(tok, H, head_size),
        preferred_element_type=jnp.float32,
    )
    window_grad = window_grad.reshape(3 * tok, width)
    window_down = jnp.dot(
        window_input, adapter_down_weight, preferred_element_type=jnp.float32
    ).astype(jnp.bfloat16)
    grad_pieces = [window_grad]
    input_pieces = [window_input.astype(jnp.float32)]
    down_segments = [window_down.astype(jnp.float32)]
    hidden_pieces = [
        jnp.dot(
            segment, up_float, precision=lax.Precision.HIGHEST, preferred_element_type=jnp.float32
        )
        for segment in grad_pieces
    ]
    summed = jnp.zeros((width // groups * lax.axis_size("context"), 2 * adapter_rank), jnp.float32)
    for inputs, hidden, grads, downs in zip(
        input_pieces, hidden_pieces, grad_pieces, down_segments
    ):
        summed = jnp.concatenate(
            [contract_rows(inputs, hidden), contract_rows(grads, downs)], axis=1
        )
    adapter = lax.psum_scatter(summed, "context", scatter_dimension=0, tiled=True)
    return (student_out, adapter[:, :adapter_rank], adapter[:, adapter_rank:])


def solution(mesh):
    placed = (
        P(("video", "context"), None),
        P(("video", "context"), None),
        P(("video", "context"), None),
        P(("video", "context"), None),
        P(),
        P(),
        P(("video", "context"), None),
    )
    return jax.shard_map(
        local,
        mesh=mesh,
        in_specs=placed,
        out_specs=(
            P(("video", "context"), None),
            P(("video", "context"), None),
            P(("video", "context"), None),
        ),
        check_vma=False,
    )
```

profile of v0, /device:TPU:0, one launch (start us, length us, event | category | flops | bytes accessed | tf_op | source)
XLA Modules:
  0.0 242.7 jit_solution(1423795878681877643)
XLA Ops:
  7.2 2.3 copy.83
  9.5 6.3 %all-to-all-start = ((bf16[128,8,4,128]{0,3,2,1:T(8,128)(2,1)}), bf16[128,8,4,128]{0,3,2,1:T(8,128)(2,1)}, u32[]{:S(2)}, u32[]{:S(2)}) async-start(bf16[128,8,4,128]{0,3,2,1:T(8,128)(2,1)} %bitcast.11), calls=%async_computation | async-start | bytes 2097152 | tf_op jit(solution)/shard_map/all_to_all | solution.py:74
  15.8 1.7 copy.85
  17.6 1.3 copy.86
  18.9 23.6 %all-to-all-done = bf16[128,8,4,128]{0,3,2,1:T(8,128)(2,1)} async-done(((bf16[128,8,4,128]{0,3,2,1:T(8,128)(2,1)}), bf16[128,8,4,128]{0,3,2,1:T(8,128)(2,1)}, u32[]{:S(2)}, u32[]{:S(2)}) %all-to-all-start) | async-done | bytes 1048608 | tf_op jit(solution)/shard_map/all_to_all | solution.py:74
  42.5 4.2 %all-to-all-start.1 = ((bf16[128,8,4,128]{3,0,2,1:T(8,128)(2,1)}), bf16[128,8,4,128]{3,0,2,1:T(8,128)(2,1)}, u32[]{:S(2)}, u32[]{:S(2)}) async-start(bf16[128,8,4,128]{3,0,2,1:T(8,128)(2,1)} %copy.86), calls=%async_computation.1 | async-start | bytes 2097152 | tf_op jit(solution)/shard_map/all_to_all | solution.py:77
  46.8 2.3 copy.88
  49.0 2.3 copy.89
  51.3 22.1 %all-to-all-done.1 = bf16[128,8,4,128]{3,0,2,1:T(8,128)(2,1)} async-done(((bf16[128,8,4,128]{3,0,2,1:T(8,128)(2,1)}), bf16[128,8,4,128]{3,0,2,1:T(8,128)(2,1)}, u32[]{:S(2)}, u32[]{:S(2)}) %all-to-all-start.1) | async-done | bytes 1048608 | tf_op jit(solution)/shard_map/all_to_all | solution.py:77
  73.4 4.2 %all-to-all-start.2 = ((bf16[128,8,4,128]{3,0,2,1:T(8,128)(2,1)}), bf16[128,8,4,128]{3,0,2,1:T(8,128)(2,1)}, u32[]{:S(2)}, u32[]{:S(2)}) async-start(bf16[128,8,4,128]{3,0,2,1:T(8,128)(2,1)} %copy.89), calls=%async_computation.2 | async-start | bytes 2097152 | tf_op jit(solution)/shard_map/all_to_all | solution.py:78
  77.7 3.6 %fusion.30 = bf16[1,128,4096]{2,1,0:T(8,128)(2,1)} fusion(bf16[4096,64]{0,1:T(8,128)(2,1)S(1)} %copy-done.6, bf16[128,4096]{1,0:T(8,128)(2,1)} %param.11, bf16[128,4096]{1,0:T(8,128)(2,1)S(1)} %copy-done.3, bf16[4096,64]{0,1:T(8,128)(2,1)S(1)} %copy-done), kind=kOutput, calls=%fused_computation.27 | convolution fusion | flops 135798784 | bytes 4194304 | tf_op jit(solution)/shard_map/dot_general | solution.py:87
  81.2 3.3 %pad_maximum_fusion.1 = bf16[3,128,4096]{2,1,0:T(8,128)(2,1)} fusion(bf16[1,128,4096]{2,1,0:T(8,128)(2,1)S(1)} %bitcast.118, bf16[1,128,4096]{2,1,0:T(8,128)(2,1)} %fusion.30, bf16[1,128,4096]{2,1,0:T(8,128)(2,1)S(1)} %bitcast.116), kind=kLoop, calls=%fused_computation.30 | loop fusion | flops 3145728 | bytes 6291456 | tf_op jit(solution)/shard_map/stack | solution.py:95
  84.5 1.3 collective-permute-start.1
  85.8 4.7 %collective-permute-start = (bf16[3,128,4096]{2,1,0:T(8,128)(2,1)}, bf16[3,128,4096]{2,1,0:T(8,128)(2,1)}, u32[]{:S(2)}, u32[]{:S(2)}) collective-permute-start(bf16[3,128,4096]{2,1,0:T(8,128)(2,1)} %pad_maximum_fusion.1), channel_id=1, source_target_pairs={{0,1},{1,2},{2,3},{3,4},{4,5},{5,6},{6,7},{8,9},{9,10},{10,11},{11... | collective-permute-start | bytes 9437192 | tf_op jit(solution)/shard_map/ppermute | solution.py:14
  91.1 2.3 copy.84
  93.4 2.3 copy.87
  95.7 8.7 %all-to-all-done.2 = bf16[128,8,4,128]{3,0,2,1:T(8,128)(2,1)} async-done(((bf16[128,8,4,128]{3,0,2,1:T(8,128)(2,1)}), bf16[128,8,4,128]{3,0,2,1:T(8,128)(2,1)}, u32[]{:S(2)}, u32[]{:S(2)}) %all-to-all-start.2) | async-done | bytes 1048608 | tf_op jit(solution)/shard_map/all_to_all | solution.py:78
  104.3 2.3 copy.90
  106.7 25.8 %while.10 = (s32[]{:T(128)}, bf16[2,512,4,128]{3,1,0,2:T(8,128)(2,1)}, bf16[2,512,4,128]{3,1,0,2:T(8,128)(2,1)}, bf16[1024,4,128]{2,0,1:T(8,128)(2,1)}, bf16[1024,4,128]{2,0,1:T(8,128)(2,1)}, /*index=5*/s32[]{:T(128)}) while((s32[]{:T(128)}, bf16[2,512,4,128]{3,1,0,2:T(8,128)(2,1)}, bf16[2,512,4,128]{3,1,0,2:T(8,128)(2,1)}, ...), condition=%wide.region_6.7_spmd, body=%wide.region_3.0_spmd.sunk | while | flops 1084490752 | bytes 19939412 | solution.py:45
  106.7 7.2 %fusion.80 = (f32[4,512]{1,0:T(4,128)S(1)}, f32[4,512,1024]{2,1,0:T(8,128)}) fusion(bf16[1024,4,128]{2,0,1:T(8,128)(2,1)} %get-tuple-element.144, bf16[2,512,4,128]{3,1,0,2:T(8,128)(2,1)} %get-tuple-element.143, s32[]{:T(128)S(6)} %copy.115), kind=kOutput, calls=%fused_computation.55.clone.1 | convolution fusion | flops 543163392 | bytes 9969668 | tf_op jit(solution)/shard_map/while/body/eval_jaxpr/sub | solution.py:39
  113.8 5.7 %fusion.81 = bf16[2,512,4,128]{3,1,0,2:T(8,128)(2,1)} fusion(bf16[2,512,4,128]{3,1,0,2:T(8,128)(2,1)} %get-tuple-element.136, s32[]{:T(128)S(6)} %copy.115, bf16[1024,4,128]{2,0,1:T(8,128)(2,1)} %get-tuple-element.145, f32[4,512,1024]{2,1,0:T(8,128)} %get-tuple-element.127, f32[4,512]{1,0:T(4,128)S(1)} %get-tuple-element.128), kind=kOutput, calls=%fused_computation.9.clone.1 | convolution fusion | flops 541327360 | bytes 9969668 | tf_op jit(solution)/shard_map/while/body/eval_jaxpr/hqk,khd->qhd/dot_general | solution.py:41
  119.5 7.2 %fusion.80 = (f32[4,512]{1,0:T(4,128)S(1)}, f32[4,512,1024]{2,1,0:T(8,128)}) fusion(bf16[1024,4,128]{2,0,1:T(8,128)(2,1)} %get-tuple-element.144, bf16[2,512,4,128]{3,1,0,2:T(8,128)(2,1)} %get-tuple-element.143, s32[]{:T(128)S(6)} %copy.115), kind=kOutput, calls=%fused_computation.55.clone.1 | convolution fusion | flops 543163392 | bytes 9969668 | tf_op jit(solution)/shard_map/while/body/eval_jaxpr/sub | solution.py:39
  126.7 5.7 %fusion.81 = bf16[2,512,4,128]{3,1,0,2:T(8,128)(2,1)} fusion(bf16[2,512,4,128]{3,1,0,2:T(8,128)(2,1)} %get-tuple-element.136, s32[]{:T(128)S(6)} %copy.115, bf16[1024,4,128]{2,0,1:T(8,128)(2,1)} %get-tuple-element.145, f32[4,512,1024]{2,1,0:T(8,128)} %get-tuple-element.127, f32[4,512]{1,0:T(4,128)S(1)} %get-tuple-element.128), kind=kOutput, calls=%fused_computation.9.clone.1 | convolution fusion | flops 541327360 | bytes 9969668 | tf_op jit(solution)/shard_map/while/body/eval_jaxpr/hqk,khd->qhd/dot_general | solution.py:41
  132.4 3.0 %copy.93 = bf16[1024,1,4,128]{3,2,1,0:T(4,128)(2,1)} copy(bf16[1024,1,4,128]{3,0,2,1:T(8,128)(2,1)} %bitcast.127) | data formatting | bytes 2097152 | tf_op jit(solution)/shard_map/reshape | solution.py:46
  135.5 4.3 %all-to-all-start.3 = ((bf16[1024,1,4,128]{3,2,1,0:T(4,128)(2,1)}), bf16[1024,1,4,128]{3,2,1,0:T(4,128)(2,1)}, u32[]{:S(2)}, u32[]{:S(2)}) async-start(bf16[1024,1,4,128]{3,2,1,0:T(4,128)(2,1)} %copy.93), calls=%async_computation.3 | async-start | bytes 2097152 | tf_op jit(solution)/shard_map/all_to_all | solution.py:81
  140.0 4.2 %pad_maximum_fusion = bf16[3,384,4096]{2,1,0:T(8,128)(2,1)S(1)} fusion(bf16[3,128,4096]{2,1,0:T(8,128)(2,1)} %collective-permute-done.1, bf16[1,128,4096]{2,1,0:T(8,128)(2,1)S(1)} %bitcast.119, bf16[1,128,4096]{2,1,0:T(8,128)(2,1)} %fusion.30, bf16[1,128,4096]{2,1,0:T(8,128)(2,1)S(1)} %bitcast.117, bf16[3,128,4096]{2,1,0:T(8,128)(2,1)} %collective-permute-done), kind=kLoop, calls=%fused_computation.20 | loop fusion | flops 47185920 | bytes 18874368 | tf_op jit(solution)/shard_map/concatenate | solution.py:18
  144.2 2.8 %slice_bitcast_fusion.1 = (bf16[48,8,32,128]{3,1,2,0:T(8,128)(2,1)S(1)}, bf16[1,384,4096]{2,1,0:T(8,128)(2,1)}) fusion(bf16[3,384,4096]{2,1,0:T(8,128)(2,1)S(1)} %pad_maximum_fusion), kind=kLoop, calls=%fused_computation.29 | loop fusion | bytes 12582912
  147.0 1.9 copy-done.1
  148.9 0.8 copy.105
  149.7 0.4 copy-done.4
  150.1 4.4 %fusion.31 = f32[32,384,128]{2,1,0:T(8,128)} fusion(bf16[384,32,128]{2,1,0:T(8,128)(2,1)S(1)} %bitcast.115, bf16[128,4096]{1,0:T(8,128)(2,1)S(1)} %copy-done.4), kind=kOutput, calls=%fused_computation.31 | convolution fusion | flops 402653184 | bytes 10485760 | tf_op jit(solution)/shard_map/qhd,khd->hqk/dot_general | solution.py:110
  154.5 4.7 %copy.100 = bf16[1,384,4096]{1,2,0:T(8,128)(2,1)} copy(bf16[1,384,4096]{2,1,0:T(8,128)(2,1)} %get-tuple-element.87) | data formatting | bytes 6291456 | tf_op jit(solution)/shard_map/reshape;squeeze | solution.py:98
  159.2 3.0 %fusion.40 = bf16[384,64]{0,1:T(8,128)(2,1)S(1)} fusion(bf16[4096,64]{0,1:T(8,128)(2,1)S(1)} %copy-done, bf16[3,384,4096]{2,1,0:T(8,128)(2,1)} %copy-done.1), kind=kOutput, calls=%fused_computation.44 | convolution fusion | flops 201351168 | bytes 3719168 | tf_op jit(solution)/shard_map/dot_general | solution.py:135
  162.2 7.2 %fusion.54 = (f32[32,128]{1,0:T(8,128)S(1)}, f32[32,128,384]{1,2,0:T(8,128)S(1)}) fusion(f32[32,384,128]{2,1,0:T(8,128)} %fusion.31, pred[128,384]{0,1:T(8,128)(4,1)S(1)} %copy.78), kind=kOutput, calls=%fused_computation.57 | output fusion | flops 9437567 | bytes 12648448 | tf_op jit(solution)/shard_map/sub | solution.py:120
  169.4 2.7 %copy-done.8 = f32[32,128,384]{1,2,0:T(8,128)} copy-done((f32[32,128,384]{1,2,0:T(8,128)}, f32[32,128,384]{1,2,0:T(8,128)S(1)}, u32[]{:S(2)}) %copy-start.8) | copy-done | bytes 6291480
  172.1 2.6 %bitcast_convert_fusion = (bf16[128,32,128]{0,2,1:T(8,128)(2,1)}, f32[32,128,128]{2,1,0:T(8,128)}) fusion(bf16[384,32,128]{0,2,1:T(8,128)(2,1)S(1)} %bitcast.123, f32[32,128,384]{1,2,0:T(8,128)S(1)} %get-tuple-element.91, f32[32,128]{1,0:T(8,128)S(1)} %get-tuple-element.90), kind=kOutput, calls=%fused_computation.43 | convolution fusion | flops 406323200 | bytes 12599296 | tf_op jit(solution)/shard_map/hqk,khd->qhd/dot_general | solution.py:122
  174.7 1.4 copy.94
  176.0 1.6 convert_bitcast_fusion
  177.6 2.1 copy.95
  179.8 2.0 fusion.39
  181.8 4.2 %fusion.46 = f32[32,128,384]{2,1,0:T(8,128)S(1)} fusion(bf16[128,32,128]{0,2,1:T(8,128)(2,1)S(1)} %fusion.39, f32[32,128,384]{1,2,0:T(8,128)} %copy-done.8, f32[32,128]{1,0:T(8,128)S(1)} %get-tuple-element.90), kind=kOutput, calls=%fused_computation.53 | convolution fusion | flops 405798912 | bytes 13647872 | tf_op jit(solution)/shard_map/hqk,qhd->khd/dot_general | solution.py:128
  186.0 2.4 %fusion.55 = f32[384,64]{0,1:T(8,128)S(1)} fusion(f32[384,4096]{0,1:T(8,128)S(1)} %bitcast.113, bf16[4096,64]{0,1:T(8,128)(2,1)S(1)} %copy-done.6), kind=kOutput, calls=%fused_computation.58 | convolution fusion | flops 1207959552 | bytes 6914048 | tf_op jit(solution)/shard_map/dot_general | solution.py:142
  188.5 3.5 %fusion.37 = f32[4096,64]{0,1:T(8,128)S(1)} fusion(f32[384,64]{0,1:T(8,128)S(1)} %fusion.55, bf16[3,384,4096]{2,1,0:T(8,128)(2,1)} %copy-done.1), kind=kOutput, calls=%fused_computation.37 | convolution fusion | flops 1207959552 | bytes 4292608 | tf_op jit(solution)/shard_map/dot_general | solution.py:50
  192.0 3.5 %fusion.56 = f32[4096,64]{0,1:T(8,128)S(1)} fusion(f32[384,4096]{0,1:T(8,128)S(1)} %bitcast.114, bf16[384,64]{0,1:T(8,128)(2,1)S(1)} %fusion.40), kind=kOutput, calls=%fused_computation.59 | convolution fusion | flops 1207959552 | bytes 7389184 | tf_op jit(solution)/shard_map/dot_general | solution.py:50
  195.5 1.5 pad_maximum_fusion.2
  197.1 2.3 copy.97
  199.3 34.8 %reduce-scatter.2.cloned.1.call-done = f32[512,128]{0,1:T(8,128)} async-done(((f32[4096,128]{0,1:T(8,128)}), f32[512,128]{0,1:T(8,128)}) %reduce-scatter.2.cloned.1.call-update) | async-done | bytes 262160 | tf_op jit(solution)/shard_map/reduce_scatter | solution.py:154
  234.2 1.7 fusion.53
  (26 shorter events, 0.9 us)
Async XLA Ops:
  7.2 70.5 %copy-start = (bf16[4096,64]{0,1:T(8,128)(2,1)S(1)}, bf16[4096,64]{0,1:T(8,128)(2,1)}, u32[]{:S(2)}) copy-start(bf16[4096,64]{0,1:T(8,128)(2,1)} %param.13) | copy-start | bytes 1572868
  9.5 33.0 %all-to-all-start = ((bf16[128,8,4,128]{0,3,2,1:T(8,128)(2,1)}), bf16[128,8,4,128]{0,3,2,1:T(8,128)(2,1)}, u32[]{:S(2)}, u32[]{:S(2)}) async-start(bf16[128,8,4,128]{0,3,2,1:T(8,128)(2,1)} %bitcast.11), calls=%async_computation | async-start | bytes 2097152 | tf_op jit(solution)/shard_map/all_to_all | solution.py:74
  15.8 61.8 %copy-start.3 = (bf16[128,4096]{1,0:T(8,128)(2,1)S(1)}, bf16[128,4096]{1,0:T(8,128)(2,1)}, u32[]{:S(2)}) copy-start(bf16[128,4096]{1,0:T(8,128)(2,1)} %param.12) | copy-start | bytes 3145732
  15.8 61.8 %copy-start.6 = (bf16[4096,64]{0,1:T(8,128)(2,1)S(1)}, bf16[4096,64]{0,1:T(8,128)(2,1)}, u32[]{:S(2)}) copy-start(bf16[4096,64]{0,1:T(8,128)(2,1)} %param.14) | copy-start | bytes 1572868
  18.9 62.3 %copy-start.2 = (bf16[128,4096]{1,0:T(8,128)(2,1)S(1)}, bf16[128,4096]{1,0:T(8,128)(2,1)}, u32[]{:S(2)}) copy-start(bf16[128,4096]{1,0:T(8,128)(2,1)} %param.10) | copy-start | bytes 3145732
  42.5 30.8 %all-to-all-start.1 = ((bf16[128,8,4,128]{3,0,2,1:T(8,128)(2,1)}), bf16[128,8,4,128]{3,0,2,1:T(8,128)(2,1)}, u32[]{:S(2)}, u32[]{:S(2)}) async-start(bf16[128,8,4,128]{3,0,2,1:T(8,128)(2,1)} %copy.86), calls=%async_computation.1 | async-start | bytes 2097152 | tf_op jit(solution)/shard_map/all_to_all | solution.py:77
  51.3 39.2 %copy-start.7 = (s32[2,4]{1,0:T(2,128)S(1)}, s32[2,4]{1,0:T(2,128)}, u32[]{:S(2)}) copy-start(s32[2,4]{1,0:T(2,128)} %param.15) | copy-start | bytes 100
  73.4 31.0 %all-to-all-start.2 = ((bf16[128,8,4,128]{3,0,2,1:T(8,128)(2,1)}), bf16[128,8,4,128]{3,0,2,1:T(8,128)(2,1)}, u32[]{:S(2)}, u32[]{:S(2)}) async-start(bf16[128,8,4,128]{3,0,2,1:T(8,128)(2,1)} %copy.89), calls=%async_computation.2 | async-start | bytes 2097152 | tf_op jit(solution)/shard_map/all_to_all | solution.py:78
  84.5 55.4 %collective-permute-start.1 = (bf16[3,128,4096]{2,1,0:T(8,128)(2,1)}, bf16[3,128,4096]{2,1,0:T(8,128)(2,1)}, u32[]{:S(2)}, u32[]{:S(2)}) collective-permute-start(bf16[3,128,4096]{2,1,0:T(8,128)(2,1)} %pad_maximum_fusion.1), channel_id=1, source_target_pairs={{1,0},{2,1},{3,2},{4,3},{5,4},{6,5},{7,6},{9,8},{10,9},{11,10},{12... | collective-permute-start | bytes 9437192 | tf_op jit(solution)/shard_map/ppermute | solution.py:17
  85.8 54.2 %collective-permute-start = (bf16[3,128,4096]{2,1,0:T(8,128)(2,1)}, bf16[3,128,4096]{2,1,0:T(8,128)(2,1)}, u32[]{:S(2)}, u32[]{:S(2)}) collective-permute-start(bf16[3,128,4096]{2,1,0:T(8,128)(2,1)} %pad_maximum_fusion.1), channel_id=1, source_target_pairs={{0,1},{1,2},{2,3},{3,4},{4,5},{5,6},{6,7},{8,9},{9,10},{10,11},{11... | collective-permute-start | bytes 9437192 | tf_op jit(solution)/shard_map/ppermute | solution.py:14
  135.5 39.2 %all-to-all-start.3 = ((bf16[1024,1,4,128]{3,2,1,0:T(4,128)(2,1)}), bf16[1024,1,4,128]{3,2,1,0:T(4,128)(2,1)}, u32[]{:S(2)}, u32[]{:S(2)}) async-start(bf16[1024,1,4,128]{3,2,1,0:T(4,128)(2,1)} %copy.93), calls=%async_computation.3 | async-start | bytes 2097152 | tf_op jit(solution)/shard_map/all_to_all | solution.py:81
  139.7 94.4 %reduce-scatter.2.cloned.1.call-start = ((), (), s32[]{:S(2)}) async-start(), calls=%async_computation.5 | async-start | bytes 2359296 | tf_op jit(solution)/shard_map/reduce_scatter | solution.py:154
  144.2 4.7 %copy-start.1 = (bf16[3,384,4096]{2,1,0:T(8,128)(2,1)}, bf16[3,384,4096]{2,1,0:T(8,128)(2,1)S(1)}, u32[]{:S(2)}) copy-start(bf16[3,384,4096]{2,1,0:T(8,128)(2,1)S(1)} %pad_maximum_fusion) | copy-start | bytes 28311556
  148.9 1.2 copy-start.4
  162.2 9.9 %copy-start.5 = (bf16[1,384,4096]{1,2,0:T(8,128)(2,1)S(1)}, bf16[1,384,4096]{1,2,0:T(8,128)(2,1)}, u32[]{:S(2)}) copy-start(bf16[1,384,4096]{1,2,0:T(8,128)(2,1)} %copy.100) | copy-start | bytes 9437188
  169.4 2.7 %copy-start.8 = (f32[32,128,384]{1,2,0:T(8,128)}, f32[32,128,384]{1,2,0:T(8,128)S(1)}, u32[]{:S(2)}) copy-start(f32[32,128,384]{1,2,0:T(8,128)S(1)} %get-tuple-element.91) | copy-start | bytes 18874372
Sparse Core Ops, SparseCore 0:
  197.2 36.9 reduce-scatter.1
where the time goes:
time: 244 us; the launch traced here: 243 us
  waiting for transfers between devices  89.2 us (37%)
  matrix products  53 us (22%)
  local copies, waits for them, and re-layouts  41.1 us (17%)
  starting transfers between devices  25.2 us (10%)
  other arithmetic  19.9 us (8%)
  between operations  14.2 us (6%)
    reduce_scatter x1, waiting for transfers between devices, local(): lax.psum_scatter(summed, 'context', scatter_dimension=0, tiled=True)  34.8 us
    all_to_all x1, waiting for transfers between devices, local(): lax.all_to_all(split_heads(queries), 'context', split_axis=1, concat_axis...  23.6 us
    all_to_all x1, waiting for transfers between devices, local(): lax.all_to_all(split_heads(keys), 'context', split_axis=1, concat_axis=0,...  22.1 us
    unnamed x24, local copies, waits for them, and re-layouts  17.2 us
    sub x2, matrix products, one_block(): expo = jnp.exp(scores - top)  14.3 us
    dot_general x2, matrix products, one_block(): jnp.einsum('hqk,khd->qhd', weights, values, preferred_element_type=jnp.fl...  11.4 us
    all_to_all x1, waiting for transfers between devices, local(): lax.all_to_all(split_heads(values), 'context', split_axis=1, concat_axis=...  8.65 us
    sub x1, other arithmetic, local(): expo = jnp.exp(scores - top)  7.18 us
  transfers between devices with their start and end apart: 7, of which 4 were waited for; matrix products, arithmetic and copies ran while one was open for 34% of the time, Pallas kernels for 0%

commit v1 on v0

v1 whole, which is shorter than its diff:
```python
import functools
import math

import jax
import jax.numpy as jnp
from jax import lax
from jax.experimental import pallas as pl
from jax.experimental.pallas import tpu as pltpu
from jax.sharding import PartitionSpec as P

H = 32
HIDDEN = -1e30
VMEM = 48 * 1024 * 1024
NT = (((1,), (1,)), ((), ()))
TN = (((0,), (0,)), ((), ()))
NN = (((1,), (0,)), ((), ()))


def mm(a, b, dims=NN):
    return lax.dot_general(a, b, dims, preferred_element_type=jnp.float32)


def params():
    return pltpu.CompilerParams(vmem_limit_bytes=VMEM)


SMEM = pl.BlockSpec(memory_space=pltpu.SMEM)
ANY = pl.BlockSpec(memory_space=pl.ANY)


def exchange(blocks, count):
    order = sorted(range(1, count), key=lambda k: -k)
    got = {0: blocks[0]}
    for k in order:
        got[k] = lax.ppermute(blocks[k], "context", [(i, i ^ k) for i in range(count)])
    return [got[k] for k in range(count)]


def pack_kernel(count, group, start, width, me_ref, q_ref, k_ref, v_ref, *rest):
    outs, sems = rest[:count], rest[count]
    me = me_ref[0]
    copies = []
    for k in range(count):
        column = pl.multiple_of((me ^ k) * group + start, 128)
        for t, ref in enumerate((q_ref, k_ref, v_ref)):
            copies.append(
                pltpu.make_async_copy(
                    ref.at[:, pl.ds(column, width)], outs[k].at[t], sems.at[3 * k + t]
                )
            )
    for copy in copies:
        copy.start()
    for copy in copies:
        copy.wait()


def pack(me, q, k, v, count, start, width):
    tok, model = q.shape
    return pl.pallas_call(
        functools.partial(pack_kernel, count, model // count, start, width),
        out_shape=[jax.ShapeDtypeStruct((3, tok, width), q.dtype)] * count,
        in_specs=[SMEM, ANY, ANY, ANY],
        out_specs=[ANY] * count,
        scratch_shapes=[pltpu.SemaphoreType.DMA((3 * count,))],
        compiler_params=params(),
        name="pack",
    )(me, q, k, v)


def unpack_kernel(count, group, spans, me_ref, *rest):
    total = count * len(spans)
    refs, out, sems = rest[:total], rest[total], rest[total + 1]
    me = me_ref[0]
    copies = []
    for c, (start, width) in enumerate(spans):
        for k in range(count):
            column = pl.multiple_of((me ^ k) * group + start, 128)
            copies.append(
                pltpu.make_async_copy(
                    refs[c * count + k],
                    out.at[:, pl.ds(column, width)],
                    sems.at[c * count + k],
                )
            )
    for copy in copies:
        copy.start()
    for copy in copies:
        copy.wait()


def unpack(me, blocks, count, spans, model):
    tok = blocks[0].shape[0]
    return pl.pallas_call(
        functools.partial(unpack_kernel, count, model // count, spans),
        out_shape=jax.ShapeDtypeStruct((tok, model), blocks[0].dtype),
        in_specs=[SMEM] + [ANY] * len(blocks),
        out_specs=ANY,
        scratch_shapes=[pltpu.SemaphoreType.DMA((len(blocks),))],
        compiler_params=params(),
        name="unpack",
    )(me, *blocks)


def attention_kernel(count, tok, hd, slots, rank, last, factor, me_ref, *rest):
    blocks, rest = rest[:count], rest[count:]
    notes, rest = rest[:count], rest[count:]
    up_ref, hid_ref, rest = rest[0], rest[1], rest[2:]
    outs, rest = rest[:count], rest[count:]
    gup_ref, rest = rest[0], rest[1:]
    nh = count if last else 1
    hid_out, rest = rest[:nh], rest[nh:]
    q_s, k_s, vt_s, svt_s, lora_s, grad_s, hid_s = rest
    head = pl.program_id(0)
    me = me_ref[0]
    tile = 3 * tok // slots
    scale = hd ** (-0.5) * math.log2(math.e)

    @pl.when(head == 0)
    def _():
        hid_s[...] = hid_ref[...]
        for p in range(count):
            lora_s[:, p * tok : (p + 1) * tok] = notes[p][:rank, :]

    for p in range(count):
        q_s[p] = blocks[p][0]
        k_s[p * tok : (p + 1) * tok, :] = blocks[p][1]
        vt_s[:, p * tok : (p + 1) * tok] = blocks[p][2].T
    up_t = up_ref[...]
    for p in range(count):
        cols = slice(p * tok, (p + 1) * tok)
        term = mm(up_t, lora_s[:, cols], TN)
        svt_s[p] = (vt_s[:, cols].astype(jnp.float32) + term).astype(jnp.bfloat16)
    grad_s[...] = jnp.zeros_like(grad_s)

    for p in range(count):
        query = q_s[p]
        scores = mm(k_s[...], query, NT)
        top = jnp.max(scores, axis=0, keepdims=True)
        expo = jnp.exp2((scores - top) * scale)
        norm = jnp.sum(expo, axis=0, keepdims=True)
        teacher = mm(vt_s[...], expo.astype(jnp.bfloat16)) / norm
        teacher = teacher.astype(jnp.bfloat16).astype(jnp.float32)

        slab = me ^ p
        low = jnp.where(slab > 0, (slab - 1) ^ me, p)
        high = jnp.where(slab < count - 1, (slab + 1) ^ me, p)
        places = (low, p, high)
        keys = jnp.concatenate(
            [k_s[pl.ds(pl.multiple_of(w * tok, tok), tok), :] for w in places], axis=0
        )
        seen = notes[p][rank:, :].astype(jnp.float32)[:slots]
        bias = (seen - 1.0) * (-HIDDEN)
        scores = mm(keys, query, NT).reshape(slots, tile, tok) + bias[:, None, :]
        scores = scores.reshape(3 * tok, tok)
        top = jnp.max(scores, axis=0, keepdims=True)
        expo = jnp.exp2((scores - top) * scale)
        norm = jnp.sum(expo, axis=0, keepdims=True)
        weights = (expo * (1.0 / norm)).astype(jnp.bfloat16)
        values = jnp.concatenate([svt_s[w] for w in places], axis=1)
        student = mm(values, weights)
        outs[p][...] = student.T.astype(jnp.bfloat16)
        delta = ((student - teacher) * factor).astype(jnp.bfloat16)
        grads = mm(weights, delta, NT)
        for n, w in enumerate(places):
            grad_s[w] += grads[n * tok : (n + 1) * tok]

    grad = grad_s[...].reshape(count * tok, hd).astype(jnp.bfloat16)
    gup_ref[...] = mm(lora_s[...], grad).T
    hid_s[...] += mm(up_t, grad, NT)

    @pl.when(head == pl.num_programs(0) - 1)
    def _():
        if last:
            for p in range(count):
                hid_out[p][...] = hid_s[:, p * tok : (p + 1) * tok].astype(jnp.bfloat16)
        else:
            hid_out[0][...] = hid_s[...]


def attention(me, blocks, notes, up_t, hid, first, hd, slots, last, total):
    count = len(blocks)
    tok = blocks[0].shape[1]
    nh = blocks[0].shape[2] // hd
    rank = up_t.shape[0]
    bf, f32 = jnp.bfloat16, jnp.float32
    whole = lambda shape: pl.BlockSpec(shape, lambda h: (0,) * len(shape))
    if last:
        hid_shape = [jax.ShapeDtypeStruct((rank, tok), bf)] * count
        hid_spec = [whole((rank, tok))] * count
    else:
        hid_shape = [jax.ShapeDtypeStruct((rank, count * tok), f32)]
        hid_spec = [whole((rank, count * tok))]
    keys = count * tok
    flops = nh * keys * (4 * keys * hd + 6 * 3 * tok * hd)
    out = pl.pallas_call(
        functools.partial(
            attention_kernel, count, tok, hd, slots, rank, last, total ** (-0.5)
        ),
        grid=(nh,),
        out_shape=[jax.ShapeDtypeStruct((tok, nh * hd), bf)] * count
        + [jax.ShapeDtypeStruct((nh * hd, rank), f32)]
        + hid_shape,
        in_specs=[SMEM]
        + [pl.BlockSpec((3, tok, hd), lambda h: (0, 0, h))] * count
        + [whole(notes[0].shape)] * count
        + [pl.BlockSpec((rank, hd), lambda h: (0, first + h)), whole((rank, keys))],
        out_specs=[pl.BlockSpec((tok, hd), lambda h: (0, h))] * count
        + [pl.BlockSpec((hd, rank), lambda h: (h, 0))]
        + hid_spec,
        scratch_shapes=[
            pltpu.VMEM((count, tok, hd), bf),
            pltpu.VMEM((keys, hd), bf),
            pltpu.VMEM((hd, keys), bf),
            pltpu.VMEM((count, hd, tok), bf),
            pltpu.VMEM((rank, keys), bf),
            pltpu.VMEM((count, tok, hd), f32),
            pltpu.VMEM((rank, keys), f32),
        ],
        compiler_params=params(),
        cost_estimate=pl.CostEstimate(
            flops=flops, bytes_accessed=4 * nh * keys * hd * 2, transcendentals=nh * keys * keys
        ),
        name="attention",
    )(me, *blocks, *notes, up_t, hid)
    return out[:count], out[count], out[count + 1 :]


def down_kernel(count, group, me_ref, *rest):
    parts, x_ref, outs = rest[:count], rest[count], rest[count + 1 :]
    me = me_ref[0]
    hidden = parts[0][...].astype(jnp.float32)
    for k in range(1, count):
        hidden += parts[k][...].astype(jnp.float32)
    hidden = hidden.astype(jnp.bfloat16)
    for k in range(count):
        column = pl.multiple_of((me ^ k) * group, 128)
        outs[k][...] = mm(hidden, x_ref[:, pl.ds(column, group)]).astype(jnp.bfloat16)


def down_terms(me, parts, x):
    count = len(parts)
    group = x.shape[1] // count
    rank = parts[0].shape[0]
    vm = pl.BlockSpec(memory_space=pltpu.VMEM)
    return pl.pallas_call(
        functools.partial(down_kernel, count, group),
        out_shape=[jax.ShapeDtypeStruct((rank, group), jnp.bfloat16)] * count,
        in_specs=[SMEM] + [vm] * (count + 1),
        out_specs=[vm] * count,
        compiler_params=params(),
        name="down_terms",
    )(me, *parts, x)


def sum_kernel(count, *refs):
    total = refs[0][...].astype(jnp.float32)
    for k in range(1, count):
        total += refs[k][...].astype(jnp.float32)
    refs[count][...] = total.T


def sum_terms(parts):
    rank, rows = parts[0].shape
    return pl.pallas_call(
        functools.partial(sum_kernel, len(parts)),
        out_shape=jax.ShapeDtypeStruct((rows, rank), jnp.float32),
        compiler_params=params(),
        name="sum_terms",
    )(*parts)


def head_chunks(per_group):
    if per_group < 2:
        return [(0, per_group)]
    return [(0, per_group - 1), (per_group - 1, 1)]


def local(
    queries, keys, values, value_layer_input, adapter_down_weight, adapter_up_weight, neighbors
):
    tok, model = queries.shape
    rank = adapter_down_weight.shape[1]
    count = lax.axis_size("context")
    index = lax.axis_index("context")
    me = index.astype(jnp.int32).reshape(1)
    hd = model // H
    group = model // count
    per_group = H // count
    tiles = neighbors.shape[0]
    slots = 3 * tiles
    tile = tok // tiles
    chunks = head_chunks(per_group)

    messages = [
        exchange(pack(me, queries, keys, values, count, first * hd, nh * hd), count)
        for first, nh in chunks
    ]

    lora = jnp.dot(
        value_layer_input, adapter_down_weight, preferred_element_type=jnp.float32
    ).astype(jnp.bfloat16)
    offsets = neighbors - (index - 1) * tiles
    seen = jnp.any(offsets[:, :, None] == jnp.arange(slots, dtype=jnp.int32), axis=1)
    seen = jnp.repeat(seen.T.astype(jnp.bfloat16), tile, axis=1)
    pad = -slots % 16
    note = jnp.concatenate([lora.T, jnp.pad(seen, ((0, pad), (0, 0)))], axis=0)
    notes = exchange([note] * count, count)

    up_t = lax.dynamic_slice_in_dim(adapter_up_weight, index * group, group, 0).T
    hid = jnp.zeros((rank, count * tok), jnp.float32)
    student, grad_up = [], []
    for c, (first, nh) in enumerate(chunks):
        last = c == len(chunks) - 1
        outs, gup, hid = attention(
            me, messages[c], notes, up_t, hid, first, hd, slots, last, tok * count
        )
        hid = hid if last else hid[0]
        student += exchange(outs, count)
        grad_up.append(gup)
    terms = exchange(down_terms(me, exchange(hid, count), value_layer_input), count)
    grad_down = sum_terms(terms)
    spans = [(first * hd, nh * hd) for first, nh in chunks]
    student_out = unpack(me, student, count, spans, model)
    return student_out, grad_down, jnp.concatenate(grad_up, axis=0)


def solution(mesh):
    rows = P(("video", "context"), None)
    return jax.shard_map(
        local,
        mesh=mesh,
        in_specs=(rows, rows, rows, rows, P(), P(), rows),
        out_specs=(rows, rows, rows),
        check_vma=False,
    )
```

time: 244 us -> 180 us (0.74)
  matrix products: 53 us -> 1.87 us
  starting transfers between devices: 25.2 us -> 66.7 us
  local copies, waits for them, and re-layouts: 41.1 us -> 12.2 us
  Pallas kernels: 0 us -> 25.2 us
  other arithmetic: 19.9 us -> 0.13 us
  waiting for transfers between devices: 89.2 us -> 69.6 us
  between operations: 14.2 us -> 1 us
    ppermute x2 -> x49, waiting for transfers between devices: 0.01 us -> 69.6 us  [exchange(): lax.ppermute(blocks[k], 'context', [(i, i ^ k) for i in range(count)])]
    ppermute x2 -> x49, starting transfers between devices: 5.94 us -> 66.7 us  [exchange(): lax.ppermute(blocks[k], 'context', [(i, i ^ k) for i in range(count)])]
    all_to_all x4 -> x0, waiting for transfers between devices: 54.3 us -> none  [the longest x1 23.6 us: local(): lax.all_to_all(split_heads(queries), 'context', split_axis=1, concat_axis...]
    dot_general x10 -> x1, matrix products: 38.7 us -> 1.87 us  [local(): jnp.dot(value_layer_input, adapter_down_weight, preferred_element_type=jn...]
    reduce_scatter x1 -> x0, waiting for transfers between devices: 34.8 us -> none  [local(): lax.psum_scatter(summed, 'context', scatter_dimension=0, tiled=True)]
    pallas_call x0 -> x7, Pallas kernels: none -> 25.2 us  [the longest x2 21.1 us: attention(): pl.pallas_call(functools.partial(attention_kernel, count, tok, hd, slots,...]
    all_to_all x4 -> x0, starting transfers between devices: 19.1 us -> none  [the longest x1 6.33 us: local(): lax.all_to_all(split_heads(queries), 'context', split_axis=1, concat_axis...]
    sub x2 -> x0, matrix products: 14.3 us -> none  [one_block(): expo = jnp.exp(scores - top)]
  transfers between devices with their start and end apart: 7 -> 49, of which waited for: 4 -> 16; matrix products, arithmetic and copies ran while one was open for 34% -> 2% of each run, Pallas kernels for 0% -> 10%
where the time goes in v1:
time: 180 us; the launch traced here: 177 us
  waiting for transfers between devices  69.6 us (39%)
  starting transfers between devices  66.7 us (37%)
  Pallas kernels  25.2 us (14%)
  local copies, waits for them, and re-layouts  12.2 us (7%)
  matrix products  1.87 us (1%)
    ppermute x49, waiting for transfers between devices, exchange(): lax.ppermute(blocks[k], 'context', [(i, i ^ k) for i in range(count)])  69.6 us
    ppermute x49, starting transfers between devices, exchange(): lax.ppermute(blocks[k], 'context', [(i, i ^ k) for i in range(count)])  66.7 us
    pallas_call x2, Pallas kernels, attention(): pl.pallas_call(functools.partial(attention_kernel, count, tok, hd, slots,...  21.1 us
    unnamed x48, local copies, waits for them, and re-layouts  12 us
  transfers between devices with their start and end apart: 49, of which 16 were waited for; matrix products, arithmetic and copies ran while one was open for 2% of the time, Pallas kernels for 10%

profile of v1, /device:TPU:0, one launch (start us, length us, event | category | flops | bytes accessed | tf_op | source)
XLA Modules:
  0.0 176.8 jit_solution(661529280361665557)
XLA Ops:
  0.7 1.3 copy-done.1
  1.9 1.2 copy-done.3
  3.2 1.2 copy-done.5
  4.4 1.5 pack.2
  6.5 2.6 %collective-permute-start.1 = (bf16[3,128,384]{2,1,0:T(8,128)(2,1)}, bf16[3,128,384]{2,1,0:T(8,128)(2,1)S(1)}, u32[]{:S(2)}, u32[]{:S(2)}) collective-permute-start(bf16[3,128,384]{2,1,0:T(8,128)(2,1)} %get-tuple-element.56), channel_id=1, source_target_pairs={{0,2},{1,3},{2,0},{3,1},{4,6},{5,7},{6,4},{7,5},{8,10},{9,11},{10,... | collective-permute-start | bytes 884744 | tf_op jit(solution)/shard_map/ppermute | solution.py:35
  9.2 1.9 %convolution_convert_fusion = bf16[64,128]{1,0:T(8,128)(2,1)S(1)} fusion(bf16[4096,64]{0,1:T(8,128)(2,1)} %param.11, bf16[128,4096]{1,0:T(8,128)(2,1)} %rest_8_.1), kind=kOutput, calls=%fused_computation | convolution fusion | flops 67117056 | bytes 1589248 | tf_op jit(solution)/shard_map/dot_general | solution.py:299
  11.4 2.6 %collective-permute-start.10 = (bf16[80,128]{1,0:T(8,128)(2,1)S(1)}, bf16[80,128]{1,0:T(8,128)(2,1)S(1)}, u32[]{:S(2)}, u32[]{:S(2)}) collective-permute-start(bf16[80,128]{1,0:T(8,128)(2,1)S(1)} %fusion.1.rest_8_), channel_id=1, source_target_pairs={{0,4},{1,5},{2,6},{3,7},{4,0},{5,1},{6,2},{7,3},{8,12},{9,13},{10,... | collective-permute-start | bytes 61448 | tf_op jit(solution)/shard_map/ppermute | solution.py:35
  14.0 2.3 %collective-permute-start.12 = (bf16[80,128]{1,0:T(8,128)(2,1)S(1)}, bf16[80,128]{1,0:T(8,128)(2,1)S(1)}, u32[]{:S(2)}, u32[]{:S(2)}) collective-permute-start(bf16[80,128]{1,0:T(8,128)(2,1)S(1)} %fusion.1.rest_8_), channel_id=1, source_target_pairs={{0,6},{1,7},{2,4},{3,5},{4,2},{5,3},{6,0},{7,1},{8,14},{9,15},{10,... | collective-permute-start | bytes 61448 | tf_op jit(solution)/shard_map/ppermute | solution.py:35
  16.3 1.2 copy-done.6
  17.5 1.0 pack.3
  20.2 1.0 collective-permute-start.22
  21.8 1.1 collective-permute-start.13
  22.8 3.9 %collective-permute-done.13.rest_15_ = bf16[80,128]{1,0:T(8,128)(2,1)S(1)} collective-permute-done((bf16[80,128]{1,0:T(8,128)(2,1)S(1)}, bf16[80,128]{1,0:T(8,128)(2,1)S(1)}, u32[]{:S(2)}, u32[]{:S(2)}) %collective-permute-start.13) | collective-permute-done | bytes 20512 | tf_op jit(solution)/shard_map/ppermute | solution.py:35
  28.0 3.8 %collective-permute-done.8.rest_10_ = bf16[80,128]{1,0:T(8,128)(2,1)S(1)} collective-permute-done((bf16[80,128]{1,0:T(8,128)(2,1)S(1)}, bf16[80,128]{1,0:T(8,128)(2,1)S(1)}, u32[]{:S(2)}, u32[]{:S(2)}) %collective-permute-start.8) | collective-permute-done | bytes 20512 | tf_op jit(solution)/shard_map/ppermute | solution.py:35
  31.8 3.2 %collective-permute-done.9.rest_11_ = bf16[80,128]{1,0:T(8,128)(2,1)S(1)} collective-permute-done((bf16[80,128]{1,0:T(8,128)(2,1)S(1)}, bf16[80,128]{1,0:T(8,128)(2,1)S(1)}, u32[]{:S(2)}, u32[]{:S(2)}) %collective-permute-start.9) | collective-permute-done | bytes 20512 | tf_op jit(solution)/shard_map/ppermute | solution.py:35
  35.7 1.7 collective-permute-start.4
  37.4 1.8 %collective-permute-start.5 = (bf16[3,128,384]{2,1,0:T(8,128)(2,1)}, bf16[3,128,384]{2,1,0:T(8,128)(2,1)S(1)}, u32[]{:S(2)}, u32[]{:S(2)}) collective-permute-start(bf16[3,128,384]{2,1,0:T(8,128)(2,1)} %get-tuple-element.60), channel_id=1, source_target_pairs={{0,6},{1,7},{2,4},{3,5},{4,2},{5,3},{6,0},{7,1},{8,14},{9,15},{10,... | collective-permute-start | bytes 884744 | tf_op jit(solution)/shard_map/ppermute | solution.py:35
  39.2 2.1 %collective-permute-start.6 = (bf16[3,128,384]{2,1,0:T(8,128)(2,1)}, bf16[3,128,384]{2,1,0:T(8,128)(2,1)S(1)}, u32[]{:S(2)}, u32[]{:S(2)}) collective-permute-start(bf16[3,128,384]{2,1,0:T(8,128)(2,1)} %get-tuple-element.61), channel_id=1, source_target_pairs={{0,7},{1,6},{2,5},{3,4},{4,3},{5,2},{6,1},{7,0},{8,15},{9,14},{10,... | collective-permute-start | bytes 884744 | tf_op jit(solution)/shard_map/ppermute | solution.py:35
  41.3 7.7 %collective-permute-done.2.rest_3_ = bf16[3,128,384]{2,1,0:T(8,128)(2,1)S(1)} collective-permute-done((bf16[3,128,384]{2,1,0:T(8,128)(2,1)}, bf16[3,128,384]{2,1,0:T(8,128)(2,1)S(1)}, u32[]{:S(2)}, u32[]{:S(2)}) %collective-permute-start.2) | collective-permute-done | bytes 294944 | tf_op jit(solution)/shard_map/ppermute | solution.py:35
  49.0 22.9 %collective-permute-done.3.rest_4_ = bf16[3,128,384]{2,1,0:T(8,128)(2,1)S(1)} collective-permute-done((bf16[3,128,384]{2,1,0:T(8,128)(2,1)}, bf16[3,128,384]{2,1,0:T(8,128)(2,1)S(1)}, u32[]{:S(2)}, u32[]{:S(2)}) %collective-permute-start.3) | collective-permute-done | bytes 294944 | tf_op jit(solution)/shard_map/ppermute | solution.py:35
  71.9 6.1 %collective-permute-done.4.rest_5_ = bf16[3,128,384]{2,1,0:T(8,128)(2,1)S(1)} collective-permute-done((bf16[3,128,384]{2,1,0:T(8,128)(2,1)}, bf16[3,128,384]{2,1,0:T(8,128)(2,1)S(1)}, u32[]{:S(2)}, u32[]{:S(2)}) %collective-permute-start.4) | collective-permute-done | bytes 294944 | tf_op jit(solution)/shard_map/ppermute | solution.py:35
  78.0 2.0 %collective-permute-start.26 = (bf16[3,128,128]{2,1,0:T(8,128)(2,1)}, bf16[3,128,128]{2,1,0:T(8,128)(2,1)S(1)}, u32[]{:S(2)}, u32[]{:S(2)}) collective-permute-start(bf16[3,128,128]{2,1,0:T(8,128)(2,1)} %get-tuple-element.76), channel_id=1, source_target_pairs={{0,6},{1,7},{2,4},{3,5},{4,2},{5,3},{6,0},{7,1},{8,14},{9,15},{10,... | collective-permute-start | bytes 294920 | tf_op jit(solution)/shard_map/ppermute | solution.py:35
  80.0 2.7 %collective-permute-start.27 = (bf16[3,128,128]{2,1,0:T(8,128)(2,1)}, bf16[3,128,128]{2,1,0:T(8,128)(2,1)S(1)}, u32[]{:S(2)}, u32[]{:S(2)}) collective-permute-start(bf16[3,128,128]{2,1,0:T(8,128)(2,1)} %get-tuple-element.77), channel_id=1, source_target_pairs={{0,7},{1,6},{2,5},{3,4},{4,3},{5,2},{6,1},{7,0},{8,15},{9,14},{10,... | collective-permute-start | bytes 294920 | tf_op jit(solution)/shard_map/ppermute | solution.py:35
  83.5 16.2 %attention.2 = (bf16[128,384]{1,0:T(8,128)(2,1)S(1)}, bf16[128,384]{1,0:T(8,128)(2,1)S(1)}, bf16[128,384]{1,0:T(8,128)(2,1)S(1)}, bf16[128,384]{1,0:T(8,128)(2,1...) custom-call(s32[1]{0:T(128)} %bitcast.me_ref, ...), custom_call_target="tpu_custom_call" | custom-call | flops 2516582400 | bytes 3145728 | tf_op jit(solution)/shard_map/attention/pallas_call | solution.py:195
  99.7 1.1 collective-permute-done.24.rest_4_
  104.1 4.9 %attention.3 = (bf16[128,128]{1,0:T(8,128)(2,1)S(1)}, bf16[128,128]{1,0:T(8,128)(2,1)S(1)}, bf16[128,128]{1,0:T(8,128)(2,1)S(1)}, bf16[128,128]{1,0:T(8,128)(2,1...) custom-call(s32[1]{0:T(128)} %bitcast.me_ref, ...), custom_call_target="tpu_custom_call" | custom-call | flops 838860800 | bytes 1048576 | tf_op jit(solution)/shard_map/attention/pallas_call | solution.py:195
  109.0 1.7 collective-permute-start.35
  110.7 13.6 %collective-permute-start.36 = (bf16[64,128]{1,0:T(8,128)(2,1)S(1)}, bf16[64,128]{1,0:T(8,128)(2,1)S(1)}, u32[]{:S(2)}, u32[]{:S(2)}) collective-permute-start(bf16[64,128]{1,0:T(8,128)(2,1)S(1)} %get-tuple-element.89), channel_id=1, source_target_pairs={{0,2},{1,3},{2,0},{3,1},{4,6},{5,7},{6,4},{7,5},{8,10},{9,11},{10,... | collective-permute-start | bytes 49160 | tf_op jit(solution)/shard_map/ppermute | solution.py:35
  124.3 2.6 %collective-permute-start.38 = (bf16[64,128]{1,0:T(8,128)(2,1)S(1)}, bf16[64,128]{1,0:T(8,128)(2,1)S(1)}, u32[]{:S(2)}, u32[]{:S(2)}) collective-permute-start(bf16[64,128]{1,0:T(8,128)(2,1)S(1)} %get-tuple-element.91), channel_id=1, source_target_pairs={{0,4},{1,5},{2,6},{3,7},{4,0},{5,1},{6,2},{7,3},{8,12},{9,13},{10,... | collective-permute-start | bytes 49160 | tf_op jit(solution)/shard_map/ppermute | solution.py:35
  127.2 1.5 collective-permute-start.39
  128.8 2.4 %collective-permute-start.40 = (bf16[64,128]{1,0:T(8,128)(2,1)S(1)}, bf16[64,128]{1,0:T(8,128)(2,1)S(1)}, u32[]{:S(2)}, u32[]{:S(2)}) collective-permute-start(bf16[64,128]{1,0:T(8,128)(2,1)S(1)} %get-tuple-element.93), channel_id=1, source_target_pairs={{0,6},{1,7},{2,4},{3,5},{4,2},{5,3},{6,0},{7,1},{8,14},{9,15},{10,... | collective-permute-start | bytes 49160 | tf_op jit(solution)/shard_map/ppermute | solution.py:35
  131.2 1.1 collective-permute-start.41
  132.9 1.5 collective-permute-done.40.rest_6_
  134.3 1.0 collective-permute-start.31
  136.3 1.9 %collective-permute-start.33 = (bf16[128,128]{1,0:T(8,128)(2,1)S(1)}, bf16[128,128]{1,0:T(8,128)(2,1)S(1)}, u32[]{:S(2)}, u32[]{:S(2)}) collective-permute-start(bf16[128,128]{1,0:T(8,128)(2,1)S(1)} %get-tuple-element.85), channel_id=1, source_target_pairs={{0,6},{1,7},{2,4},{3,5},{4,2},{5,3},{6,0},{7,1},{8,14},{9,15},{10,... | collective-permute-start | bytes 98312 | tf_op jit(solution)/shard_map/ppermute | solution.py:35
  138.5 1.4 collective-permute-start.42
  140.0 1.3 collective-permute-start.44
  142.3 1.8 collective-permute-start.34
  144.0 3.8 %collective-permute-done.34.rest_15_ = bf16[128,128]{1,0:T(8,128)(2,1)S(1)} collective-permute-done((bf16[128,128]{1,0:T(8,128)(2,1)S(1)}, bf16[128,128]{1,0:T(8,128)(2,1)S(1)}, u32[]{:S(2)}, u32[]{:S(2)}) %collective-permute-start.34) | collective-permute-done | bytes 32800 | tf_op jit(solution)/shard_map/ppermute | solution.py:35
  147.9 2.3 %collective-permute-start.15 = (bf16[128,384]{1,0:T(8,128)(2,1)S(1)}, bf16[128,384]{1,0:T(8,128)(2,1)S(1)}, u32[]{:S(2)}, u32[]{:S(2)}) collective-permute-start(bf16[128,384]{1,0:T(8,128)(2,1)S(1)} %get-tuple-element.64), channel_id=1, source_target_pairs={{0,2},{1,3},{2,0},{3,1},{4,6},{5,7},{6,4},{7,5},{8,10},{9,11},{10,... | collective-permute-start | bytes 294920 | tf_op jit(solution)/shard_map/ppermute | solution.py:35
  150.7 1.9 %collective-permute-start.47 = (bf16[64,512]{1,0:T(8,128)(2,1)S(1)}, bf16[64,512]{1,0:T(8,128)(2,1)S(1)}, u32[]{:S(2)}, u32[]{:S(2)}) collective-permute-start(bf16[64,512]{1,0:T(8,128)(2,1)S(1)} %get-tuple-element.101), channel_id=1, source_target_pairs={{0,6},{1,7},{2,4},{3,5},{4,2},{5,3},{6,0},{7,1},{8,14},{9,15},{10,... | collective-permute-start | bytes 196616 | tf_op jit(solution)/shard_map/ppermute | solution.py:35
  152.6 1.6 collective-permute-start.48
  154.2 5.3 %collective-permute-done.46.refs_5_ = bf16[64,512]{1,0:T(8,128)(2,1)S(1)} collective-permute-done((bf16[64,512]{1,0:T(8,128)(2,1)S(1)}, bf16[64,512]{1,0:T(8,128)(2,1)S(1)}, u32[]{:S(2)}, u32[]{:S(2)}) %collective-permute-start.46) | collective-permute-done | bytes 65568 | tf_op jit(solution)/shard_map/ppermute | solution.py:35
  159.5 2.4 %collective-permute-start.17 = (bf16[128,384]{1,0:T(8,128)(2,1)}, bf16[128,384]{1,0:T(8,128)(2,1)S(1)}, u32[]{:S(2)}, u32[]{:S(2)}) collective-permute-start(bf16[128,384]{1,0:T(8,128)(2,1)} %get-tuple-element.66), channel_id=1, source_target_pairs={{0,4},{1,5},{2,6},{3,7},{4,0},{5,1},{6,2},{7,3},{8,12},{9,13},{10,... | collective-permute-start | bytes 294920 | tf_op jit(solution)/shard_map/ppermute | solution.py:35
  162.8 2.3 %collective-permute-start.19 = (bf16[128,384]{1,0:T(8,128)(2,1)S(1)}, bf16[128,384]{1,0:T(8,128)(2,1)S(1)}, u32[]{:S(2)}, u32[]{:S(2)}) collective-permute-start(bf16[128,384]{1,0:T(8,128)(2,1)S(1)} %get-tuple-element.68), channel_id=1, source_target_pairs={{0,6},{1,7},{2,4},{3,5},{4,2},{5,3},{6,0},{7,1},{8,14},{9,15},{10,... | collective-permute-start | bytes 294920 | tf_op jit(solution)/shard_map/ppermute | solution.py:35
  167.8 6.7 %collective-permute-done.17.rest_4_ = bf16[128,384]{1,0:T(8,128)(2,1)S(1)} collective-permute-done((bf16[128,384]{1,0:T(8,128)(2,1)}, bf16[128,384]{1,0:T(8,128)(2,1)S(1)}, u32[]{:S(2)}, u32[]{:S(2)}) %collective-permute-start.17) | collective-permute-done | bytes 98336 | tf_op jit(solution)/shard_map/ppermute | solution.py:35
  174.5 1.0 collective-permute-done.18.rest_5_
  175.5 1.1 unpack.1
  (116 shorter events, 16.4 us)
Async XLA Ops:
  5.9 31.4 %collective-permute-start = (bf16[3,128,384]{2,1,0:T(8,128)(2,1)}, bf16[3,128,384]{2,1,0:T(8,128)(2,1)S(1)}, u32[]{:S(2)}, u32[]{:S(2)}) collective-permute-start(bf16[3,128,384]{2,1,0:T(8,128)(2,1)} %get-tuple-element.55), channel_id=1, source_target_pairs={{0,1},{1,0},{2,3},{3,2},{4,5},{5,4},{6,7},{7,6},{8,9},{9,8},{10,11... | collective-permute-start | bytes 884744 | tf_op jit(solution)/shard_map/ppermute | solution.py:35
  6.5 32.7 %collective-permute-start.1 = (bf16[3,128,384]{2,1,0:T(8,128)(2,1)}, bf16[3,128,384]{2,1,0:T(8,128)(2,1)S(1)}, u32[]{:S(2)}, u32[]{:S(2)}) collective-permute-start(bf16[3,128,384]{2,1,0:T(8,128)(2,1)} %get-tuple-element.56), channel_id=1, source_target_pairs={{0,2},{1,3},{2,0},{3,1},{4,6},{5,7},{6,4},{7,5},{8,10},{9,11},{10,... | collective-permute-start | bytes 884744 | tf_op jit(solution)/shard_map/ppermute | solution.py:35
  11.4 7.8 %collective-permute-start.10 = (bf16[80,128]{1,0:T(8,128)(2,1)S(1)}, bf16[80,128]{1,0:T(8,128)(2,1)S(1)}, u32[]{:S(2)}, u32[]{:S(2)}) collective-permute-start(bf16[80,128]{1,0:T(8,128)(2,1)S(1)} %fusion.1.rest_8_), channel_id=1, source_target_pairs={{0,4},{1,5},{2,6},{3,7},{4,0},{5,1},{6,2},{7,3},{8,12},{9,13},{10,... | collective-permute-start | bytes 61448 | tf_op jit(solution)/shard_map/ppermute | solution.py:35
  14.0 5.6 %collective-permute-start.11 = (bf16[80,128]{1,0:T(8,128)(2,1)S(1)}, bf16[80,128]{1,0:T(8,128)(2,1)S(1)}, u32[]{:S(2)}, u32[]{:S(2)}) collective-permute-start(bf16[80,128]{1,0:T(8,128)(2,1)S(1)} %fusion.1.rest_8_), channel_id=1, source_target_pairs={{0,5},{1,4},{2,7},{3,6},{4,1},{5,0},{6,3},{7,2},{8,13},{9,12},{10,... | collective-permute-start | bytes 61448 | tf_op jit(solution)/shard_map/ppermute | solution.py:35
  14.0 7.2 %collective-permute-start.12 = (bf16[80,128]{1,0:T(8,128)(2,1)S(1)}, bf16[80,128]{1,0:T(8,128)(2,1)S(1)}, u32[]{:S(2)}, u32[]{:S(2)}) collective-permute-start(bf16[80,128]{1,0:T(8,128)(2,1)S(1)} %fusion.1.rest_8_), channel_id=1, source_target_pairs={{0,6},{1,7},{2,4},{3,5},{4,2},{5,3},{6,0},{7,1},{8,14},{9,15},{10,... | collective-permute-start | bytes 61448 | tf_op jit(solution)/shard_map/ppermute | solution.py:35
  19.2 15.8 %collective-permute-start.21 = (bf16[3,128,128]{2,1,0:T(8,128)(2,1)S(1)}, bf16[3,128,128]{2,1,0:T(8,128)(2,1)S(1)}, u32[]{:S(2)}, u32[]{:S(2)}) collective-permute-start(bf16[3,128,128]{2,1,0:T(8,128)(2,1)S(1)} %get-tuple-element.71), channel_id=1, source_target_pairs={{0,1},{1,0},{2,3},{3,2},{4,5},{5,4},{6,7},{7,6},{8,9},{9,8},{10,11... | collective-permute-start | bytes 294920 | tf_op jit(solution)/shard_map/ppermute | solution.py:35
  20.2 15.5 %collective-permute-start.22 = (bf16[3,128,128]{2,1,0:T(8,128)(2,1)S(1)}, bf16[3,128,128]{2,1,0:T(8,128)(2,1)S(1)}, u32[]{:S(2)}, u32[]{:S(2)}) collective-permute-start(bf16[3,128,128]{2,1,0:T(8,128)(2,1)S(1)} %get-tuple-element.72), channel_id=1, source_target_pairs={{0,2},{1,3},{2,0},{3,1},{4,6},{5,7},{6,4},{7,5},{8,10},{9,11},{10,... | collective-permute-start | bytes 294920 | tf_op jit(solution)/shard_map/ppermute | solution.py:35
  21.8 5.0 %collective-permute-start.13 = (bf16[80,128]{1,0:T(8,128)(2,1)S(1)}, bf16[80,128]{1,0:T(8,128)(2,1)S(1)}, u32[]{:S(2)}, u32[]{:S(2)}) collective-permute-start(bf16[80,128]{1,0:T(8,128)(2,1)S(1)} %fusion.1.rest_8_), channel_id=1, source_target_pairs={{0,7},{1,6},{2,5},{3,4},{4,3},{5,2},{6,1},{7,0},{8,15},{9,14},{10,... | collective-permute-start | bytes 61448 | tf_op jit(solution)/shard_map/ppermute | solution.py:35
  28.0 3.8 %collective-permute-start.8 = (bf16[80,128]{1,0:T(8,128)(2,1)S(1)}, bf16[80,128]{1,0:T(8,128)(2,1)S(1)}, u32[]{:S(2)}, u32[]{:S(2)}) collective-permute-start(bf16[80,128]{1,0:T(8,128)(2,1)S(1)} %fusion.1.rest_8_), channel_id=1, source_target_pairs={{0,2},{1,3},{2,0},{3,1},{4,6},{5,7},{6,4},{7,5},{8,10},{9,11},{10,... | collective-permute-start | bytes 61448 | tf_op jit(solution)/shard_map/ppermute | solution.py:35
  31.8 3.2 %collective-permute-start.9 = (bf16[80,128]{1,0:T(8,128)(2,1)S(1)}, bf16[80,128]{1,0:T(8,128)(2,1)S(1)}, u32[]{:S(2)}, u32[]{:S(2)}) collective-permute-start(bf16[80,128]{1,0:T(8,128)(2,1)S(1)} %fusion.1.rest_8_), channel_id=1, source_target_pairs={{0,3},{1,2},{2,1},{3,0},{4,7},{5,6},{6,5},{7,4},{8,11},{9,10},{10,... | collective-permute-start | bytes 61448 | tf_op jit(solution)/shard_map/ppermute | solution.py:35
  35.0 14.0 %collective-permute-start.2 = (bf16[3,128,384]{2,1,0:T(8,128)(2,1)}, bf16[3,128,384]{2,1,0:T(8,128)(2,1)S(1)}, u32[]{:S(2)}, u32[]{:S(2)}) collective-permute-start(bf16[3,128,384]{2,1,0:T(8,128)(2,1)} %get-tuple-element.57), channel_id=1, source_target_pairs={{0,3},{1,2},{2,1},{3,0},{4,7},{5,6},{6,5},{7,4},{8,11},{9,10},{10,... | collective-permute-start | bytes 884744 | tf_op jit(solution)/shard_map/ppermute | solution.py:35
  35.0 36.9 %collective-permute-start.3 = (bf16[3,128,384]{2,1,0:T(8,128)(2,1)}, bf16[3,128,384]{2,1,0:T(8,128)(2,1)S(1)}, u32[]{:S(2)}, u32[]{:S(2)}) collective-permute-start(bf16[3,128,384]{2,1,0:T(8,128)(2,1)} %get-tuple-element.58), channel_id=1, source_target_pairs={{0,4},{1,5},{2,6},{3,7},{4,0},{5,1},{6,2},{7,3},{8,12},{9,13},{10,... | collective-permute-start | bytes 884744 | tf_op jit(solution)/shard_map/ppermute | solution.py:35
  35.7 42.3 %collective-permute-start.4 = (bf16[3,128,384]{2,1,0:T(8,128)(2,1)}, bf16[3,128,384]{2,1,0:T(8,128)(2,1)S(1)}, u32[]{:S(2)}, u32[]{:S(2)}) collective-permute-start(bf16[3,128,384]{2,1,0:T(8,128)(2,1)} %get-tuple-element.59), channel_id=1, source_target_pairs={{0,5},{1,4},{2,7},{3,6},{4,1},{5,0},{6,3},{7,2},{8,13},{9,12},{10,... | collective-permute-start | bytes 884744 | tf_op jit(solution)/shard_map/ppermute | solution.py:35
  37.4 40.6 %collective-permute-start.5 = (bf16[3,128,384]{2,1,0:T(8,128)(2,1)}, bf16[3,128,384]{2,1,0:T(8,128)(2,1)S(1)}, u32[]{:S(2)}, u32[]{:S(2)}) collective-permute-start(bf16[3,128,384]{2,1,0:T(8,128)(2,1)} %get-tuple-element.60), channel_id=1, source_target_pairs={{0,6},{1,7},{2,4},{3,5},{4,2},{5,3},{6,0},{7,1},{8,14},{9,15},{10,... | collective-permute-start | bytes 884744 | tf_op jit(solution)/shard_map/ppermute | solution.py:35
  39.2 40.8 %collective-permute-start.6 = (bf16[3,128,384]{2,1,0:T(8,128)(2,1)}, bf16[3,128,384]{2,1,0:T(8,128)(2,1)S(1)}, u32[]{:S(2)}, u32[]{:S(2)}) collective-permute-start(bf16[3,128,384]{2,1,0:T(8,128)(2,1)} %get-tuple-element.61), channel_id=1, source_target_pairs={{0,7},{1,6},{2,5},{3,4},{4,3},{5,2},{6,1},{7,0},{8,15},{9,14},{10,... | collective-permute-start | bytes 884744 | tf_op jit(solution)/shard_map/ppermute | solution.py:35
  49.0 50.7 %collective-permute-start.23 = (bf16[3,128,128]{2,1,0:T(8,128)(2,1)}, bf16[3,128,128]{2,1,0:T(8,128)(2,1)S(1)}, u32[]{:S(2)}, u32[]{:S(2)}) collective-permute-start(bf16[3,128,128]{2,1,0:T(8,128)(2,1)} %get-tuple-element.73), channel_id=1, source_target_pairs={{0,3},{1,2},{2,1},{3,0},{4,7},{5,6},{6,5},{7,4},{8,11},{9,10},{10,... | collective-permute-start | bytes 294920 | tf_op jit(solution)/shard_map/ppermute | solution.py:35
  71.9 29.0 %collective-permute-start.24 = (bf16[3,128,128]{2,1,0:T(8,128)(2,1)}, bf16[3,128,128]{2,1,0:T(8,128)(2,1)S(1)}, u32[]{:S(2)}, u32[]{:S(2)}) collective-permute-start(bf16[3,128,128]{2,1,0:T(8,128)(2,1)} %get-tuple-element.74), channel_id=1, source_target_pairs={{0,4},{1,5},{2,6},{3,7},{4,0},{5,1},{6,2},{7,3},{8,12},{9,13},{10,... | collective-permute-start | bytes 294920 | tf_op jit(solution)/shard_map/ppermute | solution.py:35
  78.0 23.2 %collective-permute-start.25 = (bf16[3,128,128]{2,1,0:T(8,128)(2,1)}, bf16[3,128,128]{2,1,0:T(8,128)(2,1)S(1)}, u32[]{:S(2)}, u32[]{:S(2)}) collective-permute-start(bf16[3,128,128]{2,1,0:T(8,128)(2,1)} %get-tuple-element.75), channel_id=1, source_target_pairs={{0,5},{1,4},{2,7},{3,6},{4,1},{5,0},{6,3},{7,2},{8,13},{9,12},{10,... | collective-permute-start | bytes 294920 | tf_op jit(solution)/shard_map/ppermute | solution.py:35
  78.0 23.2 %collective-permute-start.26 = (bf16[3,128,128]{2,1,0:T(8,128)(2,1)}, bf16[3,128,128]{2,1,0:T(8,128)(2,1)S(1)}, u32[]{:S(2)}, u32[]{:S(2)}) collective-permute-start(bf16[3,128,128]{2,1,0:T(8,128)(2,1)} %get-tuple-element.76), channel_id=1, source_target_pairs={{0,6},{1,7},{2,4},{3,5},{4,2},{5,3},{6,0},{7,1},{8,14},{9,15},{10,... | collective-permute-start | bytes 294920 | tf_op jit(solution)/shard_map/ppermute | solution.py:35
  80.0 21.1 %collective-permute-start.27 = (bf16[3,128,128]{2,1,0:T(8,128)(2,1)}, bf16[3,128,128]{2,1,0:T(8,128)(2,1)S(1)}, u32[]{:S(2)}, u32[]{:S(2)}) collective-permute-start(bf16[3,128,128]{2,1,0:T(8,128)(2,1)} %get-tuple-element.77), channel_id=1, source_target_pairs={{0,7},{1,6},{2,5},{3,4},{4,3},{5,2},{6,1},{7,0},{8,15},{9,14},{10,... | collective-permute-start | bytes 294920 | tf_op jit(solution)/shard_map/ppermute | solution.py:35
  109.0 18.0 %collective-permute-start.35 = (bf16[64,128]{1,0:T(8,128)(2,1)S(1)}, bf16[64,128]{1,0:T(8,128)(2,1)S(1)}, u32[]{:S(2)}, u32[]{:S(2)}) collective-permute-start(bf16[64,128]{1,0:T(8,128)(2,1)S(1)} %get-tuple-element.88), channel_id=1, source_target_pairs={{0,1},{1,0},{2,3},{3,2},{4,5},{5,4},{6,7},{7,6},{8,9},{9,8},{10,11... | collective-permute-start | bytes 49160 | tf_op jit(solution)/shard_map/ppermute | solution.py:35
  110.7 16.6 %collective-permute-start.36 = (bf16[64,128]{1,0:T(8,128)(2,1)S(1)}, bf16[64,128]{1,0:T(8,128)(2,1)S(1)}, u32[]{:S(2)}, u32[]{:S(2)}) collective-permute-start(bf16[64,128]{1,0:T(8,128)(2,1)S(1)} %get-tuple-element.89), channel_id=1, source_target_pairs={{0,2},{1,3},{2,0},{3,1},{4,6},{5,7},{6,4},{7,5},{8,10},{9,11},{10,... | collective-permute-start | bytes 49160 | tf_op jit(solution)/shard_map/ppermute | solution.py:35
  124.2 4.6 %collective-permute-start.37 = (bf16[64,128]{1,0:T(8,128)(2,1)S(1)}, bf16[64,128]{1,0:T(8,128)(2,1)S(1)}, u32[]{:S(2)}, u32[]{:S(2)}) collective-permute-start(bf16[64,128]{1,0:T(8,128)(2,1)S(1)} %get-tuple-element.90), channel_id=1, source_target_pairs={{0,3},{1,2},{2,1},{3,0},{4,7},{5,6},{6,5},{7,4},{8,11},{9,10},{10,... | collective-permute-start | bytes 49160 | tf_op jit(solution)/shard_map/ppermute | solution.py:35
  124.3 6.9 %collective-permute-start.38 = (bf16[64,128]{1,0:T(8,128)(2,1)S(1)}, bf16[64,128]{1,0:T(8,128)(2,1)S(1)}, u32[]{:S(2)}, u32[]{:S(2)}) collective-permute-start(bf16[64,128]{1,0:T(8,128)(2,1)S(1)} %get-tuple-element.91), channel_id=1, source_target_pairs={{0,4},{1,5},{2,6},{3,7},{4,0},{5,1},{6,2},{7,3},{8,12},{9,13},{10,... | collective-permute-start | bytes 49160 | tf_op jit(solution)/shard_map/ppermute | solution.py:35
  126.9 9.3 %collective-permute-start.28 = (bf16[128,128]{1,0:T(8,128)(2,1)S(1)}, bf16[128,128]{1,0:T(8,128)(2,1)S(1)}, u32[]{:S(2)}, u32[]{:S(2)}) collective-permute-start(bf16[128,128]{1,0:T(8,128)(2,1)S(1)} %get-tuple-element.80), channel_id=1, source_target_pairs={{0,1},{1,0},{2,3},{3,2},{4,5},{5,4},{6,7},{7,6},{8,9},{9,8},{10,11... | collective-permute-start | bytes 98312 | tf_op jit(solution)/shard_map/ppermute | solution.py:35
  127.0 11.5 %collective-permute-start.29 = (bf16[128,128]{1,0:T(8,128)(2,1)S(1)}, bf16[128,128]{1,0:T(8,128)(2,1)S(1)}, u32[]{:S(2)}, u32[]{:S(2)}) collective-permute-start(bf16[128,128]{1,0:T(8,128)(2,1)S(1)} %get-tuple-element.81), channel_id=1, source_target_pairs={{0,2},{1,3},{2,0},{3,1},{4,6},{5,7},{6,4},{7,5},{8,10},{9,11},{10,... | collective-permute-start | bytes 98312 | tf_op jit(solution)/shard_map/ppermute | solution.py:35
  127.2 5.0 %collective-permute-start.39 = (bf16[64,128]{1,0:T(8,128)(2,1)S(1)}, bf16[64,128]{1,0:T(8,128)(2,1)S(1)}, u32[]{:S(2)}, u32[]{:S(2)}) collective-permute-start(bf16[64,128]{1,0:T(8,128)(2,1)S(1)} %get-tuple-element.92), channel_id=1, source_target_pairs={{0,5},{1,4},{2,7},{3,6},{4,1},{5,0},{6,3},{7,2},{8,13},{9,12},{10,... | collective-permute-start | bytes 49160 | tf_op jit(solution)/shard_map/ppermute | solution.py:35
  128.8 5.5 %collective-permute-start.40 = (bf16[64,128]{1,0:T(8,128)(2,1)S(1)}, bf16[64,128]{1,0:T(8,128)(2,1)S(1)}, u32[]{:S(2)}, u32[]{:S(2)}) collective-permute-start(bf16[64,128]{1,0:T(8,128)(2,1)S(1)} %get-tuple-element.93), channel_id=1, source_target_pairs={{0,6},{1,7},{2,4},{3,5},{4,2},{5,3},{6,0},{7,1},{8,14},{9,15},{10,... | collective-permute-start | bytes 49160 | tf_op jit(solution)/shard_map/ppermute | solution.py:35
  131.2 5.1 %collective-permute-start.41 = (bf16[64,128]{1,0:T(8,128)(2,1)S(1)}, bf16[64,128]{1,0:T(8,128)(2,1)S(1)}, u32[]{:S(2)}, u32[]{:S(2)}) collective-permute-start(bf16[64,128]{1,0:T(8,128)(2,1)S(1)} %get-tuple-element.94), channel_id=1, source_target_pairs={{0,7},{1,6},{2,5},{3,4},{4,3},{5,2},{6,1},{7,0},{8,15},{9,14},{10,... | collective-permute-start | bytes 49160 | tf_op jit(solution)/shard_map/ppermute | solution.py:35
  132.3 7.6 %collective-permute-start.30 = (bf16[128,128]{1,0:T(8,128)(2,1)S(1)}, bf16[128,128]{1,0:T(8,128)(2,1)S(1)}, u32[]{:S(2)}, u32[]{:S(2)}) collective-permute-start(bf16[128,128]{1,0:T(8,128)(2,1)S(1)} %get-tuple-element.82), channel_id=1, source_target_pairs={{0,3},{1,2},{2,1},{3,0},{4,7},{5,6},{6,5},{7,4},{8,11},{9,10},{10,... | collective-permute-start | bytes 98312 | tf_op jit(solution)/shard_map/ppermute | solution.py:35
  134.3 5.6 %collective-permute-start.31 = (bf16[128,128]{1,0:T(8,128)(2,1)S(1)}, bf16[128,128]{1,0:T(8,128)(2,1)S(1)}, u32[]{:S(2)}, u32[]{:S(2)}) collective-permute-start(bf16[128,128]{1,0:T(8,128)(2,1)S(1)} %get-tuple-element.83), channel_id=1, source_target_pairs={{0,4},{1,5},{2,6},{3,7},{4,0},{5,1},{6,2},{7,3},{8,12},{9,13},{10,... | collective-permute-start | bytes 98312 | tf_op jit(solution)/shard_map/ppermute | solution.py:35
  136.2 5.1 %collective-permute-start.32 = (bf16[128,128]{1,0:T(8,128)(2,1)S(1)}, bf16[128,128]{1,0:T(8,128)(2,1)S(1)}, u32[]{:S(2)}, u32[]{:S(2)}) collective-permute-start(bf16[128,128]{1,0:T(8,128)(2,1)S(1)} %get-tuple-element.84), channel_id=1, source_target_pairs={{0,5},{1,4},{2,7},{3,6},{4,1},{5,0},{6,3},{7,2},{8,13},{9,12},{10,... | collective-permute-start | bytes 98312 | tf_op jit(solution)/shard_map/ppermute | solution.py:35
  136.3 6.0 %collective-permute-start.33 = (bf16[128,128]{1,0:T(8,128)(2,1)S(1)}, bf16[128,128]{1,0:T(8,128)(2,1)S(1)}, u32[]{:S(2)}, u32[]{:S(2)}) collective-permute-start(bf16[128,128]{1,0:T(8,128)(2,1)S(1)} %get-tuple-element.85), channel_id=1, source_target_pairs={{0,6},{1,7},{2,4},{3,5},{4,2},{5,3},{6,0},{7,1},{8,14},{9,15},{10,... | collective-permute-start | bytes 98312 | tf_op jit(solution)/shard_map/ppermute | solution.py:35
  138.5 9.4 %collective-permute-start.42 = (bf16[64,512]{1,0:T(8,128)(2,1)S(1)}, bf16[64,512]{1,0:T(8,128)(2,1)S(1)}, u32[]{:S(2)}, u32[]{:S(2)}) collective-permute-start(bf16[64,512]{1,0:T(8,128)(2,1)S(1)} %get-tuple-element.96), channel_id=1, source_target_pairs={{0,1},{1,0},{2,3},{3,2},{4,5},{5,4},{6,7},{7,6},{8,9},{9,8},{10,11... | collective-permute-start | bytes 196616 | tf_op jit(solution)/shard_map/ppermute | solution.py:35
  139.9 10.3 %collective-permute-start.43 = (bf16[64,512]{1,0:T(8,128)(2,1)S(1)}, bf16[64,512]{1,0:T(8,128)(2,1)S(1)}, u32[]{:S(2)}, u32[]{:S(2)}) collective-permute-start(bf16[64,512]{1,0:T(8,128)(2,1)S(1)} %get-tuple-element.97), channel_id=1, source_target_pairs={{0,2},{1,3},{2,0},{3,1},{4,6},{5,7},{6,4},{7,5},{8,10},{9,11},{10,... | collective-permute-start | bytes 196616 | tf_op jit(solution)/shard_map/ppermute | solution.py:35
  140.0 10.7 %collective-permute-start.44 = (bf16[64,512]{1,0:T(8,128)(2,1)S(1)}, bf16[64,512]{1,0:T(8,128)(2,1)S(1)}, u32[]{:S(2)}, u32[]{:S(2)}) collective-permute-start(bf16[64,512]{1,0:T(8,128)(2,1)S(1)} %get-tuple-element.98), channel_id=1, source_target_pairs={{0,3},{1,2},{2,1},{3,0},{4,7},{5,6},{6,5},{7,4},{8,11},{9,10},{10,... | collective-permute-start | bytes 196616 | tf_op jit(solution)/shard_map/ppermute | solution.py:35
  141.3 11.3 %collective-permute-start.45 = (bf16[64,512]{1,0:T(8,128)(2,1)S(1)}, bf16[64,512]{1,0:T(8,128)(2,1)S(1)}, u32[]{:S(2)}, u32[]{:S(2)}) collective-permute-start(bf16[64,512]{1,0:T(8,128)(2,1)S(1)} %get-tuple-element.99), channel_id=1, source_target_pairs={{0,4},{1,5},{2,6},{3,7},{4,0},{5,1},{6,2},{7,3},{8,12},{9,13},{10,... | collective-permute-start | bytes 196616 | tf_op jit(solution)/shard_map/ppermute | solution.py:35
  142.3 5.5 %collective-permute-start.34 = (bf16[128,128]{1,0:T(8,128)(2,1)S(1)}, bf16[128,128]{1,0:T(8,128)(2,1)S(1)}, u32[]{:S(2)}, u32[]{:S(2)}) collective-permute-start(bf16[128,128]{1,0:T(8,128)(2,1)S(1)} %get-tuple-element.86), channel_id=1, source_target_pairs={{0,7},{1,6},{2,5},{3,4},{4,3},{5,2},{6,1},{7,0},{8,15},{9,14},{10,... | collective-permute-start | bytes 98312 | tf_op jit(solution)/shard_map/ppermute | solution.py:35
  147.8 15.0 %collective-permute-start.14 = (bf16[128,384]{1,0:T(8,128)(2,1)S(1)}, bf16[128,384]{1,0:T(8,128)(2,1)S(1)}, u32[]{:S(2)}, u32[]{:S(2)}) collective-permute-start(bf16[128,384]{1,0:T(8,128)(2,1)S(1)} %get-tuple-element.63), channel_id=1, source_target_pairs={{0,1},{1,0},{2,3},{3,2},{4,5},{5,4},{6,7},{7,6},{8,9},{9,8},{10,11... | collective-permute-start | bytes 294920 | tf_op jit(solution)/shard_map/ppermute | solution.py:35
  147.9 17.3 %collective-permute-start.15 = (bf16[128,384]{1,0:T(8,128)(2,1)S(1)}, bf16[128,384]{1,0:T(8,128)(2,1)S(1)}, u32[]{:S(2)}, u32[]{:S(2)}) collective-permute-start(bf16[128,384]{1,0:T(8,128)(2,1)S(1)} %get-tuple-element.64), channel_id=1, source_target_pairs={{0,2},{1,3},{2,0},{3,1},{4,6},{5,7},{6,4},{7,5},{8,10},{9,11},{10,... | collective-permute-start | bytes 294920 | tf_op jit(solution)/shard_map/ppermute | solution.py:35
  150.2 9.3 %collective-permute-start.46 = (bf16[64,512]{1,0:T(8,128)(2,1)S(1)}, bf16[64,512]{1,0:T(8,128)(2,1)S(1)}, u32[]{:S(2)}, u32[]{:S(2)}) collective-permute-start(bf16[64,512]{1,0:T(8,128)(2,1)S(1)} %get-tuple-element.100), channel_id=1, source_target_pairs={{0,5},{1,4},{2,7},{3,6},{4,1},{5,0},{6,3},{7,2},{8,13},{9,12},{10,... | collective-permute-start | bytes 196616 | tf_op jit(solution)/shard_map/ppermute | solution.py:35
  150.7 8.8 %collective-permute-start.47 = (bf16[64,512]{1,0:T(8,128)(2,1)S(1)}, bf16[64,512]{1,0:T(8,128)(2,1)S(1)}, u32[]{:S(2)}, u32[]{:S(2)}) collective-permute-start(bf16[64,512]{1,0:T(8,128)(2,1)S(1)} %get-tuple-element.101), channel_id=1, source_target_pairs={{0,6},{1,7},{2,4},{3,5},{4,2},{5,3},{6,0},{7,1},{8,14},{9,15},{10,... | collective-permute-start | bytes 196616 | tf_op jit(solution)/shard_map/ppermute | solution.py:35
  152.6 9.3 %collective-permute-start.48 = (bf16[64,512]{1,0:T(8,128)(2,1)S(1)}, bf16[64,512]{1,0:T(8,128)(2,1)S(1)}, u32[]{:S(2)}, u32[]{:S(2)}) collective-permute-start(bf16[64,512]{1,0:T(8,128)(2,1)S(1)} %get-tuple-element.102), channel_id=1, source_target_pairs={{0,7},{1,6},{2,5},{3,4},{4,3},{5,2},{6,1},{7,0},{8,15},{9,14},{10,... | collective-permute-start | bytes 196616 | tf_op jit(solution)/shard_map/ppermute | solution.py:35
  159.5 8.3 %collective-permute-start.16 = (bf16[128,384]{1,0:T(8,128)(2,1)}, bf16[128,384]{1,0:T(8,128)(2,1)S(1)}, u32[]{:S(2)}, u32[]{:S(2)}) collective-permute-start(bf16[128,384]{1,0:T(8,128)(2,1)} %get-tuple-element.65), channel_id=1, source_target_pairs={{0,3},{1,2},{2,1},{3,0},{4,7},{5,6},{6,5},{7,4},{8,11},{9,10},{10,... | collective-permute-start | bytes 294920 | tf_op jit(solution)/shard_map/ppermute | solution.py:35
  159.5 15.0 %collective-permute-start.17 = (bf16[128,384]{1,0:T(8,128)(2,1)}, bf16[128,384]{1,0:T(8,128)(2,1)S(1)}, u32[]{:S(2)}, u32[]{:S(2)}) collective-permute-start(bf16[128,384]{1,0:T(8,128)(2,1)} %get-tuple-element.66), channel_id=1, source_target_pairs={{0,4},{1,5},{2,6},{3,7},{4,0},{5,1},{6,2},{7,3},{8,12},{9,13},{10,... | collective-permute-start | bytes 294920 | tf_op jit(solution)/shard_map/ppermute | solution.py:35
  161.9 13.6 %collective-permute-start.18 = (bf16[128,384]{1,0:T(8,128)(2,1)}, bf16[128,384]{1,0:T(8,128)(2,1)S(1)}, u32[]{:S(2)}, u32[]{:S(2)}) collective-permute-start(bf16[128,384]{1,0:T(8,128)(2,1)} %get-tuple-element.67), channel_id=1, source_target_pairs={{0,5},{1,4},{2,7},{3,6},{4,1},{5,0},{6,3},{7,2},{8,13},{9,12},{10,... | collective-permute-start | bytes 294920 | tf_op jit(solution)/shard_map/ppermute | solution.py:35
  162.8 12.7 %collective-permute-start.19 = (bf16[128,384]{1,0:T(8,128)(2,1)S(1)}, bf16[128,384]{1,0:T(8,128)(2,1)S(1)}, u32[]{:S(2)}, u32[]{:S(2)}) collective-permute-start(bf16[128,384]{1,0:T(8,128)(2,1)S(1)} %get-tuple-element.68), channel_id=1, source_target_pairs={{0,6},{1,7},{2,4},{3,5},{4,2},{5,3},{6,0},{7,1},{8,14},{9,15},{10,... | collective-permute-start | bytes 294920 | tf_op jit(solution)/shard_map/ppermute | solution.py:35
  165.2 10.4 %collective-permute-start.20 = (bf16[128,384]{1,0:T(8,128)(2,1)S(1)}, bf16[128,384]{1,0:T(8,128)(2,1)S(1)}, u32[]{:S(2)}, u32[]{:S(2)}) collective-permute-start(bf16[128,384]{1,0:T(8,128)(2,1)S(1)} %get-tuple-element.69), channel_id=1, source_target_pairs={{0,7},{1,6},{2,5},{3,4},{4,3},{5,2},{6,1},{7,0},{8,15},{9,14},{10,... | collective-permute-start | bytes 294920 | tf_op jit(solution)/shard_map/ppermute | solution.py:35
  (24 other events, 341.4 us)

commit v2 on v1

v2 whole, which is shorter than its diff:
```python
import functools
import math

import jax
import jax.numpy as jnp
from jax import lax
from jax.experimental import pallas as pl
from jax.experimental.pallas import tpu as pltpu
from jax.sharding import PartitionSpec as P

H = 32
HIDDEN = -1e30
VMEM = 48 * 1024 * 1024
NT = (((1,), (1,)), ((), ()))
TN = (((0,), (0,)), ((), ()))
NN = (((1,), (0,)), ((), ()))


def mm(a, b, dims=NN):
    return lax.dot_general(a, b, dims, preferred_element_type=jnp.float32)


def params():
    return pltpu.CompilerParams(vmem_limit_bytes=VMEM)


SMEM = pl.BlockSpec(memory_space=pltpu.SMEM)
HBM = pl.BlockSpec(memory_space=pltpu.HBM)
LANES = 128


def exchange(blocks, count, targets=None):
    got = {0: blocks[0]}
    for k in range(count - 1, 0, -1):
        pairs = [(i, i ^ k) for i in range(count) if targets is None or i ^ k in targets]
        got[k] = lax.ppermute(blocks[k], "context", pairs)
    return [got[k] for k in range(count)]


def pack_copies(count, group, hd, first, nh, me, refs, outs, sems):
    tok = refs[0].shape[0]
    copies = []
    for k in range(count):
        for h in range(nh):
            column = pl.multiple_of((me ^ k) * group + (first + h) * hd, LANES)
            for t, ref in enumerate(refs):
                n = h * 3 + t
                copies.append(
                    pltpu.make_async_copy(
                        ref.at[:, pl.ds(column, hd)],
                        outs[k].at[pl.ds(n * tok, tok), :],
                        sems.at[k * nh * 3 + n],
                    )
                )
    return copies


def pack_kernel(count, group, hd, first, nh, me_ref, q_ref, k_ref, v_ref, _, *rest):
    outs, sems = rest[:count], rest[count]
    copies = pack_copies(
        count, group, hd, first, nh, me_ref[0], (q_ref, k_ref, v_ref), outs, sems
    )
    for copy in copies:
        copy.start()
    for copy in copies:
        copy.wait()


def pack(me, q, k, v, after, count, hd, first, nh):
    tok, model = q.shape
    return pl.pallas_call(
        functools.partial(pack_kernel, count, model // count, hd, first, nh),
        out_shape=[jax.ShapeDtypeStruct((nh * 3 * tok, hd), q.dtype)] * count,
        in_specs=[SMEM, HBM, HBM, HBM, HBM],
        out_specs=[HBM] * count,
        scratch_shapes=[pltpu.SemaphoreType.DMA((3 * nh * count,))],
        compiler_params=params(),
        name="pack",
    )(me, q, k, v, after)


def first_kernel(count, group, hd, nh, mask_rows, tiles, me_ref, nb_ref, *rest):
    q_ref, k_ref, v_ref, x_ref, down_ref = rest[:5]
    outs, rest = rest[5 : 5 + count], rest[5 + count :]
    x_s, down_s, note_s, sems, in_sems, note_sems = rest
    me = me_ref[0]
    tok = q_ref.shape[0]
    rank = down_ref.shape[1]
    loads = [
        pltpu.make_async_copy(x_ref, x_s, in_sems.at[0]),
        pltpu.make_async_copy(down_ref, down_s, in_sems.at[1]),
    ]
    copies = pack_copies(count, group, hd, 0, nh, me, (q_ref, k_ref, v_ref), outs, sems)
    for copy in loads + copies:
        copy.start()
    rows = lax.broadcasted_iota(jnp.int32, (mask_rows, tok), 0)
    lane_tile = lax.broadcasted_iota(jnp.int32, (mask_rows, tok), 1) // (tok // tiles)
    seen = jnp.zeros((mask_rows, tok), jnp.float32)
    for t in range(tiles):
        for n in range(nb_ref.shape[1]):
            slot = nb_ref[t, n] - (me - 1) * tiles
            seen = jnp.where((rows == slot) & (lane_tile == t), 1.0, seen)
    note_s[rank:, :] = seen.astype(jnp.bfloat16)
    for copy in loads:
        copy.wait()
    note_s[:rank, :] = mm(x_s[...], down_s[...]).T.astype(jnp.bfloat16)
    notes = [
        pltpu.make_async_copy(
            note_s, outs[k].at[pl.ds(nh * 3 * tok, rank + mask_rows), :], note_sems.at[k]
        )
        for k in range(count)
    ]
    for copy in notes:
        copy.start()
    for copy in copies + notes:
        copy.wait()


def first_pack(me, nb, q, k, v, x, down, count, hd, nh, mask_rows):
    tok, model = q.shape
    rank = down.shape[1]
    rows = nh * 3 * tok + rank + mask_rows
    bf = q.dtype
    return pl.pallas_call(
        functools.partial(
            first_kernel, count, model // count, hd, nh, mask_rows, nb.shape[0]
        ),
        out_shape=[jax.ShapeDtypeStruct((rows, hd), bf)] * count,
        in_specs=[SMEM, SMEM] + [HBM] * 5,
        out_specs=[HBM] * count,
        scratch_shapes=[
            pltpu.VMEM(x.shape, bf),
            pltpu.VMEM(down.shape, bf),
            pltpu.VMEM((rank + mask_rows, tok), bf),
            pltpu.SemaphoreType.DMA((3 * nh * count,)),
            pltpu.SemaphoreType.DMA((2,)),
            pltpu.SemaphoreType.DMA((count,)),
        ],
        compiler_params=params(),
        name="first_pack",
    )(me, nb, q, k, v, x, down)


def assemble_kernel(count, group, me_ref, home_ref, *rest):
    refs, out, sems = rest[:count], rest[count], rest[count + 1]
    me = me_ref[0]

    @pl.when((me == count // 2 - 1) | (me == count // 2))
    def _():
        copies = []
        for k in range(count):
            column = pl.multiple_of((me ^ k) * group, LANES)
            copies.append(
                pltpu.make_async_copy(refs[k], out.at[:, pl.ds(column, group)], sems.at[k])
            )
        for copy in copies:
            copy.start()
        for copy in copies:
            copy.wait()


def assemble(me, home, blocks):
    count = len(blocks)
    return pl.pallas_call(
        functools.partial(assemble_kernel, count, home.shape[1] // count),
        out_shape=jax.ShapeDtypeStruct(home.shape, home.dtype),
        in_specs=[SMEM] + [HBM] * (count + 1),
        out_specs=HBM,
        input_output_aliases={1: 0},
        scratch_shapes=[pltpu.SemaphoreType.DMA((count,))],
        compiler_params=params(),
        name="assemble",
    )(me, home, *blocks)


def soft(scores, scale):
    top = jnp.max(scores, axis=0, keepdims=True)
    expo = jnp.exp2((scores - top) * scale)
    return expo, jnp.sum(expo, axis=0, keepdims=True)


def tile_weights(keys, query, mask, slots, scale):
    tok = query.shape[0]
    bias = (mask.astype(jnp.float32)[:slots] - 1.0) * (-HIDDEN)
    scores = mm(keys, query, NT).reshape(slots, 3 * tok // slots, tok) + bias[:, None, :]
    expo, norm = soft(scores.reshape(3 * tok, tok), scale)
    return (expo * (1.0 / norm)).astype(jnp.bfloat16)


def window(me, p, count):
    slab = me ^ p
    low = jnp.where(slab > 0, (slab - 1) ^ me, p)
    high = jnp.where(slab < count - 1, (slab + 1) ^ me, p)
    return low, p, high


def log_scale(hd):
    return hd ** (-0.5) * math.log2(math.e)


def home_kernel(count, slots, rank, me_ref, *rest):
    notes, rest = rest[:count], rest[count:]
    q_ref, k_refs, v_refs, up_ref, out_ref, note_s = (
        rest[0],
        rest[1:4],
        rest[4:7],
        rest[7],
        rest[8],
        rest[9],
    )
    hd = q_ref.shape[1]

    @pl.when(pl.program_id(0) == 0)
    def _():
        for p in range(count):
            note_s[p] = notes[p][...]

    keys = jnp.concatenate([ref[...] for ref in k_refs], axis=0)
    weights = tile_weights(keys, q_ref[...], notes[0][rank:, :], slots, log_scale(hd))
    values = []
    for ref, w in zip(v_refs, window(me_ref[0], 0, count)):
        term = mm(up_ref[...], note_s[w][:rank, :])
        values.append((ref[...].T.astype(jnp.float32) + term).astype(jnp.bfloat16))
    out_ref[...] = mm(jnp.concatenate(values, axis=1), weights).T.astype(jnp.bfloat16)


def home_student(me, notes, q, ks, vs, up, hd, slots):
    count = len(notes)
    tok, model = q.shape
    heads = model // hd
    rank = up.shape[1]
    column = pl.BlockSpec((tok, hd), lambda h: (0, h))
    return pl.pallas_call(
        functools.partial(home_kernel, count, slots, rank),
        grid=(heads,),
        out_shape=jax.ShapeDtypeStruct(q.shape, q.dtype),
        in_specs=[SMEM]
        + [pl.BlockSpec(notes[0].shape, lambda h: (0, 0))] * count
        + [column] * 7
        + [pl.BlockSpec((hd, rank), lambda h: (h, 0))],
        out_specs=column,
        scratch_shapes=[pltpu.VMEM((count,) + notes[0].shape, q.dtype)],
        compiler_params=params(),
        cost_estimate=pl.CostEstimate(
            flops=12 * 10**9, bytes_accessed=9 * tok * model * 2, transcendentals=0
        ),
        name="home_student",
    )(me, *notes, q, *ks, *vs, up)


def attention_kernel(count, tok, hd, slots, rank, before, last, factor, me_ref, *rest):
    blocks, rest = rest[:count], rest[count:]
    notes, rest = rest[:count], rest[count:]
    up_ref, hid_ref, rest = rest[0], rest[1], rest[2:]
    if before:
        given, rest = rest[:count], rest[count:]
    outs, rest = rest[:count], rest[count:]
    gup_ref, rest = rest[0], rest[1:]
    nh = count if last else 1
    hid_out, rest = rest[:nh], rest[nh:]
    q_s, k_s, vt_s, svt_s, lora_s, grad_s, hid_s, out_s = rest
    head = pl.program_id(0)
    me = me_ref[0]
    scale = log_scale(hd)

    @pl.when(head == 0)
    def _():
        hid_s[...] = hid_ref[...]
        for p in range(count):
            lora_s[:, p * tok : (p + 1) * tok] = notes[p][:rank, :]
            if before:
                outs[p][:, : before * hd] = given[p][...]

    start = pl.multiple_of(head * 3 * tok, tok)
    for p in range(count):
        q_s[p] = blocks[p][pl.ds(start, tok), :]
        k_s[p * tok : (p + 1) * tok, :] = blocks[p][pl.ds(start + tok, tok), :]
        vt_s[:, p * tok : (p + 1) * tok] = blocks[p][pl.ds(start + 2 * tok, tok), :].T
    up_t = up_ref[...]
    for p in range(count):
        cols = slice(p * tok, (p + 1) * tok)
        term = mm(up_t, lora_s[:, cols], TN)
        svt_s[p] = (vt_s[:, cols].astype(jnp.float32) + term).astype(jnp.bfloat16)
    grad_s[...] = jnp.zeros_like(grad_s)

    for p in range(count):
        query = q_s[p]
        expo, norm = soft(mm(k_s[...], query, NT), scale)
        teacher = mm(vt_s[...], expo.astype(jnp.bfloat16)) / norm
        teacher = teacher.astype(jnp.bfloat16).astype(jnp.float32)

        places = window(me, p, count)
        keys = jnp.concatenate(
            [k_s[pl.ds(pl.multiple_of(w * tok, tok), tok), :] for w in places], axis=0
        )
        weights = tile_weights(keys, query, notes[p][rank:, :], slots, scale)
        values = jnp.concatenate([svt_s[w] for w in places], axis=1)
        student = mm(values, weights)
        out_s[p] = student.T.astype(jnp.bfloat16)
        delta = ((student - teacher) * factor).astype(jnp.bfloat16)
        grads = mm(weights, delta, NT)
        for n, w in enumerate(places):
            grad_s[w] += grads[n * tok : (n + 1) * tok]

    column = pl.multiple_of((before + head) * hd, LANES)
    for p in range(count):
        outs[p][:, pl.ds(column, hd)] = out_s[p]
    grad = grad_s[...].reshape(count * tok, hd).astype(jnp.bfloat16)
    gup_ref[...] = mm(lora_s[...], grad).T
    hid_s[...] += mm(up_t, grad, NT)

    @pl.when(head == pl.num_programs(0) - 1)
    def _():
        if last:
            for p in range(count):
                hid_out[p][...] = hid_s[:, p * tok : (p + 1) * tok].astype(jnp.bfloat16)
        else:
            hid_out[0][...] = hid_s[...]


def attention(me, blocks, notes, up_t, hid, given, first, nh, tok, hd, slots, last):
    count = len(blocks)
    rank = up_t.shape[0]
    bf, f32 = jnp.bfloat16, jnp.float32
    whole = lambda shape: pl.BlockSpec(shape, lambda h: (0,) * len(shape))
    if last:
        hid_shape = [jax.ShapeDtypeStruct((rank, tok), bf)] * count
    else:
        hid_shape = [jax.ShapeDtypeStruct((rank, count * tok), f32)]
    keys = count * tok
    wide = (first + nh) * hd
    out = pl.pallas_call(
        functools.partial(
            attention_kernel, count, tok, hd, slots, rank, first, last, keys ** (-0.5)
        ),
        grid=(nh,),
        out_shape=[jax.ShapeDtypeStruct((tok, wide), bf)] * count
        + [jax.ShapeDtypeStruct((nh * hd, rank), f32)]
        + hid_shape,
        in_specs=[SMEM]
        + [whole(blocks[0].shape)] * count
        + [whole(notes[0].shape)] * count
        + [pl.BlockSpec((rank, hd), lambda h: (0, first + h)), whole((rank, keys))]
        + [whole(g.shape) for g in given],
        out_specs=[whole((tok, wide))] * count
        + [pl.BlockSpec((hd, rank), lambda h: (h, 0))]
        + [whole(s.shape) for s in hid_shape],
        scratch_shapes=[
            pltpu.VMEM((count, tok, hd), bf),
            pltpu.VMEM((keys, hd), bf),
            pltpu.VMEM((hd, keys), bf),
            pltpu.VMEM((count, hd, tok), bf),
            pltpu.VMEM((rank, keys), bf),
            pltpu.VMEM((count, tok, hd), f32),
            pltpu.VMEM((rank, keys), f32),
            pltpu.VMEM((count, tok, hd), bf),
        ],
        compiler_params=params(),
        cost_estimate=pl.CostEstimate(
            flops=nh * 6 * 10**9, bytes_accessed=4 * nh * keys * hd * 2, transcendentals=0
        ),
        name="attention",
    )(me, *blocks, *notes, up_t, hid, *given)
    return out[:count], out[count], out[count + 1 :]


def down_kernel(count, group, me_ref, *rest):
    parts, x_ref, outs = rest[:count], rest[count], rest[count + 1 :]
    me = me_ref[0]
    hidden = parts[0][...].astype(jnp.float32)
    for k in range(1, count):
        hidden += parts[k][...].astype(jnp.float32)
    hidden = hidden.astype(jnp.bfloat16)
    for k in range(count):
        column = pl.multiple_of((me ^ k) * group, 128)
        outs[k][...] = mm(hidden, x_ref[:, pl.ds(column, group)]).astype(jnp.bfloat16)


def down_terms(me, parts, x):
    count = len(parts)
    group = x.shape[1] // count
    rank = parts[0].shape[0]
    vm = pl.BlockSpec(memory_space=pltpu.VMEM)
    return pl.pallas_call(
        functools.partial(down_kernel, count, group),
        out_shape=[jax.ShapeDtypeStruct((rank, group), jnp.bfloat16)] * count,
        in_specs=[SMEM] + [vm] * (count + 1),
        out_specs=[vm] * count,
        compiler_params=params(),
        name="down_terms",
    )(me, *parts, x)


def sum_kernel(count, *refs):
    total = refs[0][...].astype(jnp.float32)
    for k in range(1, count):
        total += refs[k][...].astype(jnp.float32)
    refs[count][...] = total.T


def sum_terms(parts):
    rank, rows = parts[0].shape
    return pl.pallas_call(
        functools.partial(sum_kernel, len(parts)),
        out_shape=jax.ShapeDtypeStruct((rows, rank), jnp.float32),
        compiler_params=params(),
        name="sum_terms",
    )(*parts)


def head_chunks(per_group):
    if per_group < 2:
        return [(0, per_group)]
    return [(0, per_group - 1), (per_group - 1, 1)]


def local(
    queries, keys, values, value_layer_input, adapter_down_weight, adapter_up_weight, neighbors
):
    tok, model = queries.shape
    rank = adapter_down_weight.shape[1]
    count = lax.axis_size("context")
    index = lax.axis_index("context")
    me = index.astype(jnp.int32).reshape(1)
    hd = model // H
    group = model // count
    per_group = H // count
    tiles = neighbors.shape[0]
    slots = 3 * tiles
    chunks = head_chunks(per_group)

    mask_rows = slots + -slots % 16

    rows = chunks[0][1] * 3 * tok
    messages = []
    for c, (first, nh) in enumerate(chunks):
        if c == 0:
            blocks = first_pack(
                me, neighbors, queries, keys, values, value_layer_input, adapter_down_weight,
                count, hd, nh, mask_rows,
            )
        else:
            after = messages[-1][-1]
            blocks = pack(me, queries, keys, values, after, count, hd, first, nh)
        messages.append(exchange(blocks, count))
    notes = [message[rows:] for message in messages[0]]

    half = count // 2
    up_pairs = [(i, i + 1) for i in range(count - 1) if i + 1 != half]
    down_pairs = [(i + 1, i) for i, _ in up_pairs]

    def halo(array):
        low = lax.ppermute(array, "context", up_pairs)
        return low, array, lax.ppermute(array, "context", down_pairs)

    home = home_student(
        me, notes, queries, halo(keys), halo(values), adapter_up_weight, hd, slots
    )

    up_t = lax.dynamic_slice_in_dim(adapter_up_weight, index * group, group, 0).T
    hid = jnp.zeros((rank, count * tok), jnp.float32)
    outs, grad_up = [], []
    for c, (first, nh) in enumerate(chunks):
        last = c == len(chunks) - 1
        outs, gup, hid = attention(
            me, messages[c], notes, up_t, hid, outs, first, nh, tok, hd, slots, last
        )
        hid = hid if last else hid[0]
        grad_up.append(gup)
    terms = exchange(down_terms(me, exchange(hid, count), value_layer_input), count)
    grad_down = sum_terms(terms)
    student_out = assemble(me, home, exchange(outs, count, (half - 1, half)))
    return student_out, grad_down, jnp.concatenate(grad_up, axis=0)


def solution(mesh):
    rows = P(("video", "context"), None)
    return jax.shard_map(
        local,
        mesh=mesh,
        in_specs=(rows, rows, rows, rows, P(), P(), rows),
        out_specs=(rows, rows, rows),
        check_vma=False,
    )
```

time: 180 us -> 243 us (1.35)
  the two profiles are of different devices: /device:TPU:0 before, /device:TPU:11 now
where the time goes in v2:
time: 243 us; the launch traced here: 239 us
  waiting for transfers between devices  88.2 us (36%)
  Pallas kernels  56.7 us (23%)
  starting transfers between devices  56.7 us (23%)
  local copies, waits for them, and re-layouts  35.4 us (15%)
    ppermute x35, waiting for transfers between devices, exchange(): got[k] = lax.ppermute(blocks[k], 'context', pairs)  88.2 us
    ppermute x35, starting transfers between devices, exchange(): got[k] = lax.ppermute(blocks[k], 'context', pairs)  44 us
    unnamed x110, local copies, waits for them, and re-layouts  30.8 us
    pallas_call x1, Pallas kernels, home_student(): pl.pallas_call(functools.partial(home_kernel, count, slots, rank), grid=(...  24.1 us
    pallas_call x2, Pallas kernels, attention(): pl.pallas_call(functools.partial(attention_kernel, count, tok, hd, slots,...  21.9 us
    ppermute x2, starting transfers between devices, halo(): return (low, array, lax.ppermute(array, 'context', down_pairs))  9.98 us
    pallas_call x1, Pallas kernels, assemble(): pl.pallas_call(functools.partial(assemble_kernel, count, home.shape[1] //...  5.16 us
  transfers between devices with their start and end apart: 39, of which 20 were waited for; matrix products, arithmetic and copies ran while one was open for 4% of the time, Pallas kernels for 20%

profile of v2, /device:TPU:11, one launch (start us, length us, event | category | flops | bytes accessed | tf_op | source)
XLA Modules:
  0.0 239.0 jit_solution(8327707814121543577)
XLA Ops:
  0.6 2.4 %copy.11.rest_4_ = bf16[4096,64]{1,0:T(8,128)(2,1)} copy(bf16[4096,64]{0,1:T(8,128)(2,1)} %param.11) | data formatting | bytes 1048576 | tf_op args[4]
  6.2 4.6 %first_pack.1 = (bf16[1232,128]{1,0:T(8,128)(2,1)S(1)}, bf16[1232,128]{1,0:T(8,128)(2,1)S(1)}, bf16[1232,128]{1,0:T(8,128)(2,1)}, bf16[1232,128]{1,0:T(8,128)(2,...) custom-call(s32[1]{0:T(128)} %bitcast.me_ref, ...), custom_call_target="tpu_custom_call" | custom-call | tf_op jit(solution)/shard_map/first_pack/pallas_call | solution.py:124
  10.8 1.9 collective-permute-start.6
  12.8 2.2 collective-permute-start.1
  15.9 12.1 %collective-permute-done.6._.rest_7_ = bf16[1232,128]{1,0:T(8,128)(2,1)S(1)} collective-permute-done((bf16[1232,128]{1,0:T(8,128)(2,1)S(1)}, bf16[1232,128]{1,0:T(8,128)(2,1)S(1)}, u32[]{:S(2)}, u32[]{:S(2)}) %collective-permute-start.6) | collective-permute-done | bytes 315424 | tf_op jit(solution)/shard_map/ppermute | solution.py:36
  30.4 4.7 %collective-permute-done.1.rest_2_ = bf16[1232,128]{1,0:T(8,128)(2,1)} collective-permute-done((bf16[1232,128]{1,0:T(8,128)(2,1)}, bf16[1232,128]{1,0:T(8,128)(2,1)}, u32[]{:S(2)}, u32[]{:S(2)}) %collective-permute-start.1) | collective-permute-done | bytes 315424 | tf_op jit(solution)/shard_map/ppermute | solution.py:36
  35.8 6.2 %collective-permute-done.2.rest_3_ = bf16[1232,128]{1,0:T(8,128)(2,1)} collective-permute-done((bf16[1232,128]{1,0:T(8,128)(2,1)}, bf16[1232,128]{1,0:T(8,128)(2,1)}, u32[]{:S(2)}, u32[]{:S(2)}) %collective-permute-start.2) | collective-permute-done | bytes 315424 | tf_op jit(solution)/shard_map/ppermute | solution.py:36
  42.0 2.3 collective-permute-start.12
  47.6 13.1 %collective-permute-done.4.rest_5_ = bf16[1232,128]{1,0:T(8,128)(2,1)} collective-permute-done((bf16[1232,128]{1,0:T(8,128)(2,1)}, bf16[1232,128]{1,0:T(8,128)(2,1)}, u32[]{:S(2)}, u32[]{:S(2)}) %collective-permute-start.4) | collective-permute-done | bytes 315424 | tf_op jit(solution)/shard_map/ppermute | solution.py:36
  60.8 3.1 %collective-permute-start.14 = (bf16[384,128]{1,0:T(8,128)(2,1)S(1)}, bf16[384,128]{1,0:T(8,128)(2,1)S(1)}, u32[]{:S(2)}, u32[]{:S(2)}) collective-permute-start(bf16[384,128]{1,0:T(8,128)(2,1)S(1)} %get-tuple-element.66), channel_id=1, source_target_pairs={{0,4},{1,5},{2,6},{3,7},{4,0},{5,1},{6,2},{7,3},{8,12},{9,13},{10,... | collective-permute-start | bytes 294920 | tf_op jit(solution)/shard_map/ppermute | solution.py:36
  64.6 5.8 %collective-permute-done.5.rest_6_ = bf16[1232,128]{1,0:T(8,128)(2,1)} collective-permute-done((bf16[1232,128]{1,0:T(8,128)(2,1)}, bf16[1232,128]{1,0:T(8,128)(2,1)}, u32[]{:S(2)}, u32[]{:S(2)}) %collective-permute-start.5) | collective-permute-done | bytes 315424 | tf_op jit(solution)/shard_map/ppermute | solution.py:36
  71.1 1.4 collective-permute-start.16
  73.5 16.3 %attention.2 = (bf16[128,384]{1,0:T(8,128)(2,1)S(1)}, bf16[128,384]{1,0:T(8,128)(2,1)S(1)}, bf16[128,384]{1,0:T(8,128)(2,1)S(1)}, bf16[128,384]{1,0:T(8,128)(2,1...) custom-call(s32[1]{0:T(128)} %bitcast.me_ref, ...), custom_call_target="tpu_custom_call" | custom-call | flops 17999998976 | bytes 3145728 | tf_op jit(solution)/shard_map/attention/pallas_call | solution.py:332
  90.5 2.7 %collective-permute-start.10 = (bf16[128,4096]{1,0:T(8,128)(2,1)S(1)}, bf16[128,4096]{1,0:T(8,128)(2,1)}, u32[]{:S(2)}, u32[]{:S(2)}) collective-permute-start(bf16[128,4096]{1,0:T(8,128)(2,1)S(1)} %copy-done.4), channel_id=1, source_target_pairs={{1,0},{2,1},{3,2},{5,4},{6,5},{7,6},{9,8},{10,9},{11,10},{13,12},{... | collective-permute-start | bytes 3145736 | tf_op jit(solution)/shard_map/ppermute | solution.py:454
  93.3 1.3 collective-permute-start.7
  94.6 7.2 %collective-permute-start.8 = (bf16[128,4096]{1,0:T(8,128)(2,1)S(1)}, bf16[128,4096]{1,0:T(8,128)(2,1)}, u32[]{:S(2)}, u32[]{:S(2)}) collective-permute-start(bf16[128,4096]{1,0:T(8,128)(2,1)S(1)} %copy-done.2), channel_id=1, source_target_pairs={{1,0},{2,1},{3,2},{5,4},{6,5},{7,6},{9,8},{10,9},{11,10},{13,12},{... | collective-permute-start | bytes 3145736 | tf_op jit(solution)/shard_map/ppermute | solution.py:454
  101.8 1.5 collective-permute-start.9
  104.1 5.5 %attention.3 = (bf16[128,512]{1,0:T(8,128)(2,1)S(1)}, bf16[128,512]{1,0:T(8,128)(2,1)S(1)}, bf16[128,512]{1,0:T(8,128)(2,1)}, bf16[128,512]{1,0:T(8,128)(2,1)S(1...) custom-call(s32[1]{0:T(128)} %bitcast.me_ref, ...), custom_call_target="tpu_custom_call" | custom-call | flops 6000000000 | bytes 1048576 | tf_op jit(solution)/shard_map/attention/pallas_call | solution.py:332
  109.6 1.5 collective-permute-start.25
  111.9 1.7 collective-permute-start.26
  113.6 10.6 %collective-permute-done.26.rest_2_ = bf16[64,128]{1,0:T(8,128)(2,1)S(1)} collective-permute-done((bf16[64,128]{1,0:T(8,128)(2,1)S(1)}, bf16[64,128]{1,0:T(8,128)(2,1)S(1)}, u32[]{:S(2)}, u32[]{:S(2)}) %collective-permute-start.26) | collective-permute-done | bytes 16416 | tf_op jit(solution)/shard_map/ppermute | solution.py:36
  124.2 3.2 %collective-permute-done.27.rest_3_ = bf16[64,128]{1,0:T(8,128)(2,1)S(1)} collective-permute-done((bf16[64,128]{1,0:T(8,128)(2,1)S(1)}, bf16[64,128]{1,0:T(8,128)(2,1)S(1)}, u32[]{:S(2)}, u32[]{:S(2)}) %collective-permute-start.27) | collective-permute-done | bytes 16416 | tf_op jit(solution)/shard_map/ppermute | solution.py:36
  127.4 3.5 %collective-permute-done.28.rest_4_ = bf16[64,128]{1,0:T(8,128)(2,1)S(1)} collective-permute-done((bf16[64,128]{1,0:T(8,128)(2,1)S(1)}, bf16[64,128]{1,0:T(8,128)(2,1)S(1)}, u32[]{:S(2)}, u32[]{:S(2)}) %collective-permute-start.28) | collective-permute-done | bytes 16416 | tf_op jit(solution)/shard_map/ppermute | solution.py:36
  130.9 4.1 %collective-permute-done.29.rest_5_ = bf16[64,128]{1,0:T(8,128)(2,1)S(1)} collective-permute-done((bf16[64,128]{1,0:T(8,128)(2,1)S(1)}, bf16[64,128]{1,0:T(8,128)(2,1)S(1)}, u32[]{:S(2)}, u32[]{:S(2)}) %collective-permute-start.29) | collective-permute-done | bytes 16416 | tf_op jit(solution)/shard_map/ppermute | solution.py:36
  134.9 2.6 %collective-permute-done.30.rest_6_ = bf16[64,128]{1,0:T(8,128)(2,1)S(1)} collective-permute-done((bf16[64,128]{1,0:T(8,128)(2,1)S(1)}, bf16[64,128]{1,0:T(8,128)(2,1)S(1)}, u32[]{:S(2)}, u32[]{:S(2)}) %collective-permute-start.30) | collective-permute-done | bytes 16416 | tf_op jit(solution)/shard_map/ppermute | solution.py:36
  138.5 2.1 collective-permute-done.31.rest_7_
  143.5 5.7 %collective-permute-start.33 = (bf16[64,512]{1,0:T(8,128)(2,1)S(1)}, bf16[64,512]{1,0:T(8,128)(2,1)S(1)}, u32[]{:S(2)}, u32[]{:S(2)}) collective-permute-start(bf16[64,512]{1,0:T(8,128)(2,1)S(1)} %get-tuple-element.97), channel_id=1, source_target_pairs={{0,2},{1,3},{2,0},{3,1},{4,6},{5,7},{6,4},{7,5},{8,10},{9,11},{10,... | collective-permute-start | bytes 196616 | tf_op jit(solution)/shard_map/ppermute | solution.py:36
  149.3 2.2 collective-permute-done.33.refs_2_
  152.1 2.3 collective-permute-start.34
  154.4 2.2 collective-permute-done.34.refs_3_
  157.3 4.0 %collective-permute-done.35.refs_4_ = bf16[64,512]{1,0:T(8,128)(2,1)S(1)} collective-permute-done((bf16[64,512]{1,0:T(8,128)(2,1)S(1)}, bf16[64,512]{1,0:T(8,128)(2,1)S(1)}, u32[]{:S(2)}, u32[]{:S(2)}) %collective-permute-start.35) | collective-permute-done | bytes 65568 | tf_op jit(solution)/shard_map/ppermute | solution.py:36
  161.9 2.7 %collective-permute-start.36 = (bf16[64,512]{1,0:T(8,128)(2,1)S(1)}, bf16[64,512]{1,0:T(8,128)(2,1)S(1)}, u32[]{:S(2)}, u32[]{:S(2)}) collective-permute-start(bf16[64,512]{1,0:T(8,128)(2,1)S(1)} %get-tuple-element.100), channel_id=1, source_target_pairs={{0,5},{1,4},{2,7},{3,6},{4,1},{5,0},{6,3},{7,2},{8,13},{9,12},{10,... | collective-permute-start | bytes 196616 | tf_op jit(solution)/shard_map/ppermute | solution.py:36
  164.6 2.9 %collective-permute-done.36.refs_5_ = bf16[64,512]{1,0:T(8,128)(2,1)S(1)} collective-permute-done((bf16[64,512]{1,0:T(8,128)(2,1)S(1)}, bf16[64,512]{1,0:T(8,128)(2,1)S(1)}, u32[]{:S(2)}, u32[]{:S(2)}) %collective-permute-start.36) | collective-permute-done | bytes 65568 | tf_op jit(solution)/shard_map/ppermute | solution.py:36
  169.0 2.3 collective-permute-done.37.refs_6_
  171.9 2.1 collective-permute-start.38
  174.0 1.9 collective-permute-done.38.refs_7_
  176.6 1.3 collective-permute-start.18
  177.9 2.9 %collective-permute-done.18.rest_1_ = bf16[128,512]{1,0:T(8,128)(2,1)S(1)} collective-permute-done((bf16[128,512]{1,0:T(8,128)(2,1)S(1)}, bf16[128,512]{1,0:T(8,128)(2,1)S(1)}, u32[]{:S(2)}, u32[]{:S(2)}) %collective-permute-start.18) | collective-permute-done | bytes 131104 | tf_op jit(solution)/shard_map/ppermute | solution.py:36
  181.4 1.4 collective-permute-start.19
  182.9 2.4 copy.12.rest_15_
  186.0 1.7 copy.14
  195.3 1.3 collective-permute-start.20
  196.6 1.3 collective-permute-start.21
  197.9 1.3 collective-permute-start.22
  199.3 1.3 collective-permute-start.23
  200.6 3.1 %collective-permute-start.24 = (bf16[128,512]{1,0:T(8,128)(2,1)}, bf16[128,512]{1,0:T(8,128)(2,1)S(1)}, u32[]{:S(2)}, u32[]{:S(2)}) collective-permute-start(bf16[128,512]{1,0:T(8,128)(2,1)} %copy-done.48), channel_id=1, source_target_pairs={{3,4},{4,3},{11,12},{12,11},{19,20},{20,19},{27,28},{28,27}} | collective-permute-start | bytes 393224 | tf_op jit(solution)/shard_map/ppermute | solution.py:36
  209.5 24.1 %home_student.1.home_ref = bf16[128,4096]{1,0:T(8,128)(2,1)} custom-call(s32[1]{0:T(128)} %bitcast.me_ref, bf16[80,128]{1,0:T(8,128)(2,1)S(1)} %copy-done.28, bf16[80,128]{1,0:T(8,128)(2,1)S(1)} %copy-done.32, bf16[80,128]{1,0:T(8,128)(2,1)S(1)} %copy-done.34, bf16[80,128]{1,0:T(8,128)(2,1)S(1)} %copy-done.36, bf16[80,128]{1,0:T(8,128)(2,1)S(1)} %copy-done.38, ...), custom_call_target="tpu_custom_call" | custom-call | flops 12000000000 | bytes 9437184 | tf_op jit(solution)/shard_map/home_student/pallas_call | solution.py:233
  233.6 5.2 %assemble.1 = bf16[128,4096]{1,0:T(8,128)(2,1)} custom-call(s32[1]{0:T(128)} %bitcast.me_ref, bf16[128,4096]{1,0:T(8,128)(2,1)} %home_student.1.home_ref, bf16[128,512]{1,0:T(8,128)(2,1)S(1)} %get-tuple-element.79.rest_0_, bf16[128,512]{1,0:T(8,128)(2,1)S(1)} %copy-done.9, ...), custom_call_target="tpu_custom_call", output_to_operand_aliasing={{}: (1, {})} | custom-call | tf_op jit(solution)/shard_map/assemble/pallas_call | solution.py:164
  (159 shorter events, 38.4 us)
Async XLA Ops:
  10.8 17.1 %collective-permute-start.6 = (bf16[1232,128]{1,0:T(8,128)(2,1)S(1)}, bf16[1232,128]{1,0:T(8,128)(2,1)S(1)}, u32[]{:S(2)}, u32[]{:S(2)}) collective-permute-start(bf16[1232,128]{1,0:T(8,128)(2,1)S(1)} %get-tuple-element.61), channel_id=1, source_target_pairs={{0,7},{1,6},{2,5},{3,4},{4,3},{5,2},{6,1},{7,0},{8,15},{9,14},{10,... | collective-permute-start | bytes 946184 | tf_op jit(solution)/shard_map/ppermute | solution.py:36
  12.8 15.2 %collective-permute-start = (bf16[1232,128]{1,0:T(8,128)(2,1)S(1)}, bf16[1232,128]{1,0:T(8,128)(2,1)S(1)}, u32[]{:S(2)}, u32[]{:S(2)}) collective-permute-start(bf16[1232,128]{1,0:T(8,128)(2,1)S(1)} %get-tuple-element.55), channel_id=1, source_target_pairs={{0,1},{1,0},{2,3},{3,2},{4,5},{5,4},{6,7},{7,6},{8,9},{9,8},{10,11... | collective-permute-start | bytes 946184 | tf_op jit(solution)/shard_map/ppermute | solution.py:36
  12.8 22.4 %collective-permute-start.1 = (bf16[1232,128]{1,0:T(8,128)(2,1)}, bf16[1232,128]{1,0:T(8,128)(2,1)}, u32[]{:S(2)}, u32[]{:S(2)}) collective-permute-start(bf16[1232,128]{1,0:T(8,128)(2,1)} %get-tuple-element.56), channel_id=1, source_target_pairs={{0,2},{1,3},{2,0},{3,1},{4,6},{5,7},{6,4},{7,5},{8,10},{9,11},{10,... | collective-permute-start | bytes 946184 | tf_op jit(solution)/shard_map/ppermute | solution.py:36
  15.0 27.1 %collective-permute-start.2 = (bf16[1232,128]{1,0:T(8,128)(2,1)}, bf16[1232,128]{1,0:T(8,128)(2,1)}, u32[]{:S(2)}, u32[]{:S(2)}) collective-permute-start(bf16[1232,128]{1,0:T(8,128)(2,1)} %get-tuple-element.57), channel_id=1, source_target_pairs={{0,3},{1,2},{2,1},{3,0},{4,7},{5,6},{6,5},{7,4},{8,11},{9,10},{10,... | collective-permute-start | bytes 946184 | tf_op jit(solution)/shard_map/ppermute | solution.py:36
  15.4 31.3 %collective-permute-start.3 = (bf16[1232,128]{1,0:T(8,128)(2,1)}, bf16[1232,128]{1,0:T(8,128)(2,1)}, u32[]{:S(2)}, u32[]{:S(2)}) collective-permute-start(bf16[1232,128]{1,0:T(8,128)(2,1)} %get-tuple-element.58), channel_id=1, source_target_pairs={{0,4},{1,5},{2,6},{3,7},{4,0},{5,1},{6,2},{7,3},{8,12},{9,13},{10,... | collective-permute-start | bytes 946184 | tf_op jit(solution)/shard_map/ppermute | solution.py:36
  27.9 32.8 %collective-permute-start.4 = (bf16[1232,128]{1,0:T(8,128)(2,1)}, bf16[1232,128]{1,0:T(8,128)(2,1)}, u32[]{:S(2)}, u32[]{:S(2)}) collective-permute-start(bf16[1232,128]{1,0:T(8,128)(2,1)} %get-tuple-element.59), channel_id=1, source_target_pairs={{0,5},{1,4},{2,7},{3,6},{4,1},{5,0},{6,3},{7,2},{8,13},{9,12},{10,... | collective-permute-start | bytes 946184 | tf_op jit(solution)/shard_map/ppermute | solution.py:36
  27.9 42.5 %collective-permute-start.5 = (bf16[1232,128]{1,0:T(8,128)(2,1)}, bf16[1232,128]{1,0:T(8,128)(2,1)}, u32[]{:S(2)}, u32[]{:S(2)}) collective-permute-start(bf16[1232,128]{1,0:T(8,128)(2,1)} %get-tuple-element.60), channel_id=1, source_target_pairs={{0,6},{1,7},{2,4},{3,5},{4,2},{5,3},{6,0},{7,1},{8,14},{9,15},{10,... | collective-permute-start | bytes 946184 | tf_op jit(solution)/shard_map/ppermute | solution.py:36
  29.9 43.6 %copy-start.26 = (bf16[80,128]{1,0:T(8,128)(2,1)}, bf16[80,128]{1,0:T(8,128)(2,1)S(1)}, u32[]{:S(2)}) copy-start(bf16[80,128]{1,0:T(8,128)(2,1)S(1)} %slice.24.rest_0_.rest_8_) | copy-start | bytes 61444
  35.1 36.0 %collective-permute-start.11 = (bf16[384,128]{1,0:T(8,128)(2,1)S(1)}, bf16[384,128]{1,0:T(8,128)(2,1)S(1)}, u32[]{:S(2)}, u32[]{:S(2)}) collective-permute-start(bf16[384,128]{1,0:T(8,128)(2,1)S(1)} %get-tuple-element.63), channel_id=1, source_target_pairs={{0,1},{1,0},{2,3},{3,2},{4,5},{5,4},{6,7},{7,6},{8,9},{9,8},{10,11... | collective-permute-start | bytes 294920 | tf_op jit(solution)/shard_map/ppermute | solution.py:36
  42.0 30.5 %collective-permute-start.12 = (bf16[384,128]{1,0:T(8,128)(2,1)S(1)}, bf16[384,128]{1,0:T(8,128)(2,1)S(1)}, u32[]{:S(2)}, u32[]{:S(2)}) collective-permute-start(bf16[384,128]{1,0:T(8,128)(2,1)S(1)} %get-tuple-element.64), channel_id=1, source_target_pairs={{0,2},{1,3},{2,0},{3,1},{4,6},{5,7},{6,4},{7,5},{8,10},{9,11},{10,... | collective-permute-start | bytes 294920 | tf_op jit(solution)/shard_map/ppermute | solution.py:36
  45.2 58.1 %copy-start.29 = (bf16[80,128]{1,0:T(8,128)(2,1)}, bf16[80,128]{1,0:T(8,128)(2,1)S(1)}, u32[]{:S(2)}) copy-start(bf16[80,128]{1,0:T(8,128)(2,1)S(1)} %slice.38.rest_7_.rest_15_) | copy-start | bytes 61444
  45.2 58.1 %copy-start.31 = (bf16[80,128]{1,0:T(8,128)(2,1)}, bf16[80,128]{1,0:T(8,128)(2,1)S(1)}, u32[]{:S(2)}) copy-start(bf16[80,128]{1,0:T(8,128)(2,1)S(1)} %slice.32.rest_1_.rest_9_) | copy-start | bytes 61444
  45.9 57.4 %copy-start.33 = (bf16[80,128]{1,0:T(8,128)(2,1)}, bf16[80,128]{1,0:T(8,128)(2,1)S(1)}, u32[]{:S(2)}) copy-start(bf16[80,128]{1,0:T(8,128)(2,1)S(1)} %slice.33.rest_2_.rest_10_) | copy-start | bytes 61444
  46.7 56.6 %copy-start.35 = (bf16[80,128]{1,0:T(8,128)(2,1)}, bf16[80,128]{1,0:T(8,128)(2,1)S(1)}, u32[]{:S(2)}) copy-start(bf16[80,128]{1,0:T(8,128)(2,1)S(1)} %slice.34.rest_3_.rest_11_) | copy-start | bytes 61444
  46.7 43.8 %collective-permute-start.13 = (bf16[384,128]{1,0:T(8,128)(2,1)S(1)}, bf16[384,128]{1,0:T(8,128)(2,1)S(1)}, u32[]{:S(2)}, u32[]{:S(2)}) collective-permute-start(bf16[384,128]{1,0:T(8,128)(2,1)S(1)} %get-tuple-element.65), channel_id=1, source_target_pairs={{0,3},{1,2},{2,1},{3,0},{4,7},{5,6},{6,5},{7,4},{8,11},{9,10},{10,... | collective-permute-start | bytes 294920 | tf_op jit(solution)/shard_map/ppermute | solution.py:36
  47.6 55.7 %copy-start.37 = (bf16[80,128]{1,0:T(8,128)(2,1)}, bf16[80,128]{1,0:T(8,128)(2,1)S(1)}, u32[]{:S(2)}) copy-start(bf16[80,128]{1,0:T(8,128)(2,1)S(1)} %slice.35.rest_4_.rest_12_) | copy-start | bytes 61444
  60.8 32.5 %collective-permute-start.14 = (bf16[384,128]{1,0:T(8,128)(2,1)S(1)}, bf16[384,128]{1,0:T(8,128)(2,1)S(1)}, u32[]{:S(2)}, u32[]{:S(2)}) collective-permute-start(bf16[384,128]{1,0:T(8,128)(2,1)S(1)} %get-tuple-element.66), channel_id=1, source_target_pairs={{0,4},{1,5},{2,6},{3,7},{4,0},{5,1},{6,2},{7,3},{8,12},{9,13},{10,... | collective-permute-start | bytes 294920 | tf_op jit(solution)/shard_map/ppermute | solution.py:36
  64.6 38.8 %copy-start.39 = (bf16[80,128]{1,0:T(8,128)(2,1)}, bf16[80,128]{1,0:T(8,128)(2,1)S(1)}, u32[]{:S(2)}) copy-start(bf16[80,128]{1,0:T(8,128)(2,1)S(1)} %slice.36.rest_5_.rest_13_) | copy-start | bytes 61444
  70.4 24.2 %collective-permute-start.15 = (bf16[384,128]{1,0:T(8,128)(2,1)S(1)}, bf16[384,128]{1,0:T(8,128)(2,1)S(1)}, u32[]{:S(2)}, u32[]{:S(2)}) collective-permute-start(bf16[384,128]{1,0:T(8,128)(2,1)S(1)} %get-tuple-element.67), channel_id=1, source_target_pairs={{0,5},{1,4},{2,7},{3,6},{4,1},{5,0},{6,3},{7,2},{8,13},{9,12},{10,... | collective-permute-start | bytes 294920 | tf_op jit(solution)/shard_map/ppermute | solution.py:36
  71.1 30.7 %collective-permute-start.16 = (bf16[384,128]{1,0:T(8,128)(2,1)S(1)}, bf16[384,128]{1,0:T(8,128)(2,1)S(1)}, u32[]{:S(2)}, u32[]{:S(2)}) collective-permute-start(bf16[384,128]{1,0:T(8,128)(2,1)S(1)} %get-tuple-element.68), channel_id=1, source_target_pairs={{0,6},{1,7},{2,4},{3,5},{4,2},{5,3},{6,0},{7,1},{8,14},{9,15},{10,... | collective-permute-start | bytes 294920 | tf_op jit(solution)/shard_map/ppermute | solution.py:36
  72.6 30.7 %collective-permute-start.17 = (bf16[384,128]{1,0:T(8,128)(2,1)S(1)}, bf16[384,128]{1,0:T(8,128)(2,1)S(1)}, u32[]{:S(2)}, u32[]{:S(2)}) collective-permute-start(bf16[384,128]{1,0:T(8,128)(2,1)S(1)} %get-tuple-element.69), channel_id=1, source_target_pairs={{0,7},{1,6},{2,5},{3,4},{4,3},{5,2},{6,1},{7,0},{8,15},{9,14},{10,... | collective-permute-start | bytes 294920 | tf_op jit(solution)/shard_map/ppermute | solution.py:36
  90.5 106.1 %collective-permute-start.10 = (bf16[128,4096]{1,0:T(8,128)(2,1)S(1)}, bf16[128,4096]{1,0:T(8,128)(2,1)}, u32[]{:S(2)}, u32[]{:S(2)}) collective-permute-start(bf16[128,4096]{1,0:T(8,128)(2,1)S(1)} %copy-done.4), channel_id=1, source_target_pairs={{1,0},{2,1},{3,2},{5,4},{6,5},{7,6},{9,8},{10,9},{11,10},{13,12},{... | collective-permute-start | bytes 3145736 | tf_op jit(solution)/shard_map/ppermute | solution.py:454
  93.3 104.7 %collective-permute-start.7 = (bf16[128,4096]{1,0:T(8,128)(2,1)S(1)}, bf16[128,4096]{1,0:T(8,128)(2,1)}, u32[]{:S(2)}, u32[]{:S(2)}) collective-permute-start(bf16[128,4096]{1,0:T(8,128)(2,1)S(1)} %copy-done.2), channel_id=1, source_target_pairs={{0,1},{1,2},{2,3},{4,5},{5,6},{6,7},{8,9},{9,10},{10,11},{12,13},{... | collective-permute-start | bytes 3145736 | tf_op jit(solution)/shard_map/ppermute | solution.py:453
  94.6 104.7 %collective-permute-start.8 = (bf16[128,4096]{1,0:T(8,128)(2,1)S(1)}, bf16[128,4096]{1,0:T(8,128)(2,1)}, u32[]{:S(2)}, u32[]{:S(2)}) collective-permute-start(bf16[128,4096]{1,0:T(8,128)(2,1)S(1)} %copy-done.2), channel_id=1, source_target_pairs={{1,0},{2,1},{3,2},{5,4},{6,5},{7,6},{9,8},{10,9},{11,10},{13,12},{... | collective-permute-start | bytes 3145736 | tf_op jit(solution)/shard_map/ppermute | solution.py:454
  101.8 98.8 %collective-permute-start.9 = (bf16[128,4096]{1,0:T(8,128)(2,1)S(1)}, bf16[128,4096]{1,0:T(8,128)(2,1)}, u32[]{:S(2)}, u32[]{:S(2)}) collective-permute-start(bf16[128,4096]{1,0:T(8,128)(2,1)S(1)} %copy-done.4), channel_id=1, source_target_pairs={{0,1},{1,2},{2,3},{4,5},{5,6},{6,7},{8,9},{9,10},{10,11},{12,13},{... | collective-permute-start | bytes 3145736 | tf_op jit(solution)/shard_map/ppermute | solution.py:453
  104.1 36.6 %copy-start.5 = (bf16[128,4096]{1,0:T(8,128)(2,1)S(1)}, bf16[128,4096]{1,0:T(8,128)(2,1)}, u32[]{:S(2)}) copy-start(bf16[128,4096]{1,0:T(8,128)(2,1)} %rest_8_.3) | copy-start | bytes 3145732
  109.6 2.3 collective-permute-start.25
  111.9 12.3 %collective-permute-start.26 = (bf16[64,128]{1,0:T(8,128)(2,1)S(1)}, bf16[64,128]{1,0:T(8,128)(2,1)S(1)}, u32[]{:S(2)}, u32[]{:S(2)}) collective-permute-start(bf16[64,128]{1,0:T(8,128)(2,1)S(1)} %get-tuple-element.89), channel_id=1, source_target_pairs={{0,2},{1,3},{2,0},{3,1},{4,6},{5,7},{6,4},{7,5},{8,10},{9,11},{10,... | collective-permute-start | bytes 49160 | tf_op jit(solution)/shard_map/ppermute | solution.py:36
  124.2 3.2 %collective-permute-start.27 = (bf16[64,128]{1,0:T(8,128)(2,1)S(1)}, bf16[64,128]{1,0:T(8,128)(2,1)S(1)}, u32[]{:S(2)}, u32[]{:S(2)}) collective-permute-start(bf16[64,128]{1,0:T(8,128)(2,1)S(1)} %get-tuple-element.90), channel_id=1, source_target_pairs={{0,3},{1,2},{2,1},{3,0},{4,7},{5,6},{6,5},{7,4},{8,11},{9,10},{10,... | collective-permute-start | bytes 49160 | tf_op jit(solution)/shard_map/ppermute | solution.py:36
  127.4 3.5 %collective-permute-start.28 = (bf16[64,128]{1,0:T(8,128)(2,1)S(1)}, bf16[64,128]{1,0:T(8,128)(2,1)S(1)}, u32[]{:S(2)}, u32[]{:S(2)}) collective-permute-start(bf16[64,128]{1,0:T(8,128)(2,1)S(1)} %get-tuple-element.91), channel_id=1, source_target_pairs={{0,4},{1,5},{2,6},{3,7},{4,0},{5,1},{6,2},{7,3},{8,12},{9,13},{10,... | collective-permute-start | bytes 49160 | tf_op jit(solution)/shard_map/ppermute | solution.py:36
  130.9 4.1 %collective-permute-start.29 = (bf16[64,128]{1,0:T(8,128)(2,1)S(1)}, bf16[64,128]{1,0:T(8,128)(2,1)S(1)}, u32[]{:S(2)}, u32[]{:S(2)}) collective-permute-start(bf16[64,128]{1,0:T(8,128)(2,1)S(1)} %get-tuple-element.92), channel_id=1, source_target_pairs={{0,5},{1,4},{2,7},{3,6},{4,1},{5,0},{6,3},{7,2},{8,13},{9,12},{10,... | collective-permute-start | bytes 49160 | tf_op jit(solution)/shard_map/ppermute | solution.py:36
  134.9 2.6 %collective-permute-start.30 = (bf16[64,128]{1,0:T(8,128)(2,1)S(1)}, bf16[64,128]{1,0:T(8,128)(2,1)S(1)}, u32[]{:S(2)}, u32[]{:S(2)}) collective-permute-start(bf16[64,128]{1,0:T(8,128)(2,1)S(1)} %get-tuple-element.93), channel_id=1, source_target_pairs={{0,6},{1,7},{2,4},{3,5},{4,2},{5,3},{6,0},{7,1},{8,14},{9,15},{10,... | collective-permute-start | bytes 49160 | tf_op jit(solution)/shard_map/ppermute | solution.py:36
  137.5 3.2 %collective-permute-start.31 = (bf16[64,128]{1,0:T(8,128)(2,1)S(1)}, bf16[64,128]{1,0:T(8,128)(2,1)S(1)}, u32[]{:S(2)}, u32[]{:S(2)}) collective-permute-start(bf16[64,128]{1,0:T(8,128)(2,1)S(1)} %get-tuple-element.94), channel_id=1, source_target_pairs={{0,7},{1,6},{2,5},{3,4},{4,3},{5,2},{6,1},{7,0},{8,15},{9,14},{10,... | collective-permute-start | bytes 49160 | tf_op jit(solution)/shard_map/ppermute | solution.py:36
  141.7 1.3 collective-permute-start.32
  143.5 7.9 %collective-permute-start.33 = (bf16[64,512]{1,0:T(8,128)(2,1)S(1)}, bf16[64,512]{1,0:T(8,128)(2,1)S(1)}, u32[]{:S(2)}, u32[]{:S(2)}) collective-permute-start(bf16[64,512]{1,0:T(8,128)(2,1)S(1)} %get-tuple-element.97), channel_id=1, source_target_pairs={{0,2},{1,3},{2,0},{3,1},{4,6},{5,7},{6,4},{7,5},{8,10},{9,11},{10,... | collective-permute-start | bytes 196616 | tf_op jit(solution)/shard_map/ppermute | solution.py:36
  152.1 4.6 %collective-permute-start.34 = (bf16[64,512]{1,0:T(8,128)(2,1)S(1)}, bf16[64,512]{1,0:T(8,128)(2,1)S(1)}, u32[]{:S(2)}, u32[]{:S(2)}) collective-permute-start(bf16[64,512]{1,0:T(8,128)(2,1)S(1)} %get-tuple-element.98), channel_id=1, source_target_pairs={{0,3},{1,2},{2,1},{3,0},{4,7},{5,6},{6,5},{7,4},{8,11},{9,10},{10,... | collective-permute-start | bytes 196616 | tf_op jit(solution)/shard_map/ppermute | solution.py:36
  157.3 4.0 %collective-permute-start.35 = (bf16[64,512]{1,0:T(8,128)(2,1)S(1)}, bf16[64,512]{1,0:T(8,128)(2,1)S(1)}, u32[]{:S(2)}, u32[]{:S(2)}) collective-permute-start(bf16[64,512]{1,0:T(8,128)(2,1)S(1)} %get-tuple-element.99), channel_id=1, source_target_pairs={{0,4},{1,5},{2,6},{3,7},{4,0},{5,1},{6,2},{7,3},{8,12},{9,13},{10,... | collective-permute-start | bytes 196616 | tf_op jit(solution)/shard_map/ppermute | solution.py:36
  161.9 5.6 %collective-permute-start.36 = (bf16[64,512]{1,0:T(8,128)(2,1)S(1)}, bf16[64,512]{1,0:T(8,128)(2,1)S(1)}, u32[]{:S(2)}, u32[]{:S(2)}) collective-permute-start(bf16[64,512]{1,0:T(8,128)(2,1)S(1)} %get-tuple-element.100), channel_id=1, source_target_pairs={{0,5},{1,4},{2,7},{3,6},{4,1},{5,0},{6,3},{7,2},{8,13},{9,12},{10,... | collective-permute-start | bytes 196616 | tf_op jit(solution)/shard_map/ppermute | solution.py:36
  168.1 3.1 %collective-permute-start.37 = (bf16[64,512]{1,0:T(8,128)(2,1)S(1)}, bf16[64,512]{1,0:T(8,128)(2,1)S(1)}, u32[]{:S(2)}, u32[]{:S(2)}) collective-permute-start(bf16[64,512]{1,0:T(8,128)(2,1)S(1)} %get-tuple-element.101), channel_id=1, source_target_pairs={{0,6},{1,7},{2,4},{3,5},{4,2},{5,3},{6,0},{7,1},{8,14},{9,15},{10,... | collective-permute-start | bytes 196616 | tf_op jit(solution)/shard_map/ppermute | solution.py:36
  171.9 4.1 %collective-permute-start.38 = (bf16[64,512]{1,0:T(8,128)(2,1)S(1)}, bf16[64,512]{1,0:T(8,128)(2,1)S(1)}, u32[]{:S(2)}, u32[]{:S(2)}) collective-permute-start(bf16[64,512]{1,0:T(8,128)(2,1)S(1)} %get-tuple-element.102), channel_id=1, source_target_pairs={{0,7},{1,6},{2,5},{3,4},{4,3},{5,2},{6,1},{7,0},{8,15},{9,14},{10,... | collective-permute-start | bytes 196616 | tf_op jit(solution)/shard_map/ppermute | solution.py:36
  176.6 4.2 %collective-permute-start.18 = (bf16[128,512]{1,0:T(8,128)(2,1)S(1)}, bf16[128,512]{1,0:T(8,128)(2,1)S(1)}, u32[]{:S(2)}, u32[]{:S(2)}) collective-permute-start(bf16[128,512]{1,0:T(8,128)(2,1)S(1)} %get-tuple-element.80), channel_id=1, source_target_pairs={{2,3},{5,4},{10,11},{13,12},{18,19},{21,20},{26,27},{29,28}} | collective-permute-start | bytes 393224 | tf_op jit(solution)/shard_map/ppermute | solution.py:36
  181.4 13.9 %collective-permute-start.19 = (bf16[128,512]{1,0:T(8,128)(2,1)}, bf16[128,512]{1,0:T(8,128)(2,1)}, u32[]{:S(2)}, u32[]{:S(2)}) collective-permute-start(bf16[128,512]{1,0:T(8,128)(2,1)} %get-tuple-element.81), channel_id=1, source_target_pairs={{1,3},{6,4},{9,11},{14,12},{17,19},{22,20},{25,27},{30,28}} | collective-permute-start | bytes 393224 | tf_op jit(solution)/shard_map/ppermute | solution.py:36
  195.3 38.3 %collective-permute-start.20 = (bf16[128,512]{1,0:T(8,128)(2,1)}, bf16[128,512]{1,0:T(8,128)(2,1)S(1)}, u32[]{:S(2)}, u32[]{:S(2)}) collective-permute-start(bf16[128,512]{1,0:T(8,128)(2,1)} %copy-done.52), channel_id=1, source_target_pairs={{0,3},{7,4},{8,11},{15,12},{16,19},{23,20},{24,27},{31,28}} | collective-permute-start | bytes 393224 | tf_op jit(solution)/shard_map/ppermute | solution.py:36
  196.6 37.0 %collective-permute-start.21 = (bf16[128,512]{1,0:T(8,128)(2,1)}, bf16[128,512]{1,0:T(8,128)(2,1)S(1)}, u32[]{:S(2)}, u32[]{:S(2)}) collective-permute-start(bf16[128,512]{1,0:T(8,128)(2,1)} %copy-done.51), channel_id=1, source_target_pairs={{0,4},{7,3},{8,12},{15,11},{16,20},{23,19},{24,28},{31,27}} | collective-permute-start | bytes 393224 | tf_op jit(solution)/shard_map/ppermute | solution.py:36
  197.9 35.7 %collective-permute-start.22 = (bf16[128,512]{1,0:T(8,128)(2,1)}, bf16[128,512]{1,0:T(8,128)(2,1)S(1)}, u32[]{:S(2)}, u32[]{:S(2)}) collective-permute-start(bf16[128,512]{1,0:T(8,128)(2,1)} %copy-done.50), channel_id=1, source_target_pairs={{1,4},{6,3},{9,12},{14,11},{17,20},{22,19},{25,28},{30,27}} | collective-permute-start | bytes 393224 | tf_op jit(solution)/shard_map/ppermute | solution.py:36
  199.3 34.4 %collective-permute-start.23 = (bf16[128,512]{1,0:T(8,128)(2,1)}, bf16[128,512]{1,0:T(8,128)(2,1)S(1)}, u32[]{:S(2)}, u32[]{:S(2)}) collective-permute-start(bf16[128,512]{1,0:T(8,128)(2,1)} %copy-done.49), channel_id=1, source_target_pairs={{2,4},{5,3},{10,12},{13,11},{18,20},{21,19},{26,28},{29,27}} | collective-permute-start | bytes 393224 | tf_op jit(solution)/shard_map/ppermute | solution.py:36
  200.6 33.1 %copy-start.9 = (bf16[128,512]{1,0:T(8,128)(2,1)S(1)}, bf16[128,512]{1,0:T(8,128)(2,1)}, u32[]{:S(2)}) copy-start(bf16[128,512]{1,0:T(8,128)(2,1)} %copy-done.8) | copy-start | bytes 393220
  200.6 33.1 %collective-permute-start.24 = (bf16[128,512]{1,0:T(8,128)(2,1)}, bf16[128,512]{1,0:T(8,128)(2,1)S(1)}, u32[]{:S(2)}, u32[]{:S(2)}) collective-permute-start(bf16[128,512]{1,0:T(8,128)(2,1)} %copy-done.48), channel_id=1, source_target_pairs={{3,4},{4,3},{11,12},{12,11},{19,20},{20,19},{27,28},{28,27}} | collective-permute-start | bytes 393224 | tf_op jit(solution)/shard_map/ppermute | solution.py:36
  (44 other events, 314.2 us)

commit v3 on v2

v3 whole, which is shorter than its diff:
```python
import functools
import math

import jax
import jax.numpy as jnp
from jax import lax
from jax.experimental import pallas as pl
from jax.experimental.pallas import tpu as pltpu
from jax.sharding import PartitionSpec as P

H = 32
HIDDEN = -1e30
VMEM = 60 * 1024 * 1024
NT = (((1,), (1,)), ((), ()))
TN = (((0,), (0,)), ((), ()))
NN = (((1,), (0,)), ((), ()))


def mm(a, b, dims=NN):
    return lax.dot_general(a, b, dims, preferred_element_type=jnp.float32)


def params():
    return pltpu.CompilerParams(vmem_limit_bytes=VMEM)


SMEM = pl.BlockSpec(memory_space=pltpu.SMEM)
HBM = pl.BlockSpec(memory_space=pltpu.HBM)
LANES = 128


def swap(block, count, bits, targets=None):
    pairs = [(i, i ^ bits) for i in range(count) if targets is None or i ^ bits in targets]
    return lax.ppermute(block, "context", pairs)


def exchange(blocks, count):
    got = {0: blocks[0]}
    for k in range(count - 1, 0, -1):
        got[k] = swap(blocks[k], count, k)
    return [got[k] for k in range(count)]


def pack_copies(count, group, hd, first, nh, me, refs, outs, sems):
    tok = refs[0].shape[0]
    copies = []
    for k in range(count):
        for h in range(nh):
            column = pl.multiple_of((me ^ k) * group + (first + h) * hd, LANES)
            for t, ref in enumerate(refs):
                n = h * 3 + t
                copies.append(
                    pltpu.make_async_copy(
                        ref.at[:, pl.ds(column, hd)],
                        outs[k].at[pl.ds(n * tok, tok), :],
                        sems.at[k * nh * 3 + n],
                    )
                )
    return copies


def pack_kernel(count, group, hd, first, nh, me_ref, q_ref, k_ref, v_ref, _, *rest):
    outs, sems = rest[:count], rest[count]
    copies = pack_copies(
        count, group, hd, first, nh, me_ref[0], (q_ref, k_ref, v_ref), outs, sems
    )
    for copy in copies:
        copy.start()
    for copy in copies:
        copy.wait()


def pack(me, q, k, v, after, count, hd, first, nh):
    tok, model = q.shape
    return pl.pallas_call(
        functools.partial(pack_kernel, count, model // count, hd, first, nh),
        out_shape=[jax.ShapeDtypeStruct((nh * 3 * tok, hd), q.dtype)] * count,
        in_specs=[SMEM, HBM, HBM, HBM, HBM],
        out_specs=[HBM] * count,
        scratch_shapes=[pltpu.SemaphoreType.DMA((3 * nh * count,))],
        compiler_params=params(),
        name="pack",
    )(me, q, k, v, after)


def first_kernel(count, group, hd, nh, mask_rows, tiles, me_ref, nb_ref, *rest):
    q_ref, k_ref, v_ref, x_ref, down_ref = rest[:5]
    outs, rest = rest[5 : 5 + count], rest[5 + count :]
    x_s, down_s, note_s, sems, in_sems, note_sems = rest
    me = me_ref[0]
    tok = q_ref.shape[0]
    rank = down_ref.shape[0]
    loads = [
        pltpu.make_async_copy(x_ref, x_s, in_sems.at[0]),
        pltpu.make_async_copy(down_ref, down_s, in_sems.at[1]),
    ]
    copies = pack_copies(count, group, hd, 0, nh, me, (q_ref, k_ref, v_ref), outs, sems)
    for copy in loads + copies:
        copy.start()
    rows = lax.broadcasted_iota(jnp.int32, (mask_rows, tok), 0)
    lane_tile = lax.broadcasted_iota(jnp.int32, (mask_rows, tok), 1) // (tok // tiles)
    seen = jnp.zeros((mask_rows, tok), jnp.float32)
    for t in range(tiles):
        for n in range(nb_ref.shape[1]):
            slot = nb_ref[t, n] - (me - 1) * tiles
            seen = jnp.where((rows == slot) & (lane_tile == t), 1.0, seen)
    note_s[rank:, :] = seen.astype(jnp.bfloat16)
    for copy in loads:
        copy.wait()
    note_s[:rank, :] = mm(down_s[...], x_s[...], NT).astype(jnp.bfloat16)
    notes = [
        pltpu.make_async_copy(
            note_s, outs[k].at[pl.ds(nh * 3 * tok, rank + mask_rows), :], note_sems.at[k]
        )
        for k in range(count)
    ]
    for copy in notes:
        copy.start()
    for copy in copies + notes:
        copy.wait()


def first_pack(me, nb, q, k, v, x, down, count, hd, nh, mask_rows):
    tok, model = q.shape
    rank = down.shape[0]
    rows = nh * 3 * tok + rank + mask_rows
    bf = q.dtype
    return pl.pallas_call(
        functools.partial(
            first_kernel, count, model // count, hd, nh, mask_rows, nb.shape[0]
        ),
        out_shape=[jax.ShapeDtypeStruct((rows, hd), bf)] * count,
        in_specs=[SMEM, SMEM] + [HBM] * 5,
        out_specs=[HBM] * count,
        scratch_shapes=[
            pltpu.VMEM(x.shape, bf),
            pltpu.VMEM(down.shape, bf),
            pltpu.VMEM((rank + mask_rows, tok), bf),
            pltpu.SemaphoreType.DMA((3 * nh * count,)),
            pltpu.SemaphoreType.DMA((2,)),
            pltpu.SemaphoreType.DMA((count,)),
        ],
        compiler_params=params(),
        name="first_pack",
    )(me, nb, q, k, v, x, down)


def assemble_kernel(count, group, me_ref, home_ref, *rest):
    refs, out, sems = rest[: count // 2], rest[count // 2], rest[count // 2 + 1]
    me = me_ref[0]

    @pl.when((me == count // 2 - 1) | (me == count // 2))
    def _():
        copies = []
        for k in range(count):
            column = pl.multiple_of((me ^ k) * group, LANES)
            copies.append(
                pltpu.make_async_copy(
                    refs[k // 2].at[k % 2], out.at[:, pl.ds(column, group)], sems.at[k]
                )
            )
        for copy in copies:
            copy.start()
        for copy in copies:
            copy.wait()


def assemble(me, home, blocks):
    count = 2 * len(blocks)
    return pl.pallas_call(
        functools.partial(assemble_kernel, count, home.shape[1] // count),
        out_shape=jax.ShapeDtypeStruct(home.shape, home.dtype),
        in_specs=[SMEM] + [HBM] * (len(blocks) + 1),
        out_specs=HBM,
        input_output_aliases={1: 0},
        scratch_shapes=[pltpu.SemaphoreType.DMA((count,))],
        compiler_params=params(),
        name="assemble",
    )(me, home, *blocks)


def soft(scores, scale):
    top = jnp.max(scores, axis=0, keepdims=True)
    expo = jnp.exp2((scores - top) * scale)
    return expo, jnp.sum(expo, axis=0, keepdims=True)


def tile_weights(keys, query, mask, slots, scale):
    tok = query.shape[0]
    bias = (mask.astype(jnp.float32)[:slots] - 1.0) * (-HIDDEN)
    scores = mm(keys, query, NT).reshape(slots, 3 * tok // slots, tok) + bias[:, None, :]
    expo, norm = soft(scores.reshape(3 * tok, tok), scale)
    return (expo * (1.0 / norm)).astype(jnp.bfloat16)


def window(me, p, count):
    slab = me ^ p
    low = jnp.where(slab > 0, (slab - 1) ^ me, p)
    high = jnp.where(slab < count - 1, (slab + 1) ^ me, p)
    return low, p, high


def log_scale(hd):
    return hd ** (-0.5) * math.log2(math.e)


def home_kernel(count, slots, rank, hd, me_ref, *rest):
    notes, rest = rest[:count], rest[count:]
    q_ref, k_ref, v_ref, low_ref, high_ref, up_ref, out_ref, note_s, sems = rest
    tok = q_ref.shape[0]

    @pl.when(pl.program_id(0) == 0)
    def _():
        size = note_s.shape[1]
        copies = [
            pltpu.make_async_copy(
                ref.at[pl.ds(ref.shape[0] - size, size), :], note_s.at[p], sems.at[p]
            )
            for p, ref in enumerate(notes)
        ]
        for copy in copies:
            copy.start()
        for copy in copies:
            copy.wait()

    mask = note_s[0][rank:, :]
    loras = [note_s[w][:rank, :] for w in window(me_ref[0], 0, count)]
    for h in range(q_ref.shape[1] // hd):
        cols = slice(h * hd, (h + 1) * hd)
        keys = jnp.concatenate([low_ref[0, :, cols], k_ref[:, cols], high_ref[0, :, cols]], axis=0)
        weights = tile_weights(keys, q_ref[:, cols], mask, slots, log_scale(hd))
        values = []
        for value, lora in zip((low_ref[1, :, cols], v_ref[:, cols], high_ref[1, :, cols]), loras):
            term = mm(up_ref[:, cols], lora, TN)
            values.append((value.T.astype(jnp.float32) + term).astype(jnp.bfloat16))
        student = mm(jnp.concatenate(values, axis=1), weights)
        out_ref[:, cols] = student.T.astype(jnp.bfloat16)


def home_student(me, messages, mask_rows, q, k, v, low, high, up_t, hd, slots):
    count = len(messages)
    tok, model = q.shape
    rank = up_t.shape[0]
    width = min(4 * hd, model)
    column = pl.BlockSpec((tok, width), lambda h: (0, h))
    pair = pl.BlockSpec((2, tok, width), lambda h: (0, 0, h))
    return pl.pallas_call(
        functools.partial(home_kernel, count, slots, rank, hd),
        grid=(model // width,),
        out_shape=jax.ShapeDtypeStruct(q.shape, q.dtype),
        in_specs=[SMEM]
        + [HBM] * count
        + [column] * 3
        + [pair] * 2
        + [pl.BlockSpec((rank, width), lambda h: (0, h))],
        out_specs=column,
        scratch_shapes=[
            pltpu.VMEM((count, rank + mask_rows, tok), q.dtype),
            pltpu.SemaphoreType.DMA((count,)),
        ],
        compiler_params=params(),
        cost_estimate=pl.CostEstimate(
            flops=12 * 10**9, bytes_accessed=9 * tok * model * 2, transcendentals=0
        ),
        name="home_student",
    )(me, *messages, q, k, v, low, high, up_t)


def attention_kernel(
    count, tok, hd, nh, slots, rank, before, last, factor, sizes, me_ref, *rest
):
    blocks, rest = rest[:count], rest[count:]
    noted, rest = rest[:count], rest[count:]
    up_ref, _, rest = rest[0], rest[1], rest[2:]
    if before:
        (hid_ref, gup_in, out_in), rest = rest[:3], rest[3:]
    if last:
        keep_ref, send_ref, hid_keep, hid_send, gup_ref, rest = *rest[:5], rest[5:]
    else:
        hid_ref_out, gup_ref, out_ref, rest = *rest[:3], rest[3:]
    b_s, note_s, q_s, k_s, vt_s, svt_s, lora_s, grad_s, hid_s, out_s, sems, note_sems = rest
    head = pl.program_id(0)
    me = me_ref[0]
    scale = log_scale(hd)
    size, rows = note_s.shape[1], 3 * tok

    def block_copies(h):
        return [
            pltpu.make_async_copy(
                blocks[p].at[pl.ds(pl.multiple_of(h * rows, rows), rows), :],
                b_s.at[lax.rem(h, 2), p],
                sems.at[lax.rem(h, 2), p],
            )
            for p in range(count)
        ]

    @pl.when(head == 0)
    def _():
        copies = [
            pltpu.make_async_copy(
                ref.at[pl.ds(sizes - size, size), :], note_s.at[p], note_sems.at[p]
            )
            for p, ref in enumerate(noted)
        ]
        for copy in copies + block_copies(0):
            copy.start()
        for copy in copies:
            copy.wait()
        for p in range(count):
            lora_s[:, p * tok : (p + 1) * tok] = note_s[p, :rank, :]
        if before:
            hid_s[...] = hid_ref[...]
            gup_ref[:, : before * hd] = gup_in[...]
            out_s[:before] = out_in[...]
        else:
            hid_s[...] = jnp.zeros_like(hid_s)

    @pl.when(head + 1 < nh)
    def _():
        for copy in block_copies(head + 1):
            copy.start()

    for copy in block_copies(head):
        copy.wait()
    at = lax.rem(head, 2)
    for p in range(count):
        q_s[p * tok : (p + 1) * tok, :] = b_s[at, p, :tok, :]
        k_s[p * tok : (p + 1) * tok, :] = b_s[at, p, tok : 2 * tok, :]
        vt_s[:, p * tok : (p + 1) * tok] = b_s[at, p, 2 * tok :, :].T
    up_t = up_ref[...]
    for p in range(count):
        cols = slice(p * tok, (p + 1) * tok)
        term = mm(up_t, lora_s[:, cols], TN)
        svt_s[p] = (vt_s[:, cols].astype(jnp.float32) + term).astype(jnp.bfloat16)
    grad_s[...] = jnp.zeros_like(grad_s)

    for pair in range(count // 2):
        queries = q_s[2 * pair * tok : 2 * (pair + 1) * tok, :]
        expo, norm = soft(mm(k_s[...], queries, NT), scale)
        teachers = mm(vt_s[...], expo.astype(jnp.bfloat16)) / norm
        teachers = teachers.astype(jnp.bfloat16).astype(jnp.float32)
        for p in (2 * pair, 2 * pair + 1):
            teacher = teachers[:, (p % 2) * tok : (p % 2 + 1) * tok]
            places = window(me, p, count)
            keys = jnp.concatenate(
                [k_s[pl.ds(pl.multiple_of(w * tok, tok), tok), :] for w in places], axis=0
            )
            query = q_s[p * tok : (p + 1) * tok, :]
            weights = tile_weights(keys, query, note_s[p, rank:, :], slots, scale)
            values = jnp.concatenate([svt_s[w] for w in places], axis=1)
            student = mm(values, weights)
            out_s[before + head, p] = student.astype(jnp.bfloat16)
            delta = ((student - teacher) * factor).astype(jnp.bfloat16)
            grads = mm(weights, delta, NT)
            for n, w in enumerate(places):
                grad_s[w] += grads[n * tok : (n + 1) * tok]

    grad = grad_s[...].reshape(count * tok, hd).astype(jnp.bfloat16)
    column = pl.multiple_of((before + head) * hd, LANES)
    gup_ref[:, pl.ds(column, hd)] = mm(lora_s[...], grad)
    hid_s[...] += mm(up_t, grad, NT)

    @pl.when(head == nh - 1)
    def _():
        if last:
            for m in range(count // 2):
                to = slice(m * tok, (m + 1) * tok)
                hid_keep[:, to] = hid_s[:, 2 * m * tok : (2 * m + 1) * tok]
                odd = hid_s[:, (2 * m + 1) * tok : (2 * m + 2) * tok]
                hid_send[:, to] = odd.astype(jnp.bfloat16)
            core = lax.rem(me, 2)
            half = count // 2
            same = jnp.where(core == (half - 1) % 2, half - 1, half)
            other = jnp.where(core == (half - 1) % 2, half, half - 1)
            for ref, slab in ((keep_ref, same), (send_ref, other)):
                for h in range(before + nh):
                    ref[:, h * hd : (h + 1) * hd] = out_s[h, me ^ slab].T
        else:
            hid_ref_out[...] = hid_s[...]
            out_ref[...] = out_s[...]


def attention(me, blocks, noted, up_t, after, given, first, nh, tok, hd, slots, mask_rows, last):
    count = len(blocks)
    rank = up_t.shape[0]
    bf, f32 = jnp.bfloat16, jnp.float32
    whole = lambda shape: pl.BlockSpec(shape, lambda h: (0,) * len(shape))
    keys = count * tok
    heads = first + nh
    shapes = [
        jax.ShapeDtypeStruct((rank, keys), f32),
        jax.ShapeDtypeStruct((rank, heads * hd), f32),
        jax.ShapeDtypeStruct((heads, count, hd, tok), bf),
    ]
    if last:
        shapes = [
            jax.ShapeDtypeStruct((tok, heads * hd), bf),
            jax.ShapeDtypeStruct((tok, heads * hd), bf),
            jax.ShapeDtypeStruct((rank, keys // 2), f32),
            jax.ShapeDtypeStruct((rank, keys // 2), bf),
            jax.ShapeDtypeStruct((rank, heads * hd), f32),
        ]
    return pl.pallas_call(
        functools.partial(
            attention_kernel,
            count,
            tok,
            hd,
            nh,
            slots,
            rank,
            first,
            last,
            keys ** (-0.5),
            noted[0].shape[0],
        ),
        grid=(nh,),
        out_shape=shapes,
        in_specs=[SMEM]
        + [HBM] * (2 * count)
        + [pl.BlockSpec((rank, hd), lambda h: (0, first + h)), HBM]
        + [whole(g.shape) for g in given],
        out_specs=[whole(s.shape) for s in shapes],
        scratch_shapes=[
            pltpu.VMEM((2, count, 3 * tok, hd), bf),
            pltpu.VMEM((count, rank + mask_rows, tok), bf),
            pltpu.VMEM((keys, hd), bf),
            pltpu.VMEM((keys, hd), bf),
            pltpu.VMEM((hd, keys), bf),
            pltpu.VMEM((count, hd, tok), bf),
            pltpu.VMEM((rank, keys), bf),
            pltpu.VMEM((count, tok, hd), f32),
            pltpu.VMEM((rank, keys), f32),
            pltpu.VMEM((heads, count, hd, tok), bf),
            pltpu.SemaphoreType.DMA((2, count)),
            pltpu.SemaphoreType.DMA((count,)),
        ],
        compiler_params=params(),
        cost_estimate=pl.CostEstimate(
            flops=nh * 6 * 10**9, bytes_accessed=4 * nh * keys * hd * 2, transcendentals=0
        ),
        name="attention",
    )(me, *blocks, *noted, up_t, after, *given)


VM = pl.BlockSpec(memory_space=pltpu.VMEM)


def pair_kernel(parts, keep_ref, got_ref, *outs):
    width = keep_ref.shape[1] // parts
    for m in range(parts):
        cols = slice(m * width, (m + 1) * width)
        total = keep_ref[:, cols] + got_ref[:, cols].astype(jnp.float32)
        outs[m][...] = total.astype(outs[m].dtype)


def pair_sum(keep, got, parts):
    rank, width = keep.shape[0], keep.shape[1] // parts
    shapes = [
        jax.ShapeDtypeStruct((rank, width), jnp.bfloat16 if m else jnp.float32)
        for m in range(parts)
    ]
    return pl.pallas_call(
        functools.partial(pair_kernel, parts),
        out_shape=shapes,
        in_specs=[VM, VM],
        out_specs=[VM] * parts,
        compiler_params=params(),
        name="pair_sum",
    )(keep, got)


def chip_terms(keep, send, count):
    totals = pair_sum(keep, swap(send, count, 1), count // 2)
    got = {m: swap(totals[m], count, 2 * m) for m in range(count // 2 - 1, 0, -1)}
    return [totals[0]] + [got[m] for m in range(1, count // 2)]


def down_kernel(count, group, me_ref, *rest):
    parts = rest[: count // 2]
    x_ref, keep_ref, send_ref = rest[count // 2 :]
    me = me_ref[0]
    hidden = parts[0][...]
    for part in parts[1:]:
        hidden += part[...].astype(jnp.float32)
    hidden = hidden.astype(jnp.bfloat16)
    for k in range(count):
        column = pl.multiple_of((me ^ k) * group, LANES)
        term = mm(hidden, x_ref[:, pl.ds(column, group)])
        to = (send_ref, keep_ref)[k % 2 == 0]
        to[:, k // 2 * group : (k // 2 + 1) * group] = term.astype(to.dtype)


def down_terms(me, parts, x):
    count = 2 * len(parts)
    model = x.shape[1]
    rank = parts[0].shape[0]
    return pl.pallas_call(
        functools.partial(down_kernel, count, model // count),
        out_shape=[
            jax.ShapeDtypeStruct((rank, model // 2), jnp.float32),
            jax.ShapeDtypeStruct((rank, model // 2), jnp.bfloat16),
        ],
        in_specs=[SMEM] + [VM] * (len(parts) + 1),
        out_specs=[VM, VM],
        compiler_params=params(),
        name="down_terms",
    )(me, *parts, x)


def sum_kernel(*refs):
    total = refs[0][...]
    for ref in refs[1:-1]:
        total += ref[...].astype(jnp.float32)
    refs[-1][...] = total


def sum_terms(parts):
    return pl.pallas_call(
        sum_kernel,
        out_shape=jax.ShapeDtypeStruct(parts[0].shape, jnp.float32),
        in_specs=[VM] * len(parts),
        out_specs=VM,
        compiler_params=params(),
        name="sum_terms",
    )(*parts)


def head_chunks(per_group):
    if per_group < 2:
        return [(0, per_group)]
    return [(0, per_group - 1), (per_group - 1, 1)]


def local(
    queries, keys, values, value_layer_input, adapter_down_weight, adapter_up_weight, neighbors
):
    tok, model = queries.shape
    rank = adapter_down_weight.shape[1]
    count = lax.axis_size("context")
    index = lax.axis_index("context")
    me = index.astype(jnp.int32).reshape(1)
    hd = model // H
    group = model // count
    per_group = H // count
    tiles = neighbors.shape[0]
    slots = 3 * tiles
    chunks = head_chunks(per_group)

    mask_rows = slots + -slots % 16

    down_t = adapter_down_weight.T
    up_t = adapter_up_weight.T

    messages = []
    for c, (first, nh) in enumerate(chunks):
        if c == 0:
            blocks = first_pack(
                me, neighbors, queries, keys, values, value_layer_input, down_t,
                count, hd, nh, mask_rows,
            )
        else:
            after = messages[-1][-1]
            blocks = pack(me, queries, keys, values, after, count, hd, first, nh)
        messages.append(exchange(blocks, count))
    noted = messages[0]

    half = count // 2
    ups = [(i, i + 1) for i in range(count - 1) if i + 1 != half]
    both = jnp.stack([keys, values])
    low = lax.ppermute(both, "context", ups)
    high = lax.ppermute(both, "context", [(j, i) for i, j in ups])
    home = home_student(
        me, noted, mask_rows, queries, keys, values, low, high, up_t, hd, slots
    )

    own_up = lax.dynamic_slice_in_dim(up_t, index * group, group, 1)
    given = []
    for c, (first, nh) in enumerate(chunks):
        last = c == len(chunks) - 1
        given = attention(
            me, messages[c], noted, own_up, home, given, first, nh, tok, hd, slots, mask_rows, last
        )
    keep, send, hid_keep, hid_send, grad_up = given
    hidden = chip_terms(hid_keep, hid_send, count)
    grad_down = sum_terms(chip_terms(*down_terms(me, hidden, value_layer_input), count))

    middle = jnp.stack([keep, swap(send, count, 1)])
    blocks = [middle] + [swap(middle, count, 2 * m, (half - 1, half)) for m in range(1, half)]
    return assemble(me, home, blocks), grad_down.T, grad_up.T


def solution(mesh):
    rows = P(("video", "context"), None)
    return jax.shard_map(
        local,
        mesh=mesh,
        in_specs=(rows, rows, rows, rows, P(), P(), rows),
        out_specs=(rows, rows, rows),
        check_vma=False,
    )
```

time: 243 us -> 261 us (1.074)
  the two profiles are of different devices: /device:TPU:11 before, /device:TPU:13 now
where the time goes in v3:
time: 261 us; the launch traced here: 260 us
  Pallas kernels  185 us (71%)
  starting transfers between devices  36.8 us (14%)
  waiting for transfers between devices  29.5 us (11%)
  local copies, waits for them, and re-layouts  5.5 us (2%)
  other arithmetic  2.67 us (1%)
    pallas_call x1, Pallas kernels, first_pack(): pl.pallas_call(functools.partial(first_kernel, count, model // count, hd,...  74 us
    pallas_call x1, Pallas kernels, assemble(): pl.pallas_call(functools.partial(assemble_kernel, count, home.shape[1] //...  32.9 us
    ppermute x26, starting transfers between devices, swap(): return lax.ppermute(block, 'context', pairs)  31.5 us
    pallas_call x2, Pallas kernels, attention(): pl.pallas_call(functools.partial(attention_kernel, count, tok, hd, nh, sl...  29.6 us
    ppermute x26, waiting for transfers between devices, swap(): return lax.ppermute(block, 'context', pairs)  29.5 us
    pallas_call x1, Pallas kernels, pack(): pl.pallas_call(functools.partial(pack_kernel, count, model // count, hd,...  25.1 us
    pallas_call x1, Pallas kernels, home_student(): pl.pallas_call(functools.partial(home_kernel, count, slots, rank, hd), gr...  15.4 us
  transfers between devices with their start and end apart: 28, of which 9 were waited for; matrix products, arithmetic and copies ran while one was open for 1% of the time, Pallas kernels for 67%

profile of v3, /device:TPU:13, one launch (start us, length us, event | category | flops | bytes accessed | tf_op | source)
XLA Modules:
  0.0 260.0 jit_solution(7680666900762541850)
XLA Ops:
  0.6 1.7 pad_maximum_fusion
  2.4 3.9 %collective-permute-start.8 = (bf16[2,128,4096]{2,1,0:T(8,128)(2,1)S(1)}, bf16[2,128,4096]{2,1,0:T(8,128)(2,1)}, u32[]{:S(2)}, u32[]{:S(2)}) collective-permute-start(bf16[2,128,4096]{2,1,0:T(8,128)(2,1)S(1)} %pad_maximum_fusion), channel_id=1, source_target_pairs={{1,0},{2,1},{3,2},{5,4},{6,5},{7,6},{9,8},{10,9},{11,10},{13,12},{... | collective-permute-start | bytes 6291464 | tf_op jit(solution)/shard_map/ppermute | solution.py:572
  6.3 1.3 collective-permute-start.7
  7.6 74.0 %first_pack.1 = (bf16[1232,128]{1,0:T(8,128)(2,1)}, bf16[1232,128]{1,0:T(8,128)(2,1)}, bf16[1232,128]{1,0:T(8,128)(2,1)}, bf16[1232,128]{1,0:T(8,128)(2,1)}, bf1...) custom-call(s32[1]{0:T(128)} %bitcast.me_ref, ...), custom_call_target="tpu_custom_call" | custom-call | tf_op jit(solution)/shard_map/first_pack/pallas_call | solution.py:128
  81.6 1.2 collective-permute-start
  83.0 1.5 collective-permute-start.2
  84.5 1.3 collective-permute-start.6
  85.9 6.2 %collective-permute-done.1.rest_2_.rest_10_ = bf16[1232,128]{1,0:T(8,128)(2,1)S(1)} collective-permute-done((bf16[1232,128]{1,0:T(8,128)(2,1)}, bf16[1232,128]{1,0:T(8,128)(2,1)S(1)}, u32[]{:S(2)}, u32[]{:S(2)}) %collective-permute-start.1) | collective-permute-done | bytes 315424 | tf_op jit(solution)/shard_map/ppermute | solution.py:34
  92.1 2.3 collective-permute-start.3
  94.4 14.8 %collective-permute-done.2.rest_3_.rest_11_ = bf16[1232,128]{1,0:T(8,128)(2,1)S(1)} collective-permute-done((bf16[1232,128]{1,0:T(8,128)(2,1)}, bf16[1232,128]{1,0:T(8,128)(2,1)S(1)}, u32[]{:S(2)}, u32[]{:S(2)}) %collective-permute-start.2) | collective-permute-done | bytes 315424 | tf_op jit(solution)/shard_map/ppermute | solution.py:34
  109.1 2.3 collective-permute-start.4
  111.4 1.3 collective-permute-start.5
  112.7 1.5 dynamic-slice_bitcast_fusion.rest_16_
  114.2 25.1 %pack.1 = (bf16[384,128]{1,0:T(8,128)(2,1)}, bf16[384,128]{1,0:T(8,128)(2,1)}, bf16[384,128]{1,0:T(8,128)(2,1)}, bf16[384,128]{1,0:T(8,128)(2,1)}, bf16[384,128]...) custom-call(s32[1]{0:T(128)} %bitcast.me_ref, ...), custom_call_target="tpu_custom_call" | custom-call | tf_op jit(solution)/shard_map/pack/pallas_call | solution.py:75
  139.3 1.0 collective-permute-start.9
  140.3 0.8 collective-permute-done.5.rest_6_.rest_14_
  141.1 0.9 collective-permute-start.11
  142.1 4.2 %collective-permute-start.12 = (bf16[384,128]{1,0:T(8,128)(2,1)}, bf16[384,128]{1,0:T(8,128)(2,1)S(1)}, u32[]{:S(2)}, u32[]{:S(2)}) collective-permute-start(bf16[384,128]{1,0:T(8,128)(2,1)} %get-tuple-element.49), channel_id=1, source_target_pairs={{0,4},{1,5},{2,6},{3,7},{4,0},{5,1},{6,2},{7,3},{8,12},{9,13},{10,... | collective-permute-start | bytes 294920 | tf_op jit(solution)/shard_map/ppermute | solution.py:34
  146.3 15.4 %home_student.1.rest_17_.home_ref = bf16[128,4096]{1,0:T(8,128)(2,1)} custom-call(s32[1]{0:T(128)} %bitcast.me_ref, bf16[1232,128]{1,0:T(8,128)(2,1)} %get-tuple-element.37.rest_0_.rest_8_, bf16[1232,128]{1,0:T(8,128)(2,1)} %copy-done.13, bf16[1232,128]{1,0:T(8,128)(2,1)} %copy-done.14, bf16[1232,128]{1,0:T(8,128)(2,1)} %copy-done.15, ...), custom_call_target="tpu_custom_call" | custom-call | flops 12000000000 | bytes 9437184 | tf_op jit(solution)/shard_map/home_student/pallas_call | solution.py:247
  161.7 1.5 collective-permute-start.14
  163.2 0.7 collective-permute-start.15
  163.9 20.4 %attention.2 = (f32[64,1024]{1,0:T(8,128)}, f32[64,384]{1,0:T(8,128)}, bf16[3,8,128,128]{3,2,1,0:T(8,128)(2,1)}) custom-call(s32[1]{0:T(128)} %bitcast.me_ref, bf16[1232,128]{1,0:T(8,128)(2,1)} %get-tuple-element.37.rest_0_.rest_8_, bf16[1232,128]{1,0:T(8,128)(2,1)} %copy-done.13, bf16[1232,128]{1,0:T(8,128)(2,1)} %copy-done.14, ...), custom_call_target="tpu_custom_call" | custom-call | flops 17999998976 | bytes 3145728 | tf_op jit(solution)/shard_map/attention/pallas_call | solution.py:403
  184.4 0.5 copy-done.19
  185.2 9.2 %attention.3 = (bf16[128,512]{1,0:T(8,128)(2,1)}, bf16[128,512]{1,0:T(8,128)(2,1)}, f32[64,512]{1,0:T(8,128)}, bf16[64,512]{1,0:T(8,128)(2,1)}, f32[64,512]{1,0:T(8,128)}) custom-call(s32[1]{0:T(128)} %bitcast.me_ref, bf16[384,128]{1,0:T(8,128)(2,1)} %get-tuple-element.45.rest_0_, bf16[384,128]{1,0:T(8,128)(2,1)} %copy-done.16, bf16[384,128]{1,0:T(8,128)(2,1)} %copy-done.17, ...), custom_call_target="tpu_custom_call" | custom-call | flops 6000000000 | bytes 1048576 | tf_op jit(solution)/shard_map/attention/pallas_call | solution.py:403
  194.4 0.5 collective-permute-start.20
  194.9 1.1 collective-permute-done.20.got_ref
  196.1 0.6 copy-done.9
  196.7 1.5 pair_sum.2
  198.2 2.2 collective-permute-start.21
  200.4 1.9 collective-permute-start.22
  202.6 1.6 collective-permute-done.22.rest_2_
  204.3 1.2 collective-permute-done.23.rest_3_
  205.5 0.6 copy-done.12
  206.1 2.5 down_terms.1
  208.6 1.4 collective-permute-start.24
  210.0 0.9 pad_maximum_fusion.1.rest_0_
  210.9 1.3 collective-permute-start.19
  212.2 1.3 collective-permute-start.18
  213.5 1.3 collective-permute-start.17
  214.9 0.7 copy-done.2
  215.6 1.8 pair_sum.3
  217.4 2.3 collective-permute-start.25
  219.8 0.7 collective-permute-done.19.rest_3_
  221.3 2.7 %collective-permute-done.17.rest_1_ = bf16[2,128,512]{2,1,0:T(8,128)(2,1)S(1)} collective-permute-done((bf16[2,128,512]{2,1,0:T(8,128)(2,1)S(1)}, bf16[2,128,512]{2,1,0:T(8,128)(2,1)S(1)}, u32[]{:S(2)}, u32[]{:S(2)}) %collective-permute-start.17) | collective-permute-done | bytes 262176 | tf_op jit(solution)/shard_map/ppermute | solution.py:34
  224.0 0.7 copy-done.5
  224.7 32.9 %assemble.1 = bf16[128,4096]{1,0:T(8,128)(2,1)} custom-call(s32[1]{0:T(128)} %bitcast.me_ref, bf16[128,4096]{1,0:T(8,128)(2,1)} %home_student.1.rest_17_.home_ref, bf16[2,128,512]{2,1,0:T(8,128)(2,1)} %copy-done, bf16[2,128,512]{2,1,0:T(8,128)(2,1)} %copy-done.5, bf16[2,128,512]{2,1,0:T(8,128)(2,1)} %copy-done.4, ...), custom_call_target="tpu_custom_call", output_to_operand_aliasing={{}: (1, {})} | custom-call | tf_op jit(solution)/shard_map/assemble/pallas_call | solution.py:170
  257.7 0.6 copy-done.6
  258.3 1.6 sum_terms.1
  (71 shorter events, 1.9 us)
Async XLA Ops:
  2.4 139.7 %collective-permute-start.8 = (bf16[2,128,4096]{2,1,0:T(8,128)(2,1)S(1)}, bf16[2,128,4096]{2,1,0:T(8,128)(2,1)}, u32[]{:S(2)}, u32[]{:S(2)}) collective-permute-start(bf16[2,128,4096]{2,1,0:T(8,128)(2,1)S(1)} %pad_maximum_fusion), channel_id=1, source_target_pairs={{1,0},{2,1},{3,2},{5,4},{6,5},{7,6},{9,8},{10,9},{11,10},{13,12},{... | collective-permute-start | bytes 6291464 | tf_op jit(solution)/shard_map/ppermute | solution.py:572
  6.3 139.9 %collective-permute-start.7 = (bf16[2,128,4096]{2,1,0:T(8,128)(2,1)S(1)}, bf16[2,128,4096]{2,1,0:T(8,128)(2,1)}, u32[]{:S(2)}, u32[]{:S(2)}) collective-permute-start(bf16[2,128,4096]{2,1,0:T(8,128)(2,1)S(1)} %pad_maximum_fusion), channel_id=1, source_target_pairs={{0,1},{1,2},{2,3},{4,5},{5,6},{6,7},{8,9},{9,10},{10,11},{12,13},{... | collective-permute-start | bytes 6291464 | tf_op jit(solution)/shard_map/ppermute | solution.py:571
  81.6 2.9 %collective-permute-start = (bf16[1232,128]{1,0:T(8,128)(2,1)}, bf16[1232,128]{1,0:T(8,128)(2,1)S(1)}, u32[]{:S(2)}, u32[]{:S(2)}) collective-permute-start(bf16[1232,128]{1,0:T(8,128)(2,1)} %get-tuple-element.38), channel_id=1, source_target_pairs={{0,1},{1,0},{2,3},{3,2},{4,5},{5,4},{6,7},{7,6},{8,9},{9,8},{10,11... | collective-permute-start | bytes 946184 | tf_op jit(solution)/shard_map/ppermute | solution.py:34
  82.8 9.2 %collective-permute-start.1 = (bf16[1232,128]{1,0:T(8,128)(2,1)}, bf16[1232,128]{1,0:T(8,128)(2,1)S(1)}, u32[]{:S(2)}, u32[]{:S(2)}) collective-permute-start(bf16[1232,128]{1,0:T(8,128)(2,1)} %get-tuple-element.39), channel_id=1, source_target_pairs={{0,2},{1,3},{2,0},{3,1},{4,6},{5,7},{6,4},{7,5},{8,10},{9,11},{10,... | collective-permute-start | bytes 946184 | tf_op jit(solution)/shard_map/ppermute | solution.py:34
  83.0 26.1 %collective-permute-start.2 = (bf16[1232,128]{1,0:T(8,128)(2,1)}, bf16[1232,128]{1,0:T(8,128)(2,1)S(1)}, u32[]{:S(2)}, u32[]{:S(2)}) collective-permute-start(bf16[1232,128]{1,0:T(8,128)(2,1)} %get-tuple-element.40), channel_id=1, source_target_pairs={{0,3},{1,2},{2,1},{3,0},{4,7},{5,6},{6,5},{7,4},{8,11},{9,10},{10,... | collective-permute-start | bytes 946184 | tf_op jit(solution)/shard_map/ppermute | solution.py:34
  84.5 61.7 %copy-start.13 = (bf16[1232,128]{1,0:T(8,128)(2,1)}, bf16[1232,128]{1,0:T(8,128)(2,1)S(1)}, u32[]{:S(2)}) copy-start(bf16[1232,128]{1,0:T(8,128)(2,1)S(1)} %collective-permute-done.rest_1_.rest_9_) | copy-start | bytes 946180
  84.5 26.9 %collective-permute-start.6 = (bf16[1232,128]{1,0:T(8,128)(2,1)}, bf16[1232,128]{1,0:T(8,128)(2,1)S(1)}, u32[]{:S(2)}, u32[]{:S(2)}) collective-permute-start(bf16[1232,128]{1,0:T(8,128)(2,1)} %get-tuple-element.44), channel_id=1, source_target_pairs={{0,7},{1,6},{2,5},{3,4},{4,3},{5,2},{6,1},{7,0},{8,15},{9,14},{10,... | collective-permute-start | bytes 946184 | tf_op jit(solution)/shard_map/ppermute | solution.py:34
  92.1 54.2 %copy-start.14 = (bf16[1232,128]{1,0:T(8,128)(2,1)}, bf16[1232,128]{1,0:T(8,128)(2,1)S(1)}, u32[]{:S(2)}) copy-start(bf16[1232,128]{1,0:T(8,128)(2,1)S(1)} %collective-permute-done.1.rest_2_.rest_10_) | copy-start | bytes 946180
  92.1 47.2 %collective-permute-start.3 = (bf16[1232,128]{1,0:T(8,128)(2,1)}, bf16[1232,128]{1,0:T(8,128)(2,1)}, u32[]{:S(2)}, u32[]{:S(2)}) collective-permute-start(bf16[1232,128]{1,0:T(8,128)(2,1)} %get-tuple-element.41), channel_id=1, source_target_pairs={{0,4},{1,5},{2,6},{3,7},{4,0},{5,1},{6,2},{7,3},{8,12},{9,13},{10,... | collective-permute-start | bytes 946184 | tf_op jit(solution)/shard_map/ppermute | solution.py:34
  109.1 37.1 %copy-start.15 = (bf16[1232,128]{1,0:T(8,128)(2,1)}, bf16[1232,128]{1,0:T(8,128)(2,1)S(1)}, u32[]{:S(2)}) copy-start(bf16[1232,128]{1,0:T(8,128)(2,1)S(1)} %collective-permute-done.2.rest_3_.rest_11_) | copy-start | bytes 946180
  109.1 31.2 %collective-permute-start.4 = (bf16[1232,128]{1,0:T(8,128)(2,1)}, bf16[1232,128]{1,0:T(8,128)(2,1)}, u32[]{:S(2)}, u32[]{:S(2)}) collective-permute-start(bf16[1232,128]{1,0:T(8,128)(2,1)} %get-tuple-element.42), channel_id=1, source_target_pairs={{0,5},{1,4},{2,7},{3,6},{4,1},{5,0},{6,3},{7,2},{8,13},{9,12},{10,... | collective-permute-start | bytes 946184 | tf_op jit(solution)/shard_map/ppermute | solution.py:34
  111.4 2.8 %copy-start.1 = (bf16[1232,128]{1,0:T(8,128)(2,1)}, bf16[1232,128]{1,0:T(8,128)(2,1)S(1)}, u32[]{:S(2)}) copy-start(bf16[1232,128]{1,0:T(8,128)(2,1)S(1)} %collective-permute-done.6.rest_7_._.rest_15_) | copy-start | bytes 946180
  111.4 29.7 %collective-permute-start.5 = (bf16[1232,128]{1,0:T(8,128)(2,1)}, bf16[1232,128]{1,0:T(8,128)(2,1)}, u32[]{:S(2)}, u32[]{:S(2)}) collective-permute-start(bf16[1232,128]{1,0:T(8,128)(2,1)} %get-tuple-element.43), channel_id=1, source_target_pairs={{0,6},{1,7},{2,4},{3,5},{4,2},{5,3},{6,0},{7,1},{8,14},{9,15},{10,... | collective-permute-start | bytes 946184 | tf_op jit(solution)/shard_map/ppermute | solution.py:34
  139.3 22.4 %collective-permute-start.9 = (bf16[384,128]{1,0:T(8,128)(2,1)}, bf16[384,128]{1,0:T(8,128)(2,1)S(1)}, u32[]{:S(2)}, u32[]{:S(2)}) collective-permute-start(bf16[384,128]{1,0:T(8,128)(2,1)} %get-tuple-element.46), channel_id=1, source_target_pairs={{0,1},{1,0},{2,3},{3,2},{4,5},{5,4},{6,7},{7,6},{8,9},{9,8},{10,11... | collective-permute-start | bytes 294920 | tf_op jit(solution)/shard_map/ppermute | solution.py:34
  140.3 22.9 %collective-permute-start.10 = (bf16[384,128]{1,0:T(8,128)(2,1)}, bf16[384,128]{1,0:T(8,128)(2,1)S(1)}, u32[]{:S(2)}, u32[]{:S(2)}) collective-permute-start(bf16[384,128]{1,0:T(8,128)(2,1)} %get-tuple-element.47), channel_id=1, source_target_pairs={{0,2},{1,3},{2,0},{3,1},{4,6},{5,7},{6,4},{7,5},{8,10},{9,11},{10,... | collective-permute-start | bytes 294920 | tf_op jit(solution)/shard_map/ppermute | solution.py:34
  141.1 43.2 %collective-permute-start.11 = (bf16[384,128]{1,0:T(8,128)(2,1)}, bf16[384,128]{1,0:T(8,128)(2,1)S(1)}, u32[]{:S(2)}, u32[]{:S(2)}) collective-permute-start(bf16[384,128]{1,0:T(8,128)(2,1)} %get-tuple-element.48), channel_id=1, source_target_pairs={{0,3},{1,2},{2,1},{3,0},{4,7},{5,6},{6,5},{7,4},{8,11},{9,10},{10,... | collective-permute-start | bytes 294920 | tf_op jit(solution)/shard_map/ppermute | solution.py:34
  142.1 42.3 %collective-permute-start.12 = (bf16[384,128]{1,0:T(8,128)(2,1)}, bf16[384,128]{1,0:T(8,128)(2,1)S(1)}, u32[]{:S(2)}, u32[]{:S(2)}) collective-permute-start(bf16[384,128]{1,0:T(8,128)(2,1)} %get-tuple-element.49), channel_id=1, source_target_pairs={{0,4},{1,5},{2,6},{3,7},{4,0},{5,1},{6,2},{7,3},{8,12},{9,13},{10,... | collective-permute-start | bytes 294920 | tf_op jit(solution)/shard_map/ppermute | solution.py:34
  146.2 38.2 %collective-permute-start.13 = (bf16[384,128]{1,0:T(8,128)(2,1)}, bf16[384,128]{1,0:T(8,128)(2,1)S(1)}, u32[]{:S(2)}, u32[]{:S(2)}) collective-permute-start(bf16[384,128]{1,0:T(8,128)(2,1)} %get-tuple-element.50), channel_id=1, source_target_pairs={{0,5},{1,4},{2,7},{3,6},{4,1},{5,0},{6,3},{7,2},{8,13},{9,12},{10,... | collective-permute-start | bytes 294920 | tf_op jit(solution)/shard_map/ppermute | solution.py:34
  146.2 15.4 %copy-start.20 = (bf16[384,128]{1,0:T(8,128)(2,1)S(1)}, bf16[384,128]{1,0:T(8,128)(2,1)}, u32[]{:S(2)}) copy-start(bf16[384,128]{1,0:T(8,128)(2,1)} %get-tuple-element.51) | copy-start | bytes 294916
  146.3 16.9 %copy-start.18 = (bf16[384,128]{1,0:T(8,128)(2,1)S(1)}, bf16[384,128]{1,0:T(8,128)(2,1)}, u32[]{:S(2)}) copy-start(bf16[384,128]{1,0:T(8,128)(2,1)} %get-tuple-element.52) | copy-start | bytes 294916
  161.7 22.6 %copy-start.16 = (bf16[384,128]{1,0:T(8,128)(2,1)}, bf16[384,128]{1,0:T(8,128)(2,1)S(1)}, u32[]{:S(2)}) copy-start(bf16[384,128]{1,0:T(8,128)(2,1)S(1)} %collective-permute-done.9.rest_1_) | copy-start | bytes 294916
  161.7 22.7 %collective-permute-start.14 = (bf16[384,128]{1,0:T(8,128)(2,1)S(1)}, bf16[384,128]{1,0:T(8,128)(2,1)S(1)}, u32[]{:S(2)}, u32[]{:S(2)}) collective-permute-start(bf16[384,128]{1,0:T(8,128)(2,1)S(1)} %copy-done.20), channel_id=1, source_target_pairs={{0,6},{1,7},{2,4},{3,5},{4,2},{5,3},{6,0},{7,1},{8,14},{9,15},{10,... | collective-permute-start | bytes 294920 | tf_op jit(solution)/shard_map/ppermute | solution.py:34
  163.2 21.1 %copy-start.17 = (bf16[384,128]{1,0:T(8,128)(2,1)}, bf16[384,128]{1,0:T(8,128)(2,1)S(1)}, u32[]{:S(2)}) copy-start(bf16[384,128]{1,0:T(8,128)(2,1)S(1)} %collective-permute-done.10.rest_2_) | copy-start | bytes 294916
  163.2 21.2 %collective-permute-start.15 = (bf16[384,128]{1,0:T(8,128)(2,1)S(1)}, bf16[384,128]{1,0:T(8,128)(2,1)S(1)}, u32[]{:S(2)}, u32[]{:S(2)}) collective-permute-start(bf16[384,128]{1,0:T(8,128)(2,1)S(1)} %copy-done.18), channel_id=1, source_target_pairs={{0,7},{1,6},{2,5},{3,4},{4,3},{5,2},{6,1},{7,0},{8,15},{9,14},{10,... | collective-permute-start | bytes 294920 | tf_op jit(solution)/shard_map/ppermute | solution.py:34
  184.3 0.6 copy-start.19
  184.4 0.7 copy-start.21
  184.4 0.7 copy-start.22
  184.4 0.7 copy-start.23
  184.4 0.7 copy-start.24
  194.3 15.7 %collective-permute-start.16 = (bf16[128,512]{1,0:T(8,128)(2,1)}, bf16[128,512]{1,0:T(8,128)(2,1)S(1)}, u32[]{:S(2)}, u32[]{:S(2)}) collective-permute-start(bf16[128,512]{1,0:T(8,128)(2,1)} %get-tuple-element.57), channel_id=1, source_target_pairs={{0,1},{1,0},{2,3},{3,2},{4,5},{5,4},{6,7},{7,6},{8,9},{9,8},{10,11... | collective-permute-start | bytes 393224 | tf_op jit(solution)/shard_map/ppermute | solution.py:34
  194.4 1.6 collective-permute-start.20
  198.2 4.4 %collective-permute-start.21 = (bf16[64,128]{1,0:T(8,128)(2,1)}, bf16[64,128]{1,0:T(8,128)(2,1)S(1)}, u32[]{:S(2)}, u32[]{:S(2)}) collective-permute-start(bf16[64,128]{1,0:T(8,128)(2,1)} %get-tuple-element.61), channel_id=1, source_target_pairs={{0,2},{1,3},{2,0},{3,1},{4,6},{5,7},{6,4},{7,5},{8,10},{9,11},{10,... | collective-permute-start | bytes 49160 | tf_op jit(solution)/shard_map/ppermute | solution.py:34
  200.4 3.8 %collective-permute-start.22 = (bf16[64,128]{1,0:T(8,128)(2,1)}, bf16[64,128]{1,0:T(8,128)(2,1)S(1)}, u32[]{:S(2)}, u32[]{:S(2)}) collective-permute-start(bf16[64,128]{1,0:T(8,128)(2,1)} %get-tuple-element.62), channel_id=1, source_target_pairs={{0,4},{1,5},{2,6},{3,7},{4,0},{5,1},{6,2},{7,3},{8,12},{9,13},{10,... | collective-permute-start | bytes 49160 | tf_op jit(solution)/shard_map/ppermute | solution.py:34
  202.3 3.2 %collective-permute-start.23 = (bf16[64,128]{1,0:T(8,128)(2,1)}, bf16[64,128]{1,0:T(8,128)(2,1)S(1)}, u32[]{:S(2)}, u32[]{:S(2)}) collective-permute-start(bf16[64,128]{1,0:T(8,128)(2,1)} %get-tuple-element.63), channel_id=1, source_target_pairs={{0,6},{1,7},{2,4},{3,5},{4,2},{5,3},{6,0},{7,1},{8,14},{9,15},{10,... | collective-permute-start | bytes 49160 | tf_op jit(solution)/shard_map/ppermute | solution.py:34
  202.6 2.9 %copy-start.10 = (bf16[64,128]{1,0:T(8,128)(2,1)}, bf16[64,128]{1,0:T(8,128)(2,1)S(1)}, u32[]{:S(2)}) copy-start(bf16[64,128]{1,0:T(8,128)(2,1)S(1)} %collective-permute-done.21.rest_1_) | copy-start | bytes 49156
  204.3 1.2 copy-start.11
  208.6 6.2 %collective-permute-start.24 = (bf16[64,2048]{1,0:T(8,128)(2,1)}, bf16[64,2048]{1,0:T(8,128)(2,1)S(1)}, u32[]{:S(2)}, u32[]{:S(2)}) collective-permute-start(bf16[64,2048]{1,0:T(8,128)(2,1)} %get-tuple-element.65), channel_id=1, source_target_pairs={{0,1},{1,0},{2,3},{3,2},{4,5},{5,4},{6,7},{7,6},{8,9},{9,8},{10,11... | collective-permute-start | bytes 786440 | tf_op jit(solution)/shard_map/ppermute | solution.py:34
  210.9 13.1 %copy-start = (bf16[2,128,512]{2,1,0:T(8,128)(2,1)}, bf16[2,128,512]{2,1,0:T(8,128)(2,1)S(1)}, u32[]{:S(2)}) copy-start(bf16[2,128,512]{2,1,0:T(8,128)(2,1)S(1)} %pad_maximum_fusion.1.rest_0_) | copy-start | bytes 786436
  210.9 9.5 %collective-permute-start.19 = (bf16[2,128,512]{2,1,0:T(8,128)(2,1)S(1)}, bf16[2,128,512]{2,1,0:T(8,128)(2,1)S(1)}, u32[]{:S(2)}, u32[]{:S(2)}) collective-permute-start(bf16[2,128,512]{2,1,0:T(8,128)(2,1)S(1)} %pad_maximum_fusion.1.rest_0_), channel_id=1, source_target_pairs={{2,4},{5,3},{10,12},{13,11},{18,20},{21,19},{26,28},{29,27}} | collective-permute-start | bytes 786440 | tf_op jit(solution)/shard_map/ppermute | solution.py:34
  212.2 9.1 %collective-permute-start.18 = (bf16[2,128,512]{2,1,0:T(8,128)(2,1)S(1)}, bf16[2,128,512]{2,1,0:T(8,128)(2,1)S(1)}, u32[]{:S(2)}, u32[]{:S(2)}) collective-permute-start(bf16[2,128,512]{2,1,0:T(8,128)(2,1)S(1)} %pad_maximum_fusion.1.rest_0_), channel_id=1, source_target_pairs={{0,4},{7,3},{8,12},{15,11},{16,20},{23,19},{24,28},{31,27}} | collective-permute-start | bytes 786440 | tf_op jit(solution)/shard_map/ppermute | solution.py:34
  213.5 10.4 %collective-permute-start.17 = (bf16[2,128,512]{2,1,0:T(8,128)(2,1)S(1)}, bf16[2,128,512]{2,1,0:T(8,128)(2,1)S(1)}, u32[]{:S(2)}, u32[]{:S(2)}) collective-permute-start(bf16[2,128,512]{2,1,0:T(8,128)(2,1)S(1)} %pad_maximum_fusion.1.rest_0_), channel_id=1, source_target_pairs={{1,3},{6,4},{9,11},{14,12},{17,19},{22,20},{25,27},{30,28}} | collective-permute-start | bytes 786440 | tf_op jit(solution)/shard_map/ppermute | solution.py:34
  214.9 0.7 copy-start.2
  217.4 40.3 %collective-permute-start.25 = (bf16[64,512]{1,0:T(8,128)(2,1)}, bf16[64,512]{1,0:T(8,128)(2,1)S(1)}, u32[]{:S(2)}, u32[]{:S(2)}) collective-permute-start(bf16[64,512]{1,0:T(8,128)(2,1)} %get-tuple-element.67), channel_id=1, source_target_pairs={{0,2},{1,3},{2,0},{3,1},{4,6},{5,7},{6,4},{7,5},{8,10},{9,11},{10,... | collective-permute-start | bytes 196616 | tf_op jit(solution)/shard_map/ppermute | solution.py:34
  219.7 38.0 %collective-permute-start.26 = (bf16[64,512]{1,0:T(8,128)(2,1)}, bf16[64,512]{1,0:T(8,128)(2,1)S(1)}, u32[]{:S(2)}, u32[]{:S(2)}) collective-permute-start(bf16[64,512]{1,0:T(8,128)(2,1)} %get-tuple-element.68), channel_id=1, source_target_pairs={{0,4},{1,5},{2,6},{3,7},{4,0},{5,1},{6,2},{7,3},{8,12},{9,13},{10,... | collective-permute-start | bytes 196616 | tf_op jit(solution)/shard_map/ppermute | solution.py:34
  220.4 3.6 %copy-start.3 = (bf16[2,128,512]{2,1,0:T(8,128)(2,1)}, bf16[2,128,512]{2,1,0:T(8,128)(2,1)S(1)}, u32[]{:S(2)}) copy-start(bf16[2,128,512]{2,1,0:T(8,128)(2,1)S(1)} %collective-permute-done.19.rest_3_) | copy-start | bytes 786436
  220.4 37.3 %collective-permute-start.27 = (bf16[64,512]{1,0:T(8,128)(2,1)}, bf16[64,512]{1,0:T(8,128)(2,1)S(1)}, u32[]{:S(2)}, u32[]{:S(2)}) collective-permute-start(bf16[64,512]{1,0:T(8,128)(2,1)} %get-tuple-element.69), channel_id=1, source_target_pairs={{0,6},{1,7},{2,4},{3,5},{4,2},{5,3},{6,0},{7,1},{8,14},{9,15},{10,... | collective-permute-start | bytes 196616 | tf_op jit(solution)/shard_map/ppermute | solution.py:34
  221.3 2.7 %copy-start.4 = (bf16[2,128,512]{2,1,0:T(8,128)(2,1)}, bf16[2,128,512]{2,1,0:T(8,128)(2,1)S(1)}, u32[]{:S(2)}) copy-start(bf16[2,128,512]{2,1,0:T(8,128)(2,1)S(1)} %collective-permute-done.18.rest_2_) | copy-start | bytes 786436
  224.0 0.7 copy-start.5
  (5 other events, 3.1 us)

commit v4 on v3

--- a/solution.py
+++ b/solution.py
@@ -10,7 +10,6 @@
 
 H = 32
 HIDDEN = -1e30
-VMEM = 60 * 1024 * 1024
 NT = (((1,), (1,)), ((), ()))
 TN = (((0,), (0,)), ((), ()))
 NN = (((1,), (0,)), ((), ()))
@@ -20,12 +19,14 @@
     return lax.dot_general(a, b, dims, preferred_element_type=jnp.float32)
 
 
-def params():
-    return pltpu.CompilerParams(vmem_limit_bytes=VMEM)
+def params(mib):
+    return pltpu.CompilerParams(vmem_limit_bytes=mib * 1024 * 1024)
 
 
 SMEM = pl.BlockSpec(memory_space=pltpu.SMEM)
 HBM = pl.BlockSpec(memory_space=pltpu.HBM)
+ANY = pl.BlockSpec(memory_space=pl.ANY)
+VM = pl.BlockSpec(memory_space=pltpu.VMEM)
 LANES = 128
 
 
@@ -75,10 +76,10 @@
     return pl.pallas_call(
         functools.partial(pack_kernel, count, model // count, hd, first, nh),
         out_shape=[jax.ShapeDtypeStruct((nh * 3 * tok, hd), q.dtype)] * count,
-        in_specs=[SMEM, HBM, HBM, HBM, HBM],
-        out_specs=[HBM] * count,
+        in_specs=[SMEM, VM, VM, VM, ANY],
+        out_specs=[ANY] * count,
         scratch_shapes=[pltpu.SemaphoreType.DMA((3 * nh * count,))],
-        compiler_params=params(),
+        compiler_params=params(4),
         name="pack",
     )(me, q, k, v, after)
 
@@ -86,16 +87,15 @@
 def first_kernel(count, group, hd, nh, mask_rows, tiles, me_ref, nb_ref, *rest):
     q_ref, k_ref, v_ref, x_ref, down_ref = rest[:5]
     outs, rest = rest[5 : 5 + count], rest[5 + count :]
-    x_s, down_s, note_s, sems, in_sems, note_sems = rest
+    q_s, k_s, v_s, x_s, down_s, note_s, sems, in_sems, note_sems = rest
     me = me_ref[0]
     tok = q_ref.shape[0]
     rank = down_ref.shape[0]
+    pairs = ((q_ref, q_s), (k_ref, k_s), (v_ref, v_s), (x_ref, x_s), (down_ref, down_s))
     loads = [
-        pltpu.make_async_copy(x_ref, x_s, in_sems.at[0]),
-        pltpu.make_async_copy(down_ref, down_s, in_sems.at[1]),
+        pltpu.make_async_copy(ref, to, in_sems.at[n]) for n, (ref, to) in enumerate(pairs)
     ]
-    copies = pack_copies(count, group, hd, 0, nh, me, (q_ref, k_ref, v_ref), outs, sems)
-    for copy in loads + copies:
+    for copy in loads:
         copy.start()
     rows = lax.broadcasted_iota(jnp.int32, (mask_rows, tok), 0)
     lane_tile = lax.broadcasted_iota(jnp.int32, (mask_rows, tok), 1) // (tok // tiles)
@@ -105,7 +105,12 @@
             slot = nb_ref[t, n] - (me - 1) * tiles
             seen = jnp.where((rows == slot) & (lane_tile == t), 1.0, seen)
     note_s[rank:, :] = seen.astype(jnp.bfloat16)
-    for copy in loads:
+    for copy in loads[:3]:
+        copy.wait()
+    copies = pack_copies(count, group, hd, 0, nh, me, (q_s, k_s, v_s), outs, sems)
+    for copy in copies:
+        copy.start()
+    for copy in loads[3:]:
         copy.wait()
     note_s[:rank, :] = mm(down_s[...], x_s[...], NT).astype(jnp.bfloat16)
     notes = [
@@ -132,15 +137,15 @@
         out_shape=[jax.ShapeDtypeStruct((rows, hd), bf)] * count,
         in_specs=[SMEM, SMEM] + [HBM] * 5,
         out_specs=[HBM] * count,
-        scratch_shapes=[
-            pltpu.VMEM(x.shape, bf),
+        scratch_shapes=[pltpu.VMEM(x.shape, bf)] * 4
+        + [
             pltpu.VMEM(down.shape, bf),
             pltpu.VMEM((rank + mask_rows, tok), bf),
             pltpu.SemaphoreType.DMA((3 * nh * count,)),
-            pltpu.SemaphoreType.DMA((2,)),
+            pltpu.SemaphoreType.DMA((5,)),
             pltpu.SemaphoreType.DMA((count,)),
         ],
-        compiler_params=params(),
+        compiler_params=params(60),
         name="first_pack",
     )(me, nb, q, k, v, x, down)
 
@@ -170,11 +175,11 @@
     return pl.pallas_call(
         functools.partial(assemble_kernel, count, home.shape[1] // count),
         out_shape=jax.ShapeDtypeStruct(home.shape, home.dtype),
-        in_specs=[SMEM] + [HBM] * (len(blocks) + 1),
-        out_specs=HBM,
+        in_specs=[SMEM] + [ANY] * (len(blocks) + 1),
+        out_specs=ANY,
         input_output_aliases={1: 0},
         scratch_shapes=[pltpu.SemaphoreType.DMA((count,))],
-        compiler_params=params(),
+        compiler_params=params(4),
         name="assemble",
     )(me, home, *blocks)
 
@@ -206,22 +211,15 @@
 
 def home_kernel(count, slots, rank, hd, me_ref, *rest):
     notes, rest = rest[:count], rest[count:]
-    q_ref, k_ref, v_ref, low_ref, high_ref, up_ref, out_ref, note_s, sems = rest
+    q_ref, k_ref, v_ref, low_ref, high_ref, up_ref, out_ref, note_s = rest
     tok = q_ref.shape[0]
+
+    size = note_s.shape[1]
 
     @pl.when(pl.program_id(0) == 0)
     def _():
-        size = note_s.shape[1]
-        copies = [
-            pltpu.make_async_copy(
-                ref.at[pl.ds(ref.shape[0] - size, size), :], note_s.at[p], sems.at[p]
-            )
-            for p, ref in enumerate(notes)
-        ]
-        for copy in copies:
-            copy.start()
-        for copy in copies:
-            copy.wait()
+        for p, ref in enumerate(notes):
+            note_s[p] = ref[ref.shape[0] - size :, :]
 
     mask = note_s[0][rank:, :]
     loras = [note_s[w][:rank, :] for w in window(me_ref[0], 0, count)]
@@ -249,16 +247,13 @@
         grid=(model // width,),
         out_shape=jax.ShapeDtypeStruct(q.shape, q.dtype),
         in_specs=[SMEM]
-        + [HBM] * count
+        + [VM] * count
         + [column] * 3
         + [pair] * 2
         + [pl.BlockSpec((rank, width), lambda h: (0, h))],
         out_specs=column,
-        scratch_shapes=[
-            pltpu.VMEM((count, rank + mask_rows, tok), q.dtype),
-            pltpu.SemaphoreType.DMA((count,)),
-        ],
-        compiler_params=params(),
+        scratch_shapes=[pltpu.VMEM((count, rank + mask_rows, tok), q.dtype)],
+        compiler_params=params(16),
         cost_estimate=pl.CostEstimate(
             flops=12 * 10**9, bytes_accessed=9 * tok * model * 2, transcendentals=0
         ),
@@ -278,35 +273,16 @@
         keep_ref, send_ref, hid_keep, hid_send, gup_ref, rest = *rest[:5], rest[5:]
     else:
         hid_ref_out, gup_ref, out_ref, rest = *rest[:3], rest[3:]
-    b_s, note_s, q_s, k_s, vt_s, svt_s, lora_s, grad_s, hid_s, out_s, sems, note_sems = rest
+    note_s, q_s, k_s, vt_s, svt_s, lora_s, grad_s, hid_s, out_s = rest
     head = pl.program_id(0)
     me = me_ref[0]
     scale = log_scale(hd)
-    size, rows = note_s.shape[1], 3 * tok
-
-    def block_copies(h):
-        return [
-            pltpu.make_async_copy(
-                blocks[p].at[pl.ds(pl.multiple_of(h * rows, rows), rows), :],
-                b_s.at[lax.rem(h, 2), p],
-                sems.at[lax.rem(h, 2), p],
-            )
-            for p in range(count)
-        ]
+    size = note_s.shape[1]
 
     @pl.when(head == 0)
     def _():
-        copies = [
-            pltpu.make_async_copy(
-                ref.at[pl.ds(sizes - size, size), :], note_s.at[p], note_sems.at[p]
-            )
-            for p, ref in enumerate(noted)
-        ]
-        for copy in copies + block_copies(0):
-            copy.start()
-        for copy in copies:
-            copy.wait()
-        for p in range(count):
+        for p, ref in enumerate(noted):
+            note_s[p] = ref[sizes - size :, :]
             lora_s[:, p * tok : (p + 1) * tok] = note_s[p, :rank, :]
         if before:
             hid_s[...] = hid_ref[...]
@@ -315,18 +291,11 @@
         else:
             hid_s[...] = jnp.zeros_like(hid_s)
 
-    @pl.when(head + 1 < nh)
-    def _():
-        for copy in block_copies(head + 1):
-            copy.start()
-
-    for copy in block_copies(head):
-        copy.wait()
-    at = lax.rem(head, 2)
+    start = pl.multiple_of(head * 3 * tok, tok)
     for p in range(count):
-        q_s[p * tok : (p + 1) * tok, :] = b_s[at, p, :tok, :]
-        k_s[p * tok : (p + 1) * tok, :] = b_s[at, p, tok : 2 * tok, :]
-        vt_s[:, p * tok : (p + 1) * tok] = b_s[at, p, 2 * tok :, :].T
+        q_s[p * tok : (p + 1) * tok, :] = blocks[p][pl.ds(start, tok), :]
+        k_s[p * tok : (p + 1) * tok, :] = blocks[p][pl.ds(start + tok, tok), :]
+        vt_s[:, p * tok : (p + 1) * tok] = blocks[p][pl.ds(start + 2 * tok, tok), :].T
     up_t = up_ref[...]
     for p in range(count):
         cols = slice(p * tok, (p + 1) * tok)
@@ -334,26 +303,23 @@
         svt_s[p] = (vt_s[:, cols].astype(jnp.float32) + term).astype(jnp.bfloat16)
     grad_s[...] = jnp.zeros_like(grad_s)
 
-    for pair in range(count // 2):
-        queries = q_s[2 * pair * tok : 2 * (pair + 1) * tok, :]
-        expo, norm = soft(mm(k_s[...], queries, NT), scale)
-        teachers = mm(vt_s[...], expo.astype(jnp.bfloat16)) / norm
-        teachers = teachers.astype(jnp.bfloat16).astype(jnp.float32)
-        for p in (2 * pair, 2 * pair + 1):
-            teacher = teachers[:, (p % 2) * tok : (p % 2 + 1) * tok]
-            places = window(me, p, count)
-            keys = jnp.concatenate(
-                [k_s[pl.ds(pl.multiple_of(w * tok, tok), tok), :] for w in places], axis=0
-            )
-            query = q_s[p * tok : (p + 1) * tok, :]
-            weights = tile_weights(keys, query, note_s[p, rank:, :], slots, scale)
-            values = jnp.concatenate([svt_s[w] for w in places], axis=1)
-            student = mm(values, weights)
-            out_s[before + head, p] = student.astype(jnp.bfloat16)
-            delta = ((student - teacher) * factor).astype(jnp.bfloat16)
-            grads = mm(weights, delta, NT)
-            for n, w in enumerate(places):
-                grad_s[w] += grads[n * tok : (n + 1) * tok]
+    for p in range(count):
+        query = q_s[p * tok : (p + 1) * tok, :]
+        expo, norm = soft(mm(k_s[...], query, NT), scale)
+        teacher = mm(vt_s[...], expo.astype(jnp.bfloat16)) / norm
+        teacher = teacher.astype(jnp.bfloat16).astype(jnp.float32)
+        places = window(me, p, count)
+        keys = jnp.concatenate(
+            [k_s[pl.ds(pl.multiple_of(w * tok, tok), tok), :] for w in places], axis=0
+        )
+        weights = tile_weights(keys, query, note_s[p, rank:, :], slots, scale)
+        values = jnp.concatenate([svt_s[w] for w in places], axis=1)
+        student = mm(values, weights)
+        out_s[before + head, p] = student.astype(jnp.bfloat16)
+        delta = ((student - teacher) * factor).astype(jnp.bfloat16)
+        grads = mm(weights, delta, NT)
+        for n, w in enumerate(places):
+            grad_s[w] += grads[n * tok : (n + 1) * tok]
 
     grad = grad_s[...].reshape(count * tok, hd).astype(jnp.bfloat16)
     column = pl.multiple_of((before + head) * hd, LANES)
@@ -417,12 +383,11 @@
         grid=(nh,),
         out_shape=shapes,
         in_specs=[SMEM]
-        + [HBM] * (2 * count)
-        + [pl.BlockSpec((rank, hd), lambda h: (0, first + h)), HBM]
+        + [VM] * (2 * count)
+        + [pl.BlockSpec((rank, hd), lambda h: (0, first + h)), ANY]
         + [whole(g.shape) for g in given],
         out_specs=[whole(s.shape) for s in shapes],
         scratch_shapes=[
-            pltpu.VMEM((2, count, 3 * tok, hd), bf),
             pltpu.VMEM((count, rank + mask_rows, tok), bf),
             pltpu.VMEM((keys, hd), bf),
             pltpu.VMEM((keys, hd), bf),
@@ -432,18 +397,13 @@
             pltpu.VMEM((count, tok, hd), f32),
             pltpu.VMEM((rank, keys), f32),
             pltpu.VMEM((heads, count, hd, tok), bf),
-            pltpu.SemaphoreType.DMA((2, count)),
-            pltpu.SemaphoreType.DMA((count,)),
         ],
-        compiler_params=params(),
+        compiler_params=params(30),
         cost_estimate=pl.CostEstimate(
             flops=nh * 6 * 10**9, bytes_accessed=4 * nh * keys * hd * 2, transcendentals=0
         ),
         name="attention",
     )(me, *blocks, *noted, up_t, after, *given)
-
-
-VM = pl.BlockSpec(memory_space=pltpu.VMEM)
 
 
 def pair_kernel(parts, keep_ref, got_ref, *outs):
@@ -465,7 +425,7 @@
         out_shape=shapes,
         in_specs=[VM, VM],
         out_specs=[VM] * parts,
-        compiler_params=params(),
+        compiler_params=params(8),
         name="pair_sum",
     )(keep, got)
 
@@ -503,7 +463,7 @@
         ],
         in_specs=[SMEM] + [VM] * (len(parts) + 1),
         out_specs=[VM, VM],
-        compiler_params=params(),
+        compiler_params=params(8),
         name="down_terms",
     )(me, *parts, x)
 
@@ -521,7 +481,7 @@
         out_shape=jax.ShapeDtypeStruct(parts[0].shape, jnp.float32),
         in_specs=[VM] * len(parts),
         out_specs=VM,
-        compiler_params=params(),
+        compiler_params=params(8),
         name="sum_terms",
     )(*parts)
 

time: 261 us -> 168 us (0.64)
  the two profiles are of different devices: /device:TPU:13 before, /device:TPU:0 now
where the time goes in v4:
time: 168 us
  waiting for transfers between devices  62.3 us (37%)
  starting transfers between devices  52.2 us (31%)
  Pallas kernels  44.6 us (27%)
  local copies, waits for them, and re-layouts  4.43 us (3%)
  other arithmetic  3.13 us (2%)
    ppermute x26, waiting for transfers between devices, swap(): return lax.ppermute(block, 'context', pairs)  62.3 us
    ppermute x26, starting transfers between devices, swap(): return lax.ppermute(block, 'context', pairs)  46.6 us
    pallas_call x2, Pallas kernels, attention(): pl.pallas_call(functools.partial(attention_kernel, count, tok, hd, nh, sl...  23.2 us
    pallas_call x1, Pallas kernels, home_student(): pl.pallas_call(functools.partial(home_kernel, count, slots, rank, hd), gr...  14.7 us
    pallas_call x1, Pallas kernels, first_pack(): pl.pallas_call(functools.partial(first_kernel, count, model // count, hd,...  5.18 us
    ppermute x1, starting transfers between devices, local(): low = lax.ppermute(both, 'context', ups)  4.38 us
    unnamed x26, local copies, waits for them, and re-layouts  3.45 us
  transfers between devices with their start and end apart: 28, of which 10 were waited for; matrix products, arithmetic and copies ran while one was open for 1% of the time, Pallas kernels for 22%

profile of v4, /device:TPU:0, one launch (start us, length us, event | category | flops | bytes accessed | tf_op | source)
XLA Modules:
  0.0 167.6 jit_solution(8784813220883560208)
XLA Ops:
  0.6 3.1 %pad_maximum_fusion = bf16[2,128,4096]{2,1,0:T(8,128)(2,1)} fusion(bf16[1,128,4096]{2,1,0:T(8,128)(2,1)} %bitcast.12, bf16[1,128,4096]{2,1,0:T(8,128)(2,1)} %bitcast.11), kind=kLoop, calls=%fused_computation | loop fusion | flops 1048576 | bytes 4194304 | tf_op jit(solution)/shard_map/stack | solution.py:530
  3.7 1.3 collective-permute-start.8
  5.0 4.4 %collective-permute-start.7 = (bf16[2,128,4096]{2,1,0:T(8,128)(2,1)}, bf16[2,128,4096]{2,1,0:T(8,128)(2,1)}, u32[]{:S(2)}, u32[]{:S(2)}) collective-permute-start(bf16[2,128,4096]{2,1,0:T(8,128)(2,1)} %pad_maximum_fusion), channel_id=1, source_target_pairs={{0,1},{1,2},{2,3},{4,5},{5,6},{6,7},{8,9},{9,10},{10,11},{12,13},{... | collective-permute-start | bytes 6291464 | tf_op jit(solution)/shard_map/ppermute | solution.py:531
  9.4 5.2 %first_pack.1 = (bf16[1232,128]{1,0:T(8,128)(2,1)}, bf16[1232,128]{1,0:T(8,128)(2,1)}, bf16[1232,128]{1,0:T(8,128)(2,1)}, bf16[1232,128]{1,0:T(8,128)(2,1)}, bf1...) custom-call(s32[1]{0:T(128)} %bitcast.me_ref, ...), custom_call_target="tpu_custom_call" | custom-call | tf_op jit(solution)/shard_map/first_pack/pallas_call | solution.py:133
  14.6 1.4 collective-permute-start
  16.0 1.8 %collective-permute-start.1 = (bf16[1232,128]{1,0:T(8,128)(2,1)}, bf16[1232,128]{1,0:T(8,128)(2,1)S(1)}, u32[]{:S(2)}, u32[]{:S(2)}) collective-permute-start(bf16[1232,128]{1,0:T(8,128)(2,1)} %get-tuple-element.39), channel_id=1, source_target_pairs={{0,2},{1,3},{2,0},{3,1},{4,6},{5,7},{6,4},{7,5},{8,10},{9,11},{10,... | collective-permute-start | bytes 946184 | tf_op jit(solution)/shard_map/ppermute | solution.py:35
  17.9 0.7 copy-done.7
  18.6 3.7 %collective-permute-start.6 = (bf16[1232,128]{1,0:T(8,128)(2,1)}, bf16[1232,128]{1,0:T(8,128)(2,1)S(1)}, u32[]{:S(2)}, u32[]{:S(2)}) collective-permute-start(bf16[1232,128]{1,0:T(8,128)(2,1)} %get-tuple-element.44), channel_id=1, source_target_pairs={{0,7},{1,6},{2,5},{3,4},{4,3},{5,2},{6,1},{7,0},{8,15},{9,14},{10,... | collective-permute-start | bytes 946184 | tf_op jit(solution)/shard_map/ppermute | solution.py:35
  22.3 24.1 %collective-permute-done.1.rest_2_.rest_10_ = bf16[1232,128]{1,0:T(8,128)(2,1)S(1)} collective-permute-done((bf16[1232,128]{1,0:T(8,128)(2,1)}, bf16[1232,128]{1,0:T(8,128)(2,1)S(1)}, u32[]{:S(2)}, u32[]{:S(2)}) %collective-permute-start.1) | collective-permute-done | bytes 315424 | tf_op jit(solution)/shard_map/ppermute | solution.py:35
  46.4 0.7 copy-done.9
  47.1 2.6 %collective-permute-start.3 = (bf16[1232,128]{1,0:T(8,128)(2,1)}, bf16[1232,128]{1,0:T(8,128)(2,1)}, u32[]{:S(2)}, u32[]{:S(2)}) collective-permute-start(bf16[1232,128]{1,0:T(8,128)(2,1)} %get-tuple-element.41), channel_id=1, source_target_pairs={{0,4},{1,5},{2,6},{3,7},{4,0},{5,1},{6,2},{7,3},{8,12},{9,13},{10,... | collective-permute-start | bytes 946184 | tf_op jit(solution)/shard_map/ppermute | solution.py:35
  49.7 0.7 copy-done.11
  50.4 6.8 %collective-permute-start.4 = (bf16[1232,128]{1,0:T(8,128)(2,1)}, bf16[1232,128]{1,0:T(8,128)(2,1)}, u32[]{:S(2)}, u32[]{:S(2)}) collective-permute-start(bf16[1232,128]{1,0:T(8,128)(2,1)} %get-tuple-element.42), channel_id=1, source_target_pairs={{0,5},{1,4},{2,7},{3,6},{4,1},{5,0},{6,3},{7,2},{8,13},{9,12},{10,... | collective-permute-start | bytes 946184 | tf_op jit(solution)/shard_map/ppermute | solution.py:35
  57.2 4.1 %collective-permute-start.5 = (bf16[1232,128]{1,0:T(8,128)(2,1)}, bf16[1232,128]{1,0:T(8,128)(2,1)}, u32[]{:S(2)}, u32[]{:S(2)}) collective-permute-start(bf16[1232,128]{1,0:T(8,128)(2,1)} %get-tuple-element.43), channel_id=1, source_target_pairs={{0,6},{1,7},{2,4},{3,5},{4,2},{5,3},{6,0},{7,1},{8,14},{9,15},{10,... | collective-permute-start | bytes 946184 | tf_op jit(solution)/shard_map/ppermute | solution.py:35
  61.4 1.0 dynamic-slice_bitcast_fusion.rest_16_
  62.4 0.5 pack.1
  62.9 19.4 %collective-permute-done.3.rest_4_.rest_12_ = bf16[1232,128]{1,0:T(8,128)(2,1)} collective-permute-done((bf16[1232,128]{1,0:T(8,128)(2,1)}, bf16[1232,128]{1,0:T(8,128)(2,1)}, u32[]{:S(2)}, u32[]{:S(2)}) %collective-permute-start.3) | collective-permute-done | bytes 315424 | tf_op jit(solution)/shard_map/ppermute | solution.py:35
  82.3 0.1 collective-permute-start.9
  82.4 6.7 %collective-permute-done.4.rest_5_.rest_13_ = bf16[1232,128]{1,0:T(8,128)(2,1)} collective-permute-done((bf16[1232,128]{1,0:T(8,128)(2,1)}, bf16[1232,128]{1,0:T(8,128)(2,1)}, u32[]{:S(2)}, u32[]{:S(2)}) %collective-permute-start.4) | collective-permute-done | bytes 315424 | tf_op jit(solution)/shard_map/ppermute | solution.py:35
  89.1 7.0 %collective-permute-start.11 = (bf16[384,128]{1,0:T(8,128)(2,1)S(1)}, bf16[384,128]{1,0:T(8,128)(2,1)S(1)}, u32[]{:S(2)}, u32[]{:S(2)}) collective-permute-start(bf16[384,128]{1,0:T(8,128)(2,1)S(1)} %get-tuple-element.48), channel_id=1, source_target_pairs={{0,3},{1,2},{2,1},{3,0},{4,7},{5,6},{6,5},{7,4},{8,11},{9,10},{10,... | collective-permute-start | bytes 294920 | tf_op jit(solution)/shard_map/ppermute | solution.py:35
  96.1 2.7 %collective-permute-start.13 = (bf16[384,128]{1,0:T(8,128)(2,1)S(1)}, bf16[384,128]{1,0:T(8,128)(2,1)S(1)}, u32[]{:S(2)}, u32[]{:S(2)}) collective-permute-start(bf16[384,128]{1,0:T(8,128)(2,1)S(1)} %get-tuple-element.50), channel_id=1, source_target_pairs={{0,5},{1,4},{2,7},{3,6},{4,1},{5,0},{6,3},{7,2},{8,13},{9,12},{10,... | collective-permute-start | bytes 294920 | tf_op jit(solution)/shard_map/ppermute | solution.py:35
  98.8 14.7 %home_student.1.rest_17_.home_ref = bf16[128,4096]{1,0:T(8,128)(2,1)} custom-call(s32[1]{0:T(128)} %bitcast.me_ref, bf16[1232,128]{1,0:T(8,128)(2,1)S(1)} %copy-done.6, bf16[1232,128]{1,0:T(8,128)(2,1)S(1)} %copy-done.8, bf16[1232,128]{1,0:T(8,128)(2,1)S(1)} %copy-done.10, bf16[1232,128]{1,0:T(8,128)(2,1)S(1)} %copy-done.12, ...), custom_call_target="tpu_custom_call" | custom-call | flops 12000000000 | bytes 9437184 | tf_op jit(solution)/shard_map/home_student/pallas_call | solution.py:245
  113.5 0.4 collective-permute-start.14
  113.9 3.1 %collective-permute-start.15 = (bf16[384,128]{1,0:T(8,128)(2,1)S(1)}, bf16[384,128]{1,0:T(8,128)(2,1)S(1)}, u32[]{:S(2)}, u32[]{:S(2)}) collective-permute-start(bf16[384,128]{1,0:T(8,128)(2,1)S(1)} %get-tuple-element.52), channel_id=1, source_target_pairs={{0,7},{1,6},{2,5},{3,4},{4,3},{5,2},{6,1},{7,0},{8,15},{9,14},{10,... | collective-permute-start | bytes 294920 | tf_op jit(solution)/shard_map/ppermute | solution.py:35
  117.0 1.2 copy-done.4
  118.2 16.4 %attention.2 = (f32[64,1024]{1,0:T(8,128)S(1)}, f32[64,384]{1,0:T(8,128)S(1)}, bf16[3,8,128,128]{3,2,1,0:T(8,128)(2,1)S(1)}) custom-call(s32[1]{0:T(128)} %bitcast.me_ref, bf16[1232,128]{1,0:T(8,128)(2,1)S(1)} %copy-done.6, bf16[1232,128]{1,0:T(8,128)(2,1)S(1)} %copy-done.8, bf16[1232,128]{1,0:T(8,128)(2,1)S(1)} %copy-done.10, ...), custom_call_target="tpu_custom_call" | custom-call | flops 17999998976 | bytes 3145728 | tf_op jit(solution)/shard_map/attention/pallas_call | solution.py:369
  134.7 6.8 %attention.3 = (bf16[128,512]{1,0:T(8,128)(2,1)S(1)}, bf16[128,512]{1,0:T(8,128)(2,1)S(1)}, f32[64,512]{1,0:T(8,128)S(1)}, bf16[64,512]{1,0:T(8,128)(2,1)S(1)}, f32[64,512]{1,0:T(8,128)}) custom-call(s32[1]{0:T(128)} %bitcast.me_ref, bf16[384,128]{1,0:T(8,128)(2,1)S(1)} %get-tuple-element.45.rest_0_, bf16[384,128]{1,0:T(8,128)(2,1)S(1)} %collective-permute-done.9.rest_1_, ...), custom_call_target="tpu_custom_call" | custom-call | flops 6000000000 | bytes 1048576 | tf_op jit(solution)/shard_map/attention/pallas_call | solution.py:369
  141.4 0.4 collective-permute-start.16
  142.0 1.2 collective-permute-done.20.got_ref
  143.2 0.1 collective-permute-start.21
  143.2 1.8 %collective-permute-start.22 = (bf16[64,128]{1,0:T(8,128)(2,1)S(1)}, bf16[64,128]{1,0:T(8,128)(2,1)S(1)}, u32[]{:S(2)}, u32[]{:S(2)}) collective-permute-start(bf16[64,128]{1,0:T(8,128)(2,1)S(1)} %get-tuple-element.62), channel_id=1, source_target_pairs={{0,4},{1,5},{2,6},{3,7},{4,0},{5,1},{6,2},{7,3},{8,12},{9,13},{10,... | collective-permute-start | bytes 49160 | tf_op jit(solution)/shard_map/ppermute | solution.py:35
  145.0 2.6 %collective-permute-start.23 = (bf16[64,128]{1,0:T(8,128)(2,1)S(1)}, bf16[64,128]{1,0:T(8,128)(2,1)S(1)}, u32[]{:S(2)}, u32[]{:S(2)}) collective-permute-start(bf16[64,128]{1,0:T(8,128)(2,1)S(1)} %get-tuple-element.63), channel_id=1, source_target_pairs={{0,6},{1,7},{2,4},{3,5},{4,2},{5,3},{6,0},{7,1},{8,14},{9,15},{10,... | collective-permute-start | bytes 49160 | tf_op jit(solution)/shard_map/ppermute | solution.py:35
  147.6 0.3 collective-permute-done.22.rest_2_
  147.9 2.6 %collective-permute-done.23.rest_3_ = bf16[64,128]{1,0:T(8,128)(2,1)S(1)} collective-permute-done((bf16[64,128]{1,0:T(8,128)(2,1)S(1)}, bf16[64,128]{1,0:T(8,128)(2,1)S(1)}, u32[]{:S(2)}, u32[]{:S(2)}) %collective-permute-start.23) | collective-permute-done | bytes 16416 | tf_op jit(solution)/shard_map/ppermute | solution.py:35
  150.6 0.3 down_terms.1
  150.9 0.1 collective-permute-start.24
  151.0 0.7 collective-permute-start.19
  151.7 1.9 %collective-permute-start.18 = (bf16[2,128,512]{2,1,0:T(8,128)(2,1)S(1)}, bf16[2,128,512]{2,1,0:T(8,128)(2,1)S(1)}, u32[]{:S(2)}, u32[]{:S(2)}) collective-permute-start(bf16[2,128,512]{2,1,0:T(8,128)(2,1)S(1)} %pad_maximum_fusion.1.rest_0_), channel_id=1, source_target_pairs={{0,4},{7,3},{8,12},{15,11},{16,20},{23,19},{24,28},{31,27}} | collective-permute-start | bytes 786440 | tf_op jit(solution)/shard_map/ppermute | solution.py:35
  153.6 0.7 collective-permute-start.17
  154.4 0.1 collective-permute-start.25
  154.5 2.6 %collective-permute-start.26 = (bf16[64,512]{1,0:T(8,128)(2,1)S(1)}, bf16[64,512]{1,0:T(8,128)(2,1)S(1)}, u32[]{:S(2)}, u32[]{:S(2)}) collective-permute-start(bf16[64,512]{1,0:T(8,128)(2,1)S(1)} %get-tuple-element.68), channel_id=1, source_target_pairs={{0,4},{1,5},{2,6},{3,7},{4,0},{5,1},{6,2},{7,3},{8,12},{9,13},{10,... | collective-permute-start | bytes 196616 | tf_op jit(solution)/shard_map/ppermute | solution.py:35
  157.1 1.7 %collective-permute-start.27 = (bf16[64,512]{1,0:T(8,128)(2,1)S(1)}, bf16[64,512]{1,0:T(8,128)(2,1)S(1)}, u32[]{:S(2)}, u32[]{:S(2)}) collective-permute-start(bf16[64,512]{1,0:T(8,128)(2,1)S(1)} %get-tuple-element.69), channel_id=1, source_target_pairs={{0,6},{1,7},{2,4},{3,5},{4,2},{5,3},{6,0},{7,1},{8,14},{9,15},{10,... | collective-permute-start | bytes 196616 | tf_op jit(solution)/shard_map/ppermute | solution.py:35
  158.9 0.6 collective-permute-done.18.rest_2_
  159.4 0.1 assemble.1
  159.5 1.3 collective-permute-done.25.refs_1_
  160.8 1.4 collective-permute-done.26.refs_2_
  162.2 4.7 %collective-permute-done.27.refs_3_ = bf16[64,512]{1,0:T(8,128)(2,1)S(1)} collective-permute-done((bf16[64,512]{1,0:T(8,128)(2,1)S(1)}, bf16[64,512]{1,0:T(8,128)(2,1)S(1)}, u32[]{:S(2)}, u32[]{:S(2)}) %collective-permute-start.27) | collective-permute-done | bytes 65568 | tf_op jit(solution)/shard_map/ppermute | solution.py:35
  166.9 0.7 sum_terms.1
  (47 shorter events, 0.3 us)
Async XLA Ops:
  3.7 92.4 %collective-permute-start.8 = (bf16[2,128,4096]{2,1,0:T(8,128)(2,1)}, bf16[2,128,4096]{2,1,0:T(8,128)(2,1)}, u32[]{:S(2)}, u32[]{:S(2)}) collective-permute-start(bf16[2,128,4096]{2,1,0:T(8,128)(2,1)} %pad_maximum_fusion), channel_id=1, source_target_pairs={{1,0},{2,1},{3,2},{5,4},{6,5},{7,6},{9,8},{10,9},{11,10},{13,12},{... | collective-permute-start | bytes 6291464 | tf_op jit(solution)/shard_map/ppermute | solution.py:532
  5.0 91.1 %collective-permute-start.7 = (bf16[2,128,4096]{2,1,0:T(8,128)(2,1)}, bf16[2,128,4096]{2,1,0:T(8,128)(2,1)}, u32[]{:S(2)}, u32[]{:S(2)}) collective-permute-start(bf16[2,128,4096]{2,1,0:T(8,128)(2,1)} %pad_maximum_fusion), channel_id=1, source_target_pairs={{0,1},{1,2},{2,3},{4,5},{5,6},{6,7},{8,9},{9,10},{10,11},{12,13},{... | collective-permute-start | bytes 6291464 | tf_op jit(solution)/shard_map/ppermute | solution.py:531
  9.4 53.0 %copy-start = (bf16[128,4096]{1,0:T(8,128)(2,1)S(1)}, bf16[128,4096]{1,0:T(8,128)(2,1)}, u32[]{:S(2)}) copy-start(bf16[128,4096]{1,0:T(8,128)(2,1)} %k_ref.1) | copy-start | bytes 3145732
  9.4 53.0 %copy-start.1 = (bf16[128,4096]{1,0:T(8,128)(2,1)S(1)}, bf16[128,4096]{1,0:T(8,128)(2,1)}, u32[]{:S(2)}) copy-start(bf16[128,4096]{1,0:T(8,128)(2,1)} %v_ref.1) | copy-start | bytes 3145732
  9.4 53.0 %copy-start.2 = (bf16[128,4096]{1,0:T(8,128)(2,1)S(1)}, bf16[128,4096]{1,0:T(8,128)(2,1)}, u32[]{:S(2)}) copy-start(bf16[128,4096]{1,0:T(8,128)(2,1)} %q_ref.1) | copy-start | bytes 3145732
  14.6 3.3 %collective-permute-start = (bf16[1232,128]{1,0:T(8,128)(2,1)}, bf16[1232,128]{1,0:T(8,128)(2,1)S(1)}, u32[]{:S(2)}, u32[]{:S(2)}) collective-permute-start(bf16[1232,128]{1,0:T(8,128)(2,1)} %get-tuple-element.38), channel_id=1, source_target_pairs={{0,1},{1,0},{2,3},{3,2},{4,5},{5,4},{6,7},{7,6},{8,9},{9,8},{10,11... | collective-permute-start | bytes 946184 | tf_op jit(solution)/shard_map/ppermute | solution.py:35
  16.0 30.4 %collective-permute-start.1 = (bf16[1232,128]{1,0:T(8,128)(2,1)}, bf16[1232,128]{1,0:T(8,128)(2,1)S(1)}, u32[]{:S(2)}, u32[]{:S(2)}) collective-permute-start(bf16[1232,128]{1,0:T(8,128)(2,1)} %get-tuple-element.39), channel_id=1, source_target_pairs={{0,2},{1,3},{2,0},{3,1},{4,6},{5,7},{6,4},{7,5},{8,10},{9,11},{10,... | collective-permute-start | bytes 946184 | tf_op jit(solution)/shard_map/ppermute | solution.py:35
  17.8 31.9 %collective-permute-start.2 = (bf16[1232,128]{1,0:T(8,128)(2,1)}, bf16[1232,128]{1,0:T(8,128)(2,1)S(1)}, u32[]{:S(2)}, u32[]{:S(2)}) collective-permute-start(bf16[1232,128]{1,0:T(8,128)(2,1)} %get-tuple-element.40), channel_id=1, source_target_pairs={{0,3},{1,2},{2,1},{3,0},{4,7},{5,6},{6,5},{7,4},{8,11},{9,10},{10,... | collective-permute-start | bytes 946184 | tf_op jit(solution)/shard_map/ppermute | solution.py:35
  17.9 0.7 copy-start.7
  18.6 38.6 %collective-permute-start.6 = (bf16[1232,128]{1,0:T(8,128)(2,1)}, bf16[1232,128]{1,0:T(8,128)(2,1)S(1)}, u32[]{:S(2)}, u32[]{:S(2)}) collective-permute-start(bf16[1232,128]{1,0:T(8,128)(2,1)} %get-tuple-element.44), channel_id=1, source_target_pairs={{0,7},{1,6},{2,5},{3,4},{4,3},{5,2},{6,1},{7,0},{8,15},{9,14},{10,... | collective-permute-start | bytes 946184 | tf_op jit(solution)/shard_map/ppermute | solution.py:35
  46.4 0.7 copy-start.9
  47.1 35.2 %collective-permute-start.3 = (bf16[1232,128]{1,0:T(8,128)(2,1)}, bf16[1232,128]{1,0:T(8,128)(2,1)}, u32[]{:S(2)}, u32[]{:S(2)}) collective-permute-start(bf16[1232,128]{1,0:T(8,128)(2,1)} %get-tuple-element.41), channel_id=1, source_target_pairs={{0,4},{1,5},{2,6},{3,7},{4,0},{5,1},{6,2},{7,3},{8,12},{9,13},{10,... | collective-permute-start | bytes 946184 | tf_op jit(solution)/shard_map/ppermute | solution.py:35
  49.7 0.7 copy-start.11
  50.4 38.6 %collective-permute-start.4 = (bf16[1232,128]{1,0:T(8,128)(2,1)}, bf16[1232,128]{1,0:T(8,128)(2,1)}, u32[]{:S(2)}, u32[]{:S(2)}) collective-permute-start(bf16[1232,128]{1,0:T(8,128)(2,1)} %get-tuple-element.42), channel_id=1, source_target_pairs={{0,5},{1,4},{2,7},{3,6},{4,1},{5,0},{6,3},{7,2},{8,13},{9,12},{10,... | collective-permute-start | bytes 946184 | tf_op jit(solution)/shard_map/ppermute | solution.py:35
  57.2 31.9 %collective-permute-start.5 = (bf16[1232,128]{1,0:T(8,128)(2,1)}, bf16[1232,128]{1,0:T(8,128)(2,1)}, u32[]{:S(2)}, u32[]{:S(2)}) collective-permute-start(bf16[1232,128]{1,0:T(8,128)(2,1)} %get-tuple-element.43), channel_id=1, source_target_pairs={{0,6},{1,7},{2,4},{3,5},{4,2},{5,3},{6,0},{7,1},{8,14},{9,15},{10,... | collective-permute-start | bytes 946184 | tf_op jit(solution)/shard_map/ppermute | solution.py:35
  61.4 37.4 %copy-start.5 = (bf16[4096,64]{0,1:T(8,128)(2,1)S(1)}, bf16[4096,64]{0,1:T(8,128)(2,1)}, u32[]{:S(2)}) copy-start(bf16[4096,64]{0,1:T(8,128)(2,1)} %param.12) | copy-start | bytes 1572868
  61.4 37.4 %copy-start.6 = (bf16[1232,128]{1,0:T(8,128)(2,1)S(1)}, bf16[1232,128]{1,0:T(8,128)(2,1)}, u32[]{:S(2)}) copy-start(bf16[1232,128]{1,0:T(8,128)(2,1)} %get-tuple-element.37.rest_0_.rest_8_) | copy-start | bytes 946180
  61.4 37.4 %copy-start.8 = (bf16[1232,128]{1,0:T(8,128)(2,1)S(1)}, bf16[1232,128]{1,0:T(8,128)(2,1)}, u32[]{:S(2)}) copy-start(bf16[1232,128]{1,0:T(8,128)(2,1)} %copy-done.7) | copy-start | bytes 946180
  61.4 37.4 %copy-start.10 = (bf16[1232,128]{1,0:T(8,128)(2,1)S(1)}, bf16[1232,128]{1,0:T(8,128)(2,1)}, u32[]{:S(2)}) copy-start(bf16[1232,128]{1,0:T(8,128)(2,1)} %copy-done.9) | copy-start | bytes 946180
  61.4 37.4 %copy-start.12 = (bf16[1232,128]{1,0:T(8,128)(2,1)S(1)}, bf16[1232,128]{1,0:T(8,128)(2,1)}, u32[]{:S(2)}) copy-start(bf16[1232,128]{1,0:T(8,128)(2,1)} %copy-done.11) | copy-start | bytes 946180
  82.3 31.2 %collective-permute-start.9 = (bf16[384,128]{1,0:T(8,128)(2,1)S(1)}, bf16[384,128]{1,0:T(8,128)(2,1)S(1)}, u32[]{:S(2)}, u32[]{:S(2)}) collective-permute-start(bf16[384,128]{1,0:T(8,128)(2,1)S(1)} %get-tuple-element.46), channel_id=1, source_target_pairs={{0,1},{1,0},{2,3},{3,2},{4,5},{5,4},{6,7},{7,6},{8,9},{9,8},{10,11... | collective-permute-start | bytes 294920 | tf_op jit(solution)/shard_map/ppermute | solution.py:35
  89.1 24.8 %collective-permute-start.10 = (bf16[384,128]{1,0:T(8,128)(2,1)S(1)}, bf16[384,128]{1,0:T(8,128)(2,1)S(1)}, u32[]{:S(2)}, u32[]{:S(2)}) collective-permute-start(bf16[384,128]{1,0:T(8,128)(2,1)S(1)} %get-tuple-element.47), channel_id=1, source_target_pairs={{0,2},{1,3},{2,0},{3,1},{4,6},{5,7},{6,4},{7,5},{8,10},{9,11},{10,... | collective-permute-start | bytes 294920 | tf_op jit(solution)/shard_map/ppermute | solution.py:35
  89.1 45.5 %collective-permute-start.11 = (bf16[384,128]{1,0:T(8,128)(2,1)S(1)}, bf16[384,128]{1,0:T(8,128)(2,1)S(1)}, u32[]{:S(2)}, u32[]{:S(2)}) collective-permute-start(bf16[384,128]{1,0:T(8,128)(2,1)S(1)} %get-tuple-element.48), channel_id=1, source_target_pairs={{0,3},{1,2},{2,1},{3,0},{4,7},{5,6},{6,5},{7,4},{8,11},{9,10},{10,... | collective-permute-start | bytes 294920 | tf_op jit(solution)/shard_map/ppermute | solution.py:35
  96.1 38.5 %collective-permute-start.12 = (bf16[384,128]{1,0:T(8,128)(2,1)S(1)}, bf16[384,128]{1,0:T(8,128)(2,1)S(1)}, u32[]{:S(2)}, u32[]{:S(2)}) collective-permute-start(bf16[384,128]{1,0:T(8,128)(2,1)S(1)} %get-tuple-element.49), channel_id=1, source_target_pairs={{0,4},{1,5},{2,6},{3,7},{4,0},{5,1},{6,2},{7,3},{8,12},{9,13},{10,... | collective-permute-start | bytes 294920 | tf_op jit(solution)/shard_map/ppermute | solution.py:35
  96.1 38.5 %collective-permute-start.13 = (bf16[384,128]{1,0:T(8,128)(2,1)S(1)}, bf16[384,128]{1,0:T(8,128)(2,1)S(1)}, u32[]{:S(2)}, u32[]{:S(2)}) collective-permute-start(bf16[384,128]{1,0:T(8,128)(2,1)S(1)} %get-tuple-element.50), channel_id=1, source_target_pairs={{0,5},{1,4},{2,7},{3,6},{4,1},{5,0},{6,3},{7,2},{8,13},{9,12},{10,... | collective-permute-start | bytes 294920 | tf_op jit(solution)/shard_map/ppermute | solution.py:35
  113.5 21.2 %collective-permute-start.14 = (bf16[384,128]{1,0:T(8,128)(2,1)S(1)}, bf16[384,128]{1,0:T(8,128)(2,1)S(1)}, u32[]{:S(2)}, u32[]{:S(2)}) collective-permute-start(bf16[384,128]{1,0:T(8,128)(2,1)S(1)} %get-tuple-element.51), channel_id=1, source_target_pairs={{0,6},{1,7},{2,4},{3,5},{4,2},{5,3},{6,0},{7,1},{8,14},{9,15},{10,... | collective-permute-start | bytes 294920 | tf_op jit(solution)/shard_map/ppermute | solution.py:35
  113.9 20.8 %collective-permute-start.15 = (bf16[384,128]{1,0:T(8,128)(2,1)S(1)}, bf16[384,128]{1,0:T(8,128)(2,1)S(1)}, u32[]{:S(2)}, u32[]{:S(2)}) collective-permute-start(bf16[384,128]{1,0:T(8,128)(2,1)S(1)} %get-tuple-element.52), channel_id=1, source_target_pairs={{0,7},{1,6},{2,5},{3,4},{4,3},{5,2},{6,1},{7,0},{8,15},{9,14},{10,... | collective-permute-start | bytes 294920 | tf_op jit(solution)/shard_map/ppermute | solution.py:35
  117.0 1.2 copy-start.4
  134.7 15.9 %copy-start.3 = (bf16[128,4096]{1,0:T(8,128)(2,1)S(1)}, bf16[128,4096]{1,0:T(8,128)(2,1)}, u32[]{:S(2)}) copy-start(bf16[128,4096]{1,0:T(8,128)(2,1)} %rest_4_.1) | copy-start | bytes 3145732
  141.4 9.5 %collective-permute-start.16 = (bf16[128,512]{1,0:T(8,128)(2,1)S(1)}, bf16[128,512]{1,0:T(8,128)(2,1)S(1)}, u32[]{:S(2)}, u32[]{:S(2)}) collective-permute-start(bf16[128,512]{1,0:T(8,128)(2,1)S(1)} %get-tuple-element.57), channel_id=1, source_target_pairs={{0,1},{1,0},{2,3},{3,2},{4,5},{5,4},{6,7},{7,6},{8,9},{9,8},{10,11... | collective-permute-start | bytes 393224 | tf_op jit(solution)/shard_map/ppermute | solution.py:35
  141.9 1.3 collective-permute-start.20
  143.2 4.5 %collective-permute-start.21 = (bf16[64,128]{1,0:T(8,128)(2,1)S(1)}, bf16[64,128]{1,0:T(8,128)(2,1)S(1)}, u32[]{:S(2)}, u32[]{:S(2)}) collective-permute-start(bf16[64,128]{1,0:T(8,128)(2,1)S(1)} %get-tuple-element.61), channel_id=1, source_target_pairs={{0,2},{1,3},{2,0},{3,1},{4,6},{5,7},{6,4},{7,5},{8,10},{9,11},{10,... | collective-permute-start | bytes 49160 | tf_op jit(solution)/shard_map/ppermute | solution.py:35
  143.2 4.7 %collective-permute-start.22 = (bf16[64,128]{1,0:T(8,128)(2,1)S(1)}, bf16[64,128]{1,0:T(8,128)(2,1)S(1)}, u32[]{:S(2)}, u32[]{:S(2)}) collective-permute-start(bf16[64,128]{1,0:T(8,128)(2,1)S(1)} %get-tuple-element.62), channel_id=1, source_target_pairs={{0,4},{1,5},{2,6},{3,7},{4,0},{5,1},{6,2},{7,3},{8,12},{9,13},{10,... | collective-permute-start | bytes 49160 | tf_op jit(solution)/shard_map/ppermute | solution.py:35
  145.0 5.5 %collective-permute-start.23 = (bf16[64,128]{1,0:T(8,128)(2,1)S(1)}, bf16[64,128]{1,0:T(8,128)(2,1)S(1)}, u32[]{:S(2)}, u32[]{:S(2)}) collective-permute-start(bf16[64,128]{1,0:T(8,128)(2,1)S(1)} %get-tuple-element.63), channel_id=1, source_target_pairs={{0,6},{1,7},{2,4},{3,5},{4,2},{5,3},{6,0},{7,1},{8,14},{9,15},{10,... | collective-permute-start | bytes 49160 | tf_op jit(solution)/shard_map/ppermute | solution.py:35
  150.9 3.4 %collective-permute-start.24 = (bf16[64,2048]{1,0:T(8,128)(2,1)S(1)}, bf16[64,2048]{1,0:T(8,128)(2,1)S(1)}, u32[]{:S(2)}, u32[]{:S(2)}) collective-permute-start(bf16[64,2048]{1,0:T(8,128)(2,1)S(1)} %get-tuple-element.65), channel_id=1, source_target_pairs={{0,1},{1,0},{2,3},{3,2},{4,5},{5,4},{6,7},{7,6},{8,9},{9,8},{10,11... | collective-permute-start | bytes 786440 | tf_op jit(solution)/shard_map/ppermute | solution.py:35
  151.0 6.1 %collective-permute-start.19 = (bf16[2,128,512]{2,1,0:T(8,128)(2,1)S(1)}, bf16[2,128,512]{2,1,0:T(8,128)(2,1)S(1)}, u32[]{:S(2)}, u32[]{:S(2)}) collective-permute-start(bf16[2,128,512]{2,1,0:T(8,128)(2,1)S(1)} %pad_maximum_fusion.1.rest_0_), channel_id=1, source_target_pairs={{2,4},{5,3},{10,12},{13,11},{18,20},{21,19},{26,28},{29,27}} | collective-permute-start | bytes 786440 | tf_op jit(solution)/shard_map/ppermute | solution.py:35
  151.7 7.7 %collective-permute-start.18 = (bf16[2,128,512]{2,1,0:T(8,128)(2,1)S(1)}, bf16[2,128,512]{2,1,0:T(8,128)(2,1)S(1)}, u32[]{:S(2)}, u32[]{:S(2)}) collective-permute-start(bf16[2,128,512]{2,1,0:T(8,128)(2,1)S(1)} %pad_maximum_fusion.1.rest_0_), channel_id=1, source_target_pairs={{0,4},{7,3},{8,12},{15,11},{16,20},{23,19},{24,28},{31,27}} | collective-permute-start | bytes 786440 | tf_op jit(solution)/shard_map/ppermute | solution.py:35
  153.6 5.8 %collective-permute-start.17 = (bf16[2,128,512]{2,1,0:T(8,128)(2,1)S(1)}, bf16[2,128,512]{2,1,0:T(8,128)(2,1)S(1)}, u32[]{:S(2)}, u32[]{:S(2)}) collective-permute-start(bf16[2,128,512]{2,1,0:T(8,128)(2,1)S(1)} %pad_maximum_fusion.1.rest_0_), channel_id=1, source_target_pairs={{1,3},{6,4},{9,11},{14,12},{17,19},{22,20},{25,27},{30,28}} | collective-permute-start | bytes 786440 | tf_op jit(solution)/shard_map/ppermute | solution.py:35
  154.4 6.4 %collective-permute-start.25 = (bf16[64,512]{1,0:T(8,128)(2,1)S(1)}, bf16[64,512]{1,0:T(8,128)(2,1)S(1)}, u32[]{:S(2)}, u32[]{:S(2)}) collective-permute-start(bf16[64,512]{1,0:T(8,128)(2,1)S(1)} %get-tuple-element.67), channel_id=1, source_target_pairs={{0,2},{1,3},{2,0},{3,1},{4,6},{5,7},{6,4},{7,5},{8,10},{9,11},{10,... | collective-permute-start | bytes 196616 | tf_op jit(solution)/shard_map/ppermute | solution.py:35
  154.5 7.8 %collective-permute-start.26 = (bf16[64,512]{1,0:T(8,128)(2,1)S(1)}, bf16[64,512]{1,0:T(8,128)(2,1)S(1)}, u32[]{:S(2)}, u32[]{:S(2)}) collective-permute-start(bf16[64,512]{1,0:T(8,128)(2,1)S(1)} %get-tuple-element.68), channel_id=1, source_target_pairs={{0,4},{1,5},{2,6},{3,7},{4,0},{5,1},{6,2},{7,3},{8,12},{9,13},{10,... | collective-permute-start | bytes 196616 | tf_op jit(solution)/shard_map/ppermute | solution.py:35
  157.1 9.8 %collective-permute-start.27 = (bf16[64,512]{1,0:T(8,128)(2,1)S(1)}, bf16[64,512]{1,0:T(8,128)(2,1)S(1)}, u32[]{:S(2)}, u32[]{:S(2)}) collective-permute-start(bf16[64,512]{1,0:T(8,128)(2,1)S(1)} %get-tuple-element.69), channel_id=1, source_target_pairs={{0,6},{1,7},{2,4},{3,5},{4,2},{5,3},{6,0},{7,1},{8,14},{9,15},{10,... | collective-permute-start | bytes 196616 | tf_op jit(solution)/shard_map/ppermute | solution.py:35

commit v5 on v4

--- a/solution.py
+++ b/solution.py
@@ -35,9 +35,14 @@
     return lax.ppermute(block, "context", pairs)
 
 
+def far_first(count):
+    half = count // 2
+    return list(range(half, count)) + list(range(half - 1, -1, -1))
+
+
 def exchange(blocks, count):
     got = {0: blocks[0]}
-    for k in range(count - 1, 0, -1):
+    for k in far_first(count)[:-1]:
         got[k] = swap(blocks[k], count, k)
     return [got[k] for k in range(count)]
 
@@ -76,8 +81,8 @@
     return pl.pallas_call(
         functools.partial(pack_kernel, count, model // count, hd, first, nh),
         out_shape=[jax.ShapeDtypeStruct((nh * 3 * tok, hd), q.dtype)] * count,
-        in_specs=[SMEM, VM, VM, VM, ANY],
-        out_specs=[ANY] * count,
+        in_specs=[SMEM, HBM, HBM, HBM, ANY],
+        out_specs=[VM] * count,
         scratch_shapes=[pltpu.SemaphoreType.DMA((3 * nh * count,))],
         compiler_params=params(4),
         name="pack",
@@ -87,15 +92,20 @@
 def first_kernel(count, group, hd, nh, mask_rows, tiles, me_ref, nb_ref, *rest):
     q_ref, k_ref, v_ref, x_ref, down_ref = rest[:5]
     outs, rest = rest[5 : 5 + count], rest[5 + count :]
-    q_s, k_s, v_s, x_s, down_s, note_s, sems, in_sems, note_sems = rest
+    both_ref, x_s, down_s, sems, in_sems = rest
     me = me_ref[0]
     tok = q_ref.shape[0]
     rank = down_ref.shape[0]
-    pairs = ((q_ref, q_s), (k_ref, k_s), (v_ref, v_s), (x_ref, x_s), (down_ref, down_s))
+    copies = pack_copies(count, group, hd, 0, nh, me, (q_ref, k_ref, v_ref), outs, sems)
     loads = [
-        pltpu.make_async_copy(ref, to, in_sems.at[n]) for n, (ref, to) in enumerate(pairs)
+        pltpu.make_async_copy(x_ref, x_s, in_sems.at[0]),
+        pltpu.make_async_copy(down_ref, down_s, in_sems.at[1]),
     ]
-    for copy in loads:
+    pair = [
+        pltpu.make_async_copy(k_ref, both_ref.at[0], in_sems.at[2]),
+        pltpu.make_async_copy(v_ref, both_ref.at[1], in_sems.at[3]),
+    ]
+    for copy in loads + copies + pair:
         copy.start()
     rows = lax.broadcasted_iota(jnp.int32, (mask_rows, tok), 0)
     lane_tile = lax.broadcasted_iota(jnp.int32, (mask_rows, tok), 1) // (tok // tiles)
@@ -104,24 +114,13 @@
         for n in range(nb_ref.shape[1]):
             slot = nb_ref[t, n] - (me - 1) * tiles
             seen = jnp.where((rows == slot) & (lane_tile == t), 1.0, seen)
-    note_s[rank:, :] = seen.astype(jnp.bfloat16)
-    for copy in loads[:3]:
+    for copy in loads:
         copy.wait()
-    copies = pack_copies(count, group, hd, 0, nh, me, (q_s, k_s, v_s), outs, sems)
-    for copy in copies:
-        copy.start()
-    for copy in loads[3:]:
-        copy.wait()
-    note_s[:rank, :] = mm(down_s[...], x_s[...], NT).astype(jnp.bfloat16)
-    notes = [
-        pltpu.make_async_copy(
-            note_s, outs[k].at[pl.ds(nh * 3 * tok, rank + mask_rows), :], note_sems.at[k]
-        )
-        for k in range(count)
-    ]
-    for copy in notes:
-        copy.start()
-    for copy in copies + notes:
+    lora = mm(down_s[...], x_s[...], NT).astype(jnp.bfloat16)
+    note = jnp.concatenate([lora, seen.astype(jnp.bfloat16)], axis=0)
+    for out in outs:
+        out[nh * 3 * tok :, :] = note
+    for copy in copies + pair:
         copy.wait()
 
 
@@ -130,24 +129,24 @@
     rank = down.shape[0]
     rows = nh * 3 * tok + rank + mask_rows
     bf = q.dtype
-    return pl.pallas_call(
+    out = pl.pallas_call(
         functools.partial(
             first_kernel, count, model // count, hd, nh, mask_rows, nb.shape[0]
         ),
-        out_shape=[jax.ShapeDtypeStruct((rows, hd), bf)] * count,
+        out_shape=[jax.ShapeDtypeStruct((rows, hd), bf)] * count
+        + [jax.ShapeDtypeStruct((2, tok, model), bf)],
         in_specs=[SMEM, SMEM] + [HBM] * 5,
-        out_specs=[HBM] * count,
-        scratch_shapes=[pltpu.VMEM(x.shape, bf)] * 4
-        + [
+        out_specs=[VM] * (count + 1),
+        scratch_shapes=[
+            pltpu.VMEM(x.shape, bf),
             pltpu.VMEM(down.shape, bf),
-            pltpu.VMEM((rank + mask_rows, tok), bf),
             pltpu.SemaphoreType.DMA((3 * nh * count,)),
-            pltpu.SemaphoreType.DMA((5,)),
-            pltpu.SemaphoreType.DMA((count,)),
+            pltpu.SemaphoreType.DMA((4,)),
         ],
-        compiler_params=params(60),
+        compiler_params=params(50),
         name="first_pack",
     )(me, nb, q, k, v, x, down)
+    return out[:count], out[count]
 
 
 def assemble_kernel(count, group, me_ref, home_ref, *rest):
@@ -190,11 +189,11 @@
     return expo, jnp.sum(expo, axis=0, keepdims=True)
 
 
-def tile_weights(keys, query, mask, slots, scale):
-    tok = query.shape[0]
+def masked_weights(scores, mask, slots, scale):
+    rows, tok = scores.shape
     bias = (mask.astype(jnp.float32)[:slots] - 1.0) * (-HIDDEN)
-    scores = mm(keys, query, NT).reshape(slots, 3 * tok // slots, tok) + bias[:, None, :]
-    expo, norm = soft(scores.reshape(3 * tok, tok), scale)
+    scores = scores.reshape(slots, rows // slots, tok) + bias[:, None, :]
+    expo, norm = soft(scores.reshape(rows, tok), scale)
     return (expo * (1.0 / norm)).astype(jnp.bfloat16)
 
 
@@ -210,7 +209,8 @@
 
 
 def home_kernel(count, slots, rank, hd, me_ref, *rest):
-    notes, rest = rest[:count], rest[count:]
+    notes = {p: ref for p, ref in zip(far_first(count), rest)}
+    rest = rest[count:]
     q_ref, k_ref, v_ref, low_ref, high_ref, up_ref, out_ref, note_s = rest
     tok = q_ref.shape[0]
 
@@ -218,20 +218,28 @@
 
     @pl.when(pl.program_id(0) == 0)
     def _():
-        for p, ref in enumerate(notes):
+        for p, ref in notes.items():
             note_s[p] = ref[ref.shape[0] - size :, :]
 
     mask = note_s[0][rank:, :]
     loras = [note_s[w][:rank, :] for w in window(me_ref[0], 0, count)]
-    for h in range(q_ref.shape[1] // hd):
-        cols = slice(h * hd, (h + 1) * hd)
-        keys = jnp.concatenate([low_ref[0, :, cols], k_ref[:, cols], high_ref[0, :, cols]], axis=0)
-        weights = tile_weights(keys, q_ref[:, cols], mask, slots, log_scale(hd))
-        values = []
-        for value, lora in zip((low_ref[1, :, cols], v_ref[:, cols], high_ref[1, :, cols]), loras):
-            term = mm(up_ref[:, cols], lora, TN)
-            values.append((value.T.astype(jnp.float32) + term).astype(jnp.bfloat16))
-        student = mm(jnp.concatenate(values, axis=1), weights)
+    heads = [slice(h * hd, (h + 1) * hd) for h in range(q_ref.shape[1] // hd)]
+    keys = jnp.concatenate([low_ref[0], k_ref[...], high_ref[0]], axis=0)
+    scores = [mm(keys[:, cols], q_ref[:, cols], NT) for cols in heads]
+    terms = [[mm(up_ref[:, cols], lora, TN) for lora in loras] for cols in heads]
+    weights = [masked_weights(x, mask, slots, log_scale(hd)) for x in scores]
+    values = [
+        jnp.concatenate(
+            [
+                (v.T.astype(jnp.float32) + t).astype(jnp.bfloat16)
+                for v, t in zip((low_ref[1, :, cols], v_ref[:, cols], high_ref[1, :, cols]), term)
+            ],
+            axis=1,
+        )
+        for cols, term in zip(heads, terms)
+    ]
+    students = [mm(v, w) for v, w in zip(values, weights)]
+    for cols, student in zip(heads, students):
         out_ref[:, cols] = student.T.astype(jnp.bfloat16)
 
 
@@ -239,7 +247,7 @@
     count = len(messages)
     tok, model = q.shape
     rank = up_t.shape[0]
-    width = min(4 * hd, model)
+    width = min(8 * hd, model)
     column = pl.BlockSpec((tok, width), lambda h: (0, h))
     pair = pl.BlockSpec((2, tok, width), lambda h: (0, 0, h))
     return pl.pallas_call(
@@ -258,14 +266,15 @@
             flops=12 * 10**9, bytes_accessed=9 * tok * model * 2, transcendentals=0
         ),
         name="home_student",
-    )(me, *messages, q, k, v, low, high, up_t)
+    )(me, *[messages[p] for p in far_first(count)], q, k, v, low, high, up_t)
 
 
 def attention_kernel(
     count, tok, hd, nh, slots, rank, before, last, factor, sizes, me_ref, *rest
 ):
-    blocks, rest = rest[:count], rest[count:]
-    noted, rest = rest[:count], rest[count:]
+    blocks = {p: ref for p, ref in zip(far_first(count), rest)}
+    noted = {p: ref for p, ref in zip(far_first(count), rest[count:])}
+    rest = rest[2 * count :]
     up_ref, _, rest = rest[0], rest[1], rest[2:]
     if before:
         (hid_ref, gup_in, out_in), rest = rest[:3], rest[3:]
@@ -281,7 +290,7 @@
 
     @pl.when(head == 0)
     def _():
-        for p, ref in enumerate(noted):
+        for p, ref in noted.items():
             note_s[p] = ref[sizes - size :, :]
             lora_s[:, p * tok : (p + 1) * tok] = note_s[p, :rank, :]
         if before:
@@ -303,23 +312,39 @@
         svt_s[p] = (vt_s[:, cols].astype(jnp.float32) + term).astype(jnp.bfloat16)
     grad_s[...] = jnp.zeros_like(grad_s)
 
-    for p in range(count):
-        query = q_s[p * tok : (p + 1) * tok, :]
-        expo, norm = soft(mm(k_s[...], query, NT), scale)
-        teacher = mm(vt_s[...], expo.astype(jnp.bfloat16)) / norm
-        teacher = teacher.astype(jnp.bfloat16).astype(jnp.float32)
-        places = window(me, p, count)
-        keys = jnp.concatenate(
-            [k_s[pl.ds(pl.multiple_of(w * tok, tok), tok), :] for w in places], axis=0
-        )
-        weights = tile_weights(keys, query, note_s[p, rank:, :], slots, scale)
-        values = jnp.concatenate([svt_s[w] for w in places], axis=1)
-        student = mm(values, weights)
-        out_s[before + head, p] = student.astype(jnp.bfloat16)
-        delta = ((student - teacher) * factor).astype(jnp.bfloat16)
-        grads = mm(weights, delta, NT)
-        for n, w in enumerate(places):
-            grad_s[w] += grads[n * tok : (n + 1) * tok]
+    for start in range(0, count, 4):
+        slabs = range(start, min(start + 4, count))
+        queries = [q_s[p * tok : (p + 1) * tok, :] for p in slabs]
+        places = [window(me, p, count) for p in slabs]
+        full = [mm(k_s[...], query, NT) for query in queries]
+        seen = [
+            mm(
+                jnp.concatenate(
+                    [k_s[pl.ds(pl.multiple_of(w * tok, tok), tok), :] for w in place], axis=0
+                ),
+                query,
+                NT,
+            )
+            for place, query in zip(places, queries)
+        ]
+        full = [soft(x, scale) for x in full]
+        teachers = [mm(vt_s[...], expo.astype(jnp.bfloat16)) for expo, _ in full]
+        weights = [
+            masked_weights(x, note_s[p, rank:, :], slots, scale) for p, x in zip(slabs, seen)
+        ]
+        students = [
+            mm(jnp.concatenate([svt_s[w] for w in place], axis=1), weight)
+            for place, weight in zip(places, weights)
+        ]
+        deltas = []
+        for (_, norm), teacher, student in zip(full, teachers, students):
+            teacher = (teacher / norm).astype(jnp.bfloat16).astype(jnp.float32)
+            deltas.append(((student - teacher) * factor).astype(jnp.bfloat16))
+        grads = [mm(weight, delta, NT) for weight, delta in zip(weights, deltas)]
+        for p, place, student, grad in zip(slabs, places, students, grads):
+            out_s[before + head, p] = student.astype(jnp.bfloat16)
+            for n, w in enumerate(place):
+                grad_s[w] += grad[n * tok : (n + 1) * tok]
 
     grad = grad_s[...].reshape(count * tok, hd).astype(jnp.bfloat16)
     column = pl.multiple_of((before + head) * hd, LANES)
@@ -403,7 +428,14 @@
             flops=nh * 6 * 10**9, bytes_accessed=4 * nh * keys * hd * 2, transcendentals=0
         ),
         name="attention",
-    )(me, *blocks, *noted, up_t, after, *given)
+    )(
+        me,
+        *[blocks[p] for p in far_first(count)],
+        *[noted[p] for p in far_first(count)],
+        up_t,
+        after,
+        *given,
+    )
 
 
 def pair_kernel(parts, keep_ref, got_ref, *outs):
@@ -515,7 +547,7 @@
     messages = []
     for c, (first, nh) in enumerate(chunks):
         if c == 0:
-            blocks = first_pack(
+            blocks, both = first_pack(
                 me, neighbors, queries, keys, values, value_layer_input, down_t,
                 count, hd, nh, mask_rows,
             )
@@ -527,7 +559,6 @@
 
     half = count // 2
     ups = [(i, i + 1) for i in range(count - 1) if i + 1 != half]
-    both = jnp.stack([keys, values])
     low = lax.ppermute(both, "context", ups)
     high = lax.ppermute(both, "context", [(j, i) for i, j in ups])
     home = home_student(

time: 168 us -> 145 us (0.86)
  waiting for transfers between devices: 62.3 us -> 26.9 us
  starting transfers between devices: 52.2 us -> 75.8 us
  Pallas kernels: 44.6 us -> 31.6 us
  local copies, waits for them, and re-layouts: 4.43 us -> 8.09 us
  other arithmetic: 3.13 us -> 0.03 us
    ppermute x26, waiting for transfers between devices: 62.3 us -> 26.9 us  [swap(): return lax.ppermute(block, 'context', pairs)]
    ppermute x26, starting transfers between devices: 46.6 us -> 70.8 us  [swap(): return lax.ppermute(block, 'context', pairs)]
    pallas_call x1, Pallas kernels: 14.7 us -> 7.52 us  [home_student(): pl.pallas_call(functools.partial(home_kernel, count, slots, rank, hd), gr...]
    pallas_call x2, Pallas kernels: 23.2 us -> 16.8 us  [attention(): pl.pallas_call(functools.partial(attention_kernel, count, tok, hd, nh, sl...]
    unnamed x26 -> x34, local copies, waits for them, and re-layouts: 3.45 us -> 7.11 us
    another operation x1 -> x0, other arithmetic: 3.1 us -> none  [local(): both = jnp.stack([keys, values])]
  transfers between devices with their start and end apart: 28 -> 28, of which waited for: 10 -> 9; matrix products, arithmetic and copies ran while one was open for 1% -> 1% of each run, Pallas kernels for 22% -> 14%
where the time goes in v5:
time: 145 us; the launch traced here: 143 us
  starting transfers between devices  75.8 us (52%)
  Pallas kernels  31.6 us (22%)
  waiting for transfers between devices  26.9 us (19%)
  local copies, waits for them, and re-layouts  8.09 us (6%)
    ppermute x26, starting transfers between devices, swap(): return lax.ppermute(block, 'context', pairs)  70.8 us
    ppermute x26, waiting for transfers between devices, swap(): return lax.ppermute(block, 'context', pairs)  26.9 us
    pallas_call x2, Pallas kernels, attention(): pl.pallas_call(functools.partial(attention_kernel, count, tok, hd, nh, sl...  16.8 us
    pallas_call x1, Pallas kernels, home_student(): pl.pallas_call(functools.partial(home_kernel, count, slots, rank, hd), gr...  7.52 us
    unnamed x34, local copies, waits for them, and re-layouts  7.11 us
    pallas_call x1, Pallas kernels, first_pack(): pl.pallas_call(functools.partial(first_kernel, count, model // count, hd,...  5.69 us
    ppermute x1, starting transfers between devices, local(): low = lax.ppermute(both, 'context', ups)  3.69 us
  transfers between devices with their start and end apart: 28, of which 9 were waited for; matrix products, arithmetic and copies ran while one was open for 1% of the time, Pallas kernels for 14%

profile of v5, /device:TPU:0, one launch (start us, length us, event | category | flops | bytes accessed | tf_op | source)
XLA Modules:
  0.0 143.3 jit_solution(13134203842783499374)
XLA Ops:
  0.6 1.2 copy-done
  1.9 1.0 copy-done.6
  2.9 0.7 copy-done.8
  3.6 5.7 %first_pack.1 = (bf16[1232,128]{1,0:T(8,128)(2,1)S(1)}, bf16[1232,128]{1,0:T(8,128)(2,1)}, bf16[1232,128]{1,0:T(8,128)(2,1)}, bf16[1232,128]{1,0:T(8,128)(2,1)},...) custom-call(s32[1]{0:T(128)} %bitcast.me_ref, ...), custom_call_target="tpu_custom_call" | custom-call | tf_op jit(solution)/shard_map/first_pack/pallas_call | solution.py:132
  9.3 0.7 copy-done.9
  10.0 3.7 %collective-permute-start.7 = (bf16[2,128,4096]{2,1,0:T(8,128)(2,1)}, bf16[2,128,4096]{2,1,0:T(8,128)(2,1)}, u32[]{:S(2)}, u32[]{:S(2)}) collective-permute-start(bf16[2,128,4096]{2,1,0:T(8,128)(2,1)} %get-tuple-element.46), channel_id=1, source_target_pairs={{0,1},{1,2},{2,3},{4,5},{5,6},{6,7},{8,9},{9,10},{10,11},{12,13},{... | collective-permute-start | bytes 6291464 | tf_op jit(solution)/shard_map/ppermute | solution.py:562
  13.7 1.3 collective-permute-start.8
  15.0 5.4 %collective-permute-start.3 = (bf16[1232,128]{1,0:T(8,128)(2,1)S(1)}, bf16[1232,128]{1,0:T(8,128)(2,1)S(1)}, u32[]{:S(2)}, u32[]{:S(2)}) collective-permute-start(bf16[1232,128]{1,0:T(8,128)(2,1)S(1)} %get-tuple-element.41), channel_id=1, source_target_pairs={{0,7},{1,6},{2,5},{3,4},{4,3},{5,2},{6,1},{7,0},{8,15},{9,14},{10,... | collective-permute-start | bytes 946184 | tf_op jit(solution)/shard_map/ppermute | solution.py:35
  20.4 2.7 %collective-permute-start.1 = (bf16[1232,128]{1,0:T(8,128)(2,1)S(1)}, bf16[1232,128]{1,0:T(8,128)(2,1)S(1)}, u32[]{:S(2)}, u32[]{:S(2)}) collective-permute-start(bf16[1232,128]{1,0:T(8,128)(2,1)S(1)} %get-tuple-element.39), channel_id=1, source_target_pairs={{0,5},{1,4},{2,7},{3,6},{4,1},{5,0},{6,3},{7,2},{8,13},{9,12},{10,... | collective-permute-start | bytes 946184 | tf_op jit(solution)/shard_map/ppermute | solution.py:35
  23.1 5.2 %collective-permute-done.3.rest_3_._.rest_11_ = bf16[1232,128]{1,0:T(8,128)(2,1)S(1)} collective-permute-done((bf16[1232,128]{1,0:T(8,128)(2,1)S(1)}, bf16[1232,128]{1,0:T(8,128)(2,1)S(1)}, u32[]{:S(2)}, u32[]{:S(2)}) %collective-permute-start.3) | collective-permute-done | bytes 315424 | tf_op jit(solution)/shard_map/ppermute | solution.py:35
  28.3 28.9 %collective-permute-start.2 = (bf16[1232,128]{1,0:T(8,128)(2,1)S(1)}, bf16[1232,128]{1,0:T(8,128)(2,1)S(1)}, u32[]{:S(2)}, u32[]{:S(2)}) collective-permute-start(bf16[1232,128]{1,0:T(8,128)(2,1)S(1)} %get-tuple-element.40), channel_id=1, source_target_pairs={{0,6},{1,7},{2,4},{3,5},{4,2},{5,3},{6,0},{7,1},{8,14},{9,15},{10,... | collective-permute-start | bytes 946184 | tf_op jit(solution)/shard_map/ppermute | solution.py:35
  57.2 0.8 copy-done.11
  57.9 0.7 copy-done.13
  58.7 10.3 %collective-permute-start.5 = (bf16[1232,128]{1,0:T(8,128)(2,1)}, bf16[1232,128]{1,0:T(8,128)(2,1)}, u32[]{:S(2)}, u32[]{:S(2)}) collective-permute-start(bf16[1232,128]{1,0:T(8,128)(2,1)} %get-tuple-element.43), channel_id=1, source_target_pairs={{0,2},{1,3},{2,0},{3,1},{4,6},{5,7},{6,4},{7,5},{8,10},{9,11},{10,... | collective-permute-start | bytes 946184 | tf_op jit(solution)/shard_map/ppermute | solution.py:35
  69.0 4.5 %collective-permute-done.2.rest_2_.rest_10_ = bf16[1232,128]{1,0:T(8,128)(2,1)S(1)} collective-permute-done((bf16[1232,128]{1,0:T(8,128)(2,1)S(1)}, bf16[1232,128]{1,0:T(8,128)(2,1)S(1)}, u32[]{:S(2)}, u32[]{:S(2)}) %collective-permute-start.2) | collective-permute-done | bytes 315424 | tf_op jit(solution)/shard_map/ppermute | solution.py:35
  73.6 0.7 copy-done.15
  74.3 1.0 dynamic-slice_bitcast_fusion.rest_16_
  75.3 0.5 pack.1
  75.8 4.6 %collective-permute-start.10 = (bf16[384,128]{1,0:T(8,128)(2,1)S(1)}, bf16[384,128]{1,0:T(8,128)(2,1)S(1)}, u32[]{:S(2)}, u32[]{:S(2)}) collective-permute-start(bf16[384,128]{1,0:T(8,128)(2,1)S(1)} %get-tuple-element.48), channel_id=1, source_target_pairs={{0,5},{1,4},{2,7},{3,6},{4,1},{5,0},{6,3},{7,2},{8,13},{9,12},{10,... | collective-permute-start | bytes 294920 | tf_op jit(solution)/shard_map/ppermute | solution.py:35
  80.4 5.2 %collective-permute-done.5.rest_5_.rest_13_ = bf16[1232,128]{1,0:T(8,128)(2,1)} collective-permute-done((bf16[1232,128]{1,0:T(8,128)(2,1)}, bf16[1232,128]{1,0:T(8,128)(2,1)}, u32[]{:S(2)}, u32[]{:S(2)}) %collective-permute-start.5) | collective-permute-done | bytes 315424 | tf_op jit(solution)/shard_map/ppermute | solution.py:35
  85.6 0.5 collective-permute-start.11
  86.0 0.9 collective-permute-start.13
  86.9 4.2 %collective-permute-start.14 = (bf16[384,128]{1,0:T(8,128)(2,1)S(1)}, bf16[384,128]{1,0:T(8,128)(2,1)S(1)}, u32[]{:S(2)}, u32[]{:S(2)}) collective-permute-start(bf16[384,128]{1,0:T(8,128)(2,1)S(1)} %get-tuple-element.52), channel_id=1, source_target_pairs={{0,2},{1,3},{2,0},{3,1},{4,6},{5,7},{6,4},{7,5},{8,10},{9,11},{10,... | collective-permute-start | bytes 294920 | tf_op jit(solution)/shard_map/ppermute | solution.py:35
  91.2 7.5 %home_student.1.rest_17_.home_ref = bf16[128,4096]{1,0:T(8,128)(2,1)} custom-call(s32[1]{0:T(128)} %bitcast.me_ref, bf16[1232,128]{1,0:T(8,128)(2,1)S(1)} %copy-done.12, bf16[1232,128]{1,0:T(8,128)(2,1)S(1)} %copy-done.14, bf16[1232,128]{1,0:T(8,128)(2,1)S(1)} %copy-done.16, bf16[1232,128]{1,0:T(8,128)(2,1)S(1)} %collective-permute-done.3.rest_3_._.rest_11_, ...), custom_call_target="tpu_custom_call" | custom-call | flops 12000000000 | bytes 9437184 | tf_op jit(solution)/shard_map/home_student/pallas_call | solution.py:253
  98.7 0.1 collective-permute-start.9
  98.8 1.2 copy-done.5
  100.0 11.6 %attention.2 = (f32[64,1024]{1,0:T(8,128)S(1)}, f32[64,384]{1,0:T(8,128)S(1)}, bf16[3,8,128,128]{3,2,1,0:T(8,128)(2,1)S(1)}) custom-call(s32[1]{0:T(128)} %bitcast.me_ref, bf16[1232,128]{1,0:T(8,128)(2,1)S(1)} %copy-done.12, bf16[1232,128]{1,0:T(8,128)(2,1)S(1)} %copy-done.14, bf16[1232,128]{1,0:T(8,128)(2,1)S(1)} %copy-done.16, ...), custom_call_target="tpu_custom_call" | custom-call | flops 17999998976 | bytes 3145728 | tf_op jit(solution)/shard_map/attention/pallas_call | solution.py:394
  111.7 5.2 %attention.3 = (bf16[128,512]{1,0:T(8,128)(2,1)S(1)}, bf16[128,512]{1,0:T(8,128)(2,1)S(1)}, f32[64,512]{1,0:T(8,128)S(1)}, bf16[64,512]{1,0:T(8,128)(2,1)S(1)}, f32[64,512]{1,0:T(8,128)}) custom-call(s32[1]{0:T(128)} %bitcast.me_ref, bf16[384,128]{1,0:T(8,128)(2,1)S(1)} %collective-permute-done.9.rest_0_, ...), custom_call_target="tpu_custom_call" | custom-call | flops 6000000000 | bytes 1048576 | tf_op jit(solution)/shard_map/attention/pallas_call | solution.py:394
  116.9 0.4 collective-permute-start.16
  117.3 0.1 collective-permute-start.20
  117.4 1.1 collective-permute-done.20.got_ref
  118.5 0.8 collective-permute-start.21
  119.4 2.0 %collective-permute-start.22 = (bf16[64,128]{1,0:T(8,128)(2,1)S(1)}, bf16[64,128]{1,0:T(8,128)(2,1)S(1)}, u32[]{:S(2)}, u32[]{:S(2)}) collective-permute-start(bf16[64,128]{1,0:T(8,128)(2,1)S(1)} %get-tuple-element.64), channel_id=1, source_target_pairs={{0,4},{1,5},{2,6},{3,7},{4,0},{5,1},{6,2},{7,3},{8,12},{9,13},{10,... | collective-permute-start | bytes 49160 | tf_op jit(solution)/shard_map/ppermute | solution.py:35
  121.4 1.6 %collective-permute-start.23 = (bf16[64,128]{1,0:T(8,128)(2,1)S(1)}, bf16[64,128]{1,0:T(8,128)(2,1)S(1)}, u32[]{:S(2)}, u32[]{:S(2)}) collective-permute-start(bf16[64,128]{1,0:T(8,128)(2,1)S(1)} %get-tuple-element.65), channel_id=1, source_target_pairs={{0,6},{1,7},{2,4},{3,5},{4,2},{5,3},{6,0},{7,1},{8,14},{9,15},{10,... | collective-permute-start | bytes 49160 | tf_op jit(solution)/shard_map/ppermute | solution.py:35
  123.0 1.2 collective-permute-done.22.rest_2_
  124.2 2.8 %collective-permute-done.23.rest_3_ = bf16[64,128]{1,0:T(8,128)(2,1)S(1)} collective-permute-done((bf16[64,128]{1,0:T(8,128)(2,1)S(1)}, bf16[64,128]{1,0:T(8,128)(2,1)S(1)}, u32[]{:S(2)}, u32[]{:S(2)}) %collective-permute-start.23) | collective-permute-done | bytes 16416 | tf_op jit(solution)/shard_map/ppermute | solution.py:35
  126.9 0.3 down_terms.1
  127.4 0.7 collective-permute-start.17
  128.0 2.4 %collective-permute-start.18 = (bf16[2,128,512]{2,1,0:T(8,128)(2,1)S(1)}, bf16[2,128,512]{2,1,0:T(8,128)(2,1)S(1)}, u32[]{:S(2)}, u32[]{:S(2)}) collective-permute-start(bf16[2,128,512]{2,1,0:T(8,128)(2,1)S(1)} %pad_maximum_fusion.rest_0_), channel_id=1, source_target_pairs={{0,4},{7,3},{8,12},{15,11},{16,20},{23,19},{24,28},{31,27}} | collective-permute-start | bytes 786440 | tf_op jit(solution)/shard_map/ppermute | solution.py:35
  130.5 0.7 collective-permute-start.19
  131.2 1.2 collective-permute-start.25
  132.5 0.2 collective-permute-start.26
  132.7 3.0 %collective-permute-start.27 = (bf16[64,512]{1,0:T(8,128)(2,1)S(1)}, bf16[64,512]{1,0:T(8,128)(2,1)S(1)}, u32[]{:S(2)}, u32[]{:S(2)}) collective-permute-start(bf16[64,512]{1,0:T(8,128)(2,1)S(1)} %get-tuple-element.71), channel_id=1, source_target_pairs={{0,6},{1,7},{2,4},{3,5},{4,2},{5,3},{6,0},{7,1},{8,14},{9,15},{10,... | collective-permute-start | bytes 196616 | tf_op jit(solution)/shard_map/ppermute | solution.py:35
  135.7 1.6 %collective-permute-done.18.rest_2_ = bf16[2,128,512]{2,1,0:T(8,128)(2,1)S(1)} collective-permute-done((bf16[2,128,512]{2,1,0:T(8,128)(2,1)S(1)}, bf16[2,128,512]{2,1,0:T(8,128)(2,1)S(1)}, u32[]{:S(2)}, u32[]{:S(2)}) %collective-permute-start.18) | collective-permute-done | bytes 262176 | tf_op jit(solution)/shard_map/ppermute | solution.py:35
  137.3 0.1 assemble.1
  137.3 1.1 collective-permute-done.25.refs_1_
  138.5 4.2 %collective-permute-done.26.refs_2_ = bf16[64,512]{1,0:T(8,128)(2,1)S(1)} collective-permute-done((bf16[64,512]{1,0:T(8,128)(2,1)S(1)}, bf16[64,512]{1,0:T(8,128)(2,1)S(1)}, u32[]{:S(2)}, u32[]{:S(2)}) %collective-permute-start.26) | collective-permute-done | bytes 65568 | tf_op jit(solution)/shard_map/ppermute | solution.py:35
  142.6 0.7 sum_terms.1
  (54 shorter events, 0.3 us)
Async XLA Ops:
  0.6 1.2 copy-start
  1.9 1.0 copy-start.6
  2.9 0.7 copy-start.8
  3.6 71.7 %copy-start.1 = (bf16[128,4096]{1,0:T(8,128)(2,1)S(1)}, bf16[128,4096]{1,0:T(8,128)(2,1)}, u32[]{:S(2)}) copy-start(bf16[128,4096]{1,0:T(8,128)(2,1)} %q_ref.1) | copy-start | bytes 3145732
  3.6 71.7 %copy-start.2 = (bf16[128,4096]{1,0:T(8,128)(2,1)S(1)}, bf16[128,4096]{1,0:T(8,128)(2,1)}, u32[]{:S(2)}) copy-start(bf16[128,4096]{1,0:T(8,128)(2,1)} %k_ref.1) | copy-start | bytes 3145732
  3.6 71.7 %copy-start.3 = (bf16[128,4096]{1,0:T(8,128)(2,1)S(1)}, bf16[128,4096]{1,0:T(8,128)(2,1)}, u32[]{:S(2)}) copy-start(bf16[128,4096]{1,0:T(8,128)(2,1)} %v_ref.1) | copy-start | bytes 3145732
  9.3 0.7 copy-start.9
  10.0 76.0 %collective-permute-start.7 = (bf16[2,128,4096]{2,1,0:T(8,128)(2,1)}, bf16[2,128,4096]{2,1,0:T(8,128)(2,1)}, u32[]{:S(2)}, u32[]{:S(2)}) collective-permute-start(bf16[2,128,4096]{2,1,0:T(8,128)(2,1)} %get-tuple-element.46), channel_id=1, source_target_pairs={{0,1},{1,2},{2,3},{4,5},{5,6},{6,7},{8,9},{9,10},{10,11},{12,13},{... | collective-permute-start | bytes 6291464 | tf_op jit(solution)/shard_map/ppermute | solution.py:562
  13.7 73.2 %collective-permute-start.8 = (bf16[2,128,4096]{2,1,0:T(8,128)(2,1)}, bf16[2,128,4096]{2,1,0:T(8,128)(2,1)}, u32[]{:S(2)}, u32[]{:S(2)}) collective-permute-start(bf16[2,128,4096]{2,1,0:T(8,128)(2,1)} %get-tuple-element.46), channel_id=1, source_target_pairs={{1,0},{2,1},{3,2},{5,4},{6,5},{7,6},{9,8},{10,9},{11,10},{13,12},{... | collective-permute-start | bytes 6291464 | tf_op jit(solution)/shard_map/ppermute | solution.py:563
  15.0 13.3 %collective-permute-start.3 = (bf16[1232,128]{1,0:T(8,128)(2,1)S(1)}, bf16[1232,128]{1,0:T(8,128)(2,1)S(1)}, u32[]{:S(2)}, u32[]{:S(2)}) collective-permute-start(bf16[1232,128]{1,0:T(8,128)(2,1)S(1)} %get-tuple-element.41), channel_id=1, source_target_pairs={{0,7},{1,6},{2,5},{3,4},{4,3},{5,2},{6,1},{7,0},{8,15},{9,14},{10,... | collective-permute-start | bytes 946184 | tf_op jit(solution)/shard_map/ppermute | solution.py:35
  20.3 36.8 %collective-permute-start = (bf16[1232,128]{1,0:T(8,128)(2,1)S(1)}, bf16[1232,128]{1,0:T(8,128)(2,1)S(1)}, u32[]{:S(2)}, u32[]{:S(2)}) collective-permute-start(bf16[1232,128]{1,0:T(8,128)(2,1)S(1)} %get-tuple-element.38), channel_id=1, source_target_pairs={{0,4},{1,5},{2,6},{3,7},{4,0},{5,1},{6,2},{7,3},{8,12},{9,13},{10,... | collective-permute-start | bytes 946184 | tf_op jit(solution)/shard_map/ppermute | solution.py:35
  20.4 37.6 %collective-permute-start.1 = (bf16[1232,128]{1,0:T(8,128)(2,1)S(1)}, bf16[1232,128]{1,0:T(8,128)(2,1)S(1)}, u32[]{:S(2)}, u32[]{:S(2)}) collective-permute-start(bf16[1232,128]{1,0:T(8,128)(2,1)S(1)} %get-tuple-element.39), channel_id=1, source_target_pairs={{0,5},{1,4},{2,7},{3,6},{4,1},{5,0},{6,3},{7,2},{8,13},{9,12},{10,... | collective-permute-start | bytes 946184 | tf_op jit(solution)/shard_map/ppermute | solution.py:35
  28.3 45.3 %collective-permute-start.2 = (bf16[1232,128]{1,0:T(8,128)(2,1)S(1)}, bf16[1232,128]{1,0:T(8,128)(2,1)S(1)}, u32[]{:S(2)}, u32[]{:S(2)}) collective-permute-start(bf16[1232,128]{1,0:T(8,128)(2,1)S(1)} %get-tuple-element.40), channel_id=1, source_target_pairs={{0,6},{1,7},{2,4},{3,5},{4,2},{5,3},{6,0},{7,1},{8,14},{9,15},{10,... | collective-permute-start | bytes 946184 | tf_op jit(solution)/shard_map/ppermute | solution.py:35
  57.2 0.8 copy-start.11
  57.9 17.9 %collective-permute-start.4 = (bf16[1232,128]{1,0:T(8,128)(2,1)}, bf16[1232,128]{1,0:T(8,128)(2,1)}, u32[]{:S(2)}, u32[]{:S(2)}) collective-permute-start(bf16[1232,128]{1,0:T(8,128)(2,1)} %get-tuple-element.42), channel_id=1, source_target_pairs={{0,3},{1,2},{2,1},{3,0},{4,7},{5,6},{6,5},{7,4},{8,11},{9,10},{10,... | collective-permute-start | bytes 946184 | tf_op jit(solution)/shard_map/ppermute | solution.py:35
  57.9 0.7 copy-start.13
  58.7 26.9 %collective-permute-start.5 = (bf16[1232,128]{1,0:T(8,128)(2,1)}, bf16[1232,128]{1,0:T(8,128)(2,1)}, u32[]{:S(2)}, u32[]{:S(2)}) collective-permute-start(bf16[1232,128]{1,0:T(8,128)(2,1)} %get-tuple-element.43), channel_id=1, source_target_pairs={{0,2},{1,3},{2,0},{3,1},{4,6},{5,7},{6,4},{7,5},{8,10},{9,11},{10,... | collective-permute-start | bytes 946184 | tf_op jit(solution)/shard_map/ppermute | solution.py:35
  73.6 0.7 copy-start.15
  74.3 11.7 %collective-permute-start.6 = (bf16[1232,128]{1,0:T(8,128)(2,1)}, bf16[1232,128]{1,0:T(8,128)(2,1)}, u32[]{:S(2)}, u32[]{:S(2)}) collective-permute-start(bf16[1232,128]{1,0:T(8,128)(2,1)} %get-tuple-element.44), channel_id=1, source_target_pairs={{0,1},{1,0},{2,3},{3,2},{4,5},{5,4},{6,7},{7,6},{8,9},{9,8},{10,11... | collective-permute-start | bytes 946184 | tf_op jit(solution)/shard_map/ppermute | solution.py:35
  74.3 16.9 %copy-start.7 = (bf16[4096,64]{0,1:T(8,128)(2,1)S(1)}, bf16[4096,64]{0,1:T(8,128)(2,1)}, u32[]{:S(2)}) copy-start(bf16[4096,64]{0,1:T(8,128)(2,1)} %param.12) | copy-start | bytes 1572868
  74.3 16.9 %copy-start.10 = (bf16[1232,128]{1,0:T(8,128)(2,1)S(1)}, bf16[1232,128]{1,0:T(8,128)(2,1)}, u32[]{:S(2)}) copy-start(bf16[1232,128]{1,0:T(8,128)(2,1)} %copy-done.9) | copy-start | bytes 946180
  74.3 16.9 %copy-start.12 = (bf16[1232,128]{1,0:T(8,128)(2,1)S(1)}, bf16[1232,128]{1,0:T(8,128)(2,1)}, u32[]{:S(2)}) copy-start(bf16[1232,128]{1,0:T(8,128)(2,1)} %copy-done.11) | copy-start | bytes 946180
  74.3 16.9 %copy-start.14 = (bf16[1232,128]{1,0:T(8,128)(2,1)S(1)}, bf16[1232,128]{1,0:T(8,128)(2,1)}, u32[]{:S(2)}) copy-start(bf16[1232,128]{1,0:T(8,128)(2,1)} %copy-done.13) | copy-start | bytes 946180
  74.3 16.9 %copy-start.16 = (bf16[1232,128]{1,0:T(8,128)(2,1)S(1)}, bf16[1232,128]{1,0:T(8,128)(2,1)}, u32[]{:S(2)}) copy-start(bf16[1232,128]{1,0:T(8,128)(2,1)} %copy-done.15) | copy-start | bytes 946180
  75.8 22.9 %collective-permute-start.10 = (bf16[384,128]{1,0:T(8,128)(2,1)S(1)}, bf16[384,128]{1,0:T(8,128)(2,1)S(1)}, u32[]{:S(2)}, u32[]{:S(2)}) collective-permute-start(bf16[384,128]{1,0:T(8,128)(2,1)S(1)} %get-tuple-element.48), channel_id=1, source_target_pairs={{0,5},{1,4},{2,7},{3,6},{4,1},{5,0},{6,3},{7,2},{8,13},{9,12},{10,... | collective-permute-start | bytes 294920 | tf_op jit(solution)/shard_map/ppermute | solution.py:35
  85.6 13.1 %collective-permute-start.11 = (bf16[384,128]{1,0:T(8,128)(2,1)S(1)}, bf16[384,128]{1,0:T(8,128)(2,1)S(1)}, u32[]{:S(2)}, u32[]{:S(2)}) collective-permute-start(bf16[384,128]{1,0:T(8,128)(2,1)S(1)} %get-tuple-element.49), channel_id=1, source_target_pairs={{0,6},{1,7},{2,4},{3,5},{4,2},{5,3},{6,0},{7,1},{8,14},{9,15},{10,... | collective-permute-start | bytes 294920 | tf_op jit(solution)/shard_map/ppermute | solution.py:35
  86.0 25.6 %collective-permute-start.12 = (bf16[384,128]{1,0:T(8,128)(2,1)S(1)}, bf16[384,128]{1,0:T(8,128)(2,1)S(1)}, u32[]{:S(2)}, u32[]{:S(2)}) collective-permute-start(bf16[384,128]{1,0:T(8,128)(2,1)S(1)} %get-tuple-element.50), channel_id=1, source_target_pairs={{0,7},{1,6},{2,5},{3,4},{4,3},{5,2},{6,1},{7,0},{8,15},{9,14},{10,... | collective-permute-start | bytes 294920 | tf_op jit(solution)/shard_map/ppermute | solution.py:35
  86.0 25.6 %collective-permute-start.13 = (bf16[384,128]{1,0:T(8,128)(2,1)S(1)}, bf16[384,128]{1,0:T(8,128)(2,1)S(1)}, u32[]{:S(2)}, u32[]{:S(2)}) collective-permute-start(bf16[384,128]{1,0:T(8,128)(2,1)S(1)} %get-tuple-element.51), channel_id=1, source_target_pairs={{0,3},{1,2},{2,1},{3,0},{4,7},{5,6},{6,5},{7,4},{8,11},{9,10},{10,... | collective-permute-start | bytes 294920 | tf_op jit(solution)/shard_map/ppermute | solution.py:35
  86.9 24.7 %collective-permute-start.14 = (bf16[384,128]{1,0:T(8,128)(2,1)S(1)}, bf16[384,128]{1,0:T(8,128)(2,1)S(1)}, u32[]{:S(2)}, u32[]{:S(2)}) collective-permute-start(bf16[384,128]{1,0:T(8,128)(2,1)S(1)} %get-tuple-element.52), channel_id=1, source_target_pairs={{0,2},{1,3},{2,0},{3,1},{4,6},{5,7},{6,4},{7,5},{8,10},{9,11},{10,... | collective-permute-start | bytes 294920 | tf_op jit(solution)/shard_map/ppermute | solution.py:35
  98.7 12.9 %collective-permute-start.15 = (bf16[384,128]{1,0:T(8,128)(2,1)S(1)}, bf16[384,128]{1,0:T(8,128)(2,1)S(1)}, u32[]{:S(2)}, u32[]{:S(2)}) collective-permute-start(bf16[384,128]{1,0:T(8,128)(2,1)S(1)} %get-tuple-element.53), channel_id=1, source_target_pairs={{0,1},{1,0},{2,3},{3,2},{4,5},{5,4},{6,7},{7,6},{8,9},{9,8},{10,11... | collective-permute-start | bytes 294920 | tf_op jit(solution)/shard_map/ppermute | solution.py:35
  98.7 12.9 %collective-permute-start.9 = (bf16[384,128]{1,0:T(8,128)(2,1)S(1)}, bf16[384,128]{1,0:T(8,128)(2,1)S(1)}, u32[]{:S(2)}, u32[]{:S(2)}) collective-permute-start(bf16[384,128]{1,0:T(8,128)(2,1)S(1)} %get-tuple-element.47), channel_id=1, source_target_pairs={{0,4},{1,5},{2,6},{3,7},{4,0},{5,1},{6,2},{7,3},{8,12},{9,13},{10,... | collective-permute-start | bytes 294920 | tf_op jit(solution)/shard_map/ppermute | solution.py:35
  98.8 1.2 copy-start.5
  111.7 15.3 %copy-start.4 = (bf16[128,4096]{1,0:T(8,128)(2,1)S(1)}, bf16[128,4096]{1,0:T(8,128)(2,1)}, u32[]{:S(2)}) copy-start(bf16[128,4096]{1,0:T(8,128)(2,1)} %rest_4_.1) | copy-start | bytes 3145732
  116.9 10.5 %collective-permute-start.16 = (bf16[128,512]{1,0:T(8,128)(2,1)S(1)}, bf16[128,512]{1,0:T(8,128)(2,1)S(1)}, u32[]{:S(2)}, u32[]{:S(2)}) collective-permute-start(bf16[128,512]{1,0:T(8,128)(2,1)S(1)} %get-tuple-element.59), channel_id=1, source_target_pairs={{0,1},{1,0},{2,3},{3,2},{4,5},{5,4},{6,7},{7,6},{8,9},{9,8},{10,11... | collective-permute-start | bytes 393224 | tf_op jit(solution)/shard_map/ppermute | solution.py:35
  117.3 1.3 collective-permute-start.20
  118.5 4.5 %collective-permute-start.21 = (bf16[64,128]{1,0:T(8,128)(2,1)S(1)}, bf16[64,128]{1,0:T(8,128)(2,1)S(1)}, u32[]{:S(2)}, u32[]{:S(2)}) collective-permute-start(bf16[64,128]{1,0:T(8,128)(2,1)S(1)} %get-tuple-element.63), channel_id=1, source_target_pairs={{0,2},{1,3},{2,0},{3,1},{4,6},{5,7},{6,4},{7,5},{8,10},{9,11},{10,... | collective-permute-start | bytes 49160 | tf_op jit(solution)/shard_map/ppermute | solution.py:35
  119.4 4.8 %collective-permute-start.22 = (bf16[64,128]{1,0:T(8,128)(2,1)S(1)}, bf16[64,128]{1,0:T(8,128)(2,1)S(1)}, u32[]{:S(2)}, u32[]{:S(2)}) collective-permute-start(bf16[64,128]{1,0:T(8,128)(2,1)S(1)} %get-tuple-element.64), channel_id=1, source_target_pairs={{0,4},{1,5},{2,6},{3,7},{4,0},{5,1},{6,2},{7,3},{8,12},{9,13},{10,... | collective-permute-start | bytes 49160 | tf_op jit(solution)/shard_map/ppermute | solution.py:35
  121.4 5.5 %collective-permute-start.23 = (bf16[64,128]{1,0:T(8,128)(2,1)S(1)}, bf16[64,128]{1,0:T(8,128)(2,1)S(1)}, u32[]{:S(2)}, u32[]{:S(2)}) collective-permute-start(bf16[64,128]{1,0:T(8,128)(2,1)S(1)} %get-tuple-element.65), channel_id=1, source_target_pairs={{0,6},{1,7},{2,4},{3,5},{4,2},{5,3},{6,0},{7,1},{8,14},{9,15},{10,... | collective-permute-start | bytes 49160 | tf_op jit(solution)/shard_map/ppermute | solution.py:35
  127.2 3.9 %collective-permute-start.24 = (bf16[64,2048]{1,0:T(8,128)(2,1)S(1)}, bf16[64,2048]{1,0:T(8,128)(2,1)S(1)}, u32[]{:S(2)}, u32[]{:S(2)}) collective-permute-start(bf16[64,2048]{1,0:T(8,128)(2,1)S(1)} %get-tuple-element.67), channel_id=1, source_target_pairs={{0,1},{1,0},{2,3},{3,2},{4,5},{5,4},{6,7},{7,6},{8,9},{9,8},{10,11... | collective-permute-start | bytes 786440 | tf_op jit(solution)/shard_map/ppermute | solution.py:35
  127.4 5.4 %collective-permute-start.17 = (bf16[2,128,512]{2,1,0:T(8,128)(2,1)S(1)}, bf16[2,128,512]{2,1,0:T(8,128)(2,1)S(1)}, u32[]{:S(2)}, u32[]{:S(2)}) collective-permute-start(bf16[2,128,512]{2,1,0:T(8,128)(2,1)S(1)} %pad_maximum_fusion.rest_0_), channel_id=1, source_target_pairs={{1,3},{6,4},{9,11},{14,12},{17,19},{22,20},{25,27},{30,28}} | collective-permute-start | bytes 786440 | tf_op jit(solution)/shard_map/ppermute | solution.py:35
  128.0 9.2 %collective-permute-start.18 = (bf16[2,128,512]{2,1,0:T(8,128)(2,1)S(1)}, bf16[2,128,512]{2,1,0:T(8,128)(2,1)S(1)}, u32[]{:S(2)}, u32[]{:S(2)}) collective-permute-start(bf16[2,128,512]{2,1,0:T(8,128)(2,1)S(1)} %pad_maximum_fusion.rest_0_), channel_id=1, source_target_pairs={{0,4},{7,3},{8,12},{15,11},{16,20},{23,19},{24,28},{31,27}} | collective-permute-start | bytes 786440 | tf_op jit(solution)/shard_map/ppermute | solution.py:35
  130.5 6.8 %collective-permute-start.19 = (bf16[2,128,512]{2,1,0:T(8,128)(2,1)S(1)}, bf16[2,128,512]{2,1,0:T(8,128)(2,1)S(1)}, u32[]{:S(2)}, u32[]{:S(2)}) collective-permute-start(bf16[2,128,512]{2,1,0:T(8,128)(2,1)S(1)} %pad_maximum_fusion.rest_0_), channel_id=1, source_target_pairs={{2,4},{5,3},{10,12},{13,11},{18,20},{21,19},{26,28},{29,27}} | collective-permute-start | bytes 786440 | tf_op jit(solution)/shard_map/ppermute | solution.py:35
  131.2 7.2 %collective-permute-start.25 = (bf16[64,512]{1,0:T(8,128)(2,1)S(1)}, bf16[64,512]{1,0:T(8,128)(2,1)S(1)}, u32[]{:S(2)}, u32[]{:S(2)}) collective-permute-start(bf16[64,512]{1,0:T(8,128)(2,1)S(1)} %get-tuple-element.69), channel_id=1, source_target_pairs={{0,2},{1,3},{2,0},{3,1},{4,6},{5,7},{6,4},{7,5},{8,10},{9,11},{10,... | collective-permute-start | bytes 196616 | tf_op jit(solution)/shard_map/ppermute | solution.py:35
  132.5 10.2 %collective-permute-start.26 = (bf16[64,512]{1,0:T(8,128)(2,1)S(1)}, bf16[64,512]{1,0:T(8,128)(2,1)S(1)}, u32[]{:S(2)}, u32[]{:S(2)}) collective-permute-start(bf16[64,512]{1,0:T(8,128)(2,1)S(1)} %get-tuple-element.70), channel_id=1, source_target_pairs={{0,4},{1,5},{2,6},{3,7},{4,0},{5,1},{6,2},{7,3},{8,12},{9,13},{10,... | collective-permute-start | bytes 196616 | tf_op jit(solution)/shard_map/ppermute | solution.py:35
  132.7 9.9 %collective-permute-start.27 = (bf16[64,512]{1,0:T(8,128)(2,1)S(1)}, bf16[64,512]{1,0:T(8,128)(2,1)S(1)}, u32[]{:S(2)}, u32[]{:S(2)}) collective-permute-start(bf16[64,512]{1,0:T(8,128)(2,1)S(1)} %get-tuple-element.71), channel_id=1, source_target_pairs={{0,6},{1,7},{2,4},{3,5},{4,2},{5,3},{6,0},{7,1},{8,14},{9,15},{10,... | collective-permute-start | bytes 196616 | tf_op jit(solution)/shard_map/ppermute | solution.py:35

commit v6 on v5

v6 whole, which is shorter than its diff:
```python
import functools
import math

import jax
import jax.numpy as jnp
from jax import lax
from jax.experimental import pallas as pl
from jax.experimental.pallas import tpu as pltpu
from jax.sharding import PartitionSpec as P

H = 32
HIDDEN = -1e30
NT = (((1,), (1,)), ((), ()))
TN = (((0,), (0,)), ((), ()))
NN = (((1,), (0,)), ((), ()))


def mm(a, b, dims=NN):
    return lax.dot_general(a, b, dims, preferred_element_type=jnp.float32)


def params(mib):
    return pltpu.CompilerParams(vmem_limit_bytes=mib * 1024 * 1024)


SMEM = pl.BlockSpec(memory_space=pltpu.SMEM)
HBM = pl.BlockSpec(memory_space=pltpu.HBM)
ANY = pl.BlockSpec(memory_space=pl.ANY)
VM = pl.BlockSpec(memory_space=pltpu.VMEM)
LANES = 128
ROWS = 16


def swap(block, count, bits, targets=None):
    pairs = [(i, i ^ bits) for i in range(count) if targets is None or i ^ bits in targets]
    return lax.ppermute(block, "context", pairs)


def chips(blocks, count, targets=None):
    got = [blocks[0]] + [None] * (len(blocks) - 1)
    for m in sorted(range(1, len(blocks)), key=lambda m: -m):
        got[m] = swap(blocks[m], count, 2 * m, targets)
    return got


def pack_copies(count, group, hd, first, nh, me, refs, place, sems):
    tok = refs[0].shape[0]
    copies = []
    for k in range(count):
        for h in range(nh):
            column = pl.multiple_of((me ^ k) * group + (first + h) * hd, LANES)
            for t, ref in enumerate(refs):
                row = (h * 3 + t) * tok
                copies.append(
                    pltpu.make_async_copy(
                        ref.at[:, pl.ds(column, hd)],
                        place(k, row, tok),
                        sems.at[(k * nh + h) * 3 + t],
                    )
                )
    return copies


def pack_kernel(count, group, hd, first, nh, me_ref, q_ref, k_ref, v_ref, _, *rest):
    outs, sems = rest[:-1], rest[-1]
    chunk = nh * 3 * q_ref.shape[0]

    def place(k, row, size):
        if k % 2:
            return outs[-1].at[pl.ds(k // 2 * chunk + row, size), :]
        return outs[k // 2].at[pl.ds(row, size), :]

    copies = pack_copies(
        count, group, hd, first, nh, me_ref[0], (q_ref, k_ref, v_ref), place, sems
    )
    for copy in copies:
        copy.start()
    for copy in copies:
        copy.wait()


def pack(me, q, k, v, after, count, hd, first, nh):
    tok, model = q.shape
    rows = nh * 3 * tok
    shapes = [jax.ShapeDtypeStruct((2 * rows, hd), q.dtype)] * (count // 2)
    return pl.pallas_call(
        functools.partial(pack_kernel, count, model // count, hd, first, nh),
        out_shape=shapes + [jax.ShapeDtypeStruct((count // 2 * rows, hd), q.dtype)],
        in_specs=[SMEM, HBM, HBM, HBM, ANY],
        out_specs=[VM] * (count // 2 + 1),
        scratch_shapes=[pltpu.SemaphoreType.DMA((3 * nh * count,))],
        compiler_params=params(8),
        name="pack",
    )(me, q, k, v, after)


def first_kernel(count, group, hd, nh, mask_rows, tiles, me_ref, nb_ref, *rest):
    q_ref, k_ref, v_ref, x_ref, down_ref = rest[:5]
    outs, rest = rest[5 : 5 + count // 2], rest[5 + count // 2 :]
    x_s, down_s, sems, in_sems = rest
    me = me_ref[0]
    tok = q_ref.shape[0]
    rank = down_ref.shape[0]
    chunk = nh * 3 * tok

    def place(k, row, size):
        return outs[k // 2].at[pl.ds(k % 2 * chunk + row, size), :]

    copies = pack_copies(count, group, hd, 0, nh, me, (q_ref, k_ref, v_ref), place, sems)
    loads = [
        pltpu.make_async_copy(x_ref, x_s, in_sems.at[0]),
        pltpu.make_async_copy(down_ref, down_s, in_sems.at[1]),
    ]
    for copy in loads + copies:
        copy.start()
    rows = lax.broadcasted_iota(jnp.int32, (mask_rows, tok), 0)
    lane_tile = lax.broadcasted_iota(jnp.int32, (mask_rows, tok), 1) // (tok // tiles)
    seen = jnp.zeros((mask_rows, tok), jnp.float32)
    for t in range(tiles):
        for n in range(nb_ref.shape[1]):
            slot = nb_ref[t, n] - (me - 1) * tiles
            seen = jnp.where((rows == slot) & (lane_tile == t), 1.0, seen)
    for copy in loads:
        copy.wait()
    lora = mm(down_s[...], x_s[...], NT).astype(jnp.bfloat16)
    note = jnp.concatenate([lora, seen.astype(jnp.bfloat16)], axis=0)
    for out in outs:
        out[2 * chunk :, :] = note
    for copy in copies:
        copy.wait()


def first_pack(me, nb, q, k, v, x, down, count, hd, nh, mask_rows):
    tok, model = q.shape
    rows = 2 * nh * 3 * tok + down.shape[0] + mask_rows
    bf = q.dtype
    return pl.pallas_call(
        functools.partial(
            first_kernel, count, model // count, hd, nh, mask_rows, nb.shape[0]
        ),
        out_shape=[jax.ShapeDtypeStruct((rows, hd), bf)] * (count // 2),
        in_specs=[SMEM, SMEM] + [HBM] * 5,
        out_specs=[VM] * (count // 2),
        scratch_shapes=[
            pltpu.VMEM(x.shape, bf),
            pltpu.VMEM(down.shape, bf),
            pltpu.SemaphoreType.DMA((3 * nh * count,)),
            pltpu.SemaphoreType.DMA((2,)),
        ],
        compiler_params=params(60),
        name="first_pack",
    )(me, nb, q, k, v, x, down)


def forward_kernel(parts, rows, *refs):
    size = refs[0].shape[0] - rows
    for m in range(parts):
        refs[-1][m * size : (m + 1) * size, :] = refs[m][rows:, :]


def forward(blocks, note, after):
    parts = len(blocks)
    rows = (blocks[0].shape[0] - note) // 2
    size = blocks[0].shape[0] - rows
    return pl.pallas_call(
        functools.partial(forward_kernel, parts, rows),
        out_shape=jax.ShapeDtypeStruct((parts * size, blocks[0].shape[1]), blocks[0].dtype),
        in_specs=[VM] * parts + [ANY] * len(after),
        out_specs=VM,
        compiler_params=params(4),
        name="forward",
    )(*blocks, *after)


def join_kernel(parts, got_ref, *rest):
    rows = got_ref.shape[0] // parts
    for m, out in enumerate(rest[parts:]):
        out[rows:, :] = got_ref[m * rows : (m + 1) * rows, :]


def join(blocks, got):
    parts = len(blocks)
    return pl.pallas_call(
        functools.partial(join_kernel, parts),
        out_shape=[jax.ShapeDtypeStruct(block.shape, block.dtype) for block in blocks],
        in_specs=[VM] * (1 + parts),
        out_specs=[VM] * parts,
        input_output_aliases={1 + m: m for m in range(parts)},
        compiler_params=params(4),
        name="join",
    )(got, *blocks)


def forward_rows_kernel(tok, hd, pieces, *refs):
    for m, row in enumerate(pieces):
        for head, (n, start, lane) in enumerate(row):
            block = refs[n][start + tok : start + 2 * tok, lane : lane + hd]
            refs[-1][m * tok : (m + 1) * tok, head * hd : (head + 1) * hd] = block


def forward_rows(arrays, pieces, tok, hd, after):
    return pl.pallas_call(
        functools.partial(forward_rows_kernel, tok, hd, pieces),
        out_shape=jax.ShapeDtypeStruct(
            (len(pieces) * tok, len(pieces[0]) * hd), arrays[0].dtype
        ),
        in_specs=[VM] * len(arrays) + [ANY],
        out_specs=VM,
        compiler_params=params(4),
        name="forward_rows",
    )(*arrays, after)


def assemble_kernel(tok, hd, pieces, me_ref, *rest):
    refs, got, out, sems = rest[:-3], rest[-3], rest[-2], rest[-1]
    me = me_ref[0]
    heads = len(pieces[0])
    moves = []
    for m, row in enumerate(pieces):
        for head, (n, start, lane) in enumerate(row):
            column = (me ^ (2 * m)) * heads * hd + head * hd
            moves.append((refs[n].at[pl.ds(start, tok), pl.ds(lane, hd)], column, hd))
        column = (me ^ (2 * m + 1)) * heads * hd
        moves.append((got.at[pl.ds(m * tok, tok), :], column, heads * hd))
    copies = [
        pltpu.make_async_copy(
            source, out.at[:, pl.ds(pl.multiple_of(column, LANES), width)], sems.at[n]
        )
        for n, (source, column, width) in enumerate(moves)
    ]
    for copy in copies:
        copy.start()
    for copy in copies:
        copy.wait()


def assemble(me, arrays, pieces, got, tok, hd):
    half, heads = len(pieces), len(pieces[0])
    return pl.pallas_call(
        functools.partial(assemble_kernel, tok, hd, pieces),
        out_shape=jax.ShapeDtypeStruct((tok, 2 * half * heads * hd), got.dtype),
        in_specs=[SMEM] + [VM] * (len(arrays) + 1),
        out_specs=ANY,
        scratch_shapes=[pltpu.SemaphoreType.DMA((half * (heads + 1),))],
        compiler_params=params(4),
        name="assemble",
    )(me, *arrays, got)


def soft(scores, scale):
    top = jnp.max(scores, axis=0, keepdims=True)
    expo = jnp.exp2((scores - top) * scale)
    return expo, jnp.sum(expo, axis=0, keepdims=True)


def masked_weights(scores, mask, slots, scale):
    rows, tok = scores.shape
    bias = (mask.astype(jnp.float32)[:slots] - 1.0) * (-HIDDEN)
    scores = scores.reshape(slots, rows // slots, tok) + bias[:, None, :]
    expo, norm = soft(scores.reshape(rows, tok), scale)
    return (expo * (1.0 / norm)).astype(jnp.bfloat16)


def window(me, p, count):
    slab = me ^ p
    low = jnp.where(slab > 0, (slab - 1) ^ me, p)
    high = jnp.where(slab < count - 1, (slab + 1) ^ me, p)
    return low, p, high


def log_scale(hd):
    return hd ** (-0.5) * math.log2(math.e)


def attention_kernel(
    count, tok, hd, nh, slots, rank, before, last, factor, me_ref, *rest
):
    half = count // 2
    noted, rest = rest[: half + 1], rest[half + 1 :]
    if before:
        blocks, rest = rest[:half], rest[half:]
    up_ref, rest = rest[0], rest[1:]
    if before:
        hid_ref, gup_in, *rest = rest
    outs, rest = rest[:half], rest[half:]
    if last:
        hid_keep, hid_send, gup_ref, *rest = rest
    else:
        hid_out, gup_ref, *rest = rest
    note_s, q_s, k_s, vt_s, svt_s, lora_s, grad_s, hid_s, out_s = rest
    head = pl.program_id(0)
    me = me_ref[0]
    scale = log_scale(hd)
    size = note_s.shape[1]

    @pl.when(head == 0)
    def _():
        part = noted[half].shape[0] // half
        for p in range(count):
            m = p // 2
            if p % 2:
                note_s[p] = noted[half][(m + 1) * part - size : (m + 1) * part, :]
            else:
                note_s[p] = noted[m][noted[m].shape[0] - size :, :]
            lora_s[:, p * tok : (p + 1) * tok] = note_s[p, :rank, :]
        if before:
            hid_s[...] = hid_ref[...]
            gup_ref[:, : before * hd] = gup_in[...]
        else:
            hid_s[...] = jnp.zeros_like(hid_s)

    for p in range(count):
        if before:
            ref, start = blocks[p // 2], p % 2 * nh * 3 * tok
        elif p % 2:
            ref, start = noted[half], p // 2 * (noted[half].shape[0] // half)
        else:
            ref, start = noted[p // 2], 0
        start = pl.multiple_of(start + head * 3 * tok, ROWS)
        q_s[p * tok : (p + 1) * tok, :] = ref[pl.ds(start, tok), :]
        k_s[p * tok : (p + 1) * tok, :] = ref[pl.ds(start + tok, tok), :]
        vt_s[:, p * tok : (p + 1) * tok] = ref[pl.ds(start + 2 * tok, tok), :].T
    up_t = up_ref[...]
    for p in range(count):
        cols = slice(p * tok, (p + 1) * tok)
        term = mm(up_t, lora_s[:, cols], TN)
        svt_s[p] = (vt_s[:, cols].astype(jnp.float32) + term).astype(jnp.bfloat16)
    grad_s[...] = jnp.zeros_like(grad_s)

    for start in range(0, count, 4):
        slabs = range(start, min(start + 4, count))
        queries = [q_s[p * tok : (p + 1) * tok, :] for p in slabs]
        places = [window(me, p, count) for p in slabs]
        full = [mm(k_s[...], query, NT) for query in queries]
        seen = [
            mm(
                jnp.concatenate(
                    [k_s[pl.ds(pl.multiple_of(w * tok, tok), tok), :] for w in place], axis=0
                ),
                query,
                NT,
            )
            for place, query in zip(places, queries)
        ]
        full = [soft(x, scale) for x in full]
        teachers = [mm(vt_s[...], expo.astype(jnp.bfloat16)) for expo, _ in full]
        weights = [
            masked_weights(x, note_s[p, rank:, :], slots, scale) for p, x in zip(slabs, seen)
        ]
        students = [
            mm(jnp.concatenate([svt_s[w] for w in place], axis=1), weight)
            for place, weight in zip(places, weights)
        ]
        deltas = []
        for (_, norm), teacher, student in zip(full, teachers, students):
            teacher = (teacher / norm).astype(jnp.bfloat16).astype(jnp.float32)
            deltas.append(((student - teacher) * factor).astype(jnp.bfloat16))
        grads = [mm(weight, delta, NT) for weight, delta in zip(weights, deltas)]
        for p, place, student, grad in zip(slabs, places, students, grads):
            out_s[p] = student.T.astype(jnp.bfloat16)
            for n, w in enumerate(place):
                grad_s[w] += grad[n * tok : (n + 1) * tok]

    grad = grad_s[...].reshape(count * tok, hd).astype(jnp.bfloat16)
    column = pl.multiple_of(head * hd, LANES)
    for p in range(count):
        outs[p // 2][p % 2 * tok : (p % 2 + 1) * tok, pl.ds(column, hd)] = out_s[p]
    column = pl.multiple_of((before + head) * hd, LANES)
    gup_ref[:, pl.ds(column, hd)] = mm(lora_s[...], grad)
    hid_s[...] += mm(up_t, grad, NT)

    @pl.when(head == nh - 1)
    def _():
        if last:
            for m in range(half):
                to = slice(m * tok, (m + 1) * tok)
                hid_keep[:, to] = hid_s[:, 2 * m * tok : (2 * m + 1) * tok]
                odd = hid_s[:, (2 * m + 1) * tok : (2 * m + 2) * tok]
                hid_send[:, to] = odd.astype(jnp.bfloat16)
        else:
            hid_out[...] = hid_s[...]


def attention(me, blocks, noted, up_t, given, first, nh, tok, hd, slots, mask_rows, last):
    count = 2 * len(noted) - 2
    rank = up_t.shape[0]
    bf, f32 = jnp.bfloat16, jnp.float32
    keys = count * tok
    heads = first + nh
    shapes = [jax.ShapeDtypeStruct((2 * tok, nh * hd), bf)] * (count // 2)
    if last:
        shapes += [
            jax.ShapeDtypeStruct((rank, keys // 2), f32),
            jax.ShapeDtypeStruct((rank, keys // 2), bf),
        ]
    else:
        shapes += [jax.ShapeDtypeStruct((rank, keys), f32)]
    shapes += [jax.ShapeDtypeStruct((rank, heads * hd), f32)]
    return pl.pallas_call(
        functools.partial(
            attention_kernel,
            count,
            tok,
            hd,
            nh,
            slots,
            rank,
            first,
            last,
            keys ** (-0.5),
        ),
        grid=(nh,),
        out_shape=shapes,
        in_specs=[SMEM]
        + [VM] * (len(noted) + len(blocks))
        + [pl.BlockSpec((rank, hd), lambda h: (0, first + h))]
        + [VM] * len(given),
        out_specs=[VM] * len(shapes),
        scratch_shapes=[
            pltpu.VMEM((count, rank + mask_rows, tok), bf),
            pltpu.VMEM((keys, hd), bf),
            pltpu.VMEM((keys, hd), bf),
            pltpu.VMEM((hd, keys), bf),
            pltpu.VMEM((count, hd, tok), bf),
            pltpu.VMEM((rank, keys), bf),
            pltpu.VMEM((count, tok, hd), f32),
            pltpu.VMEM((rank, keys), f32),
            pltpu.VMEM((count, tok, hd), bf),
        ],
        compiler_params=params(30),
        cost_estimate=pl.CostEstimate(
            flops=nh * 4 * 10**9, bytes_accessed=4 * nh * keys * hd * 2, transcendentals=0
        ),
        name="attention",
    )(
        me,
        *noted,
        *blocks,
        up_t,
        *given,
    )


def pair_kernel(parts, counts, keep_ref, got_ref, *rest):
    riders, outs = rest[:-parts], rest[-parts:]
    rank, width = keep_ref.shape[0], keep_ref.shape[1] // parts
    for m in range(parts):
        cols = slice(m * width, (m + 1) * width)
        total = keep_ref[:, cols] + got_ref[:, cols].astype(jnp.float32)
        outs[m][:rank, :] = total.astype(outs[m].dtype)
        row = rank
        for rider in riders[sum(counts[:m]) : sum(counts[: m + 1])]:
            size = rider.shape[0]
            for lane in range(0, rider.shape[1], width):
                outs[m][row : row + size, :] = rider[:, lane : lane + width]
                row += size


def pair_sum(keep, got, parts, riders):
    rank, width = keep.shape[0], keep.shape[1] // parts
    extra = [sum(rider.size for rider in group) // width for group in riders]
    shapes = [
        jax.ShapeDtypeStruct((rank + more, width), jnp.bfloat16 if m else jnp.float32)
        for m, more in enumerate(extra)
    ]
    counts = [len(group) for group in riders]
    return pl.pallas_call(
        functools.partial(pair_kernel, parts, counts),
        out_shape=shapes,
        in_specs=[VM] * (2 + sum(counts)),
        out_specs=[VM] * parts,
        compiler_params=params(4),
        name="pair_sum",
    )(keep, got, *[rider for group in riders for rider in group])


def chip_terms(keep, send, count, riders=None):
    half = count // 2
    return chips(pair_sum(keep, swap(send, count, 1), half, riders or [[]] * half), count)


def down_kernel(count, group, me_ref, *rest):
    parts = rest[: count // 2]
    x_ref, keep_ref, send_ref = rest[count // 2 :]
    me = me_ref[0]
    hidden = parts[0][...]
    for part in parts[1:]:
        hidden += part[: hidden.shape[0], :].astype(jnp.float32)
    hidden = hidden.astype(jnp.bfloat16)
    for k in range(count):
        column = pl.multiple_of((me ^ k) * group, LANES)
        term = mm(hidden, x_ref[:, pl.ds(column, group)])
        to = (send_ref, keep_ref)[k % 2 == 0]
        to[:, k // 2 * group : (k // 2 + 1) * group] = term.astype(to.dtype)


def down_terms(me, parts, x):
    count = 2 * len(parts)
    model = x.shape[1]
    rank = parts[0].shape[0]
    return pl.pallas_call(
        functools.partial(down_kernel, count, model // count),
        out_shape=[
            jax.ShapeDtypeStruct((rank, model // 2), jnp.float32),
            jax.ShapeDtypeStruct((rank, model // 2), jnp.bfloat16),
        ],
        in_specs=[SMEM] + [VM] * (len(parts) + 1),
        out_specs=[VM, VM],
        compiler_params=params(8),
        name="down_terms",
    )(me, *parts, x)


def sum_kernel(*refs):
    total = refs[0][...]
    for ref in refs[1:-1]:
        total += ref[...].astype(jnp.float32)
    refs[-1][...] = total


def sum_terms(parts):
    return pl.pallas_call(
        sum_kernel,
        out_shape=jax.ShapeDtypeStruct(parts[0].shape, jnp.float32),
        in_specs=[VM] * len(parts),
        out_specs=VM,
        compiler_params=params(8),
        name="sum_terms",
    )(*parts)


def apart(always, phase, *operands):
    def never(*operands):
        shapes = jax.eval_shape(phase, *operands)
        return jax.tree.map(lambda shape: jnp.zeros(shape.shape, shape.dtype), shapes)

    return lax.cond(always, phase, never, *operands)


def head_chunks(per_group):
    if per_group < 2:
        return [(0, per_group)]
    return [(0, per_group - 1), (per_group - 1, 1)]


def local(
    queries, keys, values, value_layer_input, adapter_down_weight, adapter_up_weight, neighbors
):
    tok, model = queries.shape
    rank = adapter_down_weight.shape[1]
    count = lax.axis_size("context")
    index = lax.axis_index("context")
    me = index.astype(jnp.int32).reshape(1)
    hd = model // H
    group = model // count
    per_group = H // count
    tiles = neighbors.shape[0]
    slots = 3 * tiles
    chunks = head_chunks(per_group)

    mask_rows = slots + -slots % 16

    down_t = adapter_down_weight.T
    up_t = adapter_up_weight.T

    note = rank + mask_rows
    first_own = first_pack(
        me, neighbors, queries, keys, values, value_layer_input, down_t,
        count, hd, chunks[0][1], mask_rows,
    )
    joined = [[]]
    for first, nh in chunks[1:]:
        *own, send = pack(me, queries, keys, values, first_own[0], count, hd, first, nh)
        joined.append(join(own, swap(send, count, 1)))
    noted = chips(first_own, count)
    ready = [own[0] for own in joined[1:]]
    noted = noted + [swap(forward(noted, note, ready), count, 1)]
    messages = [chips(own, count) if own else [] for own in joined]

    own_up = lax.dynamic_slice_in_dim(up_t, index * group, group, 1)
    half = count // 2
    given, arrays = [], []
    riders = [[] for _ in range(half)]
    pieces = [[] for _ in range(half)]
    rows = [rank] * half
    for c, (first, nh) in enumerate(chunks):
        last = c == len(chunks) - 1
        out = attention(
            me, messages[c], noted, own_up, given, first, nh, tok, hd, slots, mask_rows, last
        )
        given = out[half:]
        for m in range(half):
            if m and (last or m == 1):
                riders[m].append(out[m])
                for _ in range(nh):
                    pieces[m].append((m - half, rows[m], 0))
                    rows[m] += 2 * tok
            else:
                pieces[m] += [(len(arrays), 0, h * hd) for h in range(nh)]
                arrays.append(swap(out[m], count, 2 * m) if m else out[0])
    hid_keep, hid_send, grad_up = given

    def hidden_phase(hid_keep, hid_send, riders):
        return chip_terms(hid_keep, hid_send, count, riders)

    def grad_phase(keep, send, _):
        return sum_terms(chip_terms(keep, send, count))

    hidden = apart(index < count, hidden_phase, hid_keep, hid_send, riders)
    keep, send = down_terms(me, hidden, value_layer_input)
    pieces = [
        [(n if n >= 0 else len(arrays) + n + half - 1, row, lane) for n, row, lane in group]
        for group in pieces
    ]
    arrays += hidden[1:]
    passed = forward_rows(arrays, pieces, tok, hd, keep)
    got = swap(passed, count, 1)
    grad_down = apart(index < count, grad_phase, keep, send, passed)
    student_out = assemble(me, arrays, pieces, got, tok, hd)
    return student_out, grad_down.T, grad_up.T


def solution(mesh):
    rows = P(("video", "context"), None)
    return jax.shard_map(
        local,
        mesh=mesh,
        in_specs=(rows, rows, rows, rows, P(), P(), rows),
        out_specs=(rows, rows, rows),
        check_vma=False,
    )
```

time: 145 us -> 127 us (0.88)
  starting transfers between devices: 75.8 us -> 22.5 us
  waiting for transfers between devices: 26.9 us -> 69.4 us
  Pallas kernels: 31.6 us -> 28.7 us
  local copies, waits for them, and re-layouts: 8.09 us -> 5.24 us
    ppermute x26 -> x19, starting transfers between devices: 70.8 us -> 22.5 us  [swap(): return lax.ppermute(block, 'context', pairs)]
    ppermute x26 -> x19, waiting for transfers between devices: 26.9 us -> 69.4 us  [swap(): return lax.ppermute(block, 'context', pairs)]
    ppermute x2 -> x0, starting transfers between devices: 4.97 us -> none  [the longest x1 3.69 us: local(): low = lax.ppermute(both, 'context', ups)]
    pallas_call x4 -> x6, Pallas kernels: 7.66 us -> 3.49 us  [the longest x1 2.19 us: assemble(): pl.pallas_call(functools.partial(assemble_kernel, tok, hd, pieces), out_s...]
    unnamed x34, local copies, waits for them, and re-layouts: 7.11 us -> 5.23 us
  transfers between devices with their start and end apart: 28 -> 19, of which waited for: 9 -> 8; matrix products, arithmetic and copies ran while one was open for 1% -> 0% of each run, Pallas kernels for 14% -> 15%
where the time goes in v6:
time: 127 us
  waiting for transfers between devices  69.4 us (55%)
  Pallas kernels  28.7 us (23%)
  starting transfers between devices  22.5 us (18%)
  local copies, waits for them, and re-layouts  5.24 us (4%)
    ppermute x19, waiting for transfers between devices, swap(): return lax.ppermute(block, 'context', pairs)  69.4 us
    ppermute x19, starting transfers between devices, swap(): return lax.ppermute(block, 'context', pairs)  22.5 us
    pallas_call x2, Pallas kernels, attention(): pl.pallas_call(functools.partial(attention_kernel, count, tok, hd, nh, sl...  17.6 us
    pallas_call x1, Pallas kernels, first_pack(): pl.pallas_call(functools.partial(first_kernel, count, model // count, hd,...  5.76 us
    unnamed x34, local copies, waits for them, and re-layouts  5.23 us
  transfers between devices with their start and end apart: 19, of which 8 were waited for; matrix products, arithmetic and copies ran while one was open for 0% of the time, Pallas kernels for 15%

profile of v6, /device:TPU:0, one launch (start us, length us, event | category | flops | bytes accessed | tf_op | source)
XLA Modules:
  0.0 126.7 jit_solution(11096348159165003594)
XLA Ops:
  0.6 0.0 copy-start
  0.7 5.8 %first_pack.1 = (bf16[2384,128]{1,0:T(8,128)(2,1)}, bf16[2384,128]{1,0:T(8,128)(2,1)}, bf16[2384,128]{1,0:T(8,128)(2,1)}, bf16[2384,128]{1,0:T(8,128)(2,1)}) custom-call(s32[1]{0:T(128)} %bitcast.me_ref, s32[2,4]{1,0:T(2,128)} %nb_ref.1, bf16[128,4096]{1,0:T(8,128)(2,1)} %q_ref.1, bf16[128,4096]{1,0:T(8,128)(2,1)} %k_ref.1, bf16[128,4096]{1,0:T(8,128)(2,1)} %v_ref.1, ...), custom_call_target="tpu_custom_call" | custom-call | tf_op jit(solution)/shard_map/first_pack/pallas_call | solution.py:137
  6.4 5.1 %collective-permute-start.10 = (bf16[2384,128]{1,0:T(8,128)(2,1)}, bf16[2384,128]{1,0:T(8,128)(2,1)S(1)}, u32[]{:S(2)}, u32[]{:S(2)}) collective-permute-start(bf16[2384,128]{1,0:T(8,128)(2,1)} %get-tuple-element.73), channel_id=1, source_target_pairs={{0,6},{1,7},{2,4},{3,5},{4,2},{5,3},{6,0},{7,1},{8,14},{9,15},{10,... | collective-permute-start | bytes 1830920 | tf_op jit(solution)/shard_map/ppermute | solution.py:36
  11.6 0.0 collective-permute-start.8
  11.6 0.6 collective-permute-start.9
  12.2 1.2 copy-done.3
  13.4 1.1 copy-done.5
  14.5 0.5 pack.1
  15.0 0.1 collective-permute-start.11
  15.1 1.7 %collective-permute-done.11.got_ref = bf16[1536,128]{1,0:T(8,128)(2,1)S(1)} collective-permute-done((bf16[1536,128]{1,0:T(8,128)(2,1)S(1)}, bf16[1536,128]{1,0:T(8,128)(2,1)S(1)}, u32[]{:S(2)}, u32[]{:S(2)}) %collective-permute-start.11) | collective-permute-done | bytes 393248 | tf_op jit(solution)/shard_map/ppermute | solution.py:36
  16.8 9.6 %collective-permute-done.10.refs_3_.rest_3_ = bf16[2384,128]{1,0:T(8,128)(2,1)S(1)} collective-permute-done((bf16[2384,128]{1,0:T(8,128)(2,1)}, bf16[2384,128]{1,0:T(8,128)(2,1)S(1)}, u32[]{:S(2)}, u32[]{:S(2)}) %collective-permute-start.10) | collective-permute-done | bytes 610336 | tf_op jit(solution)/shard_map/ppermute | solution.py:36
  26.4 13.3 %collective-permute-done.8.refs_1_.rest_1_ = bf16[2384,128]{1,0:T(8,128)(2,1)S(1)} collective-permute-done((bf16[2384,128]{1,0:T(8,128)(2,1)}, bf16[2384,128]{1,0:T(8,128)(2,1)S(1)}, u32[]{:S(2)}, u32[]{:S(2)}) %collective-permute-start.8) | collective-permute-done | bytes 610336 | tf_op jit(solution)/shard_map/ppermute | solution.py:36
  39.8 24.2 %collective-permute-done.9.refs_2_.rest_2_ = bf16[2384,128]{1,0:T(8,128)(2,1)S(1)} collective-permute-done((bf16[2384,128]{1,0:T(8,128)(2,1)}, bf16[2384,128]{1,0:T(8,128)(2,1)S(1)}, u32[]{:S(2)}, u32[]{:S(2)}) %collective-permute-start.9) | collective-permute-done | bytes 610336 | tf_op jit(solution)/shard_map/ppermute | solution.py:36
  63.9 0.1 forward.1
  64.0 0.7 copy-done.10
  64.8 0.0 collective-permute-start.12
  64.8 0.1 collective-permute-start.15
  64.9 3.0 %collective-permute-start.16 = (bf16[768,128]{1,0:T(8,128)(2,1)}, bf16[768,128]{1,0:T(8,128)(2,1)S(1)}, u32[]{:S(2)}, u32[]{:S(2)}) collective-permute-start(bf16[768,128]{1,0:T(8,128)(2,1)} %copy-done.14), channel_id=1, source_target_pairs={{0,4},{1,5},{2,6},{3,7},{4,0},{5,1},{6,2},{7,3},{8,12},{9,13},{10,... | collective-permute-start | bytes 589832 | tf_op jit(solution)/shard_map/ppermute | solution.py:36
  67.9 1.3 %collective-permute-start.17 = (bf16[768,128]{1,0:T(8,128)(2,1)}, bf16[768,128]{1,0:T(8,128)(2,1)S(1)}, u32[]{:S(2)}, u32[]{:S(2)}) collective-permute-start(bf16[768,128]{1,0:T(8,128)(2,1)} %copy-done.15), channel_id=1, source_target_pairs={{0,6},{1,7},{2,4},{3,5},{4,2},{5,3},{6,0},{7,1},{8,14},{9,15},{10,... | collective-permute-start | bytes 589832 | tf_op jit(solution)/shard_map/ppermute | solution.py:36
  69.3 0.0 collective-permute-done.12.rest_4_
  69.3 1.1 copy-done.8
  70.3 1.1 copy-done.11
  71.4 12.3 %attention.2 = (bf16[256,384]{1,0:T(8,128)(2,1)S(1)}, bf16[256,384]{1,0:T(8,128)(2,1)S(1)}, bf16[256,384]{1,0:T(8,128)(2,1)}, bf16[256,384]{1,0:T(8,128)(2,1)}, ...) custom-call(s32[1]{0:T(128)} %bitcast.me_ref, bf16[2384,128]{1,0:T(8,128)(2,1)S(1)} %copy-done.6, ...), custom_call_target="tpu_custom_call" | custom-call | flops 12000000000 | bytes 3145728 | tf_op jit(solution)/shard_map/attention/pallas_call | solution.py:399
  83.7 0.2 collective-permute-start.13
  83.9 2.3 %collective-permute-start.14 = (bf16[256,384]{1,0:T(8,128)(2,1)}, bf16[256,384]{1,0:T(8,128)(2,1)S(1)}, u32[]{:S(2)}, u32[]{:S(2)}) collective-permute-start(bf16[256,384]{1,0:T(8,128)(2,1)} %get-tuple-element.82), channel_id=1, source_target_pairs={{0,6},{1,7},{2,4},{3,5},{4,2},{5,3},{6,0},{7,1},{8,14},{9,15},{10,... | collective-permute-start | bytes 589832 | tf_op jit(solution)/shard_map/ppermute | solution.py:36
  86.2 0.0 collective-permute-done.17.rest_8_
  86.2 5.3 %attention.3 = (bf16[256,128]{1,0:T(8,128)(2,1)S(1)}, bf16[256,128]{1,0:T(8,128)(2,1)S(1)}, bf16[256,128]{1,0:T(8,128)(2,1)S(1)}, bf16[256,128]{1,0:T(8,128)(2,1...) custom-call(s32[1]{0:T(128)} %bitcast.me_ref, bf16[2384,128]{1,0:T(8,128)(2,1)S(1)} %copy-done.6, ...), custom_call_target="tpu_custom_call" | custom-call | flops 4000000000 | bytes 1048576 | tf_op jit(solution)/shard_map/attention/pallas_call | solution.py:399
  91.5 17.8 %conditional.2 = (f32[64,128]{1,0:T(8,128)S(1)}, bf16[1088,128]{1,0:T(8,128)(2,1)}, bf16[320,128]{1,0:T(8,128)(2,1)}, bf16[320,128]{1,0:T(8,128)(2,1)}) conditional(s32[]{:T(128)} %convert_element_type.4, () %tuple.22, (bf16[64,512]{1,0:T(8,128)(2,1)S(1)}, f32[64,512]{1,0:T(8,128)S(1)}, bf16[256,384]{1,0:T(8,128)(2,1)S(1)}, ...), branch_computations={%region_0.0_spmd, %region_1.0_spmd} | conditional | bytes 2031808 | solution.py:537
  91.5 1.3 collective-permute-done.got_ref
  92.8 0.1 pair_sum.2
  92.8 1.1 collective-permute-start.1
  93.9 1.1 collective-permute-start.2
  95.0 2.3 %collective-permute-start.3 = (bf16[320,128]{1,0:T(8,128)(2,1)S(1)}, bf16[320,128]{1,0:T(8,128)(2,1)}, u32[]{:S(2)}, u32[]{:S(2)}) collective-permute-start(bf16[320,128]{1,0:T(8,128)(2,1)S(1)} %get-tuple-element.28), channel_id=1, source_target_pairs={{0,6},{1,7},{2,4},{3,5},{4,2},{5,3},{6,0},{7,1},{8,14},{9,15},{10,... | collective-permute-start | bytes 245768 | tf_op jit(solution)/shard_map/cond/branch_1_fun/ppermute | solution.py:36
  97.3 12.0 %collective-permute-done.2 = bf16[320,128]{1,0:T(8,128)(2,1)} collective-permute-done((bf16[320,128]{1,0:T(8,128)(2,1)S(1)}, bf16[320,128]{1,0:T(8,128)(2,1)}, u32[]{:S(2)}, u32[]{:S(2)}) %collective-permute-start.2) | collective-permute-done | bytes 81952 | tf_op jit(solution)/shard_map/cond/branch_1_fun/ppermute | solution.py:36
  109.3 0.0 collective-permute-done.3
  109.3 0.0 collective-permute-done.1
  109.3 1.3 %down_terms.1 = (f32[64,2048]{1,0:T(8,128)S(1)}, bf16[64,2048]{1,0:T(8,128)(2,1)S(1)}) custom-call(s32[1]{0:T(128)} %bitcast.me_ref, f32[64,128]{1,0:T(8,128)S(1)} %get-tuple-element.98.rest_0_, bf16[1088,128]{1,0:T(8,128)(2,1)} %get-tuple-element.95.rest_1_.refs_4_.rest_4_, bf16[320,128]{1,0:T(8,128)(2,1)} %get-tuple-element.96.rest_2_.refs_5_.rest_5_, ...), custom_call_target="tpu_custom_call" | custom-call | tf_op jit(solution)/shard_map/down_terms/pallas_call | solution.py:501
  110.6 1.1 forward_rows.1
  111.7 0.1 collective-permute-start.18
  111.8 12.7 %conditional.3 = (f32[64,512]{1,0:T(8,128)S(1)}) conditional(s32[]{:T(128)} %convert_element_type.4, () %tuple.24, (bf16[64,2048]{1,0:T(8,128)(2,1)S(1)}, f32[64,2048]{1,0:T(8,128)S(1)}) %tuple.25), branch_computations={%region_2.0_spmd, %region_3.0_spmd} | conditional | bytes 1835176 | solution.py:537
  111.8 0.5 collective-permute-start.4
  112.3 1.8 %collective-permute-done.4.got_ref = bf16[64,2048]{1,0:T(8,128)(2,1)S(1)} collective-permute-done((bf16[64,2048]{1,0:T(8,128)(2,1)S(1)}, bf16[64,2048]{1,0:T(8,128)(2,1)S(1)}, u32[]{:S(2)}, u32[]{:S(2)}) %collective-permute-start.4) | collective-permute-done | bytes 262176 | tf_op jit(solution)/shard_map/cond/branch_1_fun/ppermute | solution.py:36
  114.1 2.3 %collective-permute-start.5 = (bf16[64,512]{1,0:T(8,128)(2,1)S(1)}, bf16[64,512]{1,0:T(8,128)(2,1)S(1)}, u32[]{:S(2)}, u32[]{:S(2)}) collective-permute-start(bf16[64,512]{1,0:T(8,128)(2,1)S(1)} %get-tuple-element.32), channel_id=1, source_target_pairs={{0,2},{1,3},{2,0},{3,1},{4,6},{5,7},{6,4},{7,5},{8,10},{9,11},{10,... | collective-permute-start | bytes 196616 | tf_op jit(solution)/shard_map/cond/branch_1_fun/ppermute | solution.py:36
  116.4 0.2 collective-permute-start.6
  116.6 2.2 %collective-permute-start.7 = (bf16[64,512]{1,0:T(8,128)(2,1)S(1)}, bf16[64,512]{1,0:T(8,128)(2,1)S(1)}, u32[]{:S(2)}, u32[]{:S(2)}) collective-permute-start(bf16[64,512]{1,0:T(8,128)(2,1)S(1)} %get-tuple-element.34), channel_id=1, source_target_pairs={{0,6},{1,7},{2,4},{3,5},{4,2},{5,3},{6,0},{7,1},{8,14},{9,15},{10,... | collective-permute-start | bytes 196616 | tf_op jit(solution)/shard_map/cond/branch_1_fun/ppermute | solution.py:36
  118.8 5.6 %collective-permute-done.6.refs_2_ = bf16[64,512]{1,0:T(8,128)(2,1)S(1)} collective-permute-done((bf16[64,512]{1,0:T(8,128)(2,1)S(1)}, bf16[64,512]{1,0:T(8,128)(2,1)S(1)}, u32[]{:S(2)}, u32[]{:S(2)}) %collective-permute-start.6) | collective-permute-done | bytes 65568 | tf_op jit(solution)/shard_map/cond/branch_1_fun/ppermute | solution.py:36
  124.5 0.0 copy-start.16
  124.5 2.2 %assemble.1 = bf16[128,4096]{1,0:T(8,128)(2,1)} custom-call(s32[1]{0:T(128)} %bitcast.me_ref, bf16[256,384]{1,0:T(8,128)(2,1)S(1)} %get-tuple-element.80.refs_0_.rest_0_, bf16[256,384]{1,0:T(8,128)(2,1)S(1)} %collective-permute-done.13.refs_1_.rest_1_, bf16[256,384]{1,0:T(8,128)(2,1)S(1)} %collective-permute-done.14.refs_2_.rest_2_, ...), custom_call_target="tpu_custom_call" | custom-call | tf_op jit(solution)/shard_map/assemble/pallas_call | solution.py:239
  (39 shorter events, 0.2 us)
Async XLA Ops:
  0.6 64.1 %copy-start = (bf16[4096,64]{0,1:T(8,128)(2,1)S(1)}, bf16[4096,64]{0,1:T(8,128)(2,1)}, u32[]{:S(2)}) copy-start(bf16[4096,64]{0,1:T(8,128)(2,1)} %param.16) | copy-start | bytes 1572868
  0.7 11.5 %copy-start.1 = (bf16[128,4096]{1,0:T(8,128)(2,1)S(1)}, bf16[128,4096]{1,0:T(8,128)(2,1)}, u32[]{:S(2)}) copy-start(bf16[128,4096]{1,0:T(8,128)(2,1)} %q_ref.1) | copy-start | bytes 3145732
  0.7 11.5 %copy-start.2 = (bf16[128,4096]{1,0:T(8,128)(2,1)S(1)}, bf16[128,4096]{1,0:T(8,128)(2,1)}, u32[]{:S(2)}) copy-start(bf16[128,4096]{1,0:T(8,128)(2,1)} %k_ref.1) | copy-start | bytes 3145732
  6.4 20.0 %collective-permute-start.10 = (bf16[2384,128]{1,0:T(8,128)(2,1)}, bf16[2384,128]{1,0:T(8,128)(2,1)S(1)}, u32[]{:S(2)}, u32[]{:S(2)}) collective-permute-start(bf16[2384,128]{1,0:T(8,128)(2,1)} %get-tuple-element.73), channel_id=1, source_target_pairs={{0,6},{1,7},{2,4},{3,5},{4,2},{5,3},{6,0},{7,1},{8,14},{9,15},{10,... | collective-permute-start | bytes 1830920 | tf_op jit(solution)/shard_map/ppermute | solution.py:36
  11.6 28.2 %collective-permute-start.8 = (bf16[2384,128]{1,0:T(8,128)(2,1)}, bf16[2384,128]{1,0:T(8,128)(2,1)S(1)}, u32[]{:S(2)}, u32[]{:S(2)}) collective-permute-start(bf16[2384,128]{1,0:T(8,128)(2,1)} %get-tuple-element.71), channel_id=1, source_target_pairs={{0,2},{1,3},{2,0},{3,1},{4,6},{5,7},{6,4},{7,5},{8,10},{9,11},{10,... | collective-permute-start | bytes 1830920 | tf_op jit(solution)/shard_map/ppermute | solution.py:36
  11.6 52.4 %collective-permute-start.9 = (bf16[2384,128]{1,0:T(8,128)(2,1)}, bf16[2384,128]{1,0:T(8,128)(2,1)S(1)}, u32[]{:S(2)}, u32[]{:S(2)}) collective-permute-start(bf16[2384,128]{1,0:T(8,128)(2,1)} %get-tuple-element.72), channel_id=1, source_target_pairs={{0,4},{1,5},{2,6},{3,7},{4,0},{5,1},{6,2},{7,3},{8,12},{9,13},{10,... | collective-permute-start | bytes 1830920 | tf_op jit(solution)/shard_map/ppermute | solution.py:36
  12.2 1.2 copy-start.3
  13.4 1.1 copy-start.5
  15.0 1.8 %collective-permute-start.11 = (bf16[1536,128]{1,0:T(8,128)(2,1)S(1)}, bf16[1536,128]{1,0:T(8,128)(2,1)S(1)}, u32[]{:S(2)}, u32[]{:S(2)}) collective-permute-start(bf16[1536,128]{1,0:T(8,128)(2,1)S(1)} %get-tuple-element.74), channel_id=1, source_target_pairs={{0,1},{1,0},{2,3},{3,2},{4,5},{5,4},{6,7},{7,6},{8,9},{9,8},{10,11... | collective-permute-start | bytes 1179656 | tf_op jit(solution)/shard_map/ppermute | solution.py:36
  16.8 47.9 %copy-start.13 = (bf16[768,128]{1,0:T(8,128)(2,1)}, bf16[768,128]{1,0:T(8,128)(2,1)S(1)}, u32[]{:S(2)}) copy-start(bf16[768,128]{1,0:T(8,128)(2,1)S(1)} %get-tuple-element.83) | copy-start | bytes 589828
  16.8 47.9 %copy-start.14 = (bf16[768,128]{1,0:T(8,128)(2,1)}, bf16[768,128]{1,0:T(8,128)(2,1)S(1)}, u32[]{:S(2)}) copy-start(bf16[768,128]{1,0:T(8,128)(2,1)S(1)} %get-tuple-element.84) | copy-start | bytes 589828
  16.8 47.9 %copy-start.15 = (bf16[768,128]{1,0:T(8,128)(2,1)}, bf16[768,128]{1,0:T(8,128)(2,1)S(1)}, u32[]{:S(2)}) copy-start(bf16[768,128]{1,0:T(8,128)(2,1)S(1)} %get-tuple-element.85) | copy-start | bytes 589828
  39.8 24.3 %copy-start.7 = (bf16[2384,128]{1,0:T(8,128)(2,1)}, bf16[2384,128]{1,0:T(8,128)(2,1)S(1)}, u32[]{:S(2)}) copy-start(bf16[2384,128]{1,0:T(8,128)(2,1)S(1)} %collective-permute-done.8.refs_1_.rest_1_) | copy-start | bytes 1830916
  63.9 0.8 copy-start.10
  63.9 5.3 %copy-start.6 = (bf16[2384,128]{1,0:T(8,128)(2,1)S(1)}, bf16[2384,128]{1,0:T(8,128)(2,1)}, u32[]{:S(2)}) copy-start(bf16[2384,128]{1,0:T(8,128)(2,1)} %get-tuple-element.70._.refs_0_.rest_0_) | copy-start | bytes 1830916
  64.8 4.5 %collective-permute-start.12 = (bf16[4928,128]{1,0:T(8,128)(2,1)S(1)}, bf16[4928,128]{1,0:T(8,128)(2,1)}, u32[]{:S(2)}, u32[]{:S(2)}) collective-permute-start(bf16[4928,128]{1,0:T(8,128)(2,1)S(1)} %forward.1), channel_id=1, source_target_pairs={{0,1},{1,0},{2,3},{3,2},{4,5},{5,4},{6,7},{7,6},{8,9},{9,8},{10,11... | collective-permute-start | bytes 3784712 | tf_op jit(solution)/shard_map/ppermute | solution.py:36
  64.8 21.4 %collective-permute-start.15 = (bf16[768,128]{1,0:T(8,128)(2,1)}, bf16[768,128]{1,0:T(8,128)(2,1)S(1)}, u32[]{:S(2)}, u32[]{:S(2)}) collective-permute-start(bf16[768,128]{1,0:T(8,128)(2,1)} %copy-done.13), channel_id=1, source_target_pairs={{0,2},{1,3},{2,0},{3,1},{4,6},{5,7},{6,4},{7,5},{8,10},{9,11},{10,... | collective-permute-start | bytes 589832 | tf_op jit(solution)/shard_map/ppermute | solution.py:36
  64.9 21.3 %collective-permute-start.16 = (bf16[768,128]{1,0:T(8,128)(2,1)}, bf16[768,128]{1,0:T(8,128)(2,1)S(1)}, u32[]{:S(2)}, u32[]{:S(2)}) collective-permute-start(bf16[768,128]{1,0:T(8,128)(2,1)} %copy-done.14), channel_id=1, source_target_pairs={{0,4},{1,5},{2,6},{3,7},{4,0},{5,1},{6,2},{7,3},{8,12},{9,13},{10,... | collective-permute-start | bytes 589832 | tf_op jit(solution)/shard_map/ppermute | solution.py:36
  67.9 18.3 %collective-permute-start.17 = (bf16[768,128]{1,0:T(8,128)(2,1)}, bf16[768,128]{1,0:T(8,128)(2,1)S(1)}, u32[]{:S(2)}, u32[]{:S(2)}) collective-permute-start(bf16[768,128]{1,0:T(8,128)(2,1)} %copy-done.15), channel_id=1, source_target_pairs={{0,6},{1,7},{2,4},{3,5},{4,2},{5,3},{6,0},{7,1},{8,14},{9,15},{10,... | collective-permute-start | bytes 589832 | tf_op jit(solution)/shard_map/ppermute | solution.py:36
  69.3 1.1 copy-start.8
  70.3 1.1 copy-start.11
  71.4 14.8 %copy-start.9 = (bf16[2384,128]{1,0:T(8,128)(2,1)S(1)}, bf16[2384,128]{1,0:T(8,128)(2,1)}, u32[]{:S(2)}) copy-start(bf16[2384,128]{1,0:T(8,128)(2,1)} %copy-done.7) | copy-start | bytes 1830916
  71.4 14.8 %copy-start.12 = (bf16[2384,128]{1,0:T(8,128)(2,1)S(1)}, bf16[2384,128]{1,0:T(8,128)(2,1)}, u32[]{:S(2)}) copy-start(bf16[2384,128]{1,0:T(8,128)(2,1)} %copy-done.10) | copy-start | bytes 1830916
  83.7 26.9 %collective-permute-start.13 = (bf16[256,384]{1,0:T(8,128)(2,1)}, bf16[256,384]{1,0:T(8,128)(2,1)S(1)}, u32[]{:S(2)}, u32[]{:S(2)}) collective-permute-start(bf16[256,384]{1,0:T(8,128)(2,1)} %get-tuple-element.81), channel_id=1, source_target_pairs={{0,4},{1,5},{2,6},{3,7},{4,0},{5,1},{6,2},{7,3},{8,12},{9,13},{10,... | collective-permute-start | bytes 589832 | tf_op jit(solution)/shard_map/ppermute | solution.py:36
  83.9 26.7 %collective-permute-start.14 = (bf16[256,384]{1,0:T(8,128)(2,1)}, bf16[256,384]{1,0:T(8,128)(2,1)S(1)}, u32[]{:S(2)}, u32[]{:S(2)}) collective-permute-start(bf16[256,384]{1,0:T(8,128)(2,1)} %get-tuple-element.82), channel_id=1, source_target_pairs={{0,6},{1,7},{2,4},{3,5},{4,2},{5,3},{6,0},{7,1},{8,14},{9,15},{10,... | collective-permute-start | bytes 589832 | tf_op jit(solution)/shard_map/ppermute | solution.py:36
  91.5 17.8 %copy-start.4 = (bf16[128,4096]{1,0:T(8,128)(2,1)S(1)}, bf16[128,4096]{1,0:T(8,128)(2,1)}, u32[]{:S(2)}) copy-start(bf16[128,4096]{1,0:T(8,128)(2,1)} %rest_4_.1) | copy-start | bytes 3145732
  91.5 1.3 collective-permute-start
  92.8 16.5 %collective-permute-start.1 = (bf16[1088,128]{1,0:T(8,128)(2,1)S(1)}, bf16[1088,128]{1,0:T(8,128)(2,1)}, u32[]{:S(2)}, u32[]{:S(2)}) collective-permute-start(bf16[1088,128]{1,0:T(8,128)(2,1)S(1)} %get-tuple-element.26), channel_id=1, source_target_pairs={{0,2},{1,3},{2,0},{3,1},{4,6},{5,7},{6,4},{7,5},{8,10},{9,11},{10,... | collective-permute-start | bytes 835592 | tf_op jit(solution)/shard_map/cond/branch_1_fun/ppermute | solution.py:36
  93.9 15.4 %collective-permute-start.2 = (bf16[320,128]{1,0:T(8,128)(2,1)S(1)}, bf16[320,128]{1,0:T(8,128)(2,1)}, u32[]{:S(2)}, u32[]{:S(2)}) collective-permute-start(bf16[320,128]{1,0:T(8,128)(2,1)S(1)} %get-tuple-element.27), channel_id=1, source_target_pairs={{0,4},{1,5},{2,6},{3,7},{4,0},{5,1},{6,2},{7,3},{8,12},{9,13},{10,... | collective-permute-start | bytes 245768 | tf_op jit(solution)/shard_map/cond/branch_1_fun/ppermute | solution.py:36
  95.0 14.3 %collective-permute-start.3 = (bf16[320,128]{1,0:T(8,128)(2,1)S(1)}, bf16[320,128]{1,0:T(8,128)(2,1)}, u32[]{:S(2)}, u32[]{:S(2)}) collective-permute-start(bf16[320,128]{1,0:T(8,128)(2,1)S(1)} %get-tuple-element.28), channel_id=1, source_target_pairs={{0,6},{1,7},{2,4},{3,5},{4,2},{5,3},{6,0},{7,1},{8,14},{9,15},{10,... | collective-permute-start | bytes 245768 | tf_op jit(solution)/shard_map/cond/branch_1_fun/ppermute | solution.py:36
  111.7 12.8 %collective-permute-start.18 = (bf16[512,512]{1,0:T(8,128)(2,1)S(1)}, bf16[512,512]{1,0:T(8,128)(2,1)S(1)}, u32[]{:S(2)}, u32[]{:S(2)}) collective-permute-start(bf16[512,512]{1,0:T(8,128)(2,1)S(1)} %forward_rows.1), channel_id=1, source_target_pairs={{0,1},{1,0},{2,3},{3,2},{4,5},{5,4},{6,7},{7,6},{8,9},{9,8},{10,11... | collective-permute-start | bytes 1572872 | tf_op jit(solution)/shard_map/ppermute | solution.py:36
  111.8 2.3 %collective-permute-start.4 = (bf16[64,2048]{1,0:T(8,128)(2,1)S(1)}, bf16[64,2048]{1,0:T(8,128)(2,1)S(1)}, u32[]{:S(2)}, u32[]{:S(2)}) collective-permute-start(bf16[64,2048]{1,0:T(8,128)(2,1)S(1)} %get-tuple-element.30), channel_id=1, source_target_pairs={{0,1},{1,0},{2,3},{3,2},{4,5},{5,4},{6,7},{7,6},{8,9},{9,8},{10,11... | collective-permute-start | bytes 786440 | tf_op jit(solution)/shard_map/cond/branch_1_fun/ppermute | solution.py:36
  114.1 4.7 %collective-permute-start.5 = (bf16[64,512]{1,0:T(8,128)(2,1)S(1)}, bf16[64,512]{1,0:T(8,128)(2,1)S(1)}, u32[]{:S(2)}, u32[]{:S(2)}) collective-permute-start(bf16[64,512]{1,0:T(8,128)(2,1)S(1)} %get-tuple-element.32), channel_id=1, source_target_pairs={{0,2},{1,3},{2,0},{3,1},{4,6},{5,7},{6,4},{7,5},{8,10},{9,11},{10,... | collective-permute-start | bytes 196616 | tf_op jit(solution)/shard_map/cond/branch_1_fun/ppermute | solution.py:36
  116.4 8.0 %collective-permute-start.6 = (bf16[64,512]{1,0:T(8,128)(2,1)S(1)}, bf16[64,512]{1,0:T(8,128)(2,1)S(1)}, u32[]{:S(2)}, u32[]{:S(2)}) collective-permute-start(bf16[64,512]{1,0:T(8,128)(2,1)S(1)} %get-tuple-element.33), channel_id=1, source_target_pairs={{0,4},{1,5},{2,6},{3,7},{4,0},{5,1},{6,2},{7,3},{8,12},{9,13},{10,... | collective-permute-start | bytes 196616 | tf_op jit(solution)/shard_map/cond/branch_1_fun/ppermute | solution.py:36
  116.6 7.8 %collective-permute-start.7 = (bf16[64,512]{1,0:T(8,128)(2,1)S(1)}, bf16[64,512]{1,0:T(8,128)(2,1)S(1)}, u32[]{:S(2)}, u32[]{:S(2)}) collective-permute-start(bf16[64,512]{1,0:T(8,128)(2,1)S(1)} %get-tuple-element.34), channel_id=1, source_target_pairs={{0,6},{1,7},{2,4},{3,5},{4,2},{5,3},{6,0},{7,1},{8,14},{9,15},{10,... | collective-permute-start | bytes 196616 | tf_op jit(solution)/shard_map/cond/branch_1_fun/ppermute | solution.py:36
  124.5 2.2 %copy-start.16 = (f32[64,512]{1,0:T(8,128)}, f32[64,512]{1,0:T(8,128)S(1)}, u32[]{:S(2)}) copy-start(f32[64,512]{1,0:T(8,128)S(1)} %get-tuple-element.110) | copy-start | bytes 393220

commit v7 on v6

--- a/solution.py
+++ b/solution.py
@@ -29,6 +29,7 @@
 VM = pl.BlockSpec(memory_space=pltpu.VMEM)
 LANES = 128
 ROWS = 16
+SMALL = pl.CostEstimate(flops=0, bytes_accessed=1 << 20, transcendentals=0)
 
 
 def swap(block, count, bits, targets=None):
@@ -90,6 +91,7 @@
         out_specs=[VM] * (count // 2 + 1),
         scratch_shapes=[pltpu.SemaphoreType.DMA((3 * nh * count,))],
         compiler_params=params(8),
+        cost_estimate=SMALL,
         name="pack",
     )(me, q, k, v, after)
 
@@ -168,6 +170,7 @@
         in_specs=[VM] * parts + [ANY] * len(after),
         out_specs=VM,
         compiler_params=params(4),
+        cost_estimate=SMALL,
         name="forward",
     )(*blocks, *after)
 
@@ -187,8 +190,26 @@
         out_specs=[VM] * parts,
         input_output_aliases={1 + m: m for m in range(parts)},
         compiler_params=params(4),
+        cost_estimate=SMALL,
         name="join",
     )(got, *blocks)
+
+
+def release_kernel(*refs):
+    pass
+
+
+def release(blocks, after):
+    return pl.pallas_call(
+        release_kernel,
+        out_shape=[jax.ShapeDtypeStruct(block.shape, block.dtype) for block in blocks],
+        in_specs=[ANY] * (len(blocks) + len(after)),
+        out_specs=[ANY] * len(blocks),
+        input_output_aliases={n: n for n in range(len(blocks))},
+        compiler_params=params(4),
+        cost_estimate=SMALL,
+        name="release",
+    )(*blocks, *after)
 
 
 def forward_rows_kernel(tok, hd, pieces, *refs):
@@ -198,53 +219,55 @@
             refs[-1][m * tok : (m + 1) * tok, head * hd : (head + 1) * hd] = block
 
 
-def forward_rows(arrays, pieces, tok, hd, after):
+def forward_rows(arrays, pieces, tok, hd):
     return pl.pallas_call(
         functools.partial(forward_rows_kernel, tok, hd, pieces),
         out_shape=jax.ShapeDtypeStruct(
             (len(pieces) * tok, len(pieces[0]) * hd), arrays[0].dtype
         ),
-        in_specs=[VM] * len(arrays) + [ANY],
+        in_specs=[VM] * len(arrays),
         out_specs=VM,
         compiler_params=params(4),
+        cost_estimate=SMALL,
         name="forward_rows",
-    )(*arrays, after)
-
-
-def assemble_kernel(tok, hd, pieces, me_ref, *rest):
-    refs, got, out, sems = rest[:-3], rest[-3], rest[-2], rest[-1]
+    )(*arrays)
+
+
+def assemble_kernel(group, moves, me_ref, *rest):
+    refs, out, sems = rest[:-2], rest[-2], rest[-1]
     me = me_ref[0]
-    heads = len(pieces[0])
-    moves = []
-    for m, row in enumerate(pieces):
-        for head, (n, start, lane) in enumerate(row):
-            column = (me ^ (2 * m)) * heads * hd + head * hd
-            moves.append((refs[n].at[pl.ds(start, tok), pl.ds(lane, hd)], column, hd))
-        column = (me ^ (2 * m + 1)) * heads * hd
-        moves.append((got.at[pl.ds(m * tok, tok), :], column, heads * hd))
-    copies = [
-        pltpu.make_async_copy(
-            source, out.at[:, pl.ds(pl.multiple_of(column, LANES), width)], sems.at[n]
+    copies = []
+    for n, (array, row, size, lane, width, k, start, to) in enumerate(moves):
+        column = pl.multiple_of((me ^ k) * group + start, LANES)
+        copies.append(
+            pltpu.make_async_copy(
+                refs[array].at[pl.ds(row, size), pl.ds(lane, width)],
+                out.at[pl.ds(to, size), pl.ds(column, width)],
+                sems.at[n],
+            )
         )
-        for n, (source, column, width) in enumerate(moves)
-    ]
     for copy in copies:
         copy.start()
     for copy in copies:
         copy.wait()
 
 
-def assemble(me, arrays, pieces, got, tok, hd):
-    half, heads = len(pieces), len(pieces[0])
-    return pl.pallas_call(
-        functools.partial(assemble_kernel, tok, hd, pieces),
-        out_shape=jax.ShapeDtypeStruct((tok, 2 * half * heads * hd), got.dtype),
-        in_specs=[SMEM] + [VM] * (len(arrays) + 1),
+def assemble(me, arrays, moves, group, tok, model, base=None):
+    given = [] if base is None else [base]
+    kernel = functools.partial(assemble_kernel, group, moves)
+    if given:
+        kernel = lambda me_ref, _, *rest: assemble_kernel(group, moves, me_ref, *rest)
+    return pl.pallas_call(
+        kernel,
+        out_shape=jax.ShapeDtypeStruct((tok, model), arrays[0].dtype),
+        in_specs=[SMEM] + [ANY] * len(given) + [VM] * len(arrays),
         out_specs=ANY,
-        scratch_shapes=[pltpu.SemaphoreType.DMA((half * (heads + 1),))],
+        input_output_aliases={1: 0} if given else {},
+        scratch_shapes=[pltpu.SemaphoreType.DMA((len(moves),))],
         compiler_params=params(4),
+        cost_estimate=SMALL,
         name="assemble",
-    )(me, *arrays, got)
+    )(me, *given, *arrays)
 
 
 def soft(scores, scale):
@@ -284,9 +307,8 @@
         hid_ref, gup_in, *rest = rest
     outs, rest = rest[:half], rest[half:]
     if last:
-        hid_keep, hid_send, gup_ref, *rest = rest
-    else:
-        hid_out, gup_ref, *rest = rest
+        send_ref, *rest = rest
+    hid_out, gup_ref, *rest = rest
     note_s, q_s, k_s, vt_s, svt_s, lora_s, grad_s, hid_s, out_s = rest
     head = pl.program_id(0)
     me = me_ref[0]
@@ -364,7 +386,10 @@
     grad = grad_s[...].reshape(count * tok, hd).astype(jnp.bfloat16)
     column = pl.multiple_of(head * hd, LANES)
     for p in range(count):
-        outs[p // 2][p % 2 * tok : (p % 2 + 1) * tok, pl.ds(column, hd)] = out_s[p]
+        to, row = outs[p // 2], p % 2 * tok
+        if last and p % 2:
+            to, row = send_ref, p // 2 * tok
+        to[row : row + tok, pl.ds(column, hd)] = out_s[p]
     column = pl.multiple_of((before + head) * hd, LANES)
     gup_ref[:, pl.ds(column, hd)] = mm(lora_s[...], grad)
     hid_s[...] += mm(up_t, grad, NT)
@@ -373,10 +398,11 @@
     def _():
         if last:
             for m in range(half):
-                to = slice(m * tok, (m + 1) * tok)
-                hid_keep[:, to] = hid_s[:, 2 * m * tok : (2 * m + 1) * tok]
-                odd = hid_s[:, (2 * m + 1) * tok : (2 * m + 2) * tok]
-                hid_send[:, to] = odd.astype(jnp.bfloat16)
+                even = slice(2 * m * tok, (2 * m + 1) * tok)
+                odd = slice((2 * m + 1) * tok, (2 * m + 2) * tok)
+                row = half * tok + m * rank
+                hid_out[:, m * tok : (m + 1) * tok] = hid_s[:, even]
+                send_ref[row : row + rank, :] = hid_s[:, odd].astype(jnp.bfloat16)
         else:
             hid_out[...] = hid_s[...]
 
@@ -387,15 +413,14 @@
     bf, f32 = jnp.bfloat16, jnp.float32
     keys = count * tok
     heads = first + nh
-    shapes = [jax.ShapeDtypeStruct((2 * tok, nh * hd), bf)] * (count // 2)
+    half = count // 2
+    shapes = [jax.ShapeDtypeStruct(((1 if last else 2) * tok, nh * hd), bf)] * half
     if last:
-        shapes += [
-            jax.ShapeDtypeStruct((rank, keys // 2), f32),
-            jax.ShapeDtypeStruct((rank, keys // 2), bf),
-        ]
-    else:
-        shapes += [jax.ShapeDtypeStruct((rank, keys), f32)]
-    shapes += [jax.ShapeDtypeStruct((rank, heads * hd), f32)]
+        shapes.append(jax.ShapeDtypeStruct((half * (tok + rank), nh * hd), bf))
+    shapes += [
+        jax.ShapeDtypeStruct((rank, keys // 2 if last else keys), f32),
+        jax.ShapeDtypeStruct((rank, heads * hd), f32),
+    ]
     return pl.pallas_call(
         functools.partial(
             attention_kernel,
@@ -441,42 +466,82 @@
     )
 
 
-def pair_kernel(parts, counts, keep_ref, got_ref, *rest):
+def pair_kernel(parts, keep_ref, got_ref, *rest):
     riders, outs = rest[:-parts], rest[-parts:]
     rank, width = keep_ref.shape[0], keep_ref.shape[1] // parts
     for m in range(parts):
         cols = slice(m * width, (m + 1) * width)
         total = keep_ref[:, cols] + got_ref[:, cols].astype(jnp.float32)
         outs[m][:rank, :] = total.astype(outs[m].dtype)
-        row = rank
-        for rider in riders[sum(counts[:m]) : sum(counts[: m + 1])]:
-            size = rider.shape[0]
-            for lane in range(0, rider.shape[1], width):
-                outs[m][row : row + size, :] = rider[:, lane : lane + width]
-                row += size
+        if m:
+            rider = riders[m - 1]
+            lanes = rider.shape[1]
+            size = outs[m].shape[0] - rank
+            for n in range(width // lanes):
+                block = rider[n * size : (n + 1) * size, :]
+                outs[m][rank:, n * lanes : (n + 1) * lanes] = block
 
 
 def pair_sum(keep, got, parts, riders):
     rank, width = keep.shape[0], keep.shape[1] // parts
-    extra = [sum(rider.size for rider in group) // width for group in riders]
-    shapes = [
-        jax.ShapeDtypeStruct((rank + more, width), jnp.bfloat16 if m else jnp.float32)
-        for m, more in enumerate(extra)
+    shapes = [jax.ShapeDtypeStruct((rank, width), jnp.float32)] + [
+        jax.ShapeDtypeStruct((rank + rider.size // width, width), rider.dtype)
+        for rider in riders
     ]
-    counts = [len(group) for group in riders]
-    return pl.pallas_call(
-        functools.partial(pair_kernel, parts, counts),
+    return pl.pallas_call(
+        functools.partial(pair_kernel, parts),
         out_shape=shapes,
-        in_specs=[VM] * (2 + sum(counts)),
+        in_specs=[VM] * (2 + len(riders)),
         out_specs=[VM] * parts,
         compiler_params=params(4),
+        cost_estimate=SMALL,
         name="pair_sum",
-    )(keep, got, *[rider for group in riders for rider in group])
-
-
-def chip_terms(keep, send, count, riders=None):
-    half = count // 2
-    return chips(pair_sum(keep, swap(send, count, 1), half, riders or [[]] * half), count)
+    )(keep, got, *riders)
+
+
+def riding_kernel(parts, keep_ref, got_ref, *rest):
+    blocks, rest = rest[:parts], rest[parts:]
+    riders, (total_ref, *outs) = rest[: -2 * parts], rest[-2 * parts :]
+    joined, sends = outs[:parts], outs[parts:]
+    rank, tok = total_ref.shape
+    for m in range(parts):
+        row = parts * tok + m * rank
+        total = keep_ref[:, m * tok : (m + 1) * tok]
+        total += got_ref[row : row + rank, :].astype(jnp.float32)
+        if m:
+            sends[m - 1][:rank, :] = total.astype(jnp.bfloat16)
+        else:
+            total_ref[...] = total
+        joined[m][:tok, :] = blocks[m][...]
+        joined[m][tok:, :] = got_ref[m * tok : (m + 1) * tok, :]
+    row = rank
+    for rider in riders:
+        for lane in range(0, rider.shape[1], tok):
+            sends[0][row : row + 2 * tok, :] = rider[:, lane : lane + tok]
+            row += 2 * tok
+
+
+def riding_sum(keep, got, blocks, riders):
+    parts = len(blocks)
+    (tok, hd), rank, bf = blocks[0].shape, keep.shape[0], blocks[0].dtype
+    extra = sum(rider.size for rider in riders) // tok
+    shapes = (
+        [jax.ShapeDtypeStruct((rank, tok), jnp.float32)]
+        + [jax.ShapeDtypeStruct((2 * tok, hd), bf)] * parts
+        + [
+            jax.ShapeDtypeStruct((rank + (extra if m == 1 else 0), tok), bf)
+            for m in range(1, parts)
+        ]
+    )
+    return pl.pallas_call(
+        functools.partial(riding_kernel, parts),
+        out_shape=shapes,
+        in_specs=[VM] * (2 + parts + len(riders)),
+        out_specs=[VM] * len(shapes),
+        compiler_params=params(4),
+        cost_estimate=SMALL,
+        name="riding_sum",
+    )(keep, got, *blocks, *riders)
 
 
 def down_kernel(count, group, me_ref, *rest):
@@ -507,26 +572,28 @@
         in_specs=[SMEM] + [VM] * (len(parts) + 1),
         out_specs=[VM, VM],
         compiler_params=params(8),
+        cost_estimate=SMALL,
         name="down_terms",
     )(me, *parts, x)
 
 
 def sum_kernel(*refs):
     total = refs[0][...]
-    for ref in refs[1:-1]:
-        total += ref[...].astype(jnp.float32)
+    for ref in refs[1:-2]:
+        total += ref[: total.shape[0], :].astype(jnp.float32)
     refs[-1][...] = total
 
 
-def sum_terms(parts):
+def sum_terms(parts, after):
     return pl.pallas_call(
         sum_kernel,
         out_shape=jax.ShapeDtypeStruct(parts[0].shape, jnp.float32),
-        in_specs=[VM] * len(parts),
+        in_specs=[VM] * len(parts) + [ANY],
         out_specs=VM,
-        compiler_params=params(8),
+        compiler_params=params(4),
+        cost_estimate=SMALL,
         name="sum_terms",
-    )(*parts)
+    )(*parts, after)
 
 
 def apart(always, phase, *operands):
@@ -579,44 +646,59 @@
 
     own_up = lax.dynamic_slice_in_dim(up_t, index * group, group, 1)
     half = count // 2
-    given, arrays = [], []
-    riders = [[] for _ in range(half)]
+    given, arrays, riders = [], [], []
     pieces = [[] for _ in range(half)]
-    rows = [rank] * half
     for c, (first, nh) in enumerate(chunks):
         last = c == len(chunks) - 1
         out = attention(
             me, messages[c], noted, own_up, given, first, nh, tok, hd, slots, mask_rows, last
         )
-        given = out[half:]
-        for m in range(half):
-            if m and (last or m == 1):
-                riders[m].append(out[m])
-                for _ in range(nh):
-                    pieces[m].append((m - half, rows[m], 0))
-                    rows[m] += 2 * tok
-            else:
-                pieces[m] += [(len(arrays), 0, h * hd) for h in range(nh)]
-                arrays.append(swap(out[m], count, 2 * m) if m else out[0])
-    hid_keep, hid_send, grad_up = given
-
-    def hidden_phase(hid_keep, hid_send, riders):
-        return chip_terms(hid_keep, hid_send, count, riders)
-
-    def grad_phase(keep, send, _):
-        return sum_terms(chip_terms(keep, send, count))
-
-    hidden = apart(index < count, hidden_phase, hid_keep, hid_send, riders)
+        blocks, given = list(out[:half]), out[-2:]
+        if last:
+            break
+        riders.append(blocks[1])
+        blocks[2:] = release(blocks[2:], messages[c + 1][1:])
+        for m in [0] + list(range(2, half)):
+            pieces[m] += [(len(arrays), 0, h * hd) for h in range(nh)]
+            arrays.append(swap(blocks[m], count, 2 * m) if m else blocks[0])
+        pieces[1] += [(-1, rank + 2 * tok * (first + h), 0) for h in range(nh)]
+    pieces = [
+        [(n if n >= 0 else len(arrays), row, lane) for n, row, lane in group] for group in pieces
+    ]
+    send, (hid, grad_up) = out[half], given
+
+    def hidden_phase(hid, send, blocks, riders):
+        total, *rest = riding_sum(hid, swap(send, count, 1), blocks, riders)
+        return chips([total] + rest[half:], count), rest[:half]
+
+    hidden, joined = apart(index < count, hidden_phase, hid, send, blocks, riders)
     keep, send = down_terms(me, hidden, value_layer_input)
-    pieces = [
-        [(n if n >= 0 else len(arrays) + n + half - 1, row, lane) for n, row, lane in group]
-        for group in pieces
-    ]
-    arrays += hidden[1:]
-    passed = forward_rows(arrays, pieces, tok, hd, keep)
-    got = swap(passed, count, 1)
-    grad_down = apart(index < count, grad_phase, keep, send, passed)
-    student_out = assemble(me, arrays, pieces, got, tok, hd)
+    before = first * hd
+
+    def grad_phase(keep, send, arrays, joined):
+        base = None
+        if before:
+            got = swap(forward_rows(arrays, pieces, tok, hd), count, 1)
+            moves = [(len(arrays), m * tok, tok, 0, before, 2 * m + 1, 0, 0) for m in range(half)]
+            for m, group_pieces in enumerate(pieces):
+                for h, (n, row, lane) in enumerate(group_pieces):
+                    moves.append((n, row, tok, lane, hd, 2 * m, h * hd, 0))
+            base = assemble(me, [*arrays, got], moves, group, tok, model)
+        totals = pair_sum(keep, swap(send, count, 1), half, joined[1:])
+        terms = chips(totals, count)
+        moves = [(0, r * tok, tok, 0, nh * hd, r, before, 0) for r in range(2)]
+        size = 2 * tok * nh * hd // group
+        for m in range(1, half):
+            step = min(size, tok)
+            for row in range(0, 2 * tok, step):
+                (r, to), (n, at) = divmod(row, tok), divmod(row, size)
+                moves.append((m, rank + at, step, n * nh * hd, nh * hd, 2 * m + r, before, to))
+        student_out = assemble(me, [joined[0], *terms[1:]], moves, group, tok, model, base)
+        return sum_terms(terms, keep if base is None else base), student_out
+
+    grad_down, student_out = apart(
+        index < count, grad_phase, keep, send, [*arrays, hidden[1]], joined
+    )
     return student_out, grad_down.T, grad_up.T
 
 

time: 127 us -> 126 us (level)
  waiting for transfers between devices: 69.4 us -> 52.1 us
  starting transfers between devices: 22.5 us -> 37.8 us
    ppermute x19, waiting for transfers between devices: 69.4 us -> 52.1 us  [swap(): return lax.ppermute(block, 'context', pairs)]
    ppermute x19, starting transfers between devices: 22.5 us -> 37.8 us  [swap(): return lax.ppermute(block, 'context', pairs)]
    pallas_call x3 -> x5, Pallas kernels: 2.3 us -> 3.53 us  [the longest x2 2.75 us: assemble(): pl.pallas_call(kernel, out_shape=jax.ShapeDtypeStruct((tok, model), array...]
    unnamed x34 -> x32, local copies, waits for them, and re-layouts: 5.23 us -> 5.84 us
  transfers between devices with their start and end apart: 19 -> 19, of which waited for: 8 -> 8; matrix products, arithmetic and copies ran while one was open for 0% -> 0% of each run, Pallas kernels for 15% -> 18%
where the time goes in v7:
time: 126 us
  waiting for transfers between devices  52.1 us (41%)
  starting transfers between devices  37.8 us (30%)
  Pallas kernels  28.9 us (23%)
  local copies, waits for them, and re-layouts  5.85 us (5%)
    ppermute x19, waiting for transfers between devices, swap(): return lax.ppermute(block, 'context', pairs)  52.1 us
    ppermute x19, starting transfers between devices, swap(): return lax.ppermute(block, 'context', pairs)  37.8 us
    pallas_call x2, Pallas kernels, attention(): pl.pallas_call(functools.partial(attention_kernel, count, tok, hd, nh, sl...  16.7 us
    unnamed x32, local copies, waits for them, and re-layouts  5.84 us
    pallas_call x1, Pallas kernels, first_pack(): pl.pallas_call(functools.partial(first_kernel, count, model // count, hd,...  5.76 us
    pallas_call x2, Pallas kernels, assemble(): pl.pallas_call(kernel, out_shape=jax.ShapeDtypeStruct((tok, model), array...  2.75 us
  transfers between devices with their start and end apart: 19, of which 8 were waited for; matrix products, arithmetic and copies ran while one was open for 0% of the time, Pallas kernels for 18%

profile of v7, /device:TPU:0, one launch (start us, length us, event | category | flops | bytes accessed | tf_op | source)
XLA Modules:
  0.0 125.6 jit_solution(14752174183047883210)
XLA Ops:
  0.6 0.0 copy-start
  0.7 5.8 %first_pack.1 = (bf16[2384,128]{1,0:T(8,128)(2,1)}, bf16[2384,128]{1,0:T(8,128)(2,1)}, bf16[2384,128]{1,0:T(8,128)(2,1)}, bf16[2384,128]{1,0:T(8,128)(2,1)}) custom-call(s32[1]{0:T(128)} %bitcast.me_ref, s32[2,4]{1,0:T(2,128)} %nb_ref.1, bf16[128,4096]{1,0:T(8,128)(2,1)} %q_ref.1, bf16[128,4096]{1,0:T(8,128)(2,1)} %k_ref.1, bf16[128,4096]{1,0:T(8,128)(2,1)} %v_ref.1, ...), custom_call_target="tpu_custom_call" | custom-call | tf_op jit(solution)/shard_map/first_pack/pallas_call | solution.py:139
  6.4 4.1 %collective-permute-start.10 = (bf16[2384,128]{1,0:T(8,128)(2,1)}, bf16[2384,128]{1,0:T(8,128)(2,1)S(1)}, u32[]{:S(2)}, u32[]{:S(2)}) collective-permute-start(bf16[2384,128]{1,0:T(8,128)(2,1)} %get-tuple-element.111), channel_id=1, source_target_pairs={{0,4},{1,5},{2,6},{3,7},{4,0},{5,1},{6,2},{7,3},{8,12},{9,13},{10,... | collective-permute-start | bytes 1830920 | tf_op jit(solution)/shard_map/ppermute | solution.py:37
  10.5 1.3 %collective-permute-start.11 = (bf16[2384,128]{1,0:T(8,128)(2,1)}, bf16[2384,128]{1,0:T(8,128)(2,1)S(1)}, u32[]{:S(2)}, u32[]{:S(2)}) collective-permute-start(bf16[2384,128]{1,0:T(8,128)(2,1)} %get-tuple-element.112), channel_id=1, source_target_pairs={{0,6},{1,7},{2,4},{3,5},{4,2},{5,3},{6,0},{7,1},{8,14},{9,15},{10,... | collective-permute-start | bytes 1830920 | tf_op jit(solution)/shard_map/ppermute | solution.py:37
  11.9 0.2 collective-permute-start.9
  12.1 1.2 copy-done.3
  13.4 1.1 copy-done.5
  14.4 0.5 pack.1
  14.9 0.1 collective-permute-start.12
  15.0 1.7 %collective-permute-done.12.got_ref = bf16[1536,128]{1,0:T(8,128)(2,1)S(1)} collective-permute-done((bf16[1536,128]{1,0:T(8,128)(2,1)S(1)}, bf16[1536,128]{1,0:T(8,128)(2,1)S(1)}, u32[]{:S(2)}, u32[]{:S(2)}) %collective-permute-start.12) | collective-permute-done | bytes 393248 | tf_op jit(solution)/shard_map/ppermute | solution.py:37
  16.8 34.8 %collective-permute-done.10.refs_2_.rest_2_ = bf16[2384,128]{1,0:T(8,128)(2,1)S(1)} collective-permute-done((bf16[2384,128]{1,0:T(8,128)(2,1)}, bf16[2384,128]{1,0:T(8,128)(2,1)S(1)}, u32[]{:S(2)}, u32[]{:S(2)}) %collective-permute-start.10) | collective-permute-done | bytes 610336 | tf_op jit(solution)/shard_map/ppermute | solution.py:37
  51.6 0.5 collective-permute-done.9.refs_1_.rest_1_
  52.1 0.1 forward.1
  52.2 0.2 copy-done.7
  52.4 0.5 copy-done.9
  52.9 0.0 collective-permute-start.13
  52.9 12.9 %collective-permute-start.14 = (bf16[768,128]{1,0:T(8,128)(2,1)}, bf16[768,128]{1,0:T(8,128)(2,1)S(1)}, u32[]{:S(2)}, u32[]{:S(2)}) collective-permute-start(bf16[768,128]{1,0:T(8,128)(2,1)} %copy-done.11), channel_id=1, source_target_pairs={{0,2},{1,3},{2,0},{3,1},{4,6},{5,7},{6,4},{7,5},{8,10},{9,11},{10,... | collective-permute-start | bytes 589832 | tf_op jit(solution)/shard_map/ppermute | solution.py:37
  65.8 1.9 %collective-permute-start.15 = (bf16[768,128]{1,0:T(8,128)(2,1)}, bf16[768,128]{1,0:T(8,128)(2,1)S(1)}, u32[]{:S(2)}, u32[]{:S(2)}) collective-permute-start(bf16[768,128]{1,0:T(8,128)(2,1)} %copy-done.12), channel_id=1, source_target_pairs={{0,4},{1,5},{2,6},{3,7},{4,0},{5,1},{6,2},{7,3},{8,12},{9,13},{10,... | collective-permute-start | bytes 589832 | tf_op jit(solution)/shard_map/ppermute | solution.py:37
  67.7 1.4 %collective-permute-start.16 = (bf16[768,128]{1,0:T(8,128)(2,1)}, bf16[768,128]{1,0:T(8,128)(2,1)S(1)}, u32[]{:S(2)}, u32[]{:S(2)}) collective-permute-start(bf16[768,128]{1,0:T(8,128)(2,1)} %copy-done.13), channel_id=1, source_target_pairs={{0,6},{1,7},{2,4},{3,5},{4,2},{5,3},{6,0},{7,1},{8,14},{9,15},{10,... | collective-permute-start | bytes 589832 | tf_op jit(solution)/shard_map/ppermute | solution.py:37
  69.1 1.1 copy-done.8
  70.1 1.1 copy-done.10
  71.2 11.5 %attention.2 = (bf16[256,384]{1,0:T(8,128)(2,1)S(1)}, bf16[256,384]{1,0:T(8,128)(2,1)S(1)}, bf16[256,384]{1,0:T(8,128)(2,1)S(1)}, bf16[256,384]{1,0:T(8,128)(2,1...) custom-call(s32[1]{0:T(128)} %bitcast.me_ref, bf16[2384,128]{1,0:T(8,128)(2,1)S(1)} %copy-done.6, ...), custom_call_target="tpu_custom_call" | custom-call | flops 12000000000 | bytes 3145728 | tf_op jit(solution)/shard_map/attention/pallas_call | solution.py:424
  82.7 0.4 collective-permute-done.15.rest_7_.refs_3_
  83.1 5.9 %collective-permute-start.17 = (bf16[256,384]{1,0:T(8,128)(2,1)S(1)}, bf16[256,384]{1,0:T(8,128)(2,1)S(1)}, u32[]{:S(2)}, u32[]{:S(2)}) collective-permute-start(bf16[256,384]{1,0:T(8,128)(2,1)S(1)} %get-tuple-element.143), channel_id=1, source_target_pairs={{0,4},{1,5},{2,6},{3,7},{4,0},{5,1},{6,2},{7,3},{8,12},{9,13},{10,... | collective-permute-start | bytes 589832 | tf_op jit(solution)/shard_map/ppermute | solution.py:37
  89.0 0.5 collective-permute-start.18
  89.6 5.2 %attention.3 = (bf16[128,128]{1,0:T(8,128)(2,1)S(1)}, bf16[128,128]{1,0:T(8,128)(2,1)S(1)}, bf16[128,128]{1,0:T(8,128)(2,1)S(1)}, bf16[128,128]{1,0:T(8,128)(2,1...) custom-call(s32[1]{0:T(128)} %bitcast.me_ref, bf16[2384,128]{1,0:T(8,128)(2,1)S(1)} %copy-done.6, ...), custom_call_target="tpu_custom_call" | custom-call | flops 4000000000 | bytes 1048576 | tf_op jit(solution)/shard_map/attention/pallas_call | solution.py:424
  94.8 12.6 %conditional.2 = (f32[64,128]{1,0:T(8,128)S(1)}, bf16[832,128]{1,0:T(8,128)(2,1)}, bf16[64,128]{1,0:T(8,128)(2,1)}, bf16[64,128]{1,0:T(8,128)(2,1)}, bf16[256,12...) conditional(s32[]{:T(128)} %convert_element_type.4, () %tuple.25, ...), branch_computations={%region_0.0_spmd, %region_1.0_spmd} | conditional | bytes 2818272 | solution.py:604
  94.8 1.4 %collective-permute-done.got_ref = bf16[768,128]{1,0:T(8,128)(2,1)S(1)} collective-permute-done((bf16[768,128]{1,0:T(8,128)(2,1)S(1)}, bf16[768,128]{1,0:T(8,128)(2,1)S(1)}, u32[]{:S(2)}, u32[]{:S(2)}) %collective-permute-start) | collective-permute-done | bytes 196640 | tf_op jit(solution)/shard_map/cond/branch_1_fun/ppermute | solution.py:37
  96.2 0.7 riding_sum.1
  96.9 0.0 collective-permute-start.1
  97.0 3.8 %collective-permute-start.2 = (bf16[64,128]{1,0:T(8,128)(2,1)S(1)}, bf16[64,128]{1,0:T(8,128)(2,1)}, u32[]{:S(2)}, u32[]{:S(2)}) collective-permute-start(bf16[64,128]{1,0:T(8,128)(2,1)S(1)} %get-tuple-element.45), channel_id=1, source_target_pairs={{0,4},{1,5},{2,6},{3,7},{4,0},{5,1},{6,2},{7,3},{8,12},{9,13},{10,... | collective-permute-start | bytes 49160 | tf_op jit(solution)/shard_map/cond/branch_1_fun/ppermute | solution.py:37
  100.8 0.6 collective-permute-start.3
  101.3 6.1 %collective-permute-done.2 = bf16[64,128]{1,0:T(8,128)(2,1)} collective-permute-done((bf16[64,128]{1,0:T(8,128)(2,1)S(1)}, bf16[64,128]{1,0:T(8,128)(2,1)}, u32[]{:S(2)}, u32[]{:S(2)}) %collective-permute-start.2) | collective-permute-done | bytes 16416 | tf_op jit(solution)/shard_map/cond/branch_1_fun/ppermute | solution.py:37
  107.5 1.3 %down_terms.1 = (f32[64,2048]{1,0:T(8,128)S(1)}, bf16[64,2048]{1,0:T(8,128)(2,1)S(1)}) custom-call(s32[1]{0:T(128)} %bitcast.me_ref, f32[64,128]{1,0:T(8,128)S(1)} %get-tuple-element.131.rest_0_, bf16[832,128]{1,0:T(8,128)(2,1)} %get-tuple-element.132.rest_1_, bf16[64,128]{1,0:T(8,128)(2,1)} %get-tuple-element.133.rest_2_, ...), custom_call_target="tpu_custom_call" | custom-call | bytes 1048576 | tf_op jit(solution)/shard_map/down_terms/pallas_call | solution.py:566
  108.8 16.1 %conditional.3 = (f32[64,512]{1,0:T(8,128)S(1)}, bf16[128,4096]{1,0:T(8,128)(2,1)}) conditional(s32[]{:T(128)} %convert_element_type.4, () %tuple.24, (bf16[64,2048]{1,0:T(8,128)(2,1)S(1)}, f32[64,2048]{1,0:T(8,128)S(1)}, bf16[256,128]{1,0:T(8,128)(2,1)S(1)}, bf16[256,128]{1,0:T(8,128)(2,1)S(1)}, bf16[256,128]{1,0:T(8,128)(2,1)S(1)}, ...), branch_computations={%region_2.0_spmd, %region_3.0_spmd} | conditional | bytes 9437400 | solution.py:604
  108.8 0.1 collective-permute-start.4
  108.9 1.0 forward_rows.1
  109.9 0.6 collective-permute-start.8
  110.4 0.1 pair_sum.1
  110.5 0.8 collective-permute-start.5
  111.3 1.1 collective-permute-start.6
  112.4 2.5 %collective-permute-start.7 = (bf16[128,512]{1,0:T(8,128)(2,1)S(1)}, bf16[128,512]{1,0:T(8,128)(2,1)S(1)}, u32[]{:S(2)}, u32[]{:S(2)}) collective-permute-start(bf16[128,512]{1,0:T(8,128)(2,1)S(1)} %get-tuple-element.59), channel_id=1, source_target_pairs={{0,6},{1,7},{2,4},{3,5},{4,2},{5,3},{6,0},{7,1},{8,14},{9,15},{10,... | collective-permute-start | bytes 393224 | tf_op jit(solution)/shard_map/cond/branch_1_fun/ppermute | solution.py:37
  115.0 1.9 %assemble.2.refs_4_._ = bf16[128,4096]{1,0:T(8,128)(2,1)} custom-call(s32[1]{0:T(128)} %get-tuple-element.60.me_ref, bf16[256,384]{1,0:T(8,128)(2,1)S(1)} %get-tuple-element.61.refs_0_.rest_0_, bf16[256,384]{1,0:T(8,128)(2,1)S(1)} %get-tuple-element.62.refs_1_.rest_1_, bf16[256,384]{1,0:T(8,128)(2,1)S(1)} %get-tuple-element.63.refs_2_.rest_2_, ...), custom_call_target="tpu_custom_call" | custom-call | bytes 1048576 | tf_op jit(solution)/shard_map/cond/branch_1_fun/assemble/pallas_call | solution.py:260
  116.9 0.3 collective-permute-done.5.refs_1_.rest_1_
  117.2 6.9 %collective-permute-done.6.refs_2_.rest_2_ = bf16[128,512]{1,0:T(8,128)(2,1)S(1)} collective-permute-done((bf16[128,512]{1,0:T(8,128)(2,1)S(1)}, bf16[128,512]{1,0:T(8,128)(2,1)S(1)}, u32[]{:S(2)}, u32[]{:S(2)}) %collective-permute-start.6) | collective-permute-done | bytes 131104 | tf_op jit(solution)/shard_map/cond/branch_1_fun/ppermute | solution.py:37
  124.1 0.8 assemble.3
  124.9 0.0 copy-start.15
  124.9 0.6 copy-done.15
  (39 shorter events, 0.1 us)
Async XLA Ops:
  0.6 52.3 %copy-start = (bf16[4096,64]{0,1:T(8,128)(2,1)S(1)}, bf16[4096,64]{0,1:T(8,128)(2,1)}, u32[]{:S(2)}) copy-start(bf16[4096,64]{0,1:T(8,128)(2,1)} %param.16) | copy-start | bytes 1572868
  0.7 11.5 %copy-start.1 = (bf16[128,4096]{1,0:T(8,128)(2,1)S(1)}, bf16[128,4096]{1,0:T(8,128)(2,1)}, u32[]{:S(2)}) copy-start(bf16[128,4096]{1,0:T(8,128)(2,1)} %q_ref.1) | copy-start | bytes 3145732
  0.7 11.5 %copy-start.2 = (bf16[128,4096]{1,0:T(8,128)(2,1)S(1)}, bf16[128,4096]{1,0:T(8,128)(2,1)}, u32[]{:S(2)}) copy-start(bf16[128,4096]{1,0:T(8,128)(2,1)} %k_ref.1) | copy-start | bytes 3145732
  6.4 45.1 %collective-permute-start.10 = (bf16[2384,128]{1,0:T(8,128)(2,1)}, bf16[2384,128]{1,0:T(8,128)(2,1)S(1)}, u32[]{:S(2)}, u32[]{:S(2)}) collective-permute-start(bf16[2384,128]{1,0:T(8,128)(2,1)} %get-tuple-element.111), channel_id=1, source_target_pairs={{0,4},{1,5},{2,6},{3,7},{4,0},{5,1},{6,2},{7,3},{8,12},{9,13},{10,... | collective-permute-start | bytes 1830920 | tf_op jit(solution)/shard_map/ppermute | solution.py:37
  10.5 41.0 %collective-permute-start.11 = (bf16[2384,128]{1,0:T(8,128)(2,1)}, bf16[2384,128]{1,0:T(8,128)(2,1)S(1)}, u32[]{:S(2)}, u32[]{:S(2)}) collective-permute-start(bf16[2384,128]{1,0:T(8,128)(2,1)} %get-tuple-element.112), channel_id=1, source_target_pairs={{0,6},{1,7},{2,4},{3,5},{4,2},{5,3},{6,0},{7,1},{8,14},{9,15},{10,... | collective-permute-start | bytes 1830920 | tf_op jit(solution)/shard_map/ppermute | solution.py:37
  11.9 40.2 %collective-permute-start.9 = (bf16[2384,128]{1,0:T(8,128)(2,1)}, bf16[2384,128]{1,0:T(8,128)(2,1)S(1)}, u32[]{:S(2)}, u32[]{:S(2)}) collective-permute-start(bf16[2384,128]{1,0:T(8,128)(2,1)} %get-tuple-element.110), channel_id=1, source_target_pairs={{0,2},{1,3},{2,0},{3,1},{4,6},{5,7},{6,4},{7,5},{8,10},{9,11},{10,... | collective-permute-start | bytes 1830920 | tf_op jit(solution)/shard_map/ppermute | solution.py:37
  12.1 1.2 copy-start.3
  13.4 1.1 copy-start.5
  14.9 1.8 %collective-permute-start.12 = (bf16[1536,128]{1,0:T(8,128)(2,1)S(1)}, bf16[1536,128]{1,0:T(8,128)(2,1)S(1)}, u32[]{:S(2)}, u32[]{:S(2)}) collective-permute-start(bf16[1536,128]{1,0:T(8,128)(2,1)S(1)} %get-tuple-element.113), channel_id=1, source_target_pairs={{0,1},{1,0},{2,3},{3,2},{4,5},{5,4},{6,7},{7,6},{8,9},{9,8},{10,11... | collective-permute-start | bytes 1179656 | tf_op jit(solution)/shard_map/ppermute | solution.py:37
  16.7 35.4 %copy-start.11 = (bf16[768,128]{1,0:T(8,128)(2,1)}, bf16[768,128]{1,0:T(8,128)(2,1)S(1)}, u32[]{:S(2)}) copy-start(bf16[768,128]{1,0:T(8,128)(2,1)S(1)} %get-tuple-element.119) | copy-start | bytes 589828
  16.7 35.4 %copy-start.12 = (bf16[768,128]{1,0:T(8,128)(2,1)}, bf16[768,128]{1,0:T(8,128)(2,1)S(1)}, u32[]{:S(2)}) copy-start(bf16[768,128]{1,0:T(8,128)(2,1)S(1)} %get-tuple-element.120) | copy-start | bytes 589828
  16.8 35.4 %copy-start.13 = (bf16[768,128]{1,0:T(8,128)(2,1)}, bf16[768,128]{1,0:T(8,128)(2,1)S(1)}, u32[]{:S(2)}) copy-start(bf16[768,128]{1,0:T(8,128)(2,1)S(1)} %get-tuple-element.121) | copy-start | bytes 589828
  51.6 0.8 copy-start.7
  52.1 0.8 copy-start.9
  52.1 17.0 %copy-start.6 = (bf16[2384,128]{1,0:T(8,128)(2,1)S(1)}, bf16[2384,128]{1,0:T(8,128)(2,1)}, u32[]{:S(2)}) copy-start(bf16[2384,128]{1,0:T(8,128)(2,1)} %get-tuple-element.109._.refs_0_.rest_0_) | copy-start | bytes 1830916
  52.9 16.2 %collective-permute-start.13 = (bf16[4928,128]{1,0:T(8,128)(2,1)S(1)}, bf16[4928,128]{1,0:T(8,128)(2,1)}, u32[]{:S(2)}, u32[]{:S(2)}) collective-permute-start(bf16[4928,128]{1,0:T(8,128)(2,1)S(1)} %forward.1), channel_id=1, source_target_pairs={{0,1},{1,0},{2,3},{3,2},{4,5},{5,4},{6,7},{7,6},{8,9},{9,8},{10,11... | collective-permute-start | bytes 3784712 | tf_op jit(solution)/shard_map/ppermute | solution.py:37
  52.9 29.8 %collective-permute-start.14 = (bf16[768,128]{1,0:T(8,128)(2,1)}, bf16[768,128]{1,0:T(8,128)(2,1)S(1)}, u32[]{:S(2)}, u32[]{:S(2)}) collective-permute-start(bf16[768,128]{1,0:T(8,128)(2,1)} %copy-done.11), channel_id=1, source_target_pairs={{0,2},{1,3},{2,0},{3,1},{4,6},{5,7},{6,4},{7,5},{8,10},{9,11},{10,... | collective-permute-start | bytes 589832 | tf_op jit(solution)/shard_map/ppermute | solution.py:37
  65.8 17.3 %collective-permute-start.15 = (bf16[768,128]{1,0:T(8,128)(2,1)}, bf16[768,128]{1,0:T(8,128)(2,1)S(1)}, u32[]{:S(2)}, u32[]{:S(2)}) collective-permute-start(bf16[768,128]{1,0:T(8,128)(2,1)} %copy-done.12), channel_id=1, source_target_pairs={{0,4},{1,5},{2,6},{3,7},{4,0},{5,1},{6,2},{7,3},{8,12},{9,13},{10,... | collective-permute-start | bytes 589832 | tf_op jit(solution)/shard_map/ppermute | solution.py:37
  67.7 15.4 %collective-permute-start.16 = (bf16[768,128]{1,0:T(8,128)(2,1)}, bf16[768,128]{1,0:T(8,128)(2,1)S(1)}, u32[]{:S(2)}, u32[]{:S(2)}) collective-permute-start(bf16[768,128]{1,0:T(8,128)(2,1)} %copy-done.13), channel_id=1, source_target_pairs={{0,6},{1,7},{2,4},{3,5},{4,2},{5,3},{6,0},{7,1},{8,14},{9,15},{10,... | collective-permute-start | bytes 589832 | tf_op jit(solution)/shard_map/ppermute | solution.py:37
  69.1 1.1 copy-start.8
  70.1 1.1 copy-start.10
  83.1 25.7 %collective-permute-start.17 = (bf16[256,384]{1,0:T(8,128)(2,1)S(1)}, bf16[256,384]{1,0:T(8,128)(2,1)S(1)}, u32[]{:S(2)}, u32[]{:S(2)}) collective-permute-start(bf16[256,384]{1,0:T(8,128)(2,1)S(1)} %get-tuple-element.143), channel_id=1, source_target_pairs={{0,4},{1,5},{2,6},{3,7},{4,0},{5,1},{6,2},{7,3},{8,12},{9,13},{10,... | collective-permute-start | bytes 589832 | tf_op jit(solution)/shard_map/ppermute | solution.py:37
  89.0 19.8 %collective-permute-start.18 = (bf16[256,384]{1,0:T(8,128)(2,1)S(1)}, bf16[256,384]{1,0:T(8,128)(2,1)S(1)}, u32[]{:S(2)}, u32[]{:S(2)}) collective-permute-start(bf16[256,384]{1,0:T(8,128)(2,1)S(1)} %get-tuple-element.144), channel_id=1, source_target_pairs={{0,6},{1,7},{2,4},{3,5},{4,2},{5,3},{6,0},{7,1},{8,14},{9,15},{10,... | collective-permute-start | bytes 589832 | tf_op jit(solution)/shard_map/ppermute | solution.py:37
  94.8 12.7 %copy-start.4 = (bf16[128,4096]{1,0:T(8,128)(2,1)S(1)}, bf16[128,4096]{1,0:T(8,128)(2,1)}, u32[]{:S(2)}) copy-start(bf16[128,4096]{1,0:T(8,128)(2,1)} %rest_4_.1) | copy-start | bytes 3145732
  94.8 1.4 %collective-permute-start = (bf16[768,128]{1,0:T(8,128)(2,1)S(1)}, bf16[768,128]{1,0:T(8,128)(2,1)S(1)}, u32[]{:S(2)}, u32[]{:S(2)}) collective-permute-start(bf16[768,128]{1,0:T(8,128)(2,1)S(1)} %get-tuple-element.37), channel_id=1, source_target_pairs={{0,1},{1,0},{2,3},{3,2},{4,5},{5,4},{6,7},{7,6},{8,9},{9,8},{10,11... | collective-permute-start | bytes 589832 | tf_op jit(solution)/shard_map/cond/branch_1_fun/ppermute | solution.py:37
  96.9 10.5 %collective-permute-start.1 = (bf16[832,128]{1,0:T(8,128)(2,1)S(1)}, bf16[832,128]{1,0:T(8,128)(2,1)}, u32[]{:S(2)}, u32[]{:S(2)}) collective-permute-start(bf16[832,128]{1,0:T(8,128)(2,1)S(1)} %get-tuple-element.44), channel_id=1, source_target_pairs={{0,2},{1,3},{2,0},{3,1},{4,6},{5,7},{6,4},{7,5},{8,10},{9,11},{10,... | collective-permute-start | bytes 638984 | tf_op jit(solution)/shard_map/cond/branch_1_fun/ppermute | solution.py:37
  97.0 10.5 %collective-permute-start.2 = (bf16[64,128]{1,0:T(8,128)(2,1)S(1)}, bf16[64,128]{1,0:T(8,128)(2,1)}, u32[]{:S(2)}, u32[]{:S(2)}) collective-permute-start(bf16[64,128]{1,0:T(8,128)(2,1)S(1)} %get-tuple-element.45), channel_id=1, source_target_pairs={{0,4},{1,5},{2,6},{3,7},{4,0},{5,1},{6,2},{7,3},{8,12},{9,13},{10,... | collective-permute-start | bytes 49160 | tf_op jit(solution)/shard_map/cond/branch_1_fun/ppermute | solution.py:37
  100.8 6.7 %collective-permute-start.3 = (bf16[64,128]{1,0:T(8,128)(2,1)S(1)}, bf16[64,128]{1,0:T(8,128)(2,1)}, u32[]{:S(2)}, u32[]{:S(2)}) collective-permute-start(bf16[64,128]{1,0:T(8,128)(2,1)S(1)} %get-tuple-element.46), channel_id=1, source_target_pairs={{0,6},{1,7},{2,4},{3,5},{4,2},{5,3},{6,0},{7,1},{8,14},{9,15},{10,... | collective-permute-start | bytes 49160 | tf_op jit(solution)/shard_map/cond/branch_1_fun/ppermute | solution.py:37
  107.4 1.3 %copy-start.14 = (bf16[256,128]{1,0:T(8,128)(2,1)S(1)}, bf16[256,128]{1,0:T(8,128)(2,1)}, u32[]{:S(2)}) copy-start(bf16[256,128]{1,0:T(8,128)(2,1)} %get-tuple-element.139) | copy-start | bytes 196612
  108.8 1.6 %collective-permute-start.4 = (bf16[64,2048]{1,0:T(8,128)(2,1)S(1)}, bf16[64,2048]{1,0:T(8,128)(2,1)S(1)}, u32[]{:S(2)}, u32[]{:S(2)}) collective-permute-start(bf16[64,2048]{1,0:T(8,128)(2,1)S(1)} %get-tuple-element.52), channel_id=1, source_target_pairs={{0,1},{1,0},{2,3},{3,2},{4,5},{5,4},{6,7},{7,6},{8,9},{9,8},{10,11... | collective-permute-start | bytes 786440 | tf_op jit(solution)/shard_map/cond/branch_1_fun/ppermute | solution.py:37
  109.9 5.1 %collective-permute-start.8 = (bf16[512,384]{1,0:T(8,128)(2,1)S(1)}, bf16[512,384]{1,0:T(8,128)(2,1)S(1)}, u32[]{:S(2)}, u32[]{:S(2)}) collective-permute-start(bf16[512,384]{1,0:T(8,128)(2,1)S(1)} %forward_rows.1), channel_id=1, source_target_pairs={{0,1},{1,0},{2,3},{3,2},{4,5},{5,4},{6,7},{7,6},{8,9},{9,8},{10,11... | collective-permute-start | bytes 1179656 | tf_op jit(solution)/shard_map/cond/branch_1_fun/ppermute | solution.py:37
  110.5 6.7 %collective-permute-start.5 = (bf16[128,512]{1,0:T(8,128)(2,1)S(1)}, bf16[128,512]{1,0:T(8,128)(2,1)S(1)}, u32[]{:S(2)}, u32[]{:S(2)}) collective-permute-start(bf16[128,512]{1,0:T(8,128)(2,1)S(1)} %get-tuple-element.57), channel_id=1, source_target_pairs={{0,2},{1,3},{2,0},{3,1},{4,6},{5,7},{6,4},{7,5},{8,10},{9,11},{10,... | collective-permute-start | bytes 393224 | tf_op jit(solution)/shard_map/cond/branch_1_fun/ppermute | solution.py:37
  111.3 12.7 %collective-permute-start.6 = (bf16[128,512]{1,0:T(8,128)(2,1)S(1)}, bf16[128,512]{1,0:T(8,128)(2,1)S(1)}, u32[]{:S(2)}, u32[]{:S(2)}) collective-permute-start(bf16[128,512]{1,0:T(8,128)(2,1)S(1)} %get-tuple-element.58), channel_id=1, source_target_pairs={{0,4},{1,5},{2,6},{3,7},{4,0},{5,1},{6,2},{7,3},{8,12},{9,13},{10,... | collective-permute-start | bytes 393224 | tf_op jit(solution)/shard_map/cond/branch_1_fun/ppermute | solution.py:37
  112.4 11.6 %collective-permute-start.7 = (bf16[128,512]{1,0:T(8,128)(2,1)S(1)}, bf16[128,512]{1,0:T(8,128)(2,1)S(1)}, u32[]{:S(2)}, u32[]{:S(2)}) collective-permute-start(bf16[128,512]{1,0:T(8,128)(2,1)S(1)} %get-tuple-element.59), channel_id=1, source_target_pairs={{0,6},{1,7},{2,4},{3,5},{4,2},{5,3},{6,0},{7,1},{8,14},{9,15},{10,... | collective-permute-start | bytes 393224 | tf_op jit(solution)/shard_map/cond/branch_1_fun/ppermute | solution.py:37
  124.9 0.7 copy-start.15

commit v8 on v7

--- a/solution.py
+++ b/solution.py
@@ -96,23 +96,23 @@
     )(me, q, k, v, after)
 
 
-def first_kernel(count, group, hd, nh, mask_rows, tiles, me_ref, nb_ref, *rest):
+def first_kernel(count, group, width, note_rows, mask_rows, tiles, me_ref, nb_ref, *rest):
     q_ref, k_ref, v_ref, x_ref, down_ref = rest[:5]
     outs, rest = rest[5 : 5 + count // 2], rest[5 + count // 2 :]
     x_s, down_s, sems, in_sems = rest
     me = me_ref[0]
     tok = q_ref.shape[0]
-    rank = down_ref.shape[0]
-    chunk = nh * 3 * tok
-
-    def place(k, row, size):
-        return outs[k // 2].at[pl.ds(k % 2 * chunk + row, size), :]
-
-    copies = pack_copies(count, group, hd, 0, nh, me, (q_ref, k_ref, v_ref), place, sems)
     loads = [
         pltpu.make_async_copy(x_ref, x_s, in_sems.at[0]),
         pltpu.make_async_copy(down_ref, down_s, in_sems.at[1]),
     ]
+    copies = []
+    for k in range(count):
+        column = pl.multiple_of((me ^ k) * group, LANES)
+        for t, ref in enumerate((q_ref, k_ref, v_ref)):
+            to = outs[k // 2].at[pl.ds((k % 2 * 3 + t) * tok, tok), :]
+            source = ref.at[:, pl.ds(column, width)]
+            copies.append(pltpu.make_async_copy(source, to, sems.at[len(copies)]))
     for copy in loads + copies:
         copy.start()
     rows = lax.broadcasted_iota(jnp.int32, (mask_rows, tok), 0)
@@ -127,26 +127,32 @@
     lora = mm(down_s[...], x_s[...], NT).astype(jnp.bfloat16)
     note = jnp.concatenate([lora, seen.astype(jnp.bfloat16)], axis=0)
     for out in outs:
-        out[2 * chunk :, :] = note
+        for n, row in enumerate(range(0, note.shape[0], note_rows)):
+            block = note[row : row + note_rows, :]
+            out[6 * tok : 6 * tok + block.shape[0], n * tok : (n + 1) * tok] = block
     for copy in copies:
         copy.wait()
 
 
-def first_pack(me, nb, q, k, v, x, down, count, hd, nh, mask_rows):
+def fold_rows(rows, parts):
+    return -(-rows // (parts * ROWS)) * ROWS
+
+
+def first_pack(me, nb, q, k, v, x, down, count, width, mask_rows):
     tok, model = q.shape
-    rows = 2 * nh * 3 * tok + down.shape[0] + mask_rows
+    note_rows = fold_rows(down.shape[0] + mask_rows, width // tok)
     bf = q.dtype
     return pl.pallas_call(
         functools.partial(
-            first_kernel, count, model // count, hd, nh, mask_rows, nb.shape[0]
+            first_kernel, count, model // count, width, note_rows, mask_rows, nb.shape[0]
         ),
-        out_shape=[jax.ShapeDtypeStruct((rows, hd), bf)] * (count // 2),
+        out_shape=[jax.ShapeDtypeStruct((6 * tok + note_rows, width), bf)] * (count // 2),
         in_specs=[SMEM, SMEM] + [HBM] * 5,
         out_specs=[VM] * (count // 2),
         scratch_shapes=[
             pltpu.VMEM(x.shape, bf),
             pltpu.VMEM(down.shape, bf),
-            pltpu.SemaphoreType.DMA((3 * nh * count,)),
+            pltpu.SemaphoreType.DMA((3 * count,)),
             pltpu.SemaphoreType.DMA((2,)),
         ],
         compiler_params=params(60),
@@ -234,8 +240,9 @@
 
 
 def assemble_kernel(group, moves, me_ref, *rest):
-    refs, out, sems = rest[:-2], rest[-2], rest[-1]
+    refs, (out, done_ref, sems) = rest[:-3], rest[-3:]
     me = me_ref[0]
+    done_ref[...] = jnp.zeros_like(done_ref)
     copies = []
     for n, (array, row, size, lane, width, k, start, to) in enumerate(moves):
         column = pl.multiple_of((me ^ k) * group + start, LANES)
@@ -259,9 +266,12 @@
         kernel = lambda me_ref, _, *rest: assemble_kernel(group, moves, me_ref, *rest)
     return pl.pallas_call(
         kernel,
-        out_shape=jax.ShapeDtypeStruct((tok, model), arrays[0].dtype),
+        out_shape=[
+            jax.ShapeDtypeStruct((tok, model), arrays[0].dtype),
+            jax.ShapeDtypeStruct((8, LANES), jnp.float32),
+        ],
         in_specs=[SMEM] + [ANY] * len(given) + [VM] * len(arrays),
-        out_specs=ANY,
+        out_specs=[ANY, VM],
         input_output_aliases={1: 0} if given else {},
         scratch_shapes=[pltpu.SemaphoreType.DMA((len(moves),))],
         compiler_params=params(4),
@@ -299,17 +309,19 @@
     count, tok, hd, nh, slots, rank, before, last, factor, me_ref, *rest
 ):
     half = count // 2
-    noted, rest = rest[: half + 1], rest[half + 1 :]
-    if before:
-        blocks, rest = rest[:half], rest[half:]
+    blocks, rest = rest[: half + (not before)], rest[half + (not before) :]
     up_ref, rest = rest[0], rest[1:]
     if before:
-        hid_ref, gup_in, *rest = rest
+        note_s, hid_ref, gup_in, *rest = rest
     outs, rest = rest[:half], rest[half:]
     if last:
         send_ref, *rest = rest
+    elif not before:
+        note_s, *rest = rest
     hid_out, gup_ref, *rest = rest
-    note_s, q_s, k_s, vt_s, svt_s, lora_s, grad_s, hid_s, out_s = rest
+    if last and not before:
+        note_s, *rest = rest
+    q_s, k_s, vt_s, svt_s, lora_s, grad_s, hid_s = rest
     head = pl.program_id(0)
     me = me_ref[0]
     scale = log_scale(hd)
@@ -317,13 +329,17 @@
 
     @pl.when(head == 0)
     def _():
-        part = noted[half].shape[0] // half
+        for p in range(count if not before else 0):
+            folded = fold_rows(size, blocks[0].shape[1] // tok)
+            part = blocks[half].shape[0] // half
+            ref, end = blocks[p // 2], 2 * part - folded
+            if p % 2:
+                ref, end = blocks[half], (p // 2 + 1) * part
+            for n, row in enumerate(range(0, size, folded)):
+                rows = min(folded, size - row)
+                block = ref[end - folded : end - folded + rows, n * tok : (n + 1) * tok]
+                note_s[p, row : row + rows, :] = block
         for p in range(count):
-            m = p // 2
-            if p % 2:
-                note_s[p] = noted[half][(m + 1) * part - size : (m + 1) * part, :]
-            else:
-                note_s[p] = noted[m][noted[m].shape[0] - size :, :]
             lora_s[:, p * tok : (p + 1) * tok] = note_s[p, :rank, :]
         if before:
             hid_s[...] = hid_ref[...]
@@ -333,15 +349,17 @@
 
     for p in range(count):
         if before:
-            ref, start = blocks[p // 2], p % 2 * nh * 3 * tok
-        elif p % 2:
-            ref, start = noted[half], p // 2 * (noted[half].shape[0] // half)
+            start = pl.multiple_of((p % 2 * nh + head) * 3 * tok, tok)
+            blocks_p = [blocks[p // 2][pl.ds(start + t * tok, tok), :] for t in range(3)]
         else:
-            ref, start = noted[p // 2], 0
-        start = pl.multiple_of(start + head * 3 * tok, ROWS)
-        q_s[p * tok : (p + 1) * tok, :] = ref[pl.ds(start, tok), :]
-        k_s[p * tok : (p + 1) * tok, :] = ref[pl.ds(start + tok, tok), :]
-        vt_s[:, p * tok : (p + 1) * tok] = ref[pl.ds(start + 2 * tok, tok), :].T
+            ref, start = blocks[p // 2], 0
+            if p % 2:
+                ref, start = blocks[half], p // 2 * (blocks[half].shape[0] // half)
+            lane = pl.ds(pl.multiple_of(head * hd, LANES), hd)
+            blocks_p = [ref[start + t * tok : start + (t + 1) * tok, lane] for t in range(3)]
+        q_s[p * tok : (p + 1) * tok, :] = blocks_p[0]
+        k_s[p * tok : (p + 1) * tok, :] = blocks_p[1]
+        vt_s[:, p * tok : (p + 1) * tok] = blocks_p[2].T
     up_t = up_ref[...]
     for p in range(count):
         cols = slice(p * tok, (p + 1) * tok)
@@ -349,8 +367,8 @@
         svt_s[p] = (vt_s[:, cols].astype(jnp.float32) + term).astype(jnp.bfloat16)
     grad_s[...] = jnp.zeros_like(grad_s)
 
-    for start in range(0, count, 4):
-        slabs = range(start, min(start + 4, count))
+    for start in range(0, count, 8):
+        slabs = range(start, min(start + 8, count))
         queries = [q_s[p * tok : (p + 1) * tok, :] for p in slabs]
         places = [window(me, p, count) for p in slabs]
         full = [mm(k_s[...], query, NT) for query in queries]
@@ -379,17 +397,16 @@
             deltas.append(((student - teacher) * factor).astype(jnp.bfloat16))
         grads = [mm(weight, delta, NT) for weight, delta in zip(weights, deltas)]
         for p, place, student, grad in zip(slabs, places, students, grads):
-            out_s[p] = student.T.astype(jnp.bfloat16)
+            to, row = outs[p // 2], p % 2 * tok
+            if last and p % 2:
+                to, row = send_ref, p // 2 * tok
+            to[row : row + tok, pl.ds(pl.multiple_of(head * hd, LANES), hd)] = student.T.astype(
+                jnp.bfloat16
+            )
             for n, w in enumerate(place):
                 grad_s[w] += grad[n * tok : (n + 1) * tok]
 
     grad = grad_s[...].reshape(count * tok, hd).astype(jnp.bfloat16)
-    column = pl.multiple_of(head * hd, LANES)
-    for p in range(count):
-        to, row = outs[p // 2], p % 2 * tok
-        if last and p % 2:
-            to, row = send_ref, p // 2 * tok
-        to[row : row + tok, pl.ds(column, hd)] = out_s[p]
     column = pl.multiple_of((before + head) * hd, LANES)
     gup_ref[:, pl.ds(column, hd)] = mm(lora_s[...], grad)
     hid_s[...] += mm(up_t, grad, NT)
@@ -407,8 +424,8 @@
             hid_out[...] = hid_s[...]
 
 
-def attention(me, blocks, noted, up_t, given, first, nh, tok, hd, slots, mask_rows, last):
-    count = 2 * len(noted) - 2
+def attention(me, blocks, up_t, given, first, nh, tok, hd, slots, mask_rows, last):
+    count = 2 * (len(blocks) - (not first))
     rank = up_t.shape[0]
     bf, f32 = jnp.bfloat16, jnp.float32
     keys = count * tok
@@ -417,6 +434,9 @@
     shapes = [jax.ShapeDtypeStruct(((1 if last else 2) * tok, nh * hd), bf)] * half
     if last:
         shapes.append(jax.ShapeDtypeStruct((half * (tok + rank), nh * hd), bf))
+    notes = (count, rank + mask_rows, tok)
+    if not first and not last:
+        shapes.append(jax.ShapeDtypeStruct(notes, bf))
     shapes += [
         jax.ShapeDtypeStruct((rank, keys // 2 if last else keys), f32),
         jax.ShapeDtypeStruct((rank, heads * hd), f32),
@@ -437,12 +457,12 @@
         grid=(nh,),
         out_shape=shapes,
         in_specs=[SMEM]
-        + [VM] * (len(noted) + len(blocks))
+        + [VM] * len(blocks)
         + [pl.BlockSpec((rank, hd), lambda h: (0, first + h))]
         + [VM] * len(given),
         out_specs=[VM] * len(shapes),
-        scratch_shapes=[
-            pltpu.VMEM((count, rank + mask_rows, tok), bf),
+        scratch_shapes=[pltpu.VMEM(notes, bf)] * (last and not first)
+        + [
             pltpu.VMEM((keys, hd), bf),
             pltpu.VMEM((keys, hd), bf),
             pltpu.VMEM((hd, keys), bf),
@@ -450,7 +470,6 @@
             pltpu.VMEM((rank, keys), bf),
             pltpu.VMEM((count, tok, hd), f32),
             pltpu.VMEM((rank, keys), f32),
-            pltpu.VMEM((count, tok, hd), bf),
         ],
         compiler_params=params(30),
         cost_estimate=pl.CostEstimate(
@@ -459,7 +478,6 @@
         name="attention",
     )(
         me,
-        *noted,
         *blocks,
         up_t,
         *given,
@@ -630,10 +648,10 @@
     down_t = adapter_down_weight.T
     up_t = adapter_up_weight.T
 
-    note = rank + mask_rows
+    width = chunks[0][1] * hd
+    note = fold_rows(rank + mask_rows, width // tok)
     first_own = first_pack(
-        me, neighbors, queries, keys, values, value_layer_input, down_t,
-        count, hd, chunks[0][1], mask_rows,
+        me, neighbors, queries, keys, values, value_layer_input, down_t, count, width, mask_rows
     )
     joined = [[]]
     for first, nh in chunks[1:]:
@@ -642,7 +660,7 @@
     noted = chips(first_own, count)
     ready = [own[0] for own in joined[1:]]
     noted = noted + [swap(forward(noted, note, ready), count, 1)]
-    messages = [chips(own, count) if own else [] for own in joined]
+    messages = [chips(own, count) if own else noted for own in joined]
 
     own_up = lax.dynamic_slice_in_dim(up_t, index * group, group, 1)
     half = count // 2
@@ -651,11 +669,13 @@
     for c, (first, nh) in enumerate(chunks):
         last = c == len(chunks) - 1
         out = attention(
-            me, messages[c], noted, own_up, given, first, nh, tok, hd, slots, mask_rows, last
+            me, messages[c], own_up, given, first, nh, tok, hd, slots, mask_rows, last
         )
-        blocks, given = list(out[:half]), out[-2:]
+        blocks, given = list(out[:half]), out[half:]
         if last:
             break
+        notes = out[half] if c == 0 else notes
+        given = [notes, *out[-2:]]
         riders.append(blocks[1])
         blocks[2:] = release(blocks[2:], messages[c + 1][1:])
         for m in [0] + list(range(2, half)):
@@ -665,7 +685,7 @@
     pieces = [
         [(n if n >= 0 else len(arrays), row, lane) for n, row, lane in group] for group in pieces
     ]
-    send, (hid, grad_up) = out[half], given
+    send, hid, grad_up = given
 
     def hidden_phase(hid, send, blocks, riders):
         total, *rest = riding_sum(hid, swap(send, count, 1), blocks, riders)
@@ -676,14 +696,14 @@
     before = first * hd
 
     def grad_phase(keep, send, arrays, joined):
-        base = None
+        base, done = None, keep
         if before:
             got = swap(forward_rows(arrays, pieces, tok, hd), count, 1)
             moves = [(len(arrays), m * tok, tok, 0, before, 2 * m + 1, 0, 0) for m in range(half)]
             for m, group_pieces in enumerate(pieces):
                 for h, (n, row, lane) in enumerate(group_pieces):
                     moves.append((n, row, tok, lane, hd, 2 * m, h * hd, 0))
-            base = assemble(me, [*arrays, got], moves, group, tok, model)
+            base, done = assemble(me, [*arrays, got], moves, group, tok, model)
         totals = pair_sum(keep, swap(send, count, 1), half, joined[1:])
         terms = chips(totals, count)
         moves = [(0, r * tok, tok, 0, nh * hd, r, before, 0) for r in range(2)]
@@ -693,12 +713,10 @@
             for row in range(0, 2 * tok, step):
                 (r, to), (n, at) = divmod(row, tok), divmod(row, size)
                 moves.append((m, rank + at, step, n * nh * hd, nh * hd, 2 * m + r, before, to))
-        student_out = assemble(me, [joined[0], *terms[1:]], moves, group, tok, model, base)
-        return sum_terms(terms, keep if base is None else base), student_out
-
-    grad_down, student_out = apart(
-        index < count, grad_phase, keep, send, [*arrays, hidden[1]], joined
-    )
+        student_out, _ = assemble(me, [joined[0], *terms[1:]], moves, group, tok, model, base)
+        return sum_terms(terms, done), student_out
+
+    grad_down, student_out = grad_phase(keep, send, [*arrays, hidden[1]], joined)
     return student_out, grad_down.T, grad_up.T
 
 

time: 126 us -> 125 us (level)
  waiting for transfers between devices: 52.1 us -> 54.9 us
  starting transfers between devices: 37.8 us -> 35.6 us
  Pallas kernels: 28.9 us -> 27.5 us
    ppermute x19, waiting for transfers between devices: 52.1 us -> 54.9 us  [swap(): return lax.ppermute(block, 'context', pairs)]
    ppermute x19, starting transfers between devices: 37.8 us -> 35.6 us  [swap(): return lax.ppermute(block, 'context', pairs)]
    pallas_call x2, Pallas kernels: 16.7 us -> 15.3 us  [attention(): pl.pallas_call(functools.partial(attention_kernel, count, tok, hd, nh, sl...]
    unnamed x32 -> x28, local copies, waits for them, and re-layouts: 5.84 us -> 5.4 us
  transfers between devices with their start and end apart: 19 -> 19, of which waited for: 8 -> 8; matrix products, arithmetic and copies ran while one was open for 0% -> 0% of each run, Pallas kernels for 18% -> 16%
where the time goes in v8:
time: 125 us; the launch traced here: 124 us
  waiting for transfers between devices  54.9 us (44%)
  starting transfers between devices  35.6 us (28%)
  Pallas kernels  27.5 us (22%)
  local copies, waits for them, and re-layouts  5.41 us (4%)
    ppermute x19, waiting for transfers between devices, swap(): return lax.ppermute(block, 'context', pairs)  54.9 us
    ppermute x19, starting transfers between devices, swap(): return lax.ppermute(block, 'context', pairs)  35.6 us
    pallas_call x2, Pallas kernels, attention(): pl.pallas_call(functools.partial(attention_kernel, count, tok, hd, nh, sl...  15.3 us
    unnamed x28, local copies, waits for them, and re-layouts  5.4 us
    pallas_call x1, Pallas kernels, first_pack(): pl.pallas_call(functools.partial(first_kernel, count, model // count, wid...  5.18 us
    pallas_call x2, Pallas kernels, assemble(): pl.pallas_call(kernel, out_shape=[jax.ShapeDtypeStruct((tok, model), arra...  3.31 us
  transfers between devices with their start and end apart: 19, of which 8 were waited for; matrix products, arithmetic and copies ran while one was open for 0% of the time, Pallas kernels for 16%

profile of v8, /device:TPU:0, one launch (start us, length us, event | category | flops | bytes accessed | tf_op | source)
XLA Modules:
  0.0 124.4 jit_solution(1975252648022853023)
XLA Ops:
  0.6 0.0 copy-start
  0.7 5.2 %first_pack.1 = (bf16[800,384]{1,0:T(8,128)(2,1)}, bf16[800,384]{1,0:T(8,128)(2,1)}, bf16[800,384]{1,0:T(8,128)(2,1)}, bf16[800,384]{1,0:T(8,128)(2,1)}) custom-call(s32[1]{0:T(128)} %bitcast.me_ref, s32[2,4]{1,0:T(2,128)} %nb_ref.1, bf16[128,4096]{1,0:T(8,128)(2,1)} %q_ref.1, bf16[128,4096]{1,0:T(8,128)(2,1)} %k_ref.1, bf16[128,4096]{1,0:T(8,128)(2,1)} %v_ref.1, ...), custom_call_target="tpu_custom_call" | custom-call | tf_op jit(solution)/shard_map/first_pack/pallas_call | solution.py:145
  5.9 3.1 %collective-permute-start.4 = (bf16[800,384]{1,0:T(8,128)(2,1)}, bf16[800,384]{1,0:T(8,128)(2,1)S(1)}, u32[]{:S(2)}, u32[]{:S(2)}) collective-permute-start(bf16[800,384]{1,0:T(8,128)(2,1)} %get-tuple-element.79), channel_id=1, source_target_pairs={{0,2},{1,3},{2,0},{3,1},{4,6},{5,7},{6,4},{7,5},{8,10},{9,11},{10,... | collective-permute-start | bytes 1843208 | tf_op jit(solution)/shard_map/ppermute | solution.py:37
  9.0 2.6 %collective-permute-start.5 = (bf16[800,384]{1,0:T(8,128)(2,1)}, bf16[800,384]{1,0:T(8,128)(2,1)S(1)}, u32[]{:S(2)}, u32[]{:S(2)}) collective-permute-start(bf16[800,384]{1,0:T(8,128)(2,1)} %get-tuple-element.80), channel_id=1, source_target_pairs={{0,4},{1,5},{2,6},{3,7},{4,0},{5,1},{6,2},{7,3},{8,12},{9,13},{10,... | collective-permute-start | bytes 1843208 | tf_op jit(solution)/shard_map/ppermute | solution.py:37
  11.5 0.0 collective-permute-start.6
  11.6 0.0 copy-start.4
  11.6 1.2 copy-done.4
  12.8 1.1 copy-done.5
  13.9 0.5 pack.1
  14.3 0.1 collective-permute-start.7
  14.4 1.7 %collective-permute-done.7.got_ref = bf16[1536,128]{1,0:T(8,128)(2,1)S(1)} collective-permute-done((bf16[1536,128]{1,0:T(8,128)(2,1)S(1)}, bf16[1536,128]{1,0:T(8,128)(2,1)S(1)}, u32[]{:S(2)}, u32[]{:S(2)}) %collective-permute-start.7) | collective-permute-done | bytes 393248 | tf_op jit(solution)/shard_map/ppermute | solution.py:37
  16.2 19.2 %collective-permute-done.4.refs_1_.rest_1_ = bf16[800,384]{1,0:T(8,128)(2,1)S(1)} collective-permute-done((bf16[800,384]{1,0:T(8,128)(2,1)}, bf16[800,384]{1,0:T(8,128)(2,1)S(1)}, u32[]{:S(2)}, u32[]{:S(2)}) %collective-permute-start.4) | collective-permute-done | bytes 614432 | tf_op jit(solution)/shard_map/ppermute | solution.py:37
  35.4 17.8 %collective-permute-done.5.refs_2_.rest_2_ = bf16[800,384]{1,0:T(8,128)(2,1)S(1)} collective-permute-done((bf16[800,384]{1,0:T(8,128)(2,1)}, bf16[800,384]{1,0:T(8,128)(2,1)S(1)}, u32[]{:S(2)}, u32[]{:S(2)}) %collective-permute-start.5) | collective-permute-done | bytes 614432 | tf_op jit(solution)/shard_map/ppermute | solution.py:37
  53.2 0.1 forward.1
  53.3 0.7 copy-done.7
  54.0 0.2 copy-done.9
  54.3 13.2 %collective-permute-start.10 = (bf16[768,128]{1,0:T(8,128)(2,1)}, bf16[768,128]{1,0:T(8,128)(2,1)S(1)}, u32[]{:S(2)}, u32[]{:S(2)}) collective-permute-start(bf16[768,128]{1,0:T(8,128)(2,1)} %copy-done.12), channel_id=1, source_target_pairs={{0,4},{1,5},{2,6},{3,7},{4,0},{5,1},{6,2},{7,3},{8,12},{9,13},{10,... | collective-permute-start | bytes 589832 | tf_op jit(solution)/shard_map/ppermute | solution.py:37
  67.5 1.3 %collective-permute-start.11 = (bf16[768,128]{1,0:T(8,128)(2,1)}, bf16[768,128]{1,0:T(8,128)(2,1)S(1)}, u32[]{:S(2)}, u32[]{:S(2)}) collective-permute-start(bf16[768,128]{1,0:T(8,128)(2,1)} %copy-done.13), channel_id=1, source_target_pairs={{0,6},{1,7},{2,4},{3,5},{4,2},{5,3},{6,0},{7,1},{8,14},{9,15},{10,... | collective-permute-start | bytes 589832 | tf_op jit(solution)/shard_map/ppermute | solution.py:37
  68.8 0.0 collective-permute-start.9
  68.8 0.0 collective-permute-done.8.rest_4_
  68.8 1.1 copy-done.8
  69.9 1.1 copy-done.10
  71.0 11.6 %attention.2 = (bf16[256,384]{1,0:T(8,128)(2,1)S(1)}, bf16[256,384]{1,0:T(8,128)(2,1)S(1)}, bf16[256,384]{1,0:T(8,128)(2,1)}, bf16[256,384]{1,0:T(8,128)(2,1)}, ...) custom-call(s32[1]{0:T(128)} %bitcast.me_ref, bf16[800,384]{1,0:T(8,128)(2,1)S(1)} %copy-done.6, ...), custom_call_target="tpu_custom_call" | custom-call | flops 12000000000 | bytes 3145728 | tf_op jit(solution)/shard_map/attention/pallas_call | solution.py:444
  82.6 0.0 collective-permute-done.10.refs_3_.rest_2_
  82.6 0.5 collective-permute-done.9.refs_2_.rest_1_
  83.0 3.3 %collective-permute-start.12 = (bf16[256,384]{1,0:T(8,128)(2,1)}, bf16[256,384]{1,0:T(8,128)(2,1)S(1)}, u32[]{:S(2)}, u32[]{:S(2)}) collective-permute-start(bf16[256,384]{1,0:T(8,128)(2,1)} %get-tuple-element.94), channel_id=1, source_target_pairs={{0,4},{1,5},{2,6},{3,7},{4,0},{5,1},{6,2},{7,3},{8,12},{9,13},{10,... | collective-permute-start | bytes 589832 | tf_op jit(solution)/shard_map/ppermute | solution.py:37
  86.4 2.5 %collective-permute-start.13 = (bf16[256,384]{1,0:T(8,128)(2,1)}, bf16[256,384]{1,0:T(8,128)(2,1)S(1)}, u32[]{:S(2)}, u32[]{:S(2)}) collective-permute-start(bf16[256,384]{1,0:T(8,128)(2,1)} %get-tuple-element.95), channel_id=1, source_target_pairs={{0,6},{1,7},{2,4},{3,5},{4,2},{5,3},{6,0},{7,1},{8,14},{9,15},{10,... | collective-permute-start | bytes 589832 | tf_op jit(solution)/shard_map/ppermute | solution.py:37
  88.8 3.7 %attention.3 = (bf16[128,128]{1,0:T(8,128)(2,1)S(1)}, bf16[128,128]{1,0:T(8,128)(2,1)S(1)}, bf16[128,128]{1,0:T(8,128)(2,1)S(1)}, bf16[128,128]{1,0:T(8,128)(2,1...) custom-call(s32[1]{0:T(128)} %bitcast.me_ref, ...), custom_call_target="tpu_custom_call" | custom-call | flops 4000000000 | bytes 1048576 | tf_op jit(solution)/shard_map/attention/pallas_call | solution.py:444
  92.6 13.0 %conditional.1 = (f32[64,128]{1,0:T(8,128)S(1)}, bf16[832,128]{1,0:T(8,128)(2,1)}, bf16[64,128]{1,0:T(8,128)(2,1)}, bf16[64,128]{1,0:T(8,128)(2,1)}, bf16[256,12...) conditional(s32[]{:T(128)} %convert_element_type.3, () %tuple.16, ...), branch_computations={%region_0.0_spmd, %region_1.0_spmd} | conditional | bytes 2818272 | solution.py:622
  92.6 1.4 %collective-permute-done.got_ref = bf16[768,128]{1,0:T(8,128)(2,1)S(1)} collective-permute-done((bf16[768,128]{1,0:T(8,128)(2,1)S(1)}, bf16[768,128]{1,0:T(8,128)(2,1)S(1)}, u32[]{:S(2)}, u32[]{:S(2)}) %collective-permute-start) | collective-permute-done | bytes 196640 | tf_op jit(solution)/shard_map/cond/branch_1_fun/ppermute | solution.py:37
  94.0 0.1 riding_sum.1
  94.1 0.1 collective-permute-start.1
  94.2 1.9 %collective-permute-start.2 = (bf16[64,128]{1,0:T(8,128)(2,1)S(1)}, bf16[64,128]{1,0:T(8,128)(2,1)}, u32[]{:S(2)}, u32[]{:S(2)}) collective-permute-start(bf16[64,128]{1,0:T(8,128)(2,1)S(1)} %get-tuple-element.23), channel_id=1, source_target_pairs={{0,4},{1,5},{2,6},{3,7},{4,0},{5,1},{6,2},{7,3},{8,12},{9,13},{10,... | collective-permute-start | bytes 49160 | tf_op jit(solution)/shard_map/cond/branch_1_fun/ppermute | solution.py:37
  96.1 2.5 %collective-permute-start.3 = (bf16[64,128]{1,0:T(8,128)(2,1)S(1)}, bf16[64,128]{1,0:T(8,128)(2,1)}, u32[]{:S(2)}, u32[]{:S(2)}) collective-permute-start(bf16[64,128]{1,0:T(8,128)(2,1)S(1)} %get-tuple-element.24), channel_id=1, source_target_pairs={{0,6},{1,7},{2,4},{3,5},{4,2},{5,3},{6,0},{7,1},{8,14},{9,15},{10,... | collective-permute-start | bytes 49160 | tf_op jit(solution)/shard_map/cond/branch_1_fun/ppermute | solution.py:37
  98.5 7.0 %collective-permute-done.2 = bf16[64,128]{1,0:T(8,128)(2,1)} collective-permute-done((bf16[64,128]{1,0:T(8,128)(2,1)S(1)}, bf16[64,128]{1,0:T(8,128)(2,1)}, u32[]{:S(2)}, u32[]{:S(2)}) %collective-permute-start.2) | collective-permute-done | bytes 16416 | tf_op jit(solution)/shard_map/cond/branch_1_fun/ppermute | solution.py:37
  105.6 1.3 %down_terms.1 = (f32[64,2048]{1,0:T(8,128)S(1)}, bf16[64,2048]{1,0:T(8,128)(2,1)S(1)}) custom-call(s32[1]{0:T(128)} %bitcast.me_ref, f32[64,128]{1,0:T(8,128)S(1)} %get-tuple-element.109.rest_0_, bf16[832,128]{1,0:T(8,128)(2,1)} %get-tuple-element.106.refs_3_.rest_3_.rest_1_, bf16[64,128]{1,0:T(8,128)(2,1)} %get-tuple-element.110.rest_2_, ...), custom_call_target="tpu_custom_call" | custom-call | bytes 1048576 | tf_op jit(solution)/shard_map/down_terms/pallas_call | solution.py:584
  106.8 0.1 collective-permute-start.15
  106.9 1.0 forward_rows.1
  107.9 0.5 collective-permute-start.14
  108.5 0.1 pair_sum.1
  108.6 0.8 collective-permute-start.16
  109.4 2.3 %collective-permute-start.17 = (bf16[128,512]{1,0:T(8,128)(2,1)S(1)}, bf16[128,512]{1,0:T(8,128)(2,1)S(1)}, u32[]{:S(2)}, u32[]{:S(2)}) collective-permute-start(bf16[128,512]{1,0:T(8,128)(2,1)S(1)} %get-tuple-element.118), channel_id=1, source_target_pairs={{0,4},{1,5},{2,6},{3,7},{4,0},{5,1},{6,2},{7,3},{8,12},{9,13},{10,... | collective-permute-start | bytes 393224 | tf_op jit(solution)/shard_map/ppermute | solution.py:37
  111.7 1.3 %collective-permute-start.18 = (bf16[128,512]{1,0:T(8,128)(2,1)S(1)}, bf16[128,512]{1,0:T(8,128)(2,1)S(1)}, u32[]{:S(2)}, u32[]{:S(2)}) collective-permute-start(bf16[128,512]{1,0:T(8,128)(2,1)S(1)} %get-tuple-element.119), channel_id=1, source_target_pairs={{0,6},{1,7},{2,4},{3,5},{4,2},{5,3},{6,0},{7,1},{8,14},{9,15},{10,... | collective-permute-start | bytes 393224 | tf_op jit(solution)/shard_map/ppermute | solution.py:37
  113.0 1.9 %assemble.2 = (bf16[128,4096]{1,0:T(8,128)(2,1)}, f32[8,128]{1,0:T(8,128)S(1)}) custom-call(s32[1]{0:T(128)} %bitcast.me_ref, bf16[256,384]{1,0:T(8,128)(2,1)S(1)} %get-tuple-element.88.refs_0_.rest_0_, bf16[256,384]{1,0:T(8,128)(2,1)S(1)} %collective-permute-done.12.refs_1_.rest_1_, bf16[256,384]{1,0:T(8,128)(2,1)S(1)} %collective-permute-done.13.refs_2_.rest_2_, ...), custom_call_target="tpu_custom_call" | custom-call | bytes 1048576 | tf_op jit(solution)/shard_map/assemble/pallas_call | solution.py:267
  115.0 1.4 %collective-permute-done.16.rest_1_.refs_1_ = bf16[128,512]{1,0:T(8,128)(2,1)S(1)} collective-permute-done((bf16[128,512]{1,0:T(8,128)(2,1)S(1)}, bf16[128,512]{1,0:T(8,128)(2,1)S(1)}, u32[]{:S(2)}, u32[]{:S(2)}) %collective-permute-start.16) | collective-permute-done | bytes 131104 | tf_op jit(solution)/shard_map/ppermute | solution.py:37
  116.3 5.9 %collective-permute-done.17.rest_2_.refs_2_ = bf16[128,512]{1,0:T(8,128)(2,1)S(1)} collective-permute-done((bf16[128,512]{1,0:T(8,128)(2,1)S(1)}, bf16[128,512]{1,0:T(8,128)(2,1)S(1)}, u32[]{:S(2)}, u32[]{:S(2)}) %collective-permute-start.17) | collective-permute-done | bytes 131104 | tf_op jit(solution)/shard_map/ppermute | solution.py:37
  122.3 0.7 sum_terms.1
  123.0 1.4 %assemble.3 = (bf16[128,4096]{1,0:T(8,128)(2,1)}, f32[8,128]{1,0:T(8,128)}) custom-call(s32[1]{0:T(128)} %bitcast.me_ref, bf16[128,4096]{1,0:T(8,128)(2,1)} %get-tuple-element.107._, bf16[256,128]{1,0:T(8,128)(2,1)S(1)} %get-tuple-element.108.rest_0_, bf16[128,512]{1,0:T(8,128)(2,1)S(1)} %collective-permute-done.16.rest_1_.refs_1_, ...), custom_call_target="tpu_custom_call", output_to_operand_aliasing={{0}: (1, {})} | custom-call | bytes 1048576 | tf_op jit(solution)/shard_map/assemble/pallas_call | solution.py:267
  (34 shorter events, 0.1 us)
Async XLA Ops:
  0.6 53.6 %copy-start = (bf16[4096,64]{0,1:T(8,128)(2,1)S(1)}, bf16[4096,64]{0,1:T(8,128)(2,1)}, u32[]{:S(2)}) copy-start(bf16[4096,64]{0,1:T(8,128)(2,1)} %param.14) | copy-start | bytes 1572868
  0.7 10.9 %copy-start.2 = (bf16[128,4096]{1,0:T(8,128)(2,1)S(1)}, bf16[128,4096]{1,0:T(8,128)(2,1)}, u32[]{:S(2)}) copy-start(bf16[128,4096]{1,0:T(8,128)(2,1)} %q_ref.1) | copy-start | bytes 3145732
  0.7 10.9 %copy-start.3 = (bf16[128,4096]{1,0:T(8,128)(2,1)S(1)}, bf16[128,4096]{1,0:T(8,128)(2,1)}, u32[]{:S(2)}) copy-start(bf16[128,4096]{1,0:T(8,128)(2,1)} %k_ref.1) | copy-start | bytes 3145732
  5.9 29.6 %collective-permute-start.4 = (bf16[800,384]{1,0:T(8,128)(2,1)}, bf16[800,384]{1,0:T(8,128)(2,1)S(1)}, u32[]{:S(2)}, u32[]{:S(2)}) collective-permute-start(bf16[800,384]{1,0:T(8,128)(2,1)} %get-tuple-element.79), channel_id=1, source_target_pairs={{0,2},{1,3},{2,0},{3,1},{4,6},{5,7},{6,4},{7,5},{8,10},{9,11},{10,... | collective-permute-start | bytes 1843208 | tf_op jit(solution)/shard_map/ppermute | solution.py:37
  9.0 44.2 %collective-permute-start.5 = (bf16[800,384]{1,0:T(8,128)(2,1)}, bf16[800,384]{1,0:T(8,128)(2,1)S(1)}, u32[]{:S(2)}, u32[]{:S(2)}) collective-permute-start(bf16[800,384]{1,0:T(8,128)(2,1)} %get-tuple-element.80), channel_id=1, source_target_pairs={{0,4},{1,5},{2,6},{3,7},{4,0},{5,1},{6,2},{7,3},{8,12},{9,13},{10,... | collective-permute-start | bytes 1843208 | tf_op jit(solution)/shard_map/ppermute | solution.py:37
  11.5 41.6 %collective-permute-start.6 = (bf16[800,384]{1,0:T(8,128)(2,1)}, bf16[800,384]{1,0:T(8,128)(2,1)S(1)}, u32[]{:S(2)}, u32[]{:S(2)}) collective-permute-start(bf16[800,384]{1,0:T(8,128)(2,1)} %get-tuple-element.81), channel_id=1, source_target_pairs={{0,6},{1,7},{2,4},{3,5},{4,2},{5,3},{6,0},{7,1},{8,14},{9,15},{10,... | collective-permute-start | bytes 1843208 | tf_op jit(solution)/shard_map/ppermute | solution.py:37
  11.6 1.2 copy-start.4
  12.8 1.1 copy-start.5
  14.3 1.8 %collective-permute-start.7 = (bf16[1536,128]{1,0:T(8,128)(2,1)S(1)}, bf16[1536,128]{1,0:T(8,128)(2,1)S(1)}, u32[]{:S(2)}, u32[]{:S(2)}) collective-permute-start(bf16[1536,128]{1,0:T(8,128)(2,1)S(1)} %get-tuple-element.82), channel_id=1, source_target_pairs={{0,1},{1,0},{2,3},{3,2},{4,5},{5,4},{6,7},{7,6},{8,9},{9,8},{10,11... | collective-permute-start | bytes 1179656 | tf_op jit(solution)/shard_map/ppermute | solution.py:37
  16.2 38.1 %copy-start.11 = (bf16[768,128]{1,0:T(8,128)(2,1)}, bf16[768,128]{1,0:T(8,128)(2,1)S(1)}, u32[]{:S(2)}) copy-start(bf16[768,128]{1,0:T(8,128)(2,1)S(1)} %get-tuple-element.91) | copy-start | bytes 589828
  16.2 38.1 %copy-start.12 = (bf16[768,128]{1,0:T(8,128)(2,1)}, bf16[768,128]{1,0:T(8,128)(2,1)S(1)}, u32[]{:S(2)}) copy-start(bf16[768,128]{1,0:T(8,128)(2,1)S(1)} %get-tuple-element.92) | copy-start | bytes 589828
  16.2 38.1 %copy-start.13 = (bf16[768,128]{1,0:T(8,128)(2,1)}, bf16[768,128]{1,0:T(8,128)(2,1)S(1)}, u32[]{:S(2)}) copy-start(bf16[768,128]{1,0:T(8,128)(2,1)S(1)} %get-tuple-element.93) | copy-start | bytes 589828
  53.2 0.8 copy-start.7
  53.2 1.1 copy-start.9
  53.2 15.6 %copy-start.6 = (bf16[800,384]{1,0:T(8,128)(2,1)S(1)}, bf16[800,384]{1,0:T(8,128)(2,1)}, u32[]{:S(2)}) copy-start(bf16[800,384]{1,0:T(8,128)(2,1)} %get-tuple-element.78._.refs_0_.rest_0_) | copy-start | bytes 1843204
  54.2 14.6 %collective-permute-start.8 = (bf16[1664,384]{1,0:T(8,128)(2,1)S(1)}, bf16[1664,384]{1,0:T(8,128)(2,1)}, u32[]{:S(2)}, u32[]{:S(2)}) collective-permute-start(bf16[1664,384]{1,0:T(8,128)(2,1)S(1)} %forward.1), channel_id=1, source_target_pairs={{0,1},{1,0},{2,3},{3,2},{4,5},{5,4},{6,7},{7,6},{8,9},{9,8},{10,11... | collective-permute-start | bytes 3833864 | tf_op jit(solution)/shard_map/ppermute | solution.py:37
  54.3 28.3 %collective-permute-start.10 = (bf16[768,128]{1,0:T(8,128)(2,1)}, bf16[768,128]{1,0:T(8,128)(2,1)S(1)}, u32[]{:S(2)}, u32[]{:S(2)}) collective-permute-start(bf16[768,128]{1,0:T(8,128)(2,1)} %copy-done.12), channel_id=1, source_target_pairs={{0,4},{1,5},{2,6},{3,7},{4,0},{5,1},{6,2},{7,3},{8,12},{9,13},{10,... | collective-permute-start | bytes 589832 | tf_op jit(solution)/shard_map/ppermute | solution.py:37
  67.5 15.1 %collective-permute-start.11 = (bf16[768,128]{1,0:T(8,128)(2,1)}, bf16[768,128]{1,0:T(8,128)(2,1)S(1)}, u32[]{:S(2)}, u32[]{:S(2)}) collective-permute-start(bf16[768,128]{1,0:T(8,128)(2,1)} %copy-done.13), channel_id=1, source_target_pairs={{0,6},{1,7},{2,4},{3,5},{4,2},{5,3},{6,0},{7,1},{8,14},{9,15},{10,... | collective-permute-start | bytes 589832 | tf_op jit(solution)/shard_map/ppermute | solution.py:37
  68.8 14.2 %collective-permute-start.9 = (bf16[768,128]{1,0:T(8,128)(2,1)}, bf16[768,128]{1,0:T(8,128)(2,1)S(1)}, u32[]{:S(2)}, u32[]{:S(2)}) collective-permute-start(bf16[768,128]{1,0:T(8,128)(2,1)} %copy-done.11), channel_id=1, source_target_pairs={{0,2},{1,3},{2,0},{3,1},{4,6},{5,7},{6,4},{7,5},{8,10},{9,11},{10,... | collective-permute-start | bytes 589832 | tf_op jit(solution)/shard_map/ppermute | solution.py:37
  68.8 1.1 copy-start.8
  69.9 1.1 copy-start.10
  83.0 23.9 %collective-permute-start.12 = (bf16[256,384]{1,0:T(8,128)(2,1)}, bf16[256,384]{1,0:T(8,128)(2,1)S(1)}, u32[]{:S(2)}, u32[]{:S(2)}) collective-permute-start(bf16[256,384]{1,0:T(8,128)(2,1)} %get-tuple-element.94), channel_id=1, source_target_pairs={{0,4},{1,5},{2,6},{3,7},{4,0},{5,1},{6,2},{7,3},{8,12},{9,13},{10,... | collective-permute-start | bytes 589832 | tf_op jit(solution)/shard_map/ppermute | solution.py:37
  86.4 20.6 %collective-permute-start.13 = (bf16[256,384]{1,0:T(8,128)(2,1)}, bf16[256,384]{1,0:T(8,128)(2,1)S(1)}, u32[]{:S(2)}, u32[]{:S(2)}) collective-permute-start(bf16[256,384]{1,0:T(8,128)(2,1)} %get-tuple-element.95), channel_id=1, source_target_pairs={{0,6},{1,7},{2,4},{3,5},{4,2},{5,3},{6,0},{7,1},{8,14},{9,15},{10,... | collective-permute-start | bytes 589832 | tf_op jit(solution)/shard_map/ppermute | solution.py:37
  92.6 13.0 %copy-start.1 = (bf16[128,4096]{1,0:T(8,128)(2,1)S(1)}, bf16[128,4096]{1,0:T(8,128)(2,1)}, u32[]{:S(2)}) copy-start(bf16[128,4096]{1,0:T(8,128)(2,1)} %rest_4_.1) | copy-start | bytes 3145732
  92.6 1.4 %collective-permute-start = (bf16[768,128]{1,0:T(8,128)(2,1)S(1)}, bf16[768,128]{1,0:T(8,128)(2,1)S(1)}, u32[]{:S(2)}, u32[]{:S(2)}) collective-permute-start(bf16[768,128]{1,0:T(8,128)(2,1)S(1)} %get-tuple-element.15), channel_id=1, source_target_pairs={{0,1},{1,0},{2,3},{3,2},{4,5},{5,4},{6,7},{7,6},{8,9},{9,8},{10,11... | collective-permute-start | bytes 589832 | tf_op jit(solution)/shard_map/cond/branch_1_fun/ppermute | solution.py:37
  94.1 11.5 %collective-permute-start.1 = (bf16[832,128]{1,0:T(8,128)(2,1)S(1)}, bf16[832,128]{1,0:T(8,128)(2,1)}, u32[]{:S(2)}, u32[]{:S(2)}) collective-permute-start(bf16[832,128]{1,0:T(8,128)(2,1)S(1)} %get-tuple-element.22), channel_id=1, source_target_pairs={{0,2},{1,3},{2,0},{3,1},{4,6},{5,7},{6,4},{7,5},{8,10},{9,11},{10,... | collective-permute-start | bytes 638984 | tf_op jit(solution)/shard_map/cond/branch_1_fun/ppermute | solution.py:37
  94.2 11.4 %collective-permute-start.2 = (bf16[64,128]{1,0:T(8,128)(2,1)S(1)}, bf16[64,128]{1,0:T(8,128)(2,1)}, u32[]{:S(2)}, u32[]{:S(2)}) collective-permute-start(bf16[64,128]{1,0:T(8,128)(2,1)S(1)} %get-tuple-element.23), channel_id=1, source_target_pairs={{0,4},{1,5},{2,6},{3,7},{4,0},{5,1},{6,2},{7,3},{8,12},{9,13},{10,... | collective-permute-start | bytes 49160 | tf_op jit(solution)/shard_map/cond/branch_1_fun/ppermute | solution.py:37
  96.1 9.5 %collective-permute-start.3 = (bf16[64,128]{1,0:T(8,128)(2,1)S(1)}, bf16[64,128]{1,0:T(8,128)(2,1)}, u32[]{:S(2)}, u32[]{:S(2)}) collective-permute-start(bf16[64,128]{1,0:T(8,128)(2,1)S(1)} %get-tuple-element.24), channel_id=1, source_target_pairs={{0,6},{1,7},{2,4},{3,5},{4,2},{5,3},{6,0},{7,1},{8,14},{9,15},{10,... | collective-permute-start | bytes 49160 | tf_op jit(solution)/shard_map/cond/branch_1_fun/ppermute | solution.py:37
  106.8 1.6 %collective-permute-start.15 = (bf16[64,2048]{1,0:T(8,128)(2,1)S(1)}, bf16[64,2048]{1,0:T(8,128)(2,1)S(1)}, u32[]{:S(2)}, u32[]{:S(2)}) collective-permute-start(bf16[64,2048]{1,0:T(8,128)(2,1)S(1)} %get-tuple-element.113), channel_id=1, source_target_pairs={{0,1},{1,0},{2,3},{3,2},{4,5},{5,4},{6,7},{7,6},{8,9},{9,8},{10,11... | collective-permute-start | bytes 786440 | tf_op jit(solution)/shard_map/ppermute | solution.py:37
  107.9 5.1 %collective-permute-start.14 = (bf16[512,384]{1,0:T(8,128)(2,1)S(1)}, bf16[512,384]{1,0:T(8,128)(2,1)S(1)}, u32[]{:S(2)}, u32[]{:S(2)}) collective-permute-start(bf16[512,384]{1,0:T(8,128)(2,1)S(1)} %forward_rows.1), channel_id=1, source_target_pairs={{0,1},{1,0},{2,3},{3,2},{4,5},{5,4},{6,7},{7,6},{8,9},{9,8},{10,11... | collective-permute-start | bytes 1179656 | tf_op jit(solution)/shard_map/ppermute | solution.py:37
  108.6 7.8 %collective-permute-start.16 = (bf16[128,512]{1,0:T(8,128)(2,1)S(1)}, bf16[128,512]{1,0:T(8,128)(2,1)S(1)}, u32[]{:S(2)}, u32[]{:S(2)}) collective-permute-start(bf16[128,512]{1,0:T(8,128)(2,1)S(1)} %get-tuple-element.117), channel_id=1, source_target_pairs={{0,2},{1,3},{2,0},{3,1},{4,6},{5,7},{6,4},{7,5},{8,10},{9,11},{10,... | collective-permute-start | bytes 393224 | tf_op jit(solution)/shard_map/ppermute | solution.py:37
  109.4 12.9 %collective-permute-start.17 = (bf16[128,512]{1,0:T(8,128)(2,1)S(1)}, bf16[128,512]{1,0:T(8,128)(2,1)S(1)}, u32[]{:S(2)}, u32[]{:S(2)}) collective-permute-start(bf16[128,512]{1,0:T(8,128)(2,1)S(1)} %get-tuple-element.118), channel_id=1, source_target_pairs={{0,4},{1,5},{2,6},{3,7},{4,0},{5,1},{6,2},{7,3},{8,12},{9,13},{10,... | collective-permute-start | bytes 393224 | tf_op jit(solution)/shard_map/ppermute | solution.py:37
  111.7 10.6 %collective-permute-start.18 = (bf16[128,512]{1,0:T(8,128)(2,1)S(1)}, bf16[128,512]{1,0:T(8,128)(2,1)S(1)}, u32[]{:S(2)}, u32[]{:S(2)}) collective-permute-start(bf16[128,512]{1,0:T(8,128)(2,1)S(1)} %get-tuple-element.119), channel_id=1, source_target_pairs={{0,6},{1,7},{2,4},{3,5},{4,2},{5,3},{6,0},{7,1},{8,14},{9,15},{10,... | collective-permute-start | bytes 393224 | tf_op jit(solution)/shard_map/ppermute | solution.py:37

commit v9 on v8

--- a/solution.py
+++ b/solution.py
@@ -239,10 +239,12 @@
     )(*arrays)
 
 
-def assemble_kernel(group, moves, me_ref, *rest):
-    refs, (out, done_ref, sems) = rest[:-3], rest[-3:]
+def assemble_kernel(group, moves, terms, me_ref, *rest):
+    if terms:
+        *rest, sum_ref, sems = rest
+        rest = [*rest[1:], sems]
+    refs, out, sems = rest[:-2], rest[-2], rest[-1]
     me = me_ref[0]
-    done_ref[...] = jnp.zeros_like(done_ref)
     copies = []
     for n, (array, row, size, lane, width, k, start, to) in enumerate(moves):
         column = pl.multiple_of((me ^ k) * group + start, LANES)
@@ -255,29 +257,44 @@
         )
     for copy in copies:
         copy.start()
+    if terms:
+        total = refs[-1][...]
+        for ref in refs[1 : terms + 1]:
+            total += ref[: total.shape[0], :].astype(jnp.float32)
+        sum_ref[...] = total
     for copy in copies:
         copy.wait()
 
 
-def assemble(me, arrays, moves, group, tok, model, base=None):
-    given = [] if base is None else [base]
-    kernel = functools.partial(assemble_kernel, group, moves)
-    if given:
-        kernel = lambda me_ref, _, *rest: assemble_kernel(group, moves, me_ref, *rest)
-    return pl.pallas_call(
-        kernel,
-        out_shape=[
-            jax.ShapeDtypeStruct((tok, model), arrays[0].dtype),
-            jax.ShapeDtypeStruct((8, LANES), jnp.float32),
-        ],
-        in_specs=[SMEM] + [ANY] * len(given) + [VM] * len(arrays),
-        out_specs=[ANY, VM],
-        input_output_aliases={1: 0} if given else {},
+def assemble(me, arrays, moves, group, tok, model):
+    return pl.pallas_call(
+        functools.partial(assemble_kernel, group, moves, 0),
+        out_shape=jax.ShapeDtypeStruct((tok, model), arrays[0].dtype),
+        in_specs=[SMEM] + [VM] * len(arrays),
+        out_specs=ANY,
         scratch_shapes=[pltpu.SemaphoreType.DMA((len(moves),))],
         compiler_params=params(4),
         cost_estimate=SMALL,
         name="assemble",
-    )(me, *given, *arrays)
+    )(me, *arrays)
+
+
+def finish(me, base, local, terms, moves, group):
+    arrays = [local, *terms[1:], terms[0]]
+    return pl.pallas_call(
+        functools.partial(assemble_kernel, group, moves, len(terms) - 1),
+        out_shape=[
+            jax.ShapeDtypeStruct(base.shape, base.dtype),
+            jax.ShapeDtypeStruct(terms[0].shape, jnp.float32),
+        ],
+        in_specs=[SMEM, ANY] + [VM] * len(arrays),
+        out_specs=[ANY, VM],
+        input_output_aliases={1: 0},
+        scratch_shapes=[pltpu.SemaphoreType.DMA((len(moves),))],
+        compiler_params=params(4),
+        cost_estimate=SMALL,
+        name="finish",
+    )(me, base, *arrays)
 
 
 def soft(scores, scale):
@@ -562,13 +579,21 @@
     )(keep, got, *blocks, *riders)
 
 
-def down_kernel(count, group, me_ref, *rest):
-    parts = rest[: count // 2]
-    x_ref, keep_ref, send_ref = rest[count // 2 :]
+def down_kernel(count, group, me_ref, own_ref, *rest):
+    parts, (x_ref, keep_ref, send_ref, own_s, part_s, sems) = rest[: count // 2 - 1], rest[-6:]
     me = me_ref[0]
-    hidden = parts[0][...]
-    for part in parts[1:]:
-        hidden += part[: hidden.shape[0], :].astype(jnp.float32)
+    rank = own_s.shape[0]
+    copies = [pltpu.make_async_copy(own_ref, own_s, sems.at[0])]
+    for n, part in enumerate(parts):
+        source = part.at[pl.ds(0, rank), :]
+        copies.append(pltpu.make_async_copy(source, part_s.at[n], sems.at[n + 1]))
+    for copy in copies:
+        copy.start()
+    for copy in copies:
+        copy.wait()
+    hidden = own_s[...]
+    for n in range(len(parts)):
+        hidden += part_s[n].astype(jnp.float32)
     hidden = hidden.astype(jnp.bfloat16)
     for k in range(count):
         column = pl.multiple_of((me ^ k) * group, LANES)
@@ -580,38 +605,24 @@
 def down_terms(me, parts, x):
     count = 2 * len(parts)
     model = x.shape[1]
-    rank = parts[0].shape[0]
+    rank, tok = parts[0].shape
     return pl.pallas_call(
         functools.partial(down_kernel, count, model // count),
         out_shape=[
             jax.ShapeDtypeStruct((rank, model // 2), jnp.float32),
             jax.ShapeDtypeStruct((rank, model // 2), jnp.bfloat16),
         ],
-        in_specs=[SMEM] + [VM] * (len(parts) + 1),
+        in_specs=[SMEM] + [ANY] * len(parts) + [VM],
         out_specs=[VM, VM],
+        scratch_shapes=[
+            pltpu.VMEM((rank, tok), jnp.float32),
+            pltpu.VMEM((len(parts) - 1, rank, tok), jnp.bfloat16),
+            pltpu.SemaphoreType.DMA((len(parts),)),
+        ],
         compiler_params=params(8),
         cost_estimate=SMALL,
         name="down_terms",
     )(me, *parts, x)
-
-
-def sum_kernel(*refs):
-    total = refs[0][...]
-    for ref in refs[1:-2]:
-        total += ref[: total.shape[0], :].astype(jnp.float32)
-    refs[-1][...] = total
-
-
-def sum_terms(parts, after):
-    return pl.pallas_call(
-        sum_kernel,
-        out_shape=jax.ShapeDtypeStruct(parts[0].shape, jnp.float32),
-        in_specs=[VM] * len(parts) + [ANY],
-        out_specs=VM,
-        compiler_params=params(4),
-        cost_estimate=SMALL,
-        name="sum_terms",
-    )(*parts, after)
 
 
 def apart(always, phase, *operands):
@@ -696,14 +707,14 @@
     before = first * hd
 
     def grad_phase(keep, send, arrays, joined):
-        base, done = None, keep
+        base = jnp.zeros((tok, model), queries.dtype) if not before else None
         if before:
             got = swap(forward_rows(arrays, pieces, tok, hd), count, 1)
             moves = [(len(arrays), m * tok, tok, 0, before, 2 * m + 1, 0, 0) for m in range(half)]
             for m, group_pieces in enumerate(pieces):
                 for h, (n, row, lane) in enumerate(group_pieces):
                     moves.append((n, row, tok, lane, hd, 2 * m, h * hd, 0))
-            base, done = assemble(me, [*arrays, got], moves, group, tok, model)
+            base = assemble(me, [*arrays, got], moves, group, tok, model)
         totals = pair_sum(keep, swap(send, count, 1), half, joined[1:])
         terms = chips(totals, count)
         moves = [(0, r * tok, tok, 0, nh * hd, r, before, 0) for r in range(2)]
@@ -713,10 +724,9 @@
             for row in range(0, 2 * tok, step):
                 (r, to), (n, at) = divmod(row, tok), divmod(row, size)
                 moves.append((m, rank + at, step, n * nh * hd, nh * hd, 2 * m + r, before, to))
-        student_out, _ = assemble(me, [joined[0], *terms[1:]], moves, group, tok, model, base)
-        return sum_terms(terms, done), student_out
-
-    grad_down, student_out = grad_phase(keep, send, [*arrays, hidden[1]], joined)
+        return finish(me, base, joined[0], terms, moves, group)
+
+    student_out, grad_down = grad_phase(keep, send, [*arrays, hidden[1]], joined)
     return student_out, grad_down.T, grad_up.T
 
 

time: 125 us -> 124 us (level)
    pallas_call x3 -> x2, Pallas kernels: 4.01 us -> 3.4 us  [the longest x1 1.93 us: assemble(): pl.pallas_call(functools.partial(assemble_kernel, group, moves, 0), out_s...]
where the time goes in v9:
time: 124 us
  waiting for transfers between devices  54.9 us (44%)
  starting transfers between devices  35.6 us (29%)
  Pallas kernels  26.8 us (22%)
  local copies, waits for them, and re-layouts  5.39 us (4%)
    ppermute x19, waiting for transfers between devices, swap(): return lax.ppermute(block, 'context', pairs)  54.9 us
    ppermute x19, starting transfers between devices, swap(): return lax.ppermute(block, 'context', pairs)  35.6 us
    pallas_call x2, Pallas kernels, attention(): pl.pallas_call(functools.partial(attention_kernel, count, tok, hd, nh, sl...  15.3 us
    unnamed x28, local copies, waits for them, and re-layouts  5.38 us
    pallas_call x1, Pallas kernels, first_pack(): pl.pallas_call(functools.partial(first_kernel, count, model // count, wid...  5.19 us
  transfers between devices with their start and end apart: 19, of which 8 were waited for; matrix products, arithmetic and copies ran while one was open for 0% of the time, Pallas kernels for 16%

profile of v9, /device:TPU:0, one launch (start us, length us, event | category | flops | bytes accessed | tf_op | source)
XLA Modules:
  0.0 123.6 jit_solution(18301395141839484813)
XLA Ops:
  0.6 0.0 copy-start
  0.7 5.2 %first_pack.1 = (bf16[800,384]{1,0:T(8,128)(2,1)}, bf16[800,384]{1,0:T(8,128)(2,1)}, bf16[800,384]{1,0:T(8,128)(2,1)}, bf16[800,384]{1,0:T(8,128)(2,1)}) custom-call(s32[1]{0:T(128)} %bitcast.me_ref, s32[2,4]{1,0:T(2,128)} %nb_ref.1, bf16[128,4096]{1,0:T(8,128)(2,1)} %q_ref.1, bf16[128,4096]{1,0:T(8,128)(2,1)} %k_ref.1, bf16[128,4096]{1,0:T(8,128)(2,1)} %v_ref.1, ...), custom_call_target="tpu_custom_call" | custom-call | tf_op jit(solution)/shard_map/first_pack/pallas_call | solution.py:145
  5.9 3.1 %collective-permute-start.4 = (bf16[800,384]{1,0:T(8,128)(2,1)}, bf16[800,384]{1,0:T(8,128)(2,1)S(1)}, u32[]{:S(2)}, u32[]{:S(2)}) collective-permute-start(bf16[800,384]{1,0:T(8,128)(2,1)} %get-tuple-element.78), channel_id=1, source_target_pairs={{0,2},{1,3},{2,0},{3,1},{4,6},{5,7},{6,4},{7,5},{8,10},{9,11},{10,... | collective-permute-start | bytes 1843208 | tf_op jit(solution)/shard_map/ppermute | solution.py:37
  9.0 2.6 %collective-permute-start.5 = (bf16[800,384]{1,0:T(8,128)(2,1)}, bf16[800,384]{1,0:T(8,128)(2,1)S(1)}, u32[]{:S(2)}, u32[]{:S(2)}) collective-permute-start(bf16[800,384]{1,0:T(8,128)(2,1)} %get-tuple-element.79), channel_id=1, source_target_pairs={{0,4},{1,5},{2,6},{3,7},{4,0},{5,1},{6,2},{7,3},{8,12},{9,13},{10,... | collective-permute-start | bytes 1843208 | tf_op jit(solution)/shard_map/ppermute | solution.py:37
  11.6 0.0 collective-permute-start.6
  11.6 0.0 copy-start.4
  11.6 1.2 copy-done.4
  12.8 1.1 copy-done.5
  13.9 0.5 pack.1
  14.4 0.1 collective-permute-start.7
  14.4 1.7 %collective-permute-done.7.got_ref = bf16[1536,128]{1,0:T(8,128)(2,1)S(1)} collective-permute-done((bf16[1536,128]{1,0:T(8,128)(2,1)S(1)}, bf16[1536,128]{1,0:T(8,128)(2,1)S(1)}, u32[]{:S(2)}, u32[]{:S(2)}) %collective-permute-start.7) | collective-permute-done | bytes 393248 | tf_op jit(solution)/shard_map/ppermute | solution.py:37
  16.2 19.2 %collective-permute-done.4.refs_1_.rest_1_ = bf16[800,384]{1,0:T(8,128)(2,1)S(1)} collective-permute-done((bf16[800,384]{1,0:T(8,128)(2,1)}, bf16[800,384]{1,0:T(8,128)(2,1)S(1)}, u32[]{:S(2)}, u32[]{:S(2)}) %collective-permute-start.4) | collective-permute-done | bytes 614432 | tf_op jit(solution)/shard_map/ppermute | solution.py:37
  35.4 17.8 %collective-permute-done.5.refs_2_.rest_2_ = bf16[800,384]{1,0:T(8,128)(2,1)S(1)} collective-permute-done((bf16[800,384]{1,0:T(8,128)(2,1)}, bf16[800,384]{1,0:T(8,128)(2,1)S(1)}, u32[]{:S(2)}, u32[]{:S(2)}) %collective-permute-start.5) | collective-permute-done | bytes 614432 | tf_op jit(solution)/shard_map/ppermute | solution.py:37
  53.2 0.0 collective-permute-done.6.refs_3_.rest_3_
  53.2 0.1 forward.1
  53.3 0.7 copy-done.7
  54.0 0.2 copy-done.9
  54.3 13.2 %collective-permute-start.10 = (bf16[768,128]{1,0:T(8,128)(2,1)}, bf16[768,128]{1,0:T(8,128)(2,1)S(1)}, u32[]{:S(2)}, u32[]{:S(2)}) collective-permute-start(bf16[768,128]{1,0:T(8,128)(2,1)} %copy-done.12), channel_id=1, source_target_pairs={{0,4},{1,5},{2,6},{3,7},{4,0},{5,1},{6,2},{7,3},{8,12},{9,13},{10,... | collective-permute-start | bytes 589832 | tf_op jit(solution)/shard_map/ppermute | solution.py:37
  67.5 1.3 %collective-permute-start.11 = (bf16[768,128]{1,0:T(8,128)(2,1)}, bf16[768,128]{1,0:T(8,128)(2,1)S(1)}, u32[]{:S(2)}, u32[]{:S(2)}) collective-permute-start(bf16[768,128]{1,0:T(8,128)(2,1)} %copy-done.13), channel_id=1, source_target_pairs={{0,6},{1,7},{2,4},{3,5},{4,2},{5,3},{6,0},{7,1},{8,14},{9,15},{10,... | collective-permute-start | bytes 589832 | tf_op jit(solution)/shard_map/ppermute | solution.py:37
  68.8 0.0 collective-permute-start.9
  68.8 1.1 copy-done.8
  69.9 1.1 copy-done.10
  71.0 11.6 %attention.2 = (bf16[256,384]{1,0:T(8,128)(2,1)S(1)}, bf16[256,384]{1,0:T(8,128)(2,1)S(1)}, bf16[256,384]{1,0:T(8,128)(2,1)}, bf16[256,384]{1,0:T(8,128)(2,1)}, ...) custom-call(s32[1]{0:T(128)} %bitcast.me_ref, bf16[800,384]{1,0:T(8,128)(2,1)S(1)} %copy-done.6, ...), custom_call_target="tpu_custom_call" | custom-call | flops 12000000000 | bytes 3145728 | tf_op jit(solution)/shard_map/attention/pallas_call | solution.py:461
  82.6 0.0 collective-permute-done.10.refs_3_.rest_2_
  82.6 0.5 collective-permute-done.9.refs_2_.rest_1_
  83.0 3.3 %collective-permute-start.12 = (bf16[256,384]{1,0:T(8,128)(2,1)}, bf16[256,384]{1,0:T(8,128)(2,1)S(1)}, u32[]{:S(2)}, u32[]{:S(2)}) collective-permute-start(bf16[256,384]{1,0:T(8,128)(2,1)} %get-tuple-element.93), channel_id=1, source_target_pairs={{0,4},{1,5},{2,6},{3,7},{4,0},{5,1},{6,2},{7,3},{8,12},{9,13},{10,... | collective-permute-start | bytes 589832 | tf_op jit(solution)/shard_map/ppermute | solution.py:37
  86.4 2.5 %collective-permute-start.13 = (bf16[256,384]{1,0:T(8,128)(2,1)}, bf16[256,384]{1,0:T(8,128)(2,1)S(1)}, u32[]{:S(2)}, u32[]{:S(2)}) collective-permute-start(bf16[256,384]{1,0:T(8,128)(2,1)} %get-tuple-element.94), channel_id=1, source_target_pairs={{0,6},{1,7},{2,4},{3,5},{4,2},{5,3},{6,0},{7,1},{8,14},{9,15},{10,... | collective-permute-start | bytes 589832 | tf_op jit(solution)/shard_map/ppermute | solution.py:37
  88.9 3.7 %attention.3 = (bf16[128,128]{1,0:T(8,128)(2,1)S(1)}, bf16[128,128]{1,0:T(8,128)(2,1)S(1)}, bf16[128,128]{1,0:T(8,128)(2,1)S(1)}, bf16[128,128]{1,0:T(8,128)(2,1...) custom-call(s32[1]{0:T(128)} %bitcast.me_ref, ...), custom_call_target="tpu_custom_call" | custom-call | flops 4000000000 | bytes 1048576 | tf_op jit(solution)/shard_map/attention/pallas_call | solution.py:461
  92.6 13.0 %conditional.1 = (f32[64,128]{1,0:T(8,128)S(1)}, bf16[832,128]{1,0:T(8,128)(2,1)}, bf16[64,128]{1,0:T(8,128)(2,1)}, bf16[64,128]{1,0:T(8,128)(2,1)}, bf16[256,12...) conditional(s32[]{:T(128)} %convert_element_type.3, () %tuple.16, ...), branch_computations={%region_0.0_spmd, %region_1.0_spmd} | conditional | bytes 2818272 | solution.py:633
  92.6 0.0 collective-permute-start
  92.6 1.4 %collective-permute-done.got_ref = bf16[768,128]{1,0:T(8,128)(2,1)S(1)} collective-permute-done((bf16[768,128]{1,0:T(8,128)(2,1)S(1)}, bf16[768,128]{1,0:T(8,128)(2,1)S(1)}, u32[]{:S(2)}, u32[]{:S(2)}) %collective-permute-start) | collective-permute-done | bytes 196640 | tf_op jit(solution)/shard_map/cond/branch_1_fun/ppermute | solution.py:37
  94.0 0.1 riding_sum.1
  94.1 0.1 collective-permute-start.1
  94.2 1.9 %collective-permute-start.2 = (bf16[64,128]{1,0:T(8,128)(2,1)S(1)}, bf16[64,128]{1,0:T(8,128)(2,1)}, u32[]{:S(2)}, u32[]{:S(2)}) collective-permute-start(bf16[64,128]{1,0:T(8,128)(2,1)S(1)} %get-tuple-element.23), channel_id=1, source_target_pairs={{0,4},{1,5},{2,6},{3,7},{4,0},{5,1},{6,2},{7,3},{8,12},{9,13},{10,... | collective-permute-start | bytes 49160 | tf_op jit(solution)/shard_map/cond/branch_1_fun/ppermute | solution.py:37
  96.1 2.5 %collective-permute-start.3 = (bf16[64,128]{1,0:T(8,128)(2,1)S(1)}, bf16[64,128]{1,0:T(8,128)(2,1)}, u32[]{:S(2)}, u32[]{:S(2)}) collective-permute-start(bf16[64,128]{1,0:T(8,128)(2,1)S(1)} %get-tuple-element.24), channel_id=1, source_target_pairs={{0,6},{1,7},{2,4},{3,5},{4,2},{5,3},{6,0},{7,1},{8,14},{9,15},{10,... | collective-permute-start | bytes 49160 | tf_op jit(solution)/shard_map/cond/branch_1_fun/ppermute | solution.py:37
  98.6 7.0 %collective-permute-done.2 = bf16[64,128]{1,0:T(8,128)(2,1)} collective-permute-done((bf16[64,128]{1,0:T(8,128)(2,1)S(1)}, bf16[64,128]{1,0:T(8,128)(2,1)}, u32[]{:S(2)}, u32[]{:S(2)}) %collective-permute-start.2) | collective-permute-done | bytes 16416 | tf_op jit(solution)/shard_map/cond/branch_1_fun/ppermute | solution.py:37
  105.6 1.1 down_terms.1
  106.7 0.1 collective-permute-start.15
  106.8 1.0 forward_rows.1
  107.8 0.5 collective-permute-start.14
  108.4 0.1 pair_sum.1
  108.5 0.8 collective-permute-start.16
  109.3 2.3 %collective-permute-start.17 = (bf16[128,512]{1,0:T(8,128)(2,1)S(1)}, bf16[128,512]{1,0:T(8,128)(2,1)S(1)}, u32[]{:S(2)}, u32[]{:S(2)}) collective-permute-start(bf16[128,512]{1,0:T(8,128)(2,1)S(1)} %get-tuple-element.116), channel_id=1, source_target_pairs={{0,4},{1,5},{2,6},{3,7},{4,0},{5,1},{6,2},{7,3},{8,12},{9,13},{10,... | collective-permute-start | bytes 393224 | tf_op jit(solution)/shard_map/ppermute | solution.py:37
  111.6 1.3 %collective-permute-start.18 = (bf16[128,512]{1,0:T(8,128)(2,1)S(1)}, bf16[128,512]{1,0:T(8,128)(2,1)S(1)}, u32[]{:S(2)}, u32[]{:S(2)}) collective-permute-start(bf16[128,512]{1,0:T(8,128)(2,1)S(1)} %get-tuple-element.117), channel_id=1, source_target_pairs={{0,6},{1,7},{2,4},{3,5},{4,2},{5,3},{6,0},{7,1},{8,14},{9,15},{10,... | collective-permute-start | bytes 393224 | tf_op jit(solution)/shard_map/ppermute | solution.py:37
  112.9 1.9 %assemble.1.rest_0_ = bf16[128,4096]{1,0:T(8,128)(2,1)} custom-call(s32[1]{0:T(128)} %bitcast.me_ref, bf16[256,384]{1,0:T(8,128)(2,1)S(1)} %get-tuple-element.87.refs_0_.rest_0_, bf16[256,384]{1,0:T(8,128)(2,1)S(1)} %collective-permute-done.12.refs_1_.rest_1_, bf16[256,384]{1,0:T(8,128)(2,1)S(1)} %collective-permute-done.13.refs_2_.rest_2_, ...), custom_call_target="tpu_custom_call" | custom-call | bytes 1048576 | tf_op jit(solution)/shard_map/assemble/pallas_call | solution.py:270
  114.9 1.4 %collective-permute-done.16.rest_2_ = bf16[128,512]{1,0:T(8,128)(2,1)S(1)} collective-permute-done((bf16[128,512]{1,0:T(8,128)(2,1)S(1)}, bf16[128,512]{1,0:T(8,128)(2,1)S(1)}, u32[]{:S(2)}, u32[]{:S(2)}) %collective-permute-start.16) | collective-permute-done | bytes 131104 | tf_op jit(solution)/shard_map/ppermute | solution.py:37
  116.2 5.9 %collective-permute-done.17.rest_3_ = bf16[128,512]{1,0:T(8,128)(2,1)S(1)} collective-permute-done((bf16[128,512]{1,0:T(8,128)(2,1)S(1)}, bf16[128,512]{1,0:T(8,128)(2,1)S(1)}, u32[]{:S(2)}, u32[]{:S(2)}) %collective-permute-start.17) | collective-permute-done | bytes 131104 | tf_op jit(solution)/shard_map/ppermute | solution.py:37
  122.2 1.5 %finish.1 = (bf16[128,4096]{1,0:T(8,128)(2,1)}, f32[64,512]{1,0:T(8,128)}) custom-call(s32[1]{0:T(128)} %bitcast.me_ref, bf16[128,4096]{1,0:T(8,128)(2,1)} %assemble.1.rest_0_, bf16[256,128]{1,0:T(8,128)(2,1)S(1)} %get-tuple-element.106.rest_1_, bf16[128,512]{1,0:T(8,128)(2,1)S(1)} %collective-permute-done.16.rest_2_, ...), custom_call_target="tpu_custom_call", output_to_operand_aliasing={{0}: (1, {})} | custom-call | bytes 1048576 | tf_op jit(solution)/shard_map/finish/pallas_call | solution.py:284
  (33 shorter events, 0.1 us)
Async XLA Ops:
  0.6 53.6 %copy-start = (bf16[4096,64]{0,1:T(8,128)(2,1)S(1)}, bf16[4096,64]{0,1:T(8,128)(2,1)}, u32[]{:S(2)}) copy-start(bf16[4096,64]{0,1:T(8,128)(2,1)} %param.14) | copy-start | bytes 1572868
  0.7 10.9 %copy-start.2 = (bf16[128,4096]{1,0:T(8,128)(2,1)S(1)}, bf16[128,4096]{1,0:T(8,128)(2,1)}, u32[]{:S(2)}) copy-start(bf16[128,4096]{1,0:T(8,128)(2,1)} %q_ref.1) | copy-start | bytes 3145732
  0.7 10.9 %copy-start.3 = (bf16[128,4096]{1,0:T(8,128)(2,1)S(1)}, bf16[128,4096]{1,0:T(8,128)(2,1)}, u32[]{:S(2)}) copy-start(bf16[128,4096]{1,0:T(8,128)(2,1)} %k_ref.1) | copy-start | bytes 3145732
  5.9 29.6 %collective-permute-start.4 = (bf16[800,384]{1,0:T(8,128)(2,1)}, bf16[800,384]{1,0:T(8,128)(2,1)S(1)}, u32[]{:S(2)}, u32[]{:S(2)}) collective-permute-start(bf16[800,384]{1,0:T(8,128)(2,1)} %get-tuple-element.78), channel_id=1, source_target_pairs={{0,2},{1,3},{2,0},{3,1},{4,6},{5,7},{6,4},{7,5},{8,10},{9,11},{10,... | collective-permute-start | bytes 1843208 | tf_op jit(solution)/shard_map/ppermute | solution.py:37
  9.0 44.2 %collective-permute-start.5 = (bf16[800,384]{1,0:T(8,128)(2,1)}, bf16[800,384]{1,0:T(8,128)(2,1)S(1)}, u32[]{:S(2)}, u32[]{:S(2)}) collective-permute-start(bf16[800,384]{1,0:T(8,128)(2,1)} %get-tuple-element.79), channel_id=1, source_target_pairs={{0,4},{1,5},{2,6},{3,7},{4,0},{5,1},{6,2},{7,3},{8,12},{9,13},{10,... | collective-permute-start | bytes 1843208 | tf_op jit(solution)/shard_map/ppermute | solution.py:37
  11.6 41.6 %collective-permute-start.6 = (bf16[800,384]{1,0:T(8,128)(2,1)}, bf16[800,384]{1,0:T(8,128)(2,1)S(1)}, u32[]{:S(2)}, u32[]{:S(2)}) collective-permute-start(bf16[800,384]{1,0:T(8,128)(2,1)} %get-tuple-element.80), channel_id=1, source_target_pairs={{0,6},{1,7},{2,4},{3,5},{4,2},{5,3},{6,0},{7,1},{8,14},{9,15},{10,... | collective-permute-start | bytes 1843208 | tf_op jit(solution)/shard_map/ppermute | solution.py:37
  11.6 1.2 copy-start.4
  12.8 1.1 copy-start.5
  14.4 1.8 %collective-permute-start.7 = (bf16[1536,128]{1,0:T(8,128)(2,1)S(1)}, bf16[1536,128]{1,0:T(8,128)(2,1)S(1)}, u32[]{:S(2)}, u32[]{:S(2)}) collective-permute-start(bf16[1536,128]{1,0:T(8,128)(2,1)S(1)} %get-tuple-element.81), channel_id=1, source_target_pairs={{0,1},{1,0},{2,3},{3,2},{4,5},{5,4},{6,7},{7,6},{8,9},{9,8},{10,11... | collective-permute-start | bytes 1179656 | tf_op jit(solution)/shard_map/ppermute | solution.py:37
  16.2 38.1 %copy-start.11 = (bf16[768,128]{1,0:T(8,128)(2,1)}, bf16[768,128]{1,0:T(8,128)(2,1)S(1)}, u32[]{:S(2)}) copy-start(bf16[768,128]{1,0:T(8,128)(2,1)S(1)} %get-tuple-element.90) | copy-start | bytes 589828
  16.2 38.1 %copy-start.12 = (bf16[768,128]{1,0:T(8,128)(2,1)}, bf16[768,128]{1,0:T(8,128)(2,1)S(1)}, u32[]{:S(2)}) copy-start(bf16[768,128]{1,0:T(8,128)(2,1)S(1)} %get-tuple-element.91) | copy-start | bytes 589828
  16.2 38.0 %copy-start.13 = (bf16[768,128]{1,0:T(8,128)(2,1)}, bf16[768,128]{1,0:T(8,128)(2,1)S(1)}, u32[]{:S(2)}) copy-start(bf16[768,128]{1,0:T(8,128)(2,1)S(1)} %get-tuple-element.92) | copy-start | bytes 589828
  53.2 0.8 copy-start.7
  53.2 1.0 copy-start.9
  53.2 15.6 %copy-start.6 = (bf16[800,384]{1,0:T(8,128)(2,1)S(1)}, bf16[800,384]{1,0:T(8,128)(2,1)}, u32[]{:S(2)}) copy-start(bf16[800,384]{1,0:T(8,128)(2,1)} %get-tuple-element.77._.refs_0_.rest_0_) | copy-start | bytes 1843204
  54.2 14.6 %collective-permute-start.8 = (bf16[1664,384]{1,0:T(8,128)(2,1)S(1)}, bf16[1664,384]{1,0:T(8,128)(2,1)}, u32[]{:S(2)}, u32[]{:S(2)}) collective-permute-start(bf16[1664,384]{1,0:T(8,128)(2,1)S(1)} %forward.1), channel_id=1, source_target_pairs={{0,1},{1,0},{2,3},{3,2},{4,5},{5,4},{6,7},{7,6},{8,9},{9,8},{10,11... | collective-permute-start | bytes 3833864 | tf_op jit(solution)/shard_map/ppermute | solution.py:37
  54.3 28.3 %collective-permute-start.10 = (bf16[768,128]{1,0:T(8,128)(2,1)}, bf16[768,128]{1,0:T(8,128)(2,1)S(1)}, u32[]{:S(2)}, u32[]{:S(2)}) collective-permute-start(bf16[768,128]{1,0:T(8,128)(2,1)} %copy-done.12), channel_id=1, source_target_pairs={{0,4},{1,5},{2,6},{3,7},{4,0},{5,1},{6,2},{7,3},{8,12},{9,13},{10,... | collective-permute-start | bytes 589832 | tf_op jit(solution)/shard_map/ppermute | solution.py:37
  67.5 15.1 %collective-permute-start.11 = (bf16[768,128]{1,0:T(8,128)(2,1)}, bf16[768,128]{1,0:T(8,128)(2,1)S(1)}, u32[]{:S(2)}, u32[]{:S(2)}) collective-permute-start(bf16[768,128]{1,0:T(8,128)(2,1)} %copy-done.13), channel_id=1, source_target_pairs={{0,6},{1,7},{2,4},{3,5},{4,2},{5,3},{6,0},{7,1},{8,14},{9,15},{10,... | collective-permute-start | bytes 589832 | tf_op jit(solution)/shard_map/ppermute | solution.py:37
  68.8 14.2 %collective-permute-start.9 = (bf16[768,128]{1,0:T(8,128)(2,1)}, bf16[768,128]{1,0:T(8,128)(2,1)S(1)}, u32[]{:S(2)}, u32[]{:S(2)}) collective-permute-start(bf16[768,128]{1,0:T(8,128)(2,1)} %copy-done.11), channel_id=1, source_target_pairs={{0,2},{1,3},{2,0},{3,1},{4,6},{5,7},{6,4},{7,5},{8,10},{9,11},{10,... | collective-permute-start | bytes 589832 | tf_op jit(solution)/shard_map/ppermute | solution.py:37
  68.8 1.1 copy-start.8
  69.9 1.1 copy-start.10
  83.0 23.8 %collective-permute-start.12 = (bf16[256,384]{1,0:T(8,128)(2,1)}, bf16[256,384]{1,0:T(8,128)(2,1)S(1)}, u32[]{:S(2)}, u32[]{:S(2)}) collective-permute-start(bf16[256,384]{1,0:T(8,128)(2,1)} %get-tuple-element.93), channel_id=1, source_target_pairs={{0,4},{1,5},{2,6},{3,7},{4,0},{5,1},{6,2},{7,3},{8,12},{9,13},{10,... | collective-permute-start | bytes 589832 | tf_op jit(solution)/shard_map/ppermute | solution.py:37
  86.4 20.4 %collective-permute-start.13 = (bf16[256,384]{1,0:T(8,128)(2,1)}, bf16[256,384]{1,0:T(8,128)(2,1)S(1)}, u32[]{:S(2)}, u32[]{:S(2)}) collective-permute-start(bf16[256,384]{1,0:T(8,128)(2,1)} %get-tuple-element.94), channel_id=1, source_target_pairs={{0,6},{1,7},{2,4},{3,5},{4,2},{5,3},{6,0},{7,1},{8,14},{9,15},{10,... | collective-permute-start | bytes 589832 | tf_op jit(solution)/shard_map/ppermute | solution.py:37
  92.6 13.0 %copy-start.1 = (bf16[128,4096]{1,0:T(8,128)(2,1)S(1)}, bf16[128,4096]{1,0:T(8,128)(2,1)}, u32[]{:S(2)}) copy-start(bf16[128,4096]{1,0:T(8,128)(2,1)} %rest_3_.3) | copy-start | bytes 3145732
  92.6 1.4 %collective-permute-start = (bf16[768,128]{1,0:T(8,128)(2,1)S(1)}, bf16[768,128]{1,0:T(8,128)(2,1)S(1)}, u32[]{:S(2)}, u32[]{:S(2)}) collective-permute-start(bf16[768,128]{1,0:T(8,128)(2,1)S(1)} %get-tuple-element.15), channel_id=1, source_target_pairs={{0,1},{1,0},{2,3},{3,2},{4,5},{5,4},{6,7},{7,6},{8,9},{9,8},{10,11... | collective-permute-start | bytes 589832 | tf_op jit(solution)/shard_map/cond/branch_1_fun/ppermute | solution.py:37
  94.1 11.5 %collective-permute-start.1 = (bf16[832,128]{1,0:T(8,128)(2,1)S(1)}, bf16[832,128]{1,0:T(8,128)(2,1)}, u32[]{:S(2)}, u32[]{:S(2)}) collective-permute-start(bf16[832,128]{1,0:T(8,128)(2,1)S(1)} %get-tuple-element.22), channel_id=1, source_target_pairs={{0,2},{1,3},{2,0},{3,1},{4,6},{5,7},{6,4},{7,5},{8,10},{9,11},{10,... | collective-permute-start | bytes 638984 | tf_op jit(solution)/shard_map/cond/branch_1_fun/ppermute | solution.py:37
  94.2 11.4 %collective-permute-start.2 = (bf16[64,128]{1,0:T(8,128)(2,1)S(1)}, bf16[64,128]{1,0:T(8,128)(2,1)}, u32[]{:S(2)}, u32[]{:S(2)}) collective-permute-start(bf16[64,128]{1,0:T(8,128)(2,1)S(1)} %get-tuple-element.23), channel_id=1, source_target_pairs={{0,4},{1,5},{2,6},{3,7},{4,0},{5,1},{6,2},{7,3},{8,12},{9,13},{10,... | collective-permute-start | bytes 49160 | tf_op jit(solution)/shard_map/cond/branch_1_fun/ppermute | solution.py:37
  96.1 9.5 %collective-permute-start.3 = (bf16[64,128]{1,0:T(8,128)(2,1)S(1)}, bf16[64,128]{1,0:T(8,128)(2,1)}, u32[]{:S(2)}, u32[]{:S(2)}) collective-permute-start(bf16[64,128]{1,0:T(8,128)(2,1)S(1)} %get-tuple-element.24), channel_id=1, source_target_pairs={{0,6},{1,7},{2,4},{3,5},{4,2},{5,3},{6,0},{7,1},{8,14},{9,15},{10,... | collective-permute-start | bytes 49160 | tf_op jit(solution)/shard_map/cond/branch_1_fun/ppermute | solution.py:37
  106.7 1.6 %collective-permute-start.15 = (bf16[64,2048]{1,0:T(8,128)(2,1)S(1)}, bf16[64,2048]{1,0:T(8,128)(2,1)S(1)}, u32[]{:S(2)}, u32[]{:S(2)}) collective-permute-start(bf16[64,2048]{1,0:T(8,128)(2,1)S(1)} %get-tuple-element.111), channel_id=1, source_target_pairs={{0,1},{1,0},{2,3},{3,2},{4,5},{5,4},{6,7},{7,6},{8,9},{9,8},{10,11... | collective-permute-start | bytes 786440 | tf_op jit(solution)/shard_map/ppermute | solution.py:37
  107.8 5.1 %collective-permute-start.14 = (bf16[512,384]{1,0:T(8,128)(2,1)S(1)}, bf16[512,384]{1,0:T(8,128)(2,1)S(1)}, u32[]{:S(2)}, u32[]{:S(2)}) collective-permute-start(bf16[512,384]{1,0:T(8,128)(2,1)S(1)} %forward_rows.1), channel_id=1, source_target_pairs={{0,1},{1,0},{2,3},{3,2},{4,5},{5,4},{6,7},{7,6},{8,9},{9,8},{10,11... | collective-permute-start | bytes 1179656 | tf_op jit(solution)/shard_map/ppermute | solution.py:37
  108.5 7.8 %collective-permute-start.16 = (bf16[128,512]{1,0:T(8,128)(2,1)S(1)}, bf16[128,512]{1,0:T(8,128)(2,1)S(1)}, u32[]{:S(2)}, u32[]{:S(2)}) collective-permute-start(bf16[128,512]{1,0:T(8,128)(2,1)S(1)} %get-tuple-element.115), channel_id=1, source_target_pairs={{0,2},{1,3},{2,0},{3,1},{4,6},{5,7},{6,4},{7,5},{8,10},{9,11},{10,... | collective-permute-start | bytes 393224 | tf_op jit(solution)/shard_map/ppermute | solution.py:37
  109.3 12.9 %collective-permute-start.17 = (bf16[128,512]{1,0:T(8,128)(2,1)S(1)}, bf16[128,512]{1,0:T(8,128)(2,1)S(1)}, u32[]{:S(2)}, u32[]{:S(2)}) collective-permute-start(bf16[128,512]{1,0:T(8,128)(2,1)S(1)} %get-tuple-element.116), channel_id=1, source_target_pairs={{0,4},{1,5},{2,6},{3,7},{4,0},{5,1},{6,2},{7,3},{8,12},{9,13},{10,... | collective-permute-start | bytes 393224 | tf_op jit(solution)/shard_map/ppermute | solution.py:37
  111.6 10.6 %collective-permute-start.18 = (bf16[128,512]{1,0:T(8,128)(2,1)S(1)}, bf16[128,512]{1,0:T(8,128)(2,1)S(1)}, u32[]{:S(2)}, u32[]{:S(2)}) collective-permute-start(bf16[128,512]{1,0:T(8,128)(2,1)S(1)} %get-tuple-element.117), channel_id=1, source_target_pairs={{0,6},{1,7},{2,4},{3,5},{4,2},{5,3},{6,0},{7,1},{8,14},{9,15},{10,... | collective-permute-start | bytes 393224 | tf_op jit(solution)/shard_map/ppermute | solution.py:37
